TPU v7x, 32 devices: a whole 2x2x4 slice. The times are simulated.
32 devices in a mesh: fsdp: 16 (over z, y, core), seq: 2 (over x).
Axes of the slice: x: 2, y: 2, z: 4, core: 2. Of those that a mesh axis runs over, the one named last changes fastest.
Arguments:
- tokens: bfloat16 [16, 1376, 1024], P('fsdp', 'seq'), may hold values from -6 to 6
- lengths: int32 [16], P('fsdp'), may hold values from 1032 to 1376
- norm1_gain: bfloat16 [1024], P('fsdp'), may hold values from 0.5 to 1.5
- norm1_bias: bfloat16 [1024], P('fsdp'), may hold values from -1.5 to 1.5
- packed_weight: bfloat16 [1024, 3072], P('fsdp'), may hold values from -0.1875 to 0.1875
- query_bias: bfloat16 [1024], P('fsdp'), may hold values from -1.5 to 1.5
- value_bias: bfloat16 [1024], P('fsdp'), may hold values from -1.5 to 1.5
- output_weight: bfloat16 [1024, 1024], P('fsdp'), may hold values from -2.5 to 2.5
- output_bias: bfloat16 [1024], P('fsdp'), may hold values from -1.5 to 1.5
- layer_scale1: bfloat16 [1024], P('fsdp'), may hold values from 0.5 to 1.5
- norm2_gain: bfloat16 [1024], P('fsdp'), may hold values from 0.5 to 1.5
- norm2_bias: bfloat16 [1024], P('fsdp'), may hold values from -1.5 to 1.5
- up_weight: bfloat16 [1024, 4096], P('fsdp'), may hold values from -0.1875 to 0.1875
- up_bias: bfloat16 [4096], P('fsdp'), may hold values from -1.5 to 1.5
- down_weight: bfloat16 [4096, 1024], P('fsdp'), may hold values from -0.125 to 0.125
- down_bias: bfloat16 [1024], P('fsdp'), may hold values from -1.5 to 1.5
- layer_scale2: bfloat16 [1024], P('fsdp'), may hold values from 0.5 to 1.5
- cotangent: bfloat16 [16, 1376, 1024], P('fsdp', 'seq'), may hold values from -6 to 6
Outputs:
- output: bfloat16 [16, 1376, 1024], P('fsdp', 'seq')
- grad_tokens: float32 [16, 1376, 1024], P('fsdp', 'seq')
- grad_norm1_gain: float32 [1024], P('fsdp')
- grad_norm1_bias: float32 [1024], P('fsdp')
- grad_packed_weight: float32 [1024, 3072], P('fsdp')
- grad_query_bias: float32 [1024], P('fsdp')
- grad_value_bias: float32 [1024], P('fsdp')
- grad_output_weight: float32 [1024, 1024], P('fsdp')
- grad_output_bias: float32 [1024], P('fsdp')
- grad_layer_scale1: float32 [1024], P('fsdp')
- grad_norm2_gain: float32 [1024], P('fsdp')
- grad_norm2_bias: float32 [1024], P('fsdp')
- grad_up_weight: float32 [1024, 4096], P('fsdp')
- grad_up_bias: float32 [4096], P('fsdp')
- grad_down_weight: float32 [4096, 1024], P('fsdp')
- grad_down_bias: float32 [1024], P('fsdp')
- grad_layer_scale2: float32 [1024], P('fsdp')
Inputs may be any that keep to these rules, and one draw needn't show every extreme that they name: Positions from lengths[b] on of image b are padding.
All inputs are finite; a program needn't handle non-finite values.
Results may differ from a plain program's by a relative error of at most 0.02.
Values may be sent and summed in bfloat16 or wider, within the bound.
No kernel may reach another device: no remote copies, remote signals or barrier semaphores. Data moves between devices by JAX's collectives and lax.ppermute only.
A program may use at most 384 MiB of HBM per device.

v0:
```python
import jax
import jax.numpy as jnp
from jax import lax
from jax.sharding import PartitionSpec as P

H = 16
HD = 64


norm_eps = 1e-06


def layer_norm(values, norm_gain, norm_shift):
    center = values - jnp.mean(values, axis=-1, keepdims=True)
    spread = jnp.mean(center * center, axis=-1, keepdims=True)
    return center * lax.rsqrt(spread + norm_eps) * norm_gain + norm_shift


def gelu_exact(values):
    return jax.nn.gelu(values, approximate=False)


def matmul(left, right):
    return jnp.dot(left, right, preferred_element_type=jnp.float32)


def left_outer(left, right):
    return jnp.einsum("ti,tj->ij", left, right, preferred_element_type=jnp.float32)


def right_back(left, right):
    return jnp.einsum("tj,ij->ti", left, right, preferred_element_type=jnp.float32)


def column_sum(values):
    return jnp.sum(values.astype(jnp.float32), axis=0)


def attention_probs(queries, key_rows, valid_count, score_scale):
    scores = score_scale * jnp.einsum(
        "qhd,khd->hqk", queries, key_rows, preferred_element_type=jnp.float32
    )
    key_valid = jnp.arange(key_rows.shape[0]) < valid_count
    scores = jnp.where(key_valid[None, None, :], scores, -jnp.inf)
    return scores


def attend(queries, key_rows, values, valid_count, score_scale):
    scores = attention_probs(queries, key_rows, valid_count, score_scale)
    largest = jnp.max(scores, axis=-1, keepdims=True)
    log_total = largest[..., 0] + jnp.log(jnp.sum(jnp.exp(scores - largest), axis=-1))
    attention = jnp.exp(scores - log_total[..., None]).astype(jnp.bfloat16)
    mixture = jnp.einsum("hqk,khd->qhd", attention, values, preferred_element_type=jnp.float32)
    return (mixture.astype(jnp.bfloat16), log_total)


def attend_back(queries, key_rows, values, valid_count, score_scale, log_total, grad_mixture):
    scores = attention_probs(queries, key_rows, valid_count, score_scale)
    probs = jnp.exp(scores - log_total[..., None])
    grad_values = jnp.einsum(
        "hqk,qhd->khd", probs.astype(jnp.bfloat16), grad_mixture, preferred_element_type=jnp.float32
    )
    grad_probs = jnp.einsum(
        "qhd,khd->hqk", grad_mixture, values, preferred_element_type=jnp.float32
    )
    inner_sum = jnp.sum(probs * grad_probs, axis=-1, keepdims=True)
    grad_scores = (probs * (grad_probs - inner_sum)).astype(jnp.bfloat16)
    grad_queries = score_scale * jnp.einsum(
        "hqk,khd->qhd", grad_scores, key_rows, preferred_element_type=jnp.float32
    )
    grad_keys = score_scale * jnp.einsum(
        "hqk,qhd->khd", grad_scores, queries, preferred_element_type=jnp.float32
    )
    return (grad_queries, grad_keys, grad_values)


def body(
    tokens,
    lengths,
    norm1_gain,
    norm1_bias,
    packed_weight,
    query_bias,
    value_bias,
    output_weight,
    output_bias,
    layer_scale1,
    norm2_gain,
    norm2_bias,
    up_weight,
    up_bias,
    down_weight,
    down_bias,
    layer_scale2,
    cotangent,
):
    gathered = (
        lax.all_gather(norm1_gain, "fsdp", axis=0, tiled=True),
        lax.all_gather(norm1_bias, "fsdp", axis=0, tiled=True),
        lax.all_gather(packed_weight, "fsdp", axis=0, tiled=True),
        lax.all_gather(query_bias, "fsdp", axis=0, tiled=True),
        lax.all_gather(value_bias, "fsdp", axis=0, tiled=True),
        lax.all_gather(output_weight, "fsdp", axis=0, tiled=True),
        lax.all_gather(output_bias, "fsdp", axis=0, tiled=True),
        lax.all_gather(layer_scale1, "fsdp", axis=0, tiled=True),
        lax.all_gather(norm2_gain, "fsdp", axis=0, tiled=True),
        lax.all_gather(norm2_bias, "fsdp", axis=0, tiled=True),
        lax.all_gather(up_weight, "fsdp", axis=0, tiled=True),
        lax.all_gather(up_bias, "fsdp", axis=0, tiled=True),
        lax.all_gather(down_weight, "fsdp", axis=0, tiled=True),
        lax.all_gather(down_bias, "fsdp", axis=0, tiled=True),
        lax.all_gather(layer_scale2, "fsdp", axis=0, tiled=True),
    )
    (
        gain_one,
        shift_one,
        packed_full,
        query_shift,
        value_shift,
        output_full,
        output_shift,
        scale_one,
        gain_two,
        shift_two,
        up_full,
        up_shift,
        down_full,
        down_shift,
        scale_two,
    ) = gathered
    gain_one = gain_one.astype(jnp.float32)
    shift_one = shift_one.astype(jnp.float32)
    query_shift = query_shift.astype(jnp.float32)
    value_shift = value_shift.astype(jnp.float32)
    output_shift = output_shift.astype(jnp.float32)
    scale_one = scale_one.astype(jnp.float32)
    gain_two = gain_two.astype(jnp.float32)
    shift_two = shift_two.astype(jnp.float32)
    up_shift = up_shift.astype(jnp.float32)
    down_shift = down_shift.astype(jnp.float32)
    scale_two = scale_two.astype(jnp.float32)
    groups = lax.axis_size("seq")
    images, local_len, model_width = tokens.shape
    seq_len = local_len * groups
    per_group = H // groups
    score_scale = HD ** (-0.5)
    token_rows = tokens.astype(jnp.float32).reshape(images * local_len, model_width)
    normed = layer_norm(token_rows, gain_one, shift_one).astype(jnp.bfloat16)
    packed_shift = jnp.concatenate([query_shift, jnp.zeros_like(query_shift), value_shift])
    packed = (matmul(normed, packed_full) + packed_shift).astype(jnp.bfloat16)
    packed = packed.reshape(images, local_len, 3, groups, per_group * HD)
    spread = lax.all_to_all(packed, "seq", split_axis=3, concat_axis=1, tiled=True)
    spread = spread.reshape(images, seq_len, 3, per_group, HD)

    def forward_image(per_image):
        image_block, valid_count = per_image
        return attend(
            image_block[:, 0], image_block[:, 1], image_block[:, 2], valid_count, score_scale
        )

    mixture, log_total = lax.map(forward_image, (spread, lengths))
    mixture = mixture.reshape(images, seq_len, 1, per_group * HD)
    mixture_rows = lax.all_to_all(mixture, "seq", split_axis=1, concat_axis=2, tiled=True).reshape(
        images * local_len, model_width
    )
    branch_one = matmul(mixture_rows, output_full) + output_shift
    middle = token_rows + scale_one * branch_one
    normed_two = layer_norm(middle, gain_two, shift_two).astype(jnp.bfloat16)
    hidden = matmul(normed_two, up_full) + up_shift
    active = gelu_exact(hidden).astype(jnp.bfloat16)
    branch_two = matmul(active, down_full) + down_shift
    output = (middle + scale_two * branch_two).astype(jnp.bfloat16).reshape(tokens.shape)
    upstream = cotangent.astype(jnp.float32).reshape(images * local_len, model_width)
    grad_scale_two = jnp.sum(upstream * branch_two, axis=0)
    delta_two = (scale_two * upstream).astype(jnp.bfloat16)
    grad_down_shift = column_sum(delta_two)
    grad_down = left_outer(active, delta_two)
    grad_active = right_back(delta_two, down_full)
    _, gelu_pull = jax.vjp(gelu_exact, hidden)
    delta_hidden = gelu_pull(grad_active)[0].astype(jnp.bfloat16)
    grad_up_shift = column_sum(delta_hidden)
    grad_up = left_outer(normed_two, delta_hidden)
    delta_normed_two = right_back(delta_hidden, up_full)
    _, norm_pull_two = jax.vjp(layer_norm, middle, gain_two, shift_two)
    grad_middle_norm, grad_gain_two, grad_shift_two = norm_pull_two(delta_normed_two)
    delta_middle = upstream + grad_middle_norm
    grad_scale_one = jnp.sum(delta_middle * branch_one, axis=0)
    delta_one = (scale_one * delta_middle).astype(jnp.bfloat16)
    grad_output_shift = column_sum(delta_one)
    grad_output = left_outer(mixture_rows, delta_one)
    delta_mixture = right_back(delta_one, output_full).astype(jnp.bfloat16)
    delta_mixture = delta_mixture.reshape(images, local_len, groups, per_group * HD)
    grad_spread = lax.all_to_all(delta_mixture, "seq", split_axis=2, concat_axis=1, tiled=True)
    grad_spread = grad_spread.reshape(images, seq_len, per_group, HD)

    def backward_image(per_image):
        image_block, valid_count, image_total, image_grad = per_image
        grad_queries, grad_keys, grad_values = attend_back(
            image_block[:, 0],
            image_block[:, 1],
            image_block[:, 2],
            valid_count,
            score_scale,
            image_total,
            image_grad,
        )
        return jnp.stack([grad_queries, grad_keys, grad_values], axis=1).astype(jnp.bfloat16)

    delta_packed = lax.map(backward_image, (spread, lengths, log_total, grad_spread))
    delta_packed = delta_packed.reshape(images, seq_len, 3, 1, per_group * HD)
    delta_back = lax.all_to_all(delta_packed, "seq", split_axis=1, concat_axis=3, tiled=True)
    delta_back = delta_back.reshape(images * local_len, 3 * model_width)
    grad_query_shift = column_sum(delta_back[:, :model_width])
    grad_value_shift = column_sum(delta_back[:, 2 * model_width :])
    grad_packed = left_outer(normed, delta_back)
    delta_normed = right_back(delta_back, packed_full)
    _, norm_pull_one = jax.vjp(layer_norm, token_rows, gain_one, shift_one)
    grad_rows_norm, grad_gain_one, grad_shift_one = norm_pull_one(delta_normed)
    grad_tokens = (delta_middle + grad_rows_norm).reshape(tokens.shape)
    local_grads = (
        grad_gain_one,
        grad_shift_one,
        grad_packed,
        grad_query_shift,
        grad_value_shift,
        grad_output,
        grad_output_shift,
        grad_scale_one,
        grad_gain_two,
        grad_shift_two,
        grad_up,
        grad_up_shift,
        grad_down,
        grad_down_shift,
        grad_scale_two,
    )
    owned_grads = (
        lax.psum_scatter(
            local_grads[0].astype(jnp.bfloat16), "fsdp", scatter_dimension=0, tiled=True
        ).astype(jnp.float32),
        lax.psum_scatter(
            local_grads[1].astype(jnp.bfloat16), "fsdp", scatter_dimension=0, tiled=True
        ).astype(jnp.float32),
        lax.psum_scatter(
            local_grads[2].astype(jnp.bfloat16), "fsdp", scatter_dimension=0, tiled=True
        ).astype(jnp.float32),
        lax.psum_scatter(
            local_grads[3].astype(jnp.bfloat16), "fsdp", scatter_dimension=0, tiled=True
        ).astype(jnp.float32),
        lax.psum_scatter(
            local_grads[4].astype(jnp.bfloat16), "fsdp", scatter_dimension=0, tiled=True
        ).astype(jnp.float32),
        lax.psum_scatter(
            local_grads[5].astype(jnp.bfloat16), "fsdp", scatter_dimension=0, tiled=True
        ).astype(jnp.float32),
        lax.psum_scatter(
            local_grads[6].astype(jnp.bfloat16), "fsdp", scatter_dimension=0, tiled=True
        ).astype(jnp.float32),
        lax.psum_scatter(
            local_grads[7].astype(jnp.bfloat16), "fsdp", scatter_dimension=0, tiled=True
        ).astype(jnp.float32),
        lax.psum_scatter(
            local_grads[8].astype(jnp.bfloat16), "fsdp", scatter_dimension=0, tiled=True
        ).astype(jnp.float32),
        lax.psum_scatter(
            local_grads[9].astype(jnp.bfloat16), "fsdp", scatter_dimension=0, tiled=True
        ).astype(jnp.float32),
        lax.psum_scatter(
            local_grads[10].astype(jnp.bfloat16), "fsdp", scatter_dimension=0, tiled=True
        ).astype(jnp.float32),
        lax.psum_scatter(
            local_grads[11].astype(jnp.bfloat16), "fsdp", scatter_dimension=0, tiled=True
        ).astype(jnp.float32),
        lax.psum_scatter(
            local_grads[12].astype(jnp.bfloat16), "fsdp", scatter_dimension=0, tiled=True
        ).astype(jnp.float32),
        lax.psum_scatter(
            local_grads[13].astype(jnp.bfloat16), "fsdp", scatter_dimension=0, tiled=True
        ).astype(jnp.float32),
        lax.psum_scatter(
            local_grads[14].astype(jnp.bfloat16), "fsdp", scatter_dimension=0, tiled=True
        ).astype(jnp.float32),
    )
    owned_grads = (
        lax.psum(owned_grads[0].astype(jnp.bfloat16), "seq").astype(jnp.float32),
        lax.psum(owned_grads[1].astype(jnp.bfloat16), "seq").astype(jnp.float32),
        lax.psum(owned_grads[2].astype(jnp.bfloat16), "seq").astype(jnp.float32),
        lax.psum(owned_grads[3].astype(jnp.bfloat16), "seq").astype(jnp.float32),
        lax.psum(owned_grads[4].astype(jnp.bfloat16), "seq").astype(jnp.float32),
        lax.psum(owned_grads[5].astype(jnp.bfloat16), "seq").astype(jnp.float32),
        lax.psum(owned_grads[6].astype(jnp.bfloat16), "seq").astype(jnp.float32),
        lax.psum(owned_grads[7].astype(jnp.bfloat16), "seq").astype(jnp.float32),
        lax.psum(owned_grads[8].astype(jnp.bfloat16), "seq").astype(jnp.float32),
        lax.psum(owned_grads[9].astype(jnp.bfloat16), "seq").astype(jnp.float32),
        lax.psum(owned_grads[10].astype(jnp.bfloat16), "seq").astype(jnp.float32),
        lax.psum(owned_grads[11].astype(jnp.bfloat16), "seq").astype(jnp.float32),
        lax.psum(owned_grads[12].astype(jnp.bfloat16), "seq").astype(jnp.float32),
        lax.psum(owned_grads[13].astype(jnp.bfloat16), "seq").astype(jnp.float32),
        lax.psum(owned_grads[14].astype(jnp.bfloat16), "seq").astype(jnp.float32),
    )
    return (output, grad_tokens) + tuple(owned_grads)


def solution(mesh):
    in_specs = (
        P("fsdp", "seq", None),
        P("fsdp"),
        P("fsdp"),
        P("fsdp"),
        P("fsdp", None),
        P("fsdp"),
        P("fsdp"),
        P("fsdp", None),
        P("fsdp"),
        P("fsdp"),
        P("fsdp"),
        P("fsdp"),
        P("fsdp", None),
        P("fsdp"),
        P("fsdp", None),
        P("fsdp"),
        P("fsdp"),
        P("fsdp", "seq", None),
    )
    out_specs = (
        P("fsdp", "seq", None),
        P("fsdp", "seq", None),
        P("fsdp"),
        P("fsdp"),
        P("fsdp", None),
        P("fsdp"),
        P("fsdp"),
        P("fsdp", None),
        P("fsdp"),
        P("fsdp"),
        P("fsdp"),
        P("fsdp"),
        P("fsdp", None),
        P("fsdp"),
        P("fsdp", None),
        P("fsdp"),
        P("fsdp"),
    )
    return jax.shard_map(body, mesh=mesh, in_specs=in_specs, out_specs=out_specs, check_vma=False)
```

profile of v0, /device:TPU:0, one launch (start us, length us, event | category | flops | bytes accessed | tf_op | source)
XLA Modules:
  0.0 1099.7 jit_solution(2834281232047310727)
XLA Ops:
  9.4 1.3 fusion.68
  19.8 64.2 %all-reduce.22 = (bf16[1024]{0:T(1024)(128)(2,1)S(1)}, bf16[1024]{0:T(1024)(128)(2,1)S(1)}, bf16[1024]{0:T(1024)(128)(2,1)S(1)}, bf16[1024]{0:T(1024)(128)(2,1)S...) all-reduce(bf16[1024]{0:T(1024)(128)(2,1)S(1)} %dynamic-update-slic, ...), channel_id=1, replica_groups=mesh['fsdp'=16,'seq'=2] {'fsdp'}, use_global_device_ids=true, to_apply=%add.4 | all-reduce | flops 10240 | bytes 40960
  84.0 1.6 convert_reduce_fusion
  86.3 9.5 add_convert_fusion.1
  95.8 10.6 reshape.235
  106.4 5.1 copy.53
  111.4 5.6 all-to-all-start
  118.3 42.4 %all-to-all-done = bf16[1,688,3,2,512]{4,1,2,0,3:T(8,128)(2,1)} async-done(((bf16[1,688,3,2,512]{4,1,2,0,3:T(8,128)(2,1)}), bf16[1,688,3,2,512]{4,1,2,0,3:T(8,128)(2,1)}, u32[]{:S(2)}, u32[]{:S(2)}) %all-to-all-start) | async-done | bytes 4227104 | tf_op jit(solution)/shard_map/all_to_all | solution.py:152
  160.7 12.5 %copy.54 = bf16[1,2,688,3,1,512]{2,1,5,3,4,0:T(2,128)(2,1)} copy(bf16[1,2,688,3,1,512]{5,2,3,1,4,0:T(8,128)(2,1)} %bitcast.3) | data formatting | bytes 8454144 | tf_op jit(solution)/shard_map/all_to_all | solution.py:152
  173.2 10.5 squeeze.40
  183.7 25.9 %fusion.69 = (f32[8,1376]{1,0:T(8,128)S(1)}, f32[8,1376,1376]{1,2,0:T(8,128)}) fusion(bf16[1376,3,8,64]{0,3,2,1:T(8,128)(2,1)} %squeeze.40, pred[1376]{0:T(1024)(128)(4,1)S(1)} %iota_compare_fusion), kind=kOutput, calls=%fused_computation.112 | convolution fusion | flops 1984247040 | bytes 63517024 | tf_op jit(solution)/shard_map/while/body/eval_jaxpr/qhd,khd->hqk/dot_general | solution.py:40
  209.6 20.2 %exponential_reduce_fusion = f32[8,1376]{1,0:T(8,128)S(1)} fusion(f32[8,1376,1376]{1,2,0:T(8,128)} %get-tuple-element.111, f32[8,1376]{1,0:T(8,128)S(1)} %get-tuple-element.110), kind=kLoop, calls=%fused_computation.5 | loop fusion | flops 30283008 | bytes 60676096 | tf_op jit(solution)/shard_map/while/body/eval_jaxpr/reduce_sum | solution.py:51
  229.8 23.3 %fusion.20 = bf16[8,64,1376]{2,1,0:T(8,128)(2,1)S(1)} fusion(f32[8,1376,1376]{1,2,0:T(8,128)} %get-tuple-element.111, f32[8,1376]{1,0:T(8,128)S(1)} %log_add_fusion, bf16[1376,3,8,64]{0,3,2,1:T(8,128)(2,1)} %squeeze.40), kind=kOutput, calls=%fused_computation.49 | convolution fusion | flops 1969815552 | bytes 64891904 | tf_op jit(solution)/shard_map/while/body/eval_jaxpr/hqk,khd->qhd/dot_general | solution.py:53
  253.2 5.4 copy.56
  259.1 10.1 reduce.6
  269.2 14.1 %reshape.310 = bf16[2,2,176128]{2,1,0:T(2,128)(2,1)} reshape(bf16[1376,512]{1,0:T(8,128)(2,1)S(1)} %reduce.6) | data formatting | bytes 2818048
  283.3 3.6 all-to-all-start.1
  287.1 18.1 %all-gather = bf16[16,1,256]{2,1,0:T(2,128)(2,1)S(1)} all-gather(bf16[1,1,256]{2,1,0:T(2,128)(2,1)S(1)} %reshape.276), channel_id=1, replica_groups=mesh['fsdp'=16,'seq'=2] {'fsdp'}, dimensions={0}, use_global_device_ids=true | all-gather | bytes 8704 | tf_op jit(solution)/shard_map/all_gather | solution.py:109
  305.2 2.3 reshape.311
  307.5 2.2 copy.72
  309.7 1.5 copy.57
  311.6 5.4 fusion.66
  317.0 1.5 copy-done.2
  319.0 35.6 %multiply_convert_fusion.1 = (bf16[688,4096]{1,0:T(8,128)(2,1)}, f32[688,4096]{1,0:T(8,128)}, f32[688,4096]{1,0:T(8,128)}) fusion(f32[4096]{0:T(1024)S(1)} %bitcast.161, bf16[1024,4096]{1,0:T(8,128)(2,1)} %all-gather.10.cloned.1.call-done, f32[688,1024]{1,0:T(8,128)} %copy-done.2, f32[1024]{0:T(1024)S(1)} %convert_element_type.224, ...), kind=kOutput, calls=%fused_computation.10 | convolution fusion | flops 5960876032 | bytes 39417216 | tf_op jit(solution)/shard_map/dot_general | solution.py:24
  354.6 19.6 %fusion.70 = (bf16[4096]{0:T(1024)(128)(2,1)}, bf16[688,4096]{1,0:T(8,128)(2,1)}) fusion(f32[688,4096]{1,0:T(8,128)} %get-tuple-element.102, bf16[4096,1024]{1,0:T(8,128)(2,1)} %all-gather.12.cloned.1.call-done, bf16[1,688,1024]{2,1,0:T(8,128)(2,1)} %param.35, f32[1024]{0:T(1024)S(1)} %convert_element_type.222, f32[688,4096]{1,0:T(8,128)} %get-tuple-element.113, ...), kind=kOutput, calls=%fused_computation.113 | convolution fusion | flops 5818560512 | bytes 38006784 | tf_op jit(solution)/shard_map/tj,ij->ti/dot_general | solution.py:32
  374.2 11.7 %multiply_reduce_fusion.1 = (bf16[1024]{0:T(1024)(128)(2,1)}, f32[688]{0:T(1024)S(1)}, bf16[1024]{0:T(1024)(128)(2,1)}, f32[688,1024]{1,0:T(8,128)S(1)}) fusion(f32[688,1024]{1,0:T(8,128)S(1)} %copy-done.3, f32[688]{0:T(1024)S(1)} %fusion.59, f32[688]{0:T(1024)S(1)} %broadcast_multiply_fusion, f32[1024]{0:T(1024)S(1)} %convert_element_type.223, ...), kind=kOutput, calls=%fused_computation.64 | convolution fusion | flops 5776995840 | bytes 19677248 | tf_op jit(solution)/shard_map/tj,ij->ti/dot_general | solution.py:32
  386.8 1.5 copy-done.4
  388.3 1.3 fusion.63
  389.7 1.1 copy-done.10
  390.8 1.7 convolution_convert_fusion.4
  393.8 21.4 %all_to_all.60 = bf16[1,688,2,512]{3,1,0,2:T(8,128)(2,1)S(1)} all-to-all(bf16[1,688,2,512]{3,1,0,2:T(8,128)(2,1)S(1)} %copy.58), channel_id=1, replica_groups=mesh['fsdp'=16,'seq'=2] {'seq'}, dimensions={2} | all-to-all | bytes 2818048 | tf_op jit(solution)/shard_map/all_to_all | solution.py:193
  415.2 1.9 copy.59
  417.0 1.2 squeeze.45
  418.2 22.8 %fusion.23 = bf16[8,64,1376]{2,1,0:T(8,128)(2,1)} fusion(bf16[1376,8,64]{0,2,1:T(8,128)(2,1)S(1)} %squeeze.45, f32[8,1376,1376]{1,2,0:T(8,128)} %get-tuple-element.111, f32[8,1376]{1,0:T(8,128)S(1)} %log_add_fusion), kind=kOutput, calls=%fused_computation.50 | convolution fusion | flops 1969815552 | bytes 63450112 | tf_op jit(solution)/shard_map/while/body/eval_jaxpr/hqk,qhd->khd/dot_general | solution.py:60
  441.1 43.0 %multiply_reduce_fusion = (f32[8,1376]{1,0:T(8,128)S(1)}, f32[8,1376,1376]{1,2,0:T(8,128)}) fusion(f32[8,1376,1376]{1,2,0:T(8,128)} %get-tuple-element.111, f32[8,1376]{1,0:T(8,128)S(1)} %log_add_fusion, bf16[1376,8,64]{0,2,1:T(8,128)(2,1)S(1)} %squeeze.45, bf16[1376,3,8,64]{0,3,2,1:T(8,128)(2,1)} %squeeze.40), kind=kOutput, calls=%fused_computation.3 | convolution fusion | flops 1984247040 | bytes 125523968 | tf_op jit(solution)/shard_map/while/body/eval_jaxpr/qhd,khd->hqk/dot_general | solution.py:63
  484.1 48.9 %multiply_convert_fusion = bf16[8,1376,1376]{1,2,0:T(8,128)(2,1)} fusion(f32[8,1376,1376]{1,2,0:T(8,128)} %get-tuple-element.116, f32[8,1376,1376]{1,2,0:T(8,128)} %get-tuple-element.111, f32[8,1376]{1,0:T(8,128)S(1)} %get-tuple-element.115, f32[8,1376]{1,0:T(8,128)S(1)} %log_add_fusion), kind=kLoop, calls=%fused_computation.2 | loop fusion | flops 60588032 | bytes 151558144 | tf_op jit(solution)/shard_map/while/body/eval_jaxpr/convert_element_type | solution.py:67
  533.0 16.5 %fusion.27 = bf16[8,64,1376]{2,1,0:T(8,128)(2,1)} fusion(bf16[8,1376,1376]{1,2,0:T(8,128)(2,1)} %multiply_convert_fusion, bf16[1376,3,8,64]{0,3,2,1:T(8,128)(2,1)} %squeeze.40), kind=kOutput, calls=%fused_computation.52 | convolution fusion | flops 1940226048 | bytes 33849344 | tf_op jit(solution)/shard_map/while/body/eval_jaxpr/hqk,qhd->khd/dot_general | solution.py:71
  549.5 16.5 %fusion.26 = bf16[8,64,1376]{2,1,0:T(8,128)(2,1)} fusion(bf16[8,1376,1376]{1,2,0:T(8,128)(2,1)} %multiply_convert_fusion, bf16[1376,3,8,64]{0,3,2,1:T(8,128)(2,1)} %squeeze.40), kind=kOutput, calls=%fused_computation.51 | convolution fusion | flops 1940226048 | bytes 33849344 | tf_op jit(solution)/shard_map/while/body/eval_jaxpr/hqk,khd->qhd/dot_general | solution.py:68
  566.0 7.0 copy.65
  573.0 7.7 copy.64
  580.7 7.7 copy.63
  588.5 12.5 %pad_maximum_fusion = bf16[1,1376,3,1,512]{4,2,3,0,1:T(4,128)(2,1)} fusion(bf16[1,1376,1,1,512]{4,2,3,0,1:T(2,128)(2,1)S(1)} %copy.65, bf16[1,1376,1,1,512]{4,2,3,0,1:T(2,128)(2,1)} %copy.64, bf16[1,1376,1,1,512]{4,2,3,0,1:T(2,128)(2,1)} %copy.63), kind=kLoop, calls=%fused_computation.30 | loop fusion | flops 12681216 | bytes 8454144 | tf_op jit(solution)/shard_map/while/body/eval_jaxpr/stack | solution.py:207
  600.9 6.3 all-to-all-start.3
  607.4 3.2 convolution_convert_fusion.3
  610.9 58.9 %all-to-all-done.3 = bf16[1,1376,3,1,512]{4,2,3,0,1:T(4,128)(2,1)} async-done(((bf16[1,1376,3,1,512]{4,2,3,0,1:T(4,128)(2,1)}), bf16[1,1376,3,1,512]{4,2,3,0,1:T(4,128)(2,1)}, u32[]{:S(2)}, u32[]{:S(2)}) %all-to-all-start.3) | async-done | bytes 4227104 | tf_op jit(solution)/shard_map/all_to_all | solution.py:211
  669.8 3.7 copy.66
  673.5 6.3 copy.67
  679.8 10.6 reshape.242
  690.4 9.6 convolution_convert_fusion.2
  700.7 12.2 %convolution_convert_fusion = bf16[1024,4096]{1,0:T(8,128)(2,1)} fusion(bf16[688,4096]{1,0:T(8,128)(2,1)} %get-tuple-element.119, f32[688,1024]{1,0:T(8,128)} %copy-done.2, f32[1024]{0:T(1024)S(1)} %copy-done.39, f32[1024]{0:T(1024)S(1)} %copy-done.24, f32[688]{0:T(1024)S(1)} %copy-done.26, f32[688]{0:T(1024)S(1)} %copy-done.16), kind=kOutput, calls=%fused_computation.27 | convolution fusion | flops 5779079168 | bytes 16856448 | tf_op jit(solution)/shard_map/ti,tj->ij/dot_general | solution.py:28
  713.0 1.4 copy-done.9
  714.4 12.0 %convolution_convert_fusion.1 = bf16[4096,1024]{1,0:T(8,128)(2,1)} fusion(bf16[688,4096]{1,0:T(8,128)(2,1)} %get-tuple-element.101, bf16[1,688,1024]{2,1,0:T(8,128)(2,1)S(1)} %copy-done.9, f32[1024]{0:T(1024)S(1)} %copy-done.28), kind=kOutput, calls=%fused_computation.28 | convolution fusion | flops 5777670144 | bytes 15437824 | tf_op jit(solution)/shard_map/ti,tj->ij/dot_general | solution.py:28
  728.2 8.8 fusion.62
  737.0 1.5 copy-done.5
  738.6 1.3 fusion.30
  740.4 41.8 %reduce-scatter.5.cloned.1.call-done = bf16[64,3072]{1,0:T(8,128)(2,1)} async-done(((bf16[1024,3072]{1,0:T(8,128)(2,1)}), bf16[64,3072]{1,0:T(8,128)(2,1)}) %reduce-scatter.5.cloned.1.call-update) | async-done | bytes 393232 | tf_op jit(solution)/shard_map/reduce_scatter | solution.py:244
  782.2 107.8 %reduce-scatter.9.cloned.1.call-done = bf16[64,4096]{1,0:T(8,128)(2,1)} async-done(((bf16[1024,4096]{1,0:T(8,128)(2,1)}), bf16[64,4096]{1,0:T(8,128)(2,1)}) %reduce-scatter.9.cloned.1.call-update) | async-done | bytes 524304 | tf_op jit(solution)/shard_map/reduce_scatter | solution.py:268
  890.0 108.5 %reduce-scatter.11.cloned.1.call-done = bf16[256,1024]{1,0:T(8,128)(2,1)} async-done(((bf16[4096,1024]{1,0:T(8,128)(2,1)}), bf16[256,1024]{1,0:T(8,128)(2,1)}) %reduce-scatter.11.cloned.1.call-update) | async-done | bytes 524304 | tf_op jit(solution)/shard_map/reduce_scatter | solution.py:274
  998.6 15.5 %fusion.38 = (bf16[1024]{0:T(1024)(128)(2,1)S(1)}, bf16[1024]{0:T(1024)(128)(2,1)S(1)}, f32[1,688,1024]{2,1,0:T(8,128)}, bf16[1,688,1024]{2,1,0:T(8,128)(2,1)}) fusion(bf16[1,688,1024]{2,1,0:T(8,128)(2,1)S(1)} %copy-done.9, f32[1024]{0:T(1024)S(1)} %convert_element_type.228, f32[688,1024]{1,0:T(8,128)} %get-tuple-element.112, f32[1024]{0:T(1024)S(1)} %copy-done.35, ...), kind=kOutput, calls=%fused_computation.63 | convolution fusion | flops 5786155008 | bytes 32376256 | tf_op jit(solution)/shard_map/dot_general | solution.py:24
  1014.1 60.3 %all-reduce.21 = (bf16[1024]{0:T(1024)(128)(2,1)S(1)}, bf16[1024]{0:T(1024)(128)(2,1)S(1)}, bf16[1024]{0:T(1024)(128)(2,1)S(1)}, bf16[1024]{0:T(1024)(128)(2,1)S...) all-reduce(bf16[1024]{0:T(1024)(128)(2,1)S(1)} %get-tuple-element.5, ...), channel_id=2, replica_groups=mesh['fsdp'=16,'seq'=2] {'fsdp'}, use_global_device_ids=true, to_apply=%region_12.13.clone | all-reduce | flops 14336 | bytes 57344
  1075.2 5.0 all-reduce.23
  1085.9 1.7 convert_element_type.246
  1087.6 1.9 convert_element_type.242
  1089.5 2.1 convert_element_type.255
  (190 shorter events, 24.9 us)
Async XLA Ops:
  7.2 78.5 %copy-start = (bf16[1,688,1024]{2,1,0:T(8,128)(2,1)S(1)}, bf16[1,688,1024]{2,1,0:T(8,128)(2,1)}, u32[]{:S(2)}) copy-start(bf16[1,688,1024]{2,1,0:T(8,128)(2,1)} %param.18) | copy-start | bytes 4227076
  7.2 79.1 %all-gather.6.cloned.1.call-start = ((), (), s32[]{:S(2)}) async-start(), calls=%async_computation.8 | async-start | bytes 6684672 | tf_op jit(solution)/shard_map/all_gather | solution.py:100
  7.9 303.6 %all-gather.8.cloned.1.call-start = ((), (), s32[]{:S(2)}) async-start(), calls=%async_computation.9 | async-start | bytes 2228224 | tf_op jit(solution)/shard_map/all_gather | solution.py:103
  8.7 310.3 %all-gather.10.cloned.1.call-start = ((), (), s32[]{:S(2)}) async-start(), calls=%async_computation.10 | async-start | bytes 8912896 | tf_op jit(solution)/shard_map/all_gather | solution.py:108
  84.0 11.8 %copy-start.19 = (f32[1024]{0:T(1024)}, f32[1024]{0:T(1024)S(1)}, u32[]{:S(2)}) copy-start(f32[1024]{0:T(1024)S(1)} %convert_element_type.212) | copy-start | bytes 12292
  84.0 11.8 %copy-start.36 = (f32[1024]{0:T(1024)}, f32[1024]{0:T(1024)S(1)}, u32[]{:S(2)}) copy-start(f32[1024]{0:T(1024)S(1)} %convert_element_type.213) | copy-start | bytes 12292
  85.7 10.1 copy-start.13
  86.2 9.6 copy-start.17
  86.2 9.6 copy-start.21
  111.4 49.3 %all-to-all-start = ((bf16[1,688,3,2,512]{4,1,2,0,3:T(8,128)(2,1)}), bf16[1,688,3,2,512]{4,1,2,0,3:T(8,128)(2,1)}, u32[]{:S(2)}, u32[]{:S(2)}) async-start(bf16[1,688,3,2,512]{4,1,2,0,3:T(8,128)(2,1)} %copy.53), calls=%async_computation | async-start | bytes 8454144 | tf_op jit(solution)/shard_map/all_to_all | solution.py:152
  117.0 237.6 %all-gather.12.cloned.1.call-start = ((), (), s32[]{:S(2)}) async-start(), calls=%async_computation.11 | async-start | bytes 8912896 | tf_op jit(solution)/shard_map/all_gather | solution.py:110
  269.2 17.8 %copy-start.44 = (bf16[256]{0:T(256)(128)(2,1)S(1)}, bf16[256]{0:T(256)(128)(2,1)}, u32[]{:S(2)}) copy-start(bf16[256]{0:T(256)(128)(2,1)} %param.31) | copy-start | bytes 1540
  283.3 21.9 %all-to-all-start.1 = ((bf16[2,2,176128]{2,1,0:T(2,128)(2,1)}), bf16[2,2,176128]{2,1,0:T(2,128)(2,1)S(1)}, u32[]{:S(2)}, u32[]{:S(2)}) async-start(bf16[2,2,176128]{2,1,0:T(2,128)(2,1)} %reshape.310), calls=%async_computation.1 | async-start | bytes 2818048 | tf_op jit(solution)/shard_map/all_to_all | solution.py:163
  287.0 98.9 %copy-start.23 = (f32[1024]{0:T(1024)}, f32[1024]{0:T(1024)S(1)}, u32[]{:S(2)}) copy-start(f32[1024]{0:T(1024)S(1)} %convert_element_type.223) | copy-start | bytes 12292
  287.0 99.8 %copy-start.27 = (f32[1024]{0:T(1024)}, f32[1024]{0:T(1024)S(1)}, u32[]{:S(2)}) copy-start(f32[1024]{0:T(1024)S(1)} %convert_element_type.222) | copy-start | bytes 12292
  287.0 24.6 %copy-start.34 = (f32[1024]{0:T(1024)}, f32[1024]{0:T(1024)S(1)}, u32[]{:S(2)}) copy-start(f32[1024]{0:T(1024)S(1)} %convert_element_type.221) | copy-start | bytes 12292
  287.0 31.9 %copy-start.38 = (f32[1024]{0:T(1024)}, f32[1024]{0:T(1024)S(1)}, u32[]{:S(2)}) copy-start(f32[1024]{0:T(1024)S(1)} %convert_element_type.224) | copy-start | bytes 12292
  311.5 5.4 copy-start.6
  317.0 1.5 copy-start.2
  317.0 68.9 %copy-start.15 = (f32[688]{0:T(1024)}, f32[688]{0:T(1024)S(1)}, u32[]{:S(2)}) copy-start(f32[688]{0:T(1024)S(1)} %broadcast_multiply_fusion) | copy-start | bytes 8260
  318.9 66.9 %copy-start.25 = (f32[688]{0:T(1024)}, f32[688]{0:T(1024)S(1)}, u32[]{:S(2)}) copy-start(f32[688]{0:T(1024)S(1)} %fusion.59) | copy-start | bytes 8260
  354.6 19.6 %copy-start.3 = (f32[688,1024]{1,0:T(8,128)S(1)}, f32[688,1024]{1,0:T(8,128)}, u32[]{:S(2)}) copy-start(f32[688,1024]{1,0:T(8,128)} %copy-done.2) | copy-start | bytes 8454148
  385.9 2.4 copy-start.8
  386.8 1.5 copy-start.4
  386.8 4.0 copy-start.43
  386.8 5.6 copy-start.29
  389.7 1.1 copy-start.10
  600.9 6.4 copy-start.7
  600.9 6.4 copy-start.11
  600.9 68.8 %all-to-all-start.3 = ((bf16[1,1376,3,1,512]{4,2,3,0,1:T(4,128)(2,1)}), bf16[1,1376,3,1,512]{4,2,3,0,1:T(4,128)(2,1)}, u32[]{:S(2)}, u32[]{:S(2)}) async-start(bf16[1,1376,3,1,512]{4,2,3,0,1:T(4,128)(2,1)} %pad_maximum_fusion), calls=%async_computation.3 | async-start | bytes 11272192 | tf_op jit(solution)/shard_map/all_to_all | solution.py:211
  607.3 133.1 %reduce-scatter.7.cloned.1.call-start = ((), (), s32[]{:S(2)}) async-start(), calls=%async_computation.13 | async-start | bytes 2228224 | tf_op jit(solution)/shard_map/reduce_scatter | solution.py:253
  610.6 171.6 %reduce-scatter.5.cloned.1.call-start = ((), (), s32[]{:S(2)}) async-start(), calls=%async_computation.12 | async-start | bytes 6684672 | tf_op jit(solution)/shard_map/reduce_scatter | solution.py:244
  679.8 10.6 copy-start.1
  679.8 10.6 copy-start.14
  679.8 10.6 copy-start.20
  679.8 10.6 copy-start.22
  679.8 10.6 copy-start.37
  700.0 0.7 copy-start.16
  700.0 0.7 copy-start.24
  700.0 0.7 copy-start.26
  700.0 0.7 copy-start.39
  700.0 190.0 %reduce-scatter.9.cloned.1.call-start = ((), (), s32[]{:S(2)}) async-start(), calls=%async_computation.14 | async-start | bytes 8912896 | tf_op jit(solution)/shard_map/reduce_scatter | solution.py:268
  712.9 1.5 copy-start.9
  712.9 1.5 copy-start.28
  712.9 285.5 %reduce-scatter.11.cloned.1.call-start = ((), (), s32[]{:S(2)}) async-start(), calls=%async_computation.15 | async-start | bytes 8912896 | tf_op jit(solution)/shard_map/reduce_scatter | solution.py:274
  726.4 1.7 copy-start.42
  726.4 359.5 %all-reduce.27.cloned.1.call-start = ((), (), s32[]{:S(2)}) async-start(), calls=%async_computation.16 | async-start | bytes 3145728 | tf_op jit(solution)/shard_map/psum | solution.py:287
  728.1 11.7 %slice-start = ((s8[4227072]{0:T(1024)(128)(4,1)}), s8[4194304]{0:T(1024)(128)(4,1)S(1)}, s32[]{:S(2)}) async-start(s8[4227072]{0:T(1024)(128)(4,1)} %bitcast.148), calls=%async_computation.17 | async-start | bytes 8388608
  728.1 8.9 copy-start.18
  728.1 11.7 %slice-start.1 = ((s8[4227072]{0:T(1024)(128)(4,1)}), s8[32768]{0:T(1024)(128)(4,1)S(1)}, s32[]{:S(2)}) async-start(s8[4227072]{0:T(1024)(128)(4,1)} %bitcast.148), calls=%async_computation.18 | async-start | bytes 65536
  737.0 1.6 copy-start.5
  739.8 258.7 %copy-start.30 = (f32[688]{0:T(1024)S(1)}, f32[688]{0:T(1024)}, u32[]{:S(2)}) copy-start(f32[688]{0:T(1024)} %copy-done.29) | copy-start | bytes 8260
  739.8 258.7 %copy-start.35 = (f32[1024]{0:T(1024)S(1)}, f32[1024]{0:T(1024)}, u32[]{:S(2)}) copy-start(f32[1024]{0:T(1024)} %copy-done.34) | copy-start | bytes 12292
  998.5 15.6 %copy-start.31 = (bf16[1024]{0:T(1024)(128)(2,1)S(1)}, bf16[1024]{0:T(1024)(128)(2,1)}, u32[]{:S(2)}) copy-start(bf16[1024]{0:T(1024)(128)(2,1)} %get-tuple-element.97) | copy-start | bytes 6148
  998.5 15.6 %copy-start.32 = (bf16[1024]{0:T(1024)(128)(2,1)S(1)}, bf16[1024]{0:T(1024)(128)(2,1)}, u32[]{:S(2)}) copy-start(bf16[1024]{0:T(1024)(128)(2,1)} %get-tuple-element.107) | copy-start | bytes 6148
  998.6 15.6 %copy-start.33 = (bf16[4096]{0:T(1024)(128)(2,1)S(1)}, bf16[4096]{0:T(1024)(128)(2,1)}, u32[]{:S(2)}) copy-start(bf16[4096]{0:T(1024)(128)(2,1)} %get-tuple-element.118) | copy-start | bytes 24580
  998.6 15.6 %copy-start.40 = (bf16[1024]{0:T(1024)(128)(2,1)S(1)}, bf16[1024]{0:T(1024)(128)(2,1)}, u32[]{:S(2)}) copy-start(bf16[1024]{0:T(1024)(128)(2,1)} %get-tuple-element.50) | copy-start | bytes 6148
  998.6 15.6 %copy-start.41 = (bf16[1024]{0:T(1024)(128)(2,1)S(1)}, bf16[1024]{0:T(1024)(128)(2,1)}, u32[]{:S(2)}) copy-start(bf16[1024]{0:T(1024)(128)(2,1)} %get-tuple-element.56) | copy-start | bytes 6148
  1085.9 5.7 copy-start.12
Sparse Core Ops, SparseCore 0:
  10.3 65.3 all-gather.5
  77.9 40.0 all-gather.7
  120.1 73.6 all-gather.9
  195.8 73.1 all-gather.11
  611.5 59.6 reduce-scatter.6
  700.1 81.9 reduce-scatter.4
  786.3 103.7 reduce-scatter.8
  894.1 104.3 reduce-scatter.10
  1001.0 51.7 all-reduce.26
where the time goes:
time: 1110 us; the launch traced here: 1100 us
  waiting for transfers between devices  362 us (33%)
  matrix products  293 us (26%)
  blocking collectives  169 us (15%)
  local copies, waits for them, and re-layouts  130 us (12%)
  other arithmetic  111 us (10%)
  between operations  17.8 us (2%)
  starting transfers between devices  16.9 us (2%)
    unnamed x2, blocking collectives  124 us
    reduce_scatter x1, waiting for transfers between devices, body(): lax.psum_scatter(local_grads[12].astype(jnp.bfloat16), 'fsdp', scatter_di...  108 us
    reduce_scatter x1, waiting for transfers between devices, body(): lax.psum_scatter(local_grads[10].astype(jnp.bfloat16), 'fsdp', scatter_di...  108 us
    dot_general x4, matrix products, matmul(): return jnp.dot(left, right, preferred_element_type=jnp.float32)  66 us
    all_to_all x1, waiting for transfers between devices, body(): lax.all_to_all(delta_packed, 'seq', split_axis=1, concat_axis=3, tiled=True)  58.9 us
    convert_element_type x1, other arithmetic, attend_back(): grad_scores = (probs * (grad_probs - inner_sum)).astype(jnp.bfloat16)  48.9 us
    dot_general x1, matrix products, attend_back(): jnp.einsum('qhd,khd->hqk', grad_mixture, values, preferred_element_type=j...  43 us
    all_to_all x1, waiting for transfers between devices, body(): lax.all_to_all(packed, 'seq', split_axis=3, concat_axis=1, tiled=True)  42.4 us
  transfers between devices with their start and end apart: 12, of which 5 were waited for; matrix products, arithmetic and copies ran while one was open for 27% of the time, Pallas kernels for 0%

commit v1 on v0

--- a/solution.py
+++ b/solution.py
@@ -1,6 +1,10 @@
+import functools
+
 import jax
 import jax.numpy as jnp
 from jax import lax
+from jax.experimental import pallas as pl
+from jax.experimental.pallas import tpu as pltpu
 from jax.sharding import PartitionSpec as P
 
 H = 16
@@ -74,7 +78,7 @@
     return (grad_queries, grad_keys, grad_values)
 
 
-def body(
+def general_body(
     tokens,
     lengths,
     norm1_gain,
@@ -301,6 +305,726 @@
     return (output, grad_tokens) + tuple(owned_grads)
 
 
+BF16 = jnp.bfloat16
+F32 = jnp.float32
+NT = (((1,), (1,)), ((), ()))
+NN = (((1,), (0,)), ((), ()))
+MASKED = -1e30
+LANES = 128
+VMEM_LIMIT = 60 * 2**20
+
+GAIN1, SHIFT1, QUERY, VALUE, OUT_SHIFT, SCALE1, GAIN2, SHIFT2, DOWN_SHIFT, SCALE2 = range(10)
+
+
+def dot(left, right, dims=NN):
+    return lax.dot_general(left, right, dims, preferred_element_type=F32)
+
+
+def turned(values):
+    return values.astype(F32).T.astype(BF16)
+
+
+def lane_ids(rows):
+    return lax.broadcasted_iota(jnp.int32, (rows, LANES), 1)
+
+
+def split3(values):
+    high = values.astype(BF16).astype(F32)
+    rest = values - high
+    mid = rest.astype(BF16).astype(F32)
+    return high, mid, rest - mid
+
+
+def params_for(flops, nbytes, transcendentals=0):
+    return dict(
+        compiler_params=pltpu.CompilerParams(vmem_limit_bytes=VMEM_LIMIT),
+        cost_estimate=pl.CostEstimate(
+            flops=flops, bytes_accessed=nbytes, transcendentals=transcendentals
+        ),
+    )
+
+
+def whole(shape):
+    return pl.BlockSpec(shape, lambda *_: (0,) * len(shape))
+
+
+def normalize(values, gain, shift):
+    center = values - jnp.mean(values, axis=-1, keepdims=True)
+    spread = jnp.mean(center * center, axis=-1, keepdims=True)
+    return center * lax.rsqrt(spread + norm_eps) * gain + shift
+
+
+def normalize_back(values, gain, delta):
+    center = values - jnp.mean(values, axis=-1, keepdims=True)
+    inverse = lax.rsqrt(jnp.mean(center * center, axis=-1, keepdims=True) + norm_eps)
+    unit = center * inverse
+    scaled = delta * gain
+    mean_scaled = jnp.mean(scaled, axis=-1, keepdims=True)
+    mean_unit = jnp.mean(scaled * unit, axis=-1, keepdims=True)
+    return inverse * (scaled - mean_scaled - unit * mean_unit), delta * unit
+
+
+def total_rows(values):
+    return jnp.sum(values, axis=0, keepdims=True)
+
+
+def project_kernel(order, x_ref, all_ref, half_ref, weight_ref, other_ref, own_ref, normed_ref):
+    step = pl.program_id(0)
+
+    @pl.when(step == 0)
+    def _():
+        normed_ref[...] = normalize(
+            x_ref[...].astype(F32), all_ref[GAIN1 : GAIN1 + 1, :], all_ref[SHIFT1 : SHIFT1 + 1, :]
+        ).astype(BF16)
+
+    kind = lax.rem(step, 3)
+    shift = jnp.where(
+        kind == 0,
+        half_ref[QUERY : QUERY + 1, :],
+        jnp.where(kind == 2, half_ref[VALUE : VALUE + 1, :], 0.0),
+    )
+    block = (dot(normed_ref[...], weight_ref[...]) + shift).astype(BF16)
+
+    @pl.when(step < 3)
+    def _():
+        other_ref[0] = block
+
+    @pl.when(step >= 3)
+    def _():
+        own_ref[0] = block
+
+
+def project(order, x, table, weight):
+    tokens, width = x.shape
+    half = width // 2
+    return pl.pallas_call(
+        project_kernel,
+        grid_spec=pltpu.PrefetchScalarGridSpec(
+            num_scalar_prefetch=1,
+            grid=(6,),
+            in_specs=[
+                whole((tokens, width)),
+                whole(table.shape),
+                pl.BlockSpec((table.shape[0], half), lambda j, order: (0, lax.rem(order[j], 2))),
+                pl.BlockSpec((width, half), lambda j, order: (0, order[j])),
+            ],
+            out_specs=[
+                pl.BlockSpec((1, tokens, half), lambda j, order: (jnp.minimum(j, 2), 0, 0)),
+                pl.BlockSpec((1, tokens, half), lambda j, order: (jnp.maximum(j - 3, 0), 0, 0)),
+                whole((tokens, width)),
+            ],
+        ),
+        out_shape=[
+            jax.ShapeDtypeStruct((3, tokens, half), BF16),
+            jax.ShapeDtypeStruct((3, tokens, half), BF16),
+            jax.ShapeDtypeStruct((tokens, width), BF16),
+        ],
+        name="project",
+        **params_for(6 * tokens * width * width, 12 * tokens * width + 6 * width * width),
+    )(order, x, table, table, weight)
+
+
+def padded_len(count, block):
+    return -(-count // block) * block
+
+
+def attend_kernel(valid, *refs, pieces, block, scale):
+    in_refs, out_refs = refs[:pieces], refs[pieces : 2 * pieces]
+    total_refs = refs[2 * pieces : 3 * pieces]
+    keys, values, queries, mixed, totals = refs[3 * pieces :]
+    pair = pl.program_id(0)
+    size = in_refs[0].shape[1]
+    count, padded = pieces * size, keys.shape[0]
+    lane = lane_ids(size)
+    row = lax.broadcasted_iota(jnp.int32, (size, LANES), 0)
+    for i in range(pieces):
+        at = pl.ds(i * size, size)
+        keys[at, :LANES] = in_refs[i][1]
+        keys[at, LANES:] = jnp.where((lane == 0) & (row >= valid[i]), MASKED, 0.0).astype(BF16)
+        values[at, :LANES] = in_refs[i][2]
+        values[at, LANES:] = jnp.where(lane == 0, 1.0, 0.0).astype(BF16)
+        for j in range(2):
+            mine = lane // HD == j
+            queries[j, at, :LANES] = jnp.where(mine, in_refs[i][0].astype(F32) * scale, 0.0).astype(BF16)
+            queries[j, at, LANES:] = jnp.where(lane == 0, 1.0, 0.0).astype(BF16)
+    if padded > count:
+        rest = pl.ds(count, padded - count)
+        rest_lane = lane_ids(padded - count)
+        keys[rest, :LANES] = jnp.zeros((padded - count, LANES), BF16)
+        keys[rest, LANES:] = jnp.where(rest_lane == 0, MASKED, 0.0).astype(BF16)
+        values[rest, :] = jnp.zeros((padded - count, 2 * LANES), BF16)
+        for j in range(2):
+            queries[j, rest, :] = jnp.zeros((padded - count, 2 * LANES), BF16)
+
+    @pl.when(pair == 0)
+    def _():
+        for i in range(pieces):
+            total_refs[i][...] = jnp.zeros_like(total_refs[i])
+
+    block_lane = lane_ids(block)
+    for b in range(padded // block):
+        at = pl.ds(b * block, block)
+        results, logs = [], 0.0
+        for j in range(2):
+            scores = dot(queries[j, at, :], keys[...], NT)
+            largest = jnp.max(scores, axis=1, keepdims=True)
+            weights = jnp.exp(scores - largest).astype(BF16)
+            result = dot(weights, values[...])
+            total = result[:, LANES : LANES + 1]
+            results.append(result[:, :LANES] * (1.0 / total))
+            logs += jnp.where(block_lane == 2 * pair + j, largest + jnp.log(total), 0.0)
+        mixed[at, :] = jnp.where(block_lane < HD, results[0], results[1])
+        totals[at, :] = logs
+    for i in range(pieces):
+        at = pl.ds(i * size, size)
+        out_refs[i][...] = mixed[at, :].astype(BF16)
+        total_refs[i][...] += totals[at, :]
+
+
+def attention(valid, parts, block):
+    pieces = len(parts)
+    _, size, width = parts[0].shape
+    pairs = width // LANES
+    padded = padded_len(pieces * size, block)
+    outs = pl.pallas_call(
+        functools.partial(attend_kernel, pieces=pieces, block=block, scale=HD**-0.5),
+        grid_spec=pltpu.PrefetchScalarGridSpec(
+            num_scalar_prefetch=1,
+            grid=(pairs,),
+            in_specs=[pl.BlockSpec((3, size, LANES), lambda h, _: (0, 0, h))] * pieces,
+            out_specs=[pl.BlockSpec((size, LANES), lambda h, _: (0, h))] * pieces
+            + [whole((size, LANES))] * pieces,
+            scratch_shapes=[
+                pltpu.VMEM((padded, 2 * LANES), BF16),
+                pltpu.VMEM((padded, 2 * LANES), BF16),
+                pltpu.VMEM((2, padded, 2 * LANES), BF16),
+                pltpu.VMEM((padded, LANES), F32),
+                pltpu.VMEM((padded, LANES), F32),
+            ],
+        ),
+        out_shape=[jax.ShapeDtypeStruct((size, width), BF16)] * pieces
+        + [jax.ShapeDtypeStruct((size, LANES), F32)] * pieces,
+        name="attend",
+        **params_for(16 * pairs * LANES * padded * padded, 8 * size * width * pieces, pairs * 2 * padded * padded),
+    )(valid, *parts)
+    return outs[:pieces], outs[pieces:]
+
+
+def attend_back_kernel(valid, *refs, pieces, block, scale):
+    in_refs, mix_refs = refs[:pieces], refs[pieces : 2 * pieces]
+    grad_refs, total_refs = refs[2 * pieces : 3 * pieces], refs[3 * pieces : 4 * pieces]
+    out_refs = refs[4 * pieces : 5 * pieces]
+    keys, values, queries, grads, queries_t, grads_t, dq, dk_t, dv_t = refs[5 * pieces :]
+    pair = pl.program_id(0)
+    size = in_refs[0].shape[1]
+    count, padded = pieces * size, keys.shape[0]
+    blocks = padded // block
+    lane = lane_ids(size)
+    row = lax.broadcasted_iota(jnp.int32, (size, LANES), 0)
+    for i in range(pieces):
+        at = pl.ds(i * size, size)
+        keys[at, :LANES] = in_refs[i][1]
+        keys[at, LANES:] = jnp.where(
+            lane == 0, jnp.where(row >= valid[i], MASKED, 0.0), jnp.where(lane < 4, 1.0, 0.0)
+        ).astype(BF16)
+        values[at, :LANES] = in_refs[i][2]
+        values[at, LANES:] = jnp.where((lane > 0) & (lane < 4), 1.0, 0.0).astype(BF16)
+        queries[0, at, :LANES] = in_refs[i][0]
+        grads[0, at, :LANES] = grad_refs[i][...]
+    if padded > count:
+        left = padded - count
+        rest = pl.ds(count, left)
+        keys[rest, :LANES] = jnp.zeros((left, LANES), BF16)
+        keys[rest, LANES:] = jnp.where(lane_ids(left) == 0, MASKED, 0.0).astype(BF16)
+        values[rest, :] = jnp.zeros((left, 2 * LANES), BF16)
+        for j in range(2):
+            queries[j, rest, :] = jnp.zeros((left, 2 * LANES), BF16)
+            grads[j, rest, :] = jnp.zeros((left, 2 * LANES), BF16)
+    for b in range(blocks):
+        at = pl.ds(b * block, block)
+        queries_t[b] = (queries[0, at, :LANES].astype(F32) * scale).T.astype(BF16)
+        grads_t[b] = turned(grads[0, at, :LANES])
+    for j in range(2):
+        mine = lane // HD == j
+        for i in range(pieces):
+            at = pl.ds(i * size, size)
+            grad = jnp.where(mine, grad_refs[i][...].astype(F32), 0.0)
+            queries[j, at, :LANES] = jnp.where(mine, in_refs[i][0].astype(F32) * scale, 0.0).astype(BF16)
+            grads[j, at, :LANES] = grad.astype(BF16)
+            log_total = jnp.sum(
+                jnp.where(lane == 2 * pair + j, total_refs[i][...], 0.0), axis=1, keepdims=True
+            )
+            high, mid, low = split3(-log_total)
+            queries[j, at, LANES:] = jnp.where(
+                lane == 0,
+                1.0,
+                jnp.where(lane == 1, high, jnp.where(lane == 2, mid, jnp.where(lane == 3, low, 0.0))),
+            ).astype(BF16)
+            inner = jnp.sum(grad * mix_refs[i][...].astype(F32), axis=1, keepdims=True)
+            high, mid, low = split3(-inner)
+            grads[j, at, LANES:] = jnp.where(
+                lane == 1, high, jnp.where(lane == 2, mid, jnp.where(lane == 3, low, 0.0))
+            ).astype(BF16)
+    dk_t[...] = jnp.zeros_like(dk_t)
+    dv_t[...] = jnp.zeros_like(dv_t)
+    block_lane = lane_ids(block)
+    for b in range(blocks):
+        at = pl.ds(b * block, block)
+        results = []
+        for j in range(2):
+            mine = pl.ds(j * HD, HD)
+            probs = jnp.exp(dot(queries[j, at, :], keys[...], NT))
+            grad_scores = (probs * dot(grads[j, at, :], values[...], NT)).astype(BF16)
+            results.append(dot(grad_scores, keys[:, :LANES]) * scale)
+            dv_t[mine, :] += dot(grads_t[b, mine, :], probs.astype(BF16))
+            dk_t[mine, :] += dot(queries_t[b, mine, :], grad_scores)
+        dq[at, :] = jnp.where(block_lane < HD, results[0], results[1])
+    dk, dv = dk_t[...].T, dv_t[...].T
+    for i in range(pieces):
+        at = slice(i * size, (i + 1) * size)
+        out_refs[i][0] = dq[at, :].astype(BF16)
+        out_refs[i][1] = dk[at, :].astype(BF16)
+        out_refs[i][2] = dv[at, :].astype(BF16)
+
+
+def attention_back(valid, parts, mixtures, grads, totals, block):
+    pieces = len(parts)
+    _, size, width = parts[0].shape
+    pairs = width // LANES
+    padded = padded_len(pieces * size, block)
+    triple = pl.BlockSpec((3, size, LANES), lambda h, _: (0, 0, h))
+    single = pl.BlockSpec((size, LANES), lambda h, _: (0, h))
+    return pl.pallas_call(
+        functools.partial(attend_back_kernel, pieces=pieces, block=block, scale=HD**-0.5),
+        grid_spec=pltpu.PrefetchScalarGridSpec(
+            num_scalar_prefetch=1,
+            grid=(pairs,),
+            in_specs=[triple] * pieces + [single] * 2 * pieces + [whole((size, LANES))] * pieces,
+            out_specs=[triple] * pieces,
+            scratch_shapes=[
+                pltpu.VMEM((padded, 2 * LANES), BF16),
+                pltpu.VMEM((padded, 2 * LANES), BF16),
+                pltpu.VMEM((2, padded, 2 * LANES), BF16),
+                pltpu.VMEM((2, padded, 2 * LANES), BF16),
+                pltpu.VMEM((padded // block, LANES, block), BF16),
+                pltpu.VMEM((padded // block, LANES, block), BF16),
+                pltpu.VMEM((padded, LANES), F32),
+                pltpu.VMEM((LANES, padded), F32),
+                pltpu.VMEM((LANES, padded), F32),
+            ],
+        ),
+        out_shape=[jax.ShapeDtypeStruct((3, size, width), BF16)] * pieces,
+        name="attend_back",
+        **params_for(30 * pairs * LANES * padded * padded, 16 * size * width * pieces, pairs * 2 * padded * padded),
+    )(valid, *parts, *mixtures, *grads, *totals)
+
+
+def merge_kernel(order, x_ref, own_ref, far_ref, table, own_w, far_w, middle_ref, branch_ref, normed_ref):
+    branch = dot(own_ref[...], own_w[...]) + dot(far_ref[...], far_w[...])
+    branch += table[OUT_SHIFT : OUT_SHIFT + 1, :]
+    middle = x_ref[...].astype(F32) + table[SCALE1 : SCALE1 + 1, :] * branch
+    middle_ref[...] = middle
+    branch_ref[...] = branch
+    normed_ref[...] = normalize(
+        middle, table[GAIN2 : GAIN2 + 1, :], table[SHIFT2 : SHIFT2 + 1, :]
+    ).astype(BF16)
+
+
+ROWS = 352
+
+
+def row_steps(tokens):
+    return -(-tokens // ROWS)
+
+
+def merge(order, x, own, far, table, weight):
+    tokens, width = x.shape
+    half = width // 2
+    wide = pl.BlockSpec((ROWS, width), lambda i, _: (i, 0))
+    narrow = pl.BlockSpec((ROWS, half), lambda i, _: (i, 0))
+    return pl.pallas_call(
+        merge_kernel,
+        grid_spec=pltpu.PrefetchScalarGridSpec(
+            num_scalar_prefetch=1,
+            grid=(row_steps(tokens),),
+            in_specs=[
+                wide,
+                narrow,
+                narrow,
+                whole(table.shape),
+                pl.BlockSpec((half, width), lambda i, order: (order[3], 0)),
+                pl.BlockSpec((half, width), lambda i, order: (order[0], 0)),
+            ],
+            out_specs=[wide, wide, wide],
+        ),
+        out_shape=[
+            jax.ShapeDtypeStruct((tokens, width), F32),
+            jax.ShapeDtypeStruct((tokens, width), F32),
+            jax.ShapeDtypeStruct((tokens, width), BF16),
+        ],
+        name="merge",
+        **params_for(2 * tokens * width * width, 14 * tokens * width + 2 * width * width),
+    )(order, x, own, far, table, weight, weight)
+
+
+def gelu_and_slope(values):
+    size = jnp.abs(values) * 0.7071067811865476
+    t = 1.0 / (1.0 + 0.3275911 * size)
+    bell = jnp.exp(-0.5 * (values * values))
+    poly = t * (0.254829592 + t * (-0.284496736 + t * (1.421413741 + t * (-1.453152027 + t * 1.061405429))))
+    tail = 0.5 * poly * bell
+    phi = jnp.where(values < 0, tail, 1.0 - tail)
+    return values * phi, phi + values * bell * 0.3989422804014327
+
+
+def mlp_kernel(
+    normed_ref, cotangent_ref, table, up_ref, shift_ref, down_ref,
+    branch_ref, delta_ref, grad_up_ref, grad_down_ref, grad_shift_ref,
+    upstream, upstream_t, normed_t,
+):
+    @pl.when(pl.program_id(0) == 0)
+    def _():
+        scaled = (cotangent_ref[...].astype(F32) * table[SCALE2 : SCALE2 + 1, :]).astype(BF16)
+        upstream[...] = scaled
+        upstream_t[...] = turned(scaled)
+        normed_t[...] = turned(normed_ref[...])
+        branch_ref[...] = jnp.zeros_like(branch_ref)
+        delta_ref[...] = jnp.zeros_like(delta_ref)
+
+    up, down = up_ref[...], down_ref[...]
+    hidden = dot(normed_ref[...], up) + shift_ref[...]
+    grad_active = dot(upstream[...], down, NT)
+    active, slope = gelu_and_slope(hidden)
+    active = active.astype(BF16)
+    delta_hidden = (grad_active * slope).astype(BF16)
+    branch_ref[...] += dot(active, down)
+    delta_ref[...] += dot(delta_hidden, up, NT)
+    grad_up_ref[...] = dot(normed_t[...], delta_hidden).astype(BF16)
+    grad_down = dot(upstream_t[...], active).astype(BF16)
+    each = grad_down_ref.shape[2]
+    for i in range(grad_down_ref.shape[0]):
+        grad_down_ref[i] = grad_down[:, i * each : (i + 1) * each]
+    grad_shift_ref[...] = total_rows(delta_hidden.astype(F32))
+
+
+def mlp(normed, cotangent, table, up, up_shift, down, owners, block=512):
+    tokens, width = normed.shape
+    hidden = up.shape[1]
+    each = hidden // owners
+    held = block // each
+    return pl.pallas_call(
+        mlp_kernel,
+        grid=(hidden // block,),
+        in_specs=[
+            whole((tokens, width)),
+            whole((tokens, width)),
+            whole(table.shape),
+            pl.BlockSpec((width, block), lambda j: (0, j)),
+            pl.BlockSpec((1, block), lambda j: (0, j)),
+            pl.BlockSpec((block, width), lambda j: (j, 0)),
+        ],
+        out_specs=[
+            whole((tokens, width)),
+            whole((tokens, width)),
+            pl.BlockSpec((width, block), lambda j: (0, j)),
+            pl.BlockSpec((held, width, each), lambda j: (j, 0, 0)),
+            pl.BlockSpec((1, block), lambda j: (0, j)),
+        ],
+        out_shape=[
+            jax.ShapeDtypeStruct((tokens, width), F32),
+            jax.ShapeDtypeStruct((tokens, width), F32),
+            jax.ShapeDtypeStruct((width, hidden), BF16),
+            jax.ShapeDtypeStruct((owners, width, each), BF16),
+            jax.ShapeDtypeStruct((1, hidden), F32),
+        ],
+        scratch_shapes=[
+            pltpu.VMEM((tokens, width), BF16),
+            pltpu.VMEM((width, tokens), BF16),
+            pltpu.VMEM((width, tokens), BF16),
+        ],
+        name="mlp",
+        **params_for(12 * tokens * width * hidden, 12 * tokens * width + 8 * width * hidden, 2 * tokens * hidden),
+    )(normed, cotangent, table, up, up_shift, down)
+
+
+SUM_ROWS = 8
+
+
+def unmerge_kernel(
+    order, middle_ref, branch1_ref, branch2_ref, delta_ref, cotangent_ref, own_ref, far_ref, table, own_w, far_w,
+    output_ref, delta_middle_ref, own_grad_ref, far_grad_ref, weight_ref, sums_ref,
+    delta1_all,
+    *, tokens,
+):
+    step = pl.program_id(0)
+
+    @pl.when(step == 0)
+    def _():
+        sums_ref[...] = jnp.zeros_like(sums_ref)
+
+    rows, width = middle_ref.shape
+    inside = lax.broadcasted_iota(jnp.int32, (rows, width), 0) + step * rows < tokens
+
+    def kept(values):
+        return jnp.where(inside, values, 0.0)
+
+    upstream = cotangent_ref[...].astype(F32)
+    scale2 = table[SCALE2 : SCALE2 + 1, :]
+    middle = middle_ref[...]
+    branch2 = branch2_ref[...] + table[DOWN_SHIFT : DOWN_SHIFT + 1, :]
+    output_ref[...] = (middle + scale2 * branch2).astype(BF16)
+    delta2 = (scale2 * upstream).astype(BF16).astype(F32)
+    delta = delta_ref[...]
+    inner, gain_terms = normalize_back(middle, table[GAIN2 : GAIN2 + 1, :], delta)
+    delta_middle = upstream + inner
+    delta_middle_ref[...] = delta_middle
+    delta1 = kept(table[SCALE1 : SCALE1 + 1, :] * delta_middle).astype(BF16)
+    delta1_all[pl.ds(pl.multiple_of(step * rows, 16), rows), :] = delta1
+    own_grad_ref[...] = dot(delta1, own_w[...], NT).astype(BF16)
+    far_grad_ref[...] = dot(delta1, far_w[...], NT).astype(BF16)
+    terms = (
+        upstream * branch2,
+        delta2,
+        gain_terms,
+        delta,
+        delta_middle * branch1_ref[...],
+        delta1.astype(F32),
+    )
+    for i, term in enumerate(terms):
+        sums_ref[i : i + 1, :] += total_rows(kept(term))
+
+    @pl.when(step == pl.num_programs(0) - 1)
+    def _():
+        delta1_kept = delta1_all[:tokens, :]
+        half = own_ref.shape[1]
+        own_at = pl.multiple_of(order[3] * half, half)
+        far_at = pl.multiple_of(order[0] * half, half)
+        weight_ref[pl.ds(own_at, half), :] = dot(turned(own_ref[...]), delta1_kept).astype(BF16)
+        weight_ref[pl.ds(far_at, half), :] = dot(turned(far_ref[...]), delta1_kept).astype(BF16)
+
+
+def unmerge(order, middle, branch1, branch2, delta, cotangent, own, far, table, weight):
+    tokens, width = middle.shape
+    half = width // 2
+    steps = row_steps(tokens)
+    wide = pl.BlockSpec((ROWS, width), lambda i, _: (i, 0))
+    narrow = pl.BlockSpec((ROWS, half), lambda i, _: (i, 0))
+    return pl.pallas_call(
+        functools.partial(unmerge_kernel, tokens=tokens),
+        grid_spec=pltpu.PrefetchScalarGridSpec(
+            num_scalar_prefetch=1,
+            grid=(steps,),
+            in_specs=[wide] * 5
+            + [whole((tokens, half))] * 2
+            + [
+                whole(table.shape),
+                pl.BlockSpec((half, width), lambda i, order: (order[3], 0)),
+                pl.BlockSpec((half, width), lambda i, order: (order[0], 0)),
+            ],
+            out_specs=[wide, wide, narrow, narrow, whole((width, width)), whole((SUM_ROWS, width))],
+            scratch_shapes=[pltpu.VMEM((steps * ROWS, width), BF16)],
+        ),
+        out_shape=[
+            jax.ShapeDtypeStruct((tokens, width), BF16),
+            jax.ShapeDtypeStruct((tokens, width), F32),
+            jax.ShapeDtypeStruct((tokens, half), BF16),
+            jax.ShapeDtypeStruct((tokens, half), BF16),
+            jax.ShapeDtypeStruct((width, width), BF16),
+            jax.ShapeDtypeStruct((SUM_ROWS, width), F32),
+        ],
+        name="unmerge",
+        **params_for(4 * tokens * width * width, 30 * tokens * width + 4 * width * width),
+    )(order, middle, branch1, branch2, delta, cotangent, own, far, table, weight, weight)
+
+
+def packed_grad_kernel(order, normed_ref, far_ref, own_ref, grad_ref, sums_ref, normed_t):
+    step = pl.program_id(0)
+
+    @pl.when(step == 0)
+    def _():
+        normed_t[...] = turned(normed_ref[...])
+
+    block = jnp.where(step < 3, far_ref[0], own_ref[0])
+    grad_ref[...] = dot(normed_t[...], block).astype(BF16)
+    sums_ref[...] = jnp.broadcast_to(total_rows(block.astype(F32)), sums_ref.shape)
+
+
+def far_block(j, _):
+    return (jnp.minimum(j, 2), 0, 0)
+
+
+def own_block(j, _):
+    return (jnp.maximum(j - 3, 0), 0, 0)
+
+
+def packed_grad(order, normed, far, own):
+    tokens, width = normed.shape
+    half = width // 2
+    return pl.pallas_call(
+        packed_grad_kernel,
+        grid_spec=pltpu.PrefetchScalarGridSpec(
+            num_scalar_prefetch=1,
+            grid=(6,),
+            in_specs=[
+                whole((tokens, width)),
+                pl.BlockSpec((1, tokens, half), far_block),
+                pl.BlockSpec((1, tokens, half), own_block),
+            ],
+            out_specs=[
+                pl.BlockSpec((width, half), lambda j, order: (0, order[j])),
+                pl.BlockSpec((8, half), lambda j, order: (0, order[j])),
+            ],
+            scratch_shapes=[pltpu.VMEM((width, tokens), BF16)],
+        ),
+        out_shape=[
+            jax.ShapeDtypeStruct((width, 3 * width), BF16),
+            jax.ShapeDtypeStruct((8, 3 * width), F32),
+        ],
+        name="packed_grad",
+        **params_for(6 * tokens * width * width, 8 * tokens * width + 6 * width * width),
+    )(order, normed, far, own)
+
+
+def unproject_kernel(
+    order, x_ref, delta_middle_ref, table, far_ref, own_ref, weight_ref, out_ref, sums_ref, delta
+):
+    step = pl.program_id(0)
+
+    @pl.when(step == 0)
+    def _():
+        delta[...] = jnp.zeros_like(delta)
+
+    block = jnp.where(step < 3, far_ref[0], own_ref[0])
+    delta[...] += dot(block, weight_ref[...], NT)
+
+    @pl.when(step == pl.num_programs(0) - 1)
+    def _():
+        delta_normed = delta[...]
+        inner, gain_terms = normalize_back(
+            x_ref[...].astype(F32), table[GAIN1 : GAIN1 + 1, :], delta_normed
+        )
+        out_ref[...] = (delta_middle_ref[...] + inner).astype(BF16)
+        sums_ref[...] = jnp.zeros_like(sums_ref)
+        sums_ref[0:1, :] = total_rows(gain_terms)
+        sums_ref[1:2, :] = total_rows(delta_normed)
+
+
+def unproject(order, x, delta_middle, table, far, own, weight):
+    tokens, width = x.shape
+    half = width // 2
+    return pl.pallas_call(
+        unproject_kernel,
+        grid_spec=pltpu.PrefetchScalarGridSpec(
+            num_scalar_prefetch=1,
+            grid=(6,),
+            in_specs=[
+                whole((tokens, width)),
+                whole((tokens, width)),
+                whole(table.shape),
+                pl.BlockSpec((1, tokens, half), far_block),
+                pl.BlockSpec((1, tokens, half), own_block),
+                pl.BlockSpec((width, half), lambda j, order: (0, order[j])),
+            ],
+            out_specs=[whole((tokens, width)), whole((SUM_ROWS, width))],
+            scratch_shapes=[pltpu.VMEM((tokens, width), F32)],
+        ),
+        out_shape=[
+            jax.ShapeDtypeStruct((tokens, width), BF16),
+            jax.ShapeDtypeStruct((SUM_ROWS, width), F32),
+        ],
+        name="unproject",
+        **params_for(6 * tokens * width * width, 12 * tokens * width + 6 * width * width),
+    )(order, x, delta_middle, table, far, own, weight)
+
+
+def paired_body(
+    tokens, lengths, norm1_gain, norm1_bias, packed_weight, query_bias, value_bias, output_weight, output_bias,
+    layer_scale1, norm2_gain, norm2_bias, up_weight, up_bias, down_weight, down_bias, layer_scale2, cotangent,
+):
+    owners = lax.axis_size("fsdp")
+    images, local_len, width = tokens.shape
+    core = lax.rem(lax.axis_index("fsdp"), 2)
+    regroup = [(f * 2 + s, (f - f % 2 + s) * 2 + f % 2) for f in range(owners) for s in range(2)]
+    twin = [(f, f ^ 1) for f in range(owners)]
+
+    def regrouped(values):
+        return lax.ppermute(values, ("fsdp", "seq"), regroup)
+
+    def to_twin(values):
+        return lax.ppermute(values, "fsdp", twin)
+
+    x = regrouped(tokens.reshape(local_len, width))
+    valid_count = regrouped(lengths)
+    vectors = (
+        norm1_gain, norm1_bias, query_bias, value_bias, output_bias, layer_scale1, norm2_gain, norm2_bias,
+        down_bias, layer_scale2,
+    )
+    rows = norm1_gain.shape[0]
+    small = jnp.concatenate(vectors + (up_bias,))
+    first_rows = packed_weight.shape[0]
+    small_block = jnp.zeros((first_rows * LANES,), BF16).at[: small.shape[0]].set(small)
+    first = jnp.concatenate([packed_weight, small_block.reshape(first_rows, LANES)], axis=1)
+    first_full = lax.all_gather(first, "fsdp", axis=0, tiled=True)
+    small_full = first_full[:, 3 * width :].reshape(owners, first_rows * LANES)
+    table = small_full[:, : 10 * rows].reshape(owners, 10, rows).transpose(1, 0, 2).reshape(10, width)
+    table = jnp.pad(table, ((0, 6), (0, 0))).astype(F32)
+    up_shift = small_full[:, 10 * rows : small.shape[0]].reshape(1, -1).astype(F32)
+    output_full = lax.all_gather(output_weight, "fsdp", axis=0, tiled=True)
+    up_full = lax.all_gather(up_weight, "fsdp", axis=0, tiled=True)
+    down_full = lax.all_gather(down_weight, "fsdp", axis=0, tiled=True)
+
+    order = jnp.stack([1 - core, 3 - core, 5 - core, core, 2 + core, 4 + core]).astype(jnp.int32)
+    starts = jnp.stack([core, 1 - core]) * local_len
+    valid = jnp.clip(valid_count - starts, 0, local_len).astype(jnp.int32)
+
+    far_out, own_part, normed = project(order, x, table, first_full)
+    far_part = to_twin(far_out)
+    parts = [own_part, far_part]
+    (own_mix, far_mix_out), totals = attention(valid, parts, 352)
+    far_mix = to_twin(far_mix_out)
+    middle, branch1, normed2 = merge(order, x, own_mix, far_mix, table, output_full)
+    upstream = regrouped(cotangent.reshape(local_len, width))
+    branch2, delta_normed2, grad_up, grad_down, grad_up_shift = mlp(
+        normed2, upstream, table, up_full, up_shift, down_full, owners
+    )
+    output, delta_middle, own_grad, far_grad_out, grad_output, sums2 = unmerge(
+        order, middle, branch1, branch2, delta_normed2, upstream, own_mix, far_mix, table, output_full
+    )
+    output = regrouped(output).reshape(tokens.shape)
+    far_grad = to_twin(far_grad_out)
+    own_delta, far_delta_out = attention_back(
+        valid, parts, [own_mix, far_mix_out], [own_grad, far_grad], totals, 352
+    )
+    far_delta = to_twin(far_delta_out)
+    grad_packed, packed_sums = packed_grad(order, normed, far_delta, own_delta)
+    grad_x, sums1 = unproject(order, x, delta_middle, table, far_delta, own_delta, first_full)
+    grad_tokens = regrouped(grad_x).astype(F32).reshape(tokens.shape)
+
+    def owned(grad):
+        part = lax.psum_scatter(grad, "fsdp", scatter_dimension=0, tiled=True)
+        return part.astype(F32) + lax.ppermute(part, "seq", [(0, 1), (1, 0)]).astype(F32)
+
+    grad_up = owned(grad_up)
+    grad_down = owned(grad_down)[0].T
+    grad_output = owned(grad_output)
+    grad_packed = owned(grad_packed)
+    sums = jnp.concatenate(
+        [
+            sums1[0], sums1[1], packed_sums[0, :width], packed_sums[0, 2 * width :], sums2[5], sums2[4], sums2[2],
+            sums2[3], sums2[1], sums2[0], grad_up_shift[0],
+        ]
+    )
+    all_sums = lax.psum(sums, ("fsdp", "seq"))
+    me = lax.axis_index("fsdp")
+    mine = [lax.dynamic_slice(all_sums, (i * width + me * rows,), (rows,)) for i in range(10)]
+    each = up_bias.shape[0]
+    mine_up = lax.dynamic_slice(all_sums, (10 * width + me * each,), (each,))
+    return (
+        output, grad_tokens, mine[0], mine[1], grad_packed, mine[2], mine[3], grad_output, mine[4], mine[5],
+        mine[6], mine[7], grad_up, mine_up, grad_down, mine[8], mine[9],
+    )
+
+
 def solution(mesh):
     in_specs = (
         P("fsdp", "seq", None),
@@ -341,4 +1065,6 @@
         P("fsdp"),
         P("fsdp"),
     )
-    return jax.shard_map(body, mesh=mesh, in_specs=in_specs, out_specs=out_specs, check_vma=False)
+    paired = mesh.shape["seq"] == 2 and mesh.shape["fsdp"] % 2 == 0
+    chosen = paired_body if paired else general_body
+    return jax.shard_map(chosen, mesh=mesh, in_specs=in_specs, out_specs=out_specs, check_vma=False)

time: 1110 us -> 741 us (0.67)
  matrix products: 293 us -> 0 us
  Pallas kernels: 0 us -> 182 us
  blocking collectives: 169 us -> 50.7 us
  local copies, waits for them, and re-layouts: 130 us -> 20.1 us
  other arithmetic: 111 us -> 11.9 us
  waiting for transfers between devices: 362 us -> 414 us
  starting transfers between devices: 16.9 us -> 37.6 us
    dot_general x18 -> x0, matrix products: 293 us -> none  [the longest x4 66 us: matmul(): return jnp.dot(left, right, preferred_element_type=jnp.float32)]
    all_gather x4, waiting for transfers between devices: 0.06 us -> 194 us  [the longest x1 75.2 us: paired_body(): down_full = lax.all_gather(down_weight, 'fsdp', axis=0, tiled=True)]
    pallas_call x0 -> x8, Pallas kernels: none -> 182 us  [the longest x1 48.1 us: mlp(): pl.pallas_call(mlp_kernel, grid=(hidden // block,), in_specs=[whole((toke...]
    unnamed x2 -> x0, blocking collectives: 124 us -> none
    all_to_all x3 -> x0, waiting for transfers between devices: 101 us -> none  [the longest x1 58.9 us: body(): lax.all_to_all(delta_packed, 'seq', split_axis=1, concat_axis=3, tiled=True)]
    convert_element_type x27 -> x1, other arithmetic: 61.4 us -> 0.63 us  [paired_body(): table = jnp.pad(table, ((0, 6), (0, 0))).astype(F32)]
    reduce_scatter x4, waiting for transfers between devices: 258 us -> 198 us  [owned(): part = lax.psum_scatter(grad, 'fsdp', scatter_dimension=0, tiled=True)]
    psum x1, blocking collectives: 4.98 us -> 50.7 us  [paired_body(): all_sums = lax.psum(sums, ('fsdp', 'seq'))]
  transfers between devices with their start and end apart: 12 -> 21, of which waited for: 5 -> 9; matrix products, arithmetic and copies ran while one was open for 27% -> 2% of each run, Pallas kernels for 0% -> 16%
where the time goes in v1:
time: 741 us; the launch traced here: 731 us
  waiting for transfers between devices  414 us (56%)
  Pallas kernels  182 us (25%)
  blocking collectives  50.7 us (7%)
  starting transfers between devices  37.6 us (5%)
  local copies, waits for them, and re-layouts  20.1 us (3%)
  between operations  14.8 us (2%)
  other arithmetic  11.9 us (2%)
    reduce_scatter x4, waiting for transfers between devices, owned(): part = lax.psum_scatter(grad, 'fsdp', scatter_dimension=0, tiled=True)  198 us
    all_gather x1, waiting for transfers between devices, paired_body(): down_full = lax.all_gather(down_weight, 'fsdp', axis=0, tiled=True)  75.2 us
    all_gather x1, waiting for transfers between devices, paired_body(): first_full = lax.all_gather(first, 'fsdp', axis=0, tiled=True)  61.5 us
    all_gather x1, waiting for transfers between devices, paired_body(): up_full = lax.all_gather(up_weight, 'fsdp', axis=0, tiled=True)  57.1 us
    psum x1, blocking collectives, paired_body(): all_sums = lax.psum(sums, ('fsdp', 'seq'))  50.7 us
    pallas_call x1, Pallas kernels, mlp(): pl.pallas_call(mlp_kernel, grid=(hidden // block,), in_specs=[whole((toke...  48.1 us
    pallas_call x1, Pallas kernels, attention_back(): pl.pallas_call(functools.partial(attend_back_kernel, pieces=pieces, block...  45.9 us
    pallas_call x1, Pallas kernels, attention(): pl.pallas_call(functools.partial(attend_kernel, pieces=pieces, block=bloc...  28.3 us
  transfers between devices with their start and end apart: 21, of which 9 were waited for; matrix products, arithmetic and copies ran while one was open for 2% of the time, Pallas kernels for 16%

profile of v1, /device:TPU:0, one launch (start us, length us, event | category | flops | bytes accessed | tf_op | source)
XLA Modules:
  0.0 731.4 jit_solution(8187065102545561533)
XLA Ops:
  7.2 7.4 %concatenate.11 = bf16[896]{0:T(1024)(128)(2,1)S(1)} concatenate(bf16[64]{0:T(256)(128)(2,1)} %param.22, bf16[64]{0:T(256)(128)(2,1)} %param.23, bf16[64]{0:T(256)(128)(2,1)} %param.25, bf16[64]{0:T(256)(128)(2,1)} %param.26, bf16[64]{0:T(256)(128)(2,1)} %param.28, bf16[64]{0:T(256)(128)(2,1)} %param.29, bf16[64]{0:T(256)(128)(2,1)} %param.30, bf16[64]{0:T(256)(128)(2,1)} %param.31, ...), dimensions={0} | concatenate | bytes 3584 | tf_op jit(solution)/shard_map/concatenate | solution.py:963
  14.7 1.8 pad_maximum_fusion
  16.5 0.0 all-gather.7.cloned.1.call-start
  16.5 0.7 all-gather.7.cloned.1.call-update
  17.3 0.7 all-gather.9.cloned.1.call-update
  18.0 0.5 all-gather.11.cloned.1.call-update
  18.6 2.0 collective-permute-start
  20.6 0.6 stack.32.order
  21.2 61.5 %all-gather.5.cloned.1.call-done.weight_ref = bf16[1024,3200]{1,0:T(8,128)(2,1)} async-done(((bf16[64,3200]{1,0:T(8,128)(2,1)}), bf16[1024,3200]{1,0:T(8,128)(2,1)}) %all-gather.5.cloned.1.call-update) | async-done | bytes 6553616 | tf_op jit(solution)/shard_map/all_gather | solution.py:967
  82.7 1.0 slice.63
  83.7 0.1 reshape.100
  83.8 0.1 reshape.101
  83.9 0.1 reshape.102
  84.1 0.6 pad_convert_fusion.all_ref.half_ref.table
  84.7 1.1 copy-done.1
  85.8 12.0 %project.1 = (bf16[3,688,512]{2,1,0:T(8,128)(2,1)}, bf16[3,688,512]{2,1,0:T(8,128)(2,1)}, bf16[688,1024]{1,0:T(8,128)(2,1)}) custom-call(s32[6]{0:T(128)} %stack.32.order, bf16[688,1024]{1,0:T(8,128)(2,1)} %copy-done.1, f32[16,1024]{1,0:T(8,128)} %pad_convert_fusion.all_ref.half_ref.table, f32[16,1024]{1,0:T(8,128)} %pad_convert_fusion.all_ref.half_ref.table, ...), custom_call_target="tpu_custom_call" | custom-call | flops 4328521728 | bytes 14745600 | tf_op jit(solution)/shard_map/project/pallas_call | solution.py:400
  97.8 0.3 collective-permute-start.2
  98.2 1.9 collective-permute-start.1
  100.0 2.0 collective-permute-start.4
  102.0 1.2 fusion.1.valid
  103.2 28.3 %attend.1 = (bf16[688,512]{1,0:T(8,128)(2,1)}, bf16[688,512]{1,0:T(8,128)(2,1)}, f32[688,128]{1,0:T(8,128)}, f32[688,128]{1,0:T(8,128)}) custom-call(s32[2]{0:T(128)} %fusion.1.valid, bf16[3,688,512]{2,1,0:T(8,128)(2,1)} %get-tuple-element.56.refs_0_, bf16[3,688,512]{2,1,0:T(8,128)(2,1)} %collective-permute-done.2.refs_1_), custom_call_target="tpu_custom_call" | custom-call | flops 16240345088 | bytes 5636096 | tf_op jit(solution)/shard_map/attend/pallas_call | solution.py:489
  131.6 2.0 collective-permute-start.3
  133.6 0.6 copy.39
  134.2 1.4 collective-permute-done.3.far_ref
  135.6 0.8 copy-done
  136.4 7.1 merge.1
  143.6 57.1 %all-gather.9.cloned.1.call-done.up_ref = bf16[1024,4096]{1,0:T(8,128)(2,1)} async-done(((bf16[64,4096]{1,0:T(8,128)(2,1)}), bf16[1024,4096]{1,0:T(8,128)(2,1)}) %all-gather.9.cloned.1.call-update) | async-done | bytes 8388624 | tf_op jit(solution)/shard_map/all_gather | solution.py:973
  200.7 75.2 %all-gather.11.cloned.1.call-done.down_ref = bf16[4096,1024]{1,0:T(8,128)(2,1)} async-done(((bf16[256,1024]{1,0:T(8,128)(2,1)}), bf16[4096,1024]{1,0:T(8,128)(2,1)}) %all-gather.11.cloned.1.call-update) | async-done | bytes 8388624 | tf_op jit(solution)/shard_map/all_gather | solution.py:974
  275.9 48.1 %mlp.1 = (f32[688,1024]{1,0:T(8,128)}, f32[688,1024]{1,0:T(8,128)}, bf16[1024,4096]{1,0:T(8,128)(2,1)}, bf16[16,1024,256]{2,1,0:T(8,128)(2,1)}, f32[1,4096]{1,0:T(1,128)}) custom-call(bf16[688,1024]{1,0:T(8,128)(2,1)} %get-tuple-element.62.normed_ref, bf16[688,1024]{1,0:T(8,128)(2,1)} %copy-done.2, f32[16,1024]{1,0:T(8,128)} %pad_convert_fusion.all_ref.half_ref.table, ...), custom_call_target="tpu_custom_call" | custom-call | flops 34628173824 | bytes 42008576 | tf_op jit(solution)/shard_map/mlp/pallas_call | solution.py:715
  324.0 14.5 %unmerge.1 = (bf16[688,1024]{1,0:T(8,128)(2,1)}, f32[688,1024]{1,0:T(8,128)}, bf16[688,512]{1,0:T(8,128)(2,1)}, bf16[688,512]{1,0:T(8,128)(2,1)}, bf16[1024,1024]{1,0:T(8,128)(2,1)}, /*index=5*/f32[8,1024]{1,0:T(8,128)}) custom-call(s32[6]{0:T(128)} %stack.32.order, f32[688,1024]{1,0:T(8,128)} %get-tuple-element.60.middle_ref, ...), custom_call_target="tpu_custom_call" | custom-call | flops 2885681152 | bytes 25329664 | tf_op jit(solution)/shard_map/unmerge/pallas_call | solution.py:812
  338.5 0.3 collective-permute-start.6
  338.9 0.0 reduce-scatter.5.cloned.1.call-start
  338.9 2.0 collective-permute-done.6.refs_5_
  341.0 0.9 copy-done.9
  341.8 45.9 %attend_back.1 = (bf16[3,688,512]{2,1,0:T(8,128)(2,1)}, bf16[3,688,512]{2,1,0:T(8,128)(2,1)}) custom-call(s32[2]{0:T(128)} %fusion.1.valid, bf16[3,688,512]{2,1,0:T(8,128)(2,1)} %get-tuple-element.56.refs_0_, bf16[3,688,512]{2,1,0:T(8,128)(2,1)} %collective-permute-done.2.refs_1_, bf16[688,512]{1,0:T(8,128)(2,1)} %get-tuple-element.58.own_ref.refs_2_, ...), custom_call_target="tpu_custom_call" | custom-call | flops 30450647040 | bytes 11272192 | tf_op jit(solution)/shard_map/attend_back/pallas_call | solution.py:597
  387.7 0.3 collective-permute-start.7
  388.0 4.1 collective-permute-done.7.far_ref
  392.1 1.3 copy-done.7
  393.4 11.2 %packed_grad.1 = (bf16[1024,3072]{1,0:T(8,128)(2,1)}, f32[8,3072]{1,0:T(8,128)}) custom-call(s32[6]{0:T(128)} %stack.32.order, bf16[688,1024]{1,0:T(8,128)(2,1)} %get-tuple-element.75.normed_ref, bf16[3,688,512]{2,1,0:T(8,128)(2,1)} %copy-done.7, bf16[3,688,512]{2,1,0:T(8,128)(2,1)} %get-tuple-element.72.own_ref), custom_call_target="tpu_custom_call" | custom-call | flops 4328521728 | bytes 11927552 | tf_op jit(solution)/shard_map/packed_grad/pallas_call | solution.py:863
  404.6 0.7 reduce-scatter.9.cloned.1.call-update
  405.4 0.7 reduce-scatter.11.cloned.1.call-update
  406.1 0.6 copy-done.8
  406.7 0.7 collective-permute-start.5
  407.5 15.1 %unproject.1 = (bf16[688,1024]{1,0:T(8,128)(2,1)}, f32[8,1024]{1,0:T(8,128)}) custom-call(s32[6]{0:T(128)} %stack.32.order, bf16[688,1024]{1,0:T(8,128)(2,1)} %copy-done.1, f32[688,1024]{1,0:T(8,128)} %get-tuple-element.66.delta_middle_ref, f32[16,1024]{1,0:T(8,128)} %pad_convert_fusion.all_ref.half_ref.table, bf16[3,688,512]{2,1,0:T(8,128)(2,1)} %copy-done.7, ...), custom_call_target="tpu_custom_call" | custom-call | flops 4328521728 | bytes 14745600 | tf_op jit(solution)/shard_map/unproject/pallas_call | solution.py:915
  422.6 12.4 %collective-permute-start.8 = (bf16[688,1024]{1,0:T(8,128)(2,1)}, bf16[688,1024]{1,0:T(8,128)(2,1)}, u32[]{:S(2)}, u32[]{:S(2)}) collective-permute-start(bf16[688,1024]{1,0:T(8,128)(2,1)} %get-tuple-element.73), channel_id=1, source_target_pairs={{0,0},{1,2},{2,1},{3,3},{4,4},{5,6},{6,5},{7,7},{8,8},{9,10},{10,9... | collective-permute-start | bytes 4227080 | tf_op jit(solution)/shard_map/ppermute | solution.py:951
  435.0 0.8 fusion.5
  435.8 0.8 fusion.2
  436.7 10.1 %collective-permute-start.10 = (bf16[64,1024]{1,0:T(8,128)(2,1)}, bf16[64,1024]{1,0:T(8,128)(2,1)S(1)}, u32[]{:S(2)}, u32[]{:S(2)}) collective-permute-start(bf16[64,1024]{1,0:T(8,128)(2,1)} %reduce-scatter.7.cloned.1.call-done), channel_id=1, source_target_pairs={{0,1},{1,0},{2,3},{3,2},{4,5},{5,4},{6,7},{7,6},{8,9},{9,8},{10,11... | collective-permute-start | bytes 393224 | tf_op jit(solution)/shard_map/ppermute | solution.py:1005
  446.8 50.7 %psum.7 = f32[14336]{0:T(1024)S(1)} all-reduce(f32[14336]{0:T(1024)S(1)} %constant_dynamic-update-slice_fusion), channel_id=1, replica_groups=mesh['fsdp'=16,'seq'=2] {'fsdp','seq'}, use_global_device_ids=true, to_apply=%region_0.0 | all-reduce | flops 14336 | bytes 114688 | tf_op jit(solution)/shard_map/psum | solution.py:1017
  497.5 0.6 dynamic_slice.41
  498.1 0.6 fusion.3
  498.8 2.3 collective-permute-start.9
  501.1 1.7 convert_add_fusion.2
  502.7 3.5 bitcast_convert_fusion
  506.2 90.9 %reduce-scatter.9.cloned.1.call-done = bf16[64,4096]{1,0:T(8,128)(2,1)} async-done(((bf16[1024,4096]{1,0:T(8,128)(2,1)}), bf16[64,4096]{1,0:T(8,128)(2,1)}) %reduce-scatter.9.cloned.1.call-update) | async-done | bytes 524304 | tf_op jit(solution)/shard_map/reduce_scatter | solution.py:1004
  597.1 1.5 collective-permute-start.11
  598.6 107.0 %reduce-scatter.11.cloned.1.call-done = bf16[1,1024,256]{2,1,0:T(8,128)(2,1)} async-done(((bf16[16,1024,256]{2,1,0:T(8,128)(2,1)}), bf16[1,1024,256]{2,1,0:T(8,128)(2,1)}) %reduce-scatter.11.cloned.1.call-update) | async-done | bytes 524304 | tf_op jit(solution)/shard_map/reduce_scatter | solution.py:1004
  705.5 1.5 collective-permute-start.12
  707.0 1.0 convert_add_fusion.1
  708.0 11.5 %collective-permute-done.12 = bf16[1,1024,256]{2,1,0:T(8,128)(2,1)S(1)} collective-permute-done((bf16[1,1024,256]{2,1,0:T(8,128)(2,1)}, bf16[1,1024,256]{2,1,0:T(8,128)(2,1)S(1)}, u32[]{:S(2)}, u32[]{:S(2)}) %collective-permute-start.12) | collective-permute-done | bytes 524320 | tf_op jit(solution)/shard_map/ppermute | solution.py:1005
  719.5 1.2 add_bitcast_fusion
  720.6 1.3 copy.38
  721.9 1.1 convert_add_fusion
  723.0 1.1 copy.51
  (52 shorter events, 0.4 us)
Async XLA Ops:
  7.2 75.5 %all-gather.5.cloned.1.call-start = ((), (), s32[]{:S(2)}) async-start(), calls=%async_computation.4 | async-start | bytes 6963200 | tf_op jit(solution)/shard_map/all_gather | solution.py:967
  16.5 117.8 %all-gather.7.cloned.1.call-start = ((), (), s32[]{:S(2)}) async-start(), calls=%async_computation.5 | async-start | bytes 2228224 | tf_op jit(solution)/shard_map/all_gather | solution.py:972
  17.2 183.5 %all-gather.9.cloned.1.call-start = ((), (), s32[]{:S(2)}) async-start(), calls=%async_computation.6 | async-start | bytes 8912896 | tf_op jit(solution)/shard_map/all_gather | solution.py:973
  18.0 258.0 %all-gather.11.cloned.1.call-start = ((), (), s32[]{:S(2)}) async-start(), calls=%async_computation.7 | async-start | bytes 8912896 | tf_op jit(solution)/shard_map/all_gather | solution.py:974
  18.5 418.2 %reduce-scatter.7.cloned.1.call-start = ((), (), s32[]{:S(2)}) async-start(), calls=%async_computation.9 | async-start | bytes 2228224 | tf_op jit(solution)/shard_map/reduce_scatter | solution.py:1004
  18.6 66.1 %collective-permute-start = (bf16[688,1024]{1,0:T(8,128)(2,1)}, bf16[688,1024]{1,0:T(8,128)(2,1)S(1)}, u32[]{:S(2)}, u32[]{:S(2)}) collective-permute-start(bf16[688,1024]{1,0:T(8,128)(2,1)} %bitcast.6), channel_id=1, source_target_pairs={{0,0},{1,2},{2,1},{3,3},{4,4},{5,6},{6,5},{7,7},{8,8},{9,10},{10,9... | collective-permute-start | bytes 4227080 | tf_op jit(solution)/shard_map/ppermute | solution.py:951
  84.7 1.1 copy-start.1
  97.8 5.4 collective-permute-start.2
  98.2 3.9 collective-permute-start.1
  100.0 43.6 %collective-permute-start.4 = (bf16[688,1024]{1,0:T(8,128)(2,1)}, bf16[688,1024]{1,0:T(8,128)(2,1)S(1)}, u32[]{:S(2)}, u32[]{:S(2)}) collective-permute-start(bf16[688,1024]{1,0:T(8,128)(2,1)} %bitcast.49), channel_id=1, source_target_pairs={{0,0},{1,2},{2,1},{3,3},{4,4},{5,6},{6,5},{7,7},{8,8},{9,10},{10,9... | collective-permute-start | bytes 4227080 | tf_op jit(solution)/shard_map/ppermute | solution.py:951
  131.6 4.0 collective-permute-start.3
  135.6 0.9 copy-start
  143.6 132.3 %copy-start.2 = (bf16[688,1024]{1,0:T(8,128)(2,1)}, bf16[688,1024]{1,0:T(8,128)(2,1)S(1)}, u32[]{:S(2)}) copy-start(bf16[688,1024]{1,0:T(8,128)(2,1)S(1)} %collective-permute-done.4.cotangent_ref) | copy-start | bytes 4227076
  338.5 2.4 collective-permute-start.6
  338.9 159.9 %reduce-scatter.5.cloned.1.call-start = ((), (), s32[]{:S(2)}) async-start(), calls=%async_computation.8 | async-start | bytes 6684672 | tf_op jit(solution)/shard_map/reduce_scatter | solution.py:1004
  341.0 0.9 copy-start.9
  387.7 4.4 collective-permute-start.7
  392.1 1.3 copy-start.7
  404.6 192.5 %reduce-scatter.9.cloned.1.call-start = ((), (), s32[]{:S(2)}) async-start(), calls=%async_computation.10 | async-start | bytes 8912896 | tf_op jit(solution)/shard_map/reduce_scatter | solution.py:1004
  405.3 300.2 %reduce-scatter.11.cloned.1.call-start = ((), (), s32[]{:S(2)}) async-start(), calls=%async_computation.11 | async-start | bytes 8912896 | tf_op jit(solution)/shard_map/reduce_scatter | solution.py:1004
  405.4 1.4 copy-start.8
  405.4 2.1 copy-start.5
  406.7 0.8 collective-permute-start.5
  407.5 29.1 %copy-start.6 = (f32[1,4096]{1,0:T(1,128)S(1)}, f32[1,4096]{1,0:T(1,128)}, u32[]{:S(2)}) copy-start(f32[1,4096]{1,0:T(1,128)} %get-tuple-element.78) | copy-start | bytes 49156
  422.6 80.1 %collective-permute-start.8 = (bf16[688,1024]{1,0:T(8,128)(2,1)}, bf16[688,1024]{1,0:T(8,128)(2,1)}, u32[]{:S(2)}, u32[]{:S(2)}) collective-permute-start(bf16[688,1024]{1,0:T(8,128)(2,1)} %get-tuple-element.73), channel_id=1, source_target_pairs={{0,0},{1,2},{2,1},{3,3},{4,4},{5,6},{6,5},{7,7},{8,8},{9,10},{10,9... | collective-permute-start | bytes 4227080 | tf_op jit(solution)/shard_map/ppermute | solution.py:951
  436.7 64.4 %collective-permute-start.10 = (bf16[64,1024]{1,0:T(8,128)(2,1)}, bf16[64,1024]{1,0:T(8,128)(2,1)S(1)}, u32[]{:S(2)}, u32[]{:S(2)}) collective-permute-start(bf16[64,1024]{1,0:T(8,128)(2,1)} %reduce-scatter.7.cloned.1.call-done), channel_id=1, source_target_pairs={{0,1},{1,0},{2,3},{3,2},{4,5},{5,4},{6,7},{7,6},{8,9},{9,8},{10,11... | collective-permute-start | bytes 393224 | tf_op jit(solution)/shard_map/ppermute | solution.py:1005
  498.8 208.3 %collective-permute-start.9 = (bf16[64,3072]{1,0:T(8,128)(2,1)}, bf16[64,3072]{1,0:T(8,128)(2,1)S(1)}, u32[]{:S(2)}, u32[]{:S(2)}) collective-permute-start(bf16[64,3072]{1,0:T(8,128)(2,1)} %reduce-scatter.5.cloned.1.call-done), channel_id=1, source_target_pairs={{0,1},{1,0},{2,3},{3,2},{4,5},{5,4},{6,7},{7,6},{8,9},{9,8},{10,11... | collective-permute-start | bytes 1179656 | tf_op jit(solution)/shard_map/ppermute | solution.py:1005
  502.7 204.3 %copy-start.4 = (bf16[64,3072]{1,0:T(8,128)(2,1)S(1)}, bf16[64,3072]{1,0:T(8,128)(2,1)}, u32[]{:S(2)}) copy-start(bf16[64,3072]{1,0:T(8,128)(2,1)} %reduce-scatter.5.cloned.1.call-done) | copy-start | bytes 1179652
  597.1 124.9 %collective-permute-start.11 = (bf16[64,4096]{1,0:T(8,128)(2,1)}, bf16[64,4096]{1,0:T(8,128)(2,1)S(1)}, u32[]{:S(2)}, u32[]{:S(2)}) collective-permute-start(bf16[64,4096]{1,0:T(8,128)(2,1)} %reduce-scatter.9.cloned.1.call-done), channel_id=1, source_target_pairs={{0,1},{1,0},{2,3},{3,2},{4,5},{5,4},{6,7},{7,6},{8,9},{9,8},{10,11... | collective-permute-start | bytes 1572872 | tf_op jit(solution)/shard_map/ppermute | solution.py:1005
  705.5 13.9 %collective-permute-start.12 = (bf16[1,1024,256]{2,1,0:T(8,128)(2,1)}, bf16[1,1024,256]{2,1,0:T(8,128)(2,1)S(1)}, u32[]{:S(2)}, u32[]{:S(2)}) collective-permute-start(bf16[1,1024,256]{2,1,0:T(8,128)(2,1)} %reduce-scatter.11.cloned.1.call-done), channel_id=1, source_target_pairs={{0,1},{1,0},{2,3},{3,2},{4,5},{5,4},{6,7},{7,6},{8,9},{9,8},{10,11... | collective-permute-start | bytes 1572872 | tf_op jit(solution)/shard_map/ppermute | solution.py:1005
  708.0 14.0 %copy-start.3 = (bf16[64,4096]{1,0:T(8,128)(2,1)S(1)}, bf16[64,4096]{1,0:T(8,128)(2,1)}, u32[]{:S(2)}) copy-start(bf16[64,4096]{1,0:T(8,128)(2,1)} %reduce-scatter.9.cloned.1.call-done) | copy-start | bytes 1572868
Sparse Core Ops, SparseCore 0:
  16.6 66.0 all-gather.4
  84.9 39.9 all-gather.6
  127.0 73.6 all-gather.8
  202.8 73.1 all-gather.10
  339.0 59.8 reduce-scatter.6
  404.7 84.3 reduce-scatter.4
  493.2 103.8 reduce-scatter.8
  601.1 104.3 reduce-scatter.10

commit v2 on v1

--- a/solution.py
+++ b/solution.py
@@ -2,6 +2,7 @@
 
 import jax
 import jax.numpy as jnp
+import numpy as np
 from jax import lax
 from jax.experimental import pallas as pl
 from jax.experimental.pallas import tpu as pltpu
@@ -321,7 +322,7 @@
 
 
 def turned(values):
-    return values.astype(F32).T.astype(BF16)
+    return values.T
 
 
 def lane_ids(rows):
@@ -335,7 +336,11 @@
     return high, mid, rest - mid
 
 
-def params_for(flops, nbytes, transcendentals=0):
+LONG, SHORT = 16.0, 1 / 64
+
+
+def params_for(flops, nbytes, transcendentals=0, weight=1.0):
+    flops, nbytes, transcendentals = (int(weight * count) for count in (flops, nbytes, transcendentals))
     return dict(
         compiler_params=pltpu.CompilerParams(vmem_limit_bytes=VMEM_LIMIT),
         cost_estimate=pl.CostEstimate(
@@ -368,60 +373,129 @@
     return jnp.sum(values, axis=0, keepdims=True)
 
 
-def project_kernel(order, x_ref, all_ref, half_ref, weight_ref, other_ref, own_ref, normed_ref):
+VECTORS = 10
+
+
+def pack_kernel(place, weight_ref, up_ref, down_ref, output_ref, *refs):
+    vector_refs, shift_ref = refs[:VECTORS], refs[VECTORS]
+    first_ref, rest_ref = refs[VECTORS + 1 :]
+    rows, width = weight_ref.shape
+    first_ref[:, :width] = weight_ref[...]
+    first_ref[:, width:] = jnp.zeros((rows, LANES), BF16)
+    for i, ref in enumerate(vector_refs):
+        values = ref[...].astype(F32).reshape(1, -1)
+        empty = jnp.zeros_like(values)
+        first, second = jnp.concatenate([values, empty], 1), jnp.concatenate([empty, values], 1)
+        first_ref[i : i + 1, width:] = jnp.where(place[CORE] == 0, first, second).astype(BF16)
+    shift = shift_ref[...].astype(F32).reshape(-1, LANES)
+    first_ref[VECTORS : VECTORS + shift.shape[0], width:] = shift.astype(BF16)
+    at = 0
+    for ref in (up_ref, down_ref, output_ref):
+        for g in range(ref.shape[0] // rows):
+            rest_ref[:, at : at + ref.shape[1]] = ref[g * rows : (g + 1) * rows, :]
+            at += ref.shape[1]
+
+
+def pack(place, weight, up, down, output, vectors, up_shift):
+    in_vmem = pl.BlockSpec(memory_space=pltpu.VMEM)
+    rows, width = weight.shape
+    others = (up.size + down.size + output.size) // rows
+    return pl.pallas_call(
+        pack_kernel,
+        in_specs=[pl.BlockSpec(memory_space=pltpu.SMEM)] + [in_vmem] * (VECTORS + 5),
+        out_specs=[in_vmem, in_vmem],
+        out_shape=[
+            jax.ShapeDtypeStruct((rows, width + LANES), BF16),
+            jax.ShapeDtypeStruct((rows, others), BF16),
+        ],
+        name="pack",
+        **params_for(0, 4 * rows * (width + others)),
+    )(place, weight, up, down, output, *vectors, up_shift)
+
+
+CORE, CHIPS = 6, 7
+
+
+def project_kernel(place, x_ref, *refs, chips):
+    own_refs, far_refs = refs[:chips], refs[chips : 2 * chips]
+    far_out_ref, own_ref, normed_ref, weight_ref, table_ref, up_ref = refs[2 * chips :]
     step = pl.program_id(0)
+    rows, block = own_refs[0].shape[0], weight_ref.shape[1]
+    packed = own_refs[0].shape[1] - LANES
+    core = place[CORE]
 
     @pl.when(step == 0)
     def _():
+        vector = lax.broadcasted_iota(jnp.int32, (table_ref.shape[0], LANES), 0) < VECTORS
+        each = up_ref.shape[1] // (2 * chips)
+        for k in range(chips):
+            chip = place[CHIPS + k]
+            own = own_refs[k][: table_ref.shape[0], packed:].astype(F32)
+            far = far_refs[k][: table_ref.shape[0], packed:].astype(F32)
+            at = pl.ds(pl.multiple_of(chip * LANES, LANES), LANES)
+            table_ref[:, at] = jnp.where(vector, own + far, 0.0)
+            for part, side in ((own, core), (far, 1 - core)):
+                for r in range(each // LANES):
+                    at = pl.multiple_of((2 * chip + side) * each + r * LANES, LANES)
+                    up_ref[:, pl.ds(at, LANES)] = part[VECTORS + r : VECTORS + r + 1, :]
         normed_ref[...] = normalize(
-            x_ref[...].astype(F32), all_ref[GAIN1 : GAIN1 + 1, :], all_ref[SHIFT1 : SHIFT1 + 1, :]
+            x_ref[...].astype(F32), table_ref[GAIN1 : GAIN1 + 1, :], table_ref[SHIFT1 : SHIFT1 + 1, :]
         ).astype(BF16)
 
+    columns = pl.ds(pl.multiple_of(place[step] * block, block), block)
+    for k in range(chips):
+        start = 2 * place[CHIPS + k]
+        weight_ref[pl.ds(pl.multiple_of((start + core) * rows, rows), rows), :] = own_refs[k][:, columns]
+        weight_ref[pl.ds(pl.multiple_of((start + 1 - core) * rows, rows), rows), :] = far_refs[k][:, columns]
     kind = lax.rem(step, 3)
+    side = pl.ds(pl.multiple_of(lax.rem(place[step], 2) * block, block), block)
     shift = jnp.where(
         kind == 0,
-        half_ref[QUERY : QUERY + 1, :],
-        jnp.where(kind == 2, half_ref[VALUE : VALUE + 1, :], 0.0),
-    )
-    block = (dot(normed_ref[...], weight_ref[...]) + shift).astype(BF16)
+        table_ref[QUERY : QUERY + 1, side],
+        jnp.where(kind == 2, table_ref[VALUE : VALUE + 1, side], 0.0),
+    )
+    result = (dot(normed_ref[...], weight_ref[...]) + shift).astype(BF16)
 
     @pl.when(step < 3)
     def _():
-        other_ref[0] = block
+        far_out_ref[0] = result
 
     @pl.when(step >= 3)
     def _():
-        own_ref[0] = block
-
-
-def project(order, x, table, weight):
+        own_ref[0] = result
+
+
+def project(place, x, own_pieces, far_pieces, hidden):
+    chips = len(own_pieces)
     tokens, width = x.shape
     half = width // 2
+    piece = own_pieces[0].shape
     return pl.pallas_call(
-        project_kernel,
+        functools.partial(project_kernel, chips=chips),
         grid_spec=pltpu.PrefetchScalarGridSpec(
             num_scalar_prefetch=1,
             grid=(6,),
-            in_specs=[
+            in_specs=[whole((tokens, width))] + [whole(piece)] * 2 * chips,
+            out_specs=[
+                pl.BlockSpec((1, tokens, half), lambda j, _: (jnp.minimum(j, 2), 0, 0)),
+                pl.BlockSpec((1, tokens, half), lambda j, _: (jnp.maximum(j - 3, 0), 0, 0)),
                 whole((tokens, width)),
-                whole(table.shape),
-                pl.BlockSpec((table.shape[0], half), lambda j, order: (0, lax.rem(order[j], 2))),
-                pl.BlockSpec((width, half), lambda j, order: (0, order[j])),
-            ],
-            out_specs=[
-                pl.BlockSpec((1, tokens, half), lambda j, order: (jnp.minimum(j, 2), 0, 0)),
-                pl.BlockSpec((1, tokens, half), lambda j, order: (jnp.maximum(j - 3, 0), 0, 0)),
-                whole((tokens, width)),
+                pl.BlockSpec((width, half), lambda j, place: (0, place[j])),
+                whole((16, width)),
+                whole((1, hidden)),
             ],
         ),
         out_shape=[
             jax.ShapeDtypeStruct((3, tokens, half), BF16),
             jax.ShapeDtypeStruct((3, tokens, half), BF16),
             jax.ShapeDtypeStruct((tokens, width), BF16),
+            jax.ShapeDtypeStruct((width, 3 * width), BF16),
+            jax.ShapeDtypeStruct((16, width), F32),
+            jax.ShapeDtypeStruct((1, hidden), F32),
         ],
         name="project",
-        **params_for(6 * tokens * width * width, 12 * tokens * width + 6 * width * width),
-    )(order, x, table, table, weight)
+        **params_for(6 * tokens * width * width, 12 * tokens * width + 12 * width * width),
+    )(place, x, *own_pieces, *far_pieces)
 
 
 def padded_len(count, block):
@@ -510,12 +584,12 @@
     return outs[:pieces], outs[pieces:]
 
 
-def attend_back_kernel(valid, *refs, pieces, block, scale):
+def attend_back_kernel(valid, *refs, pieces, block, scale, first):
     in_refs, mix_refs = refs[:pieces], refs[pieces : 2 * pieces]
     grad_refs, total_refs = refs[2 * pieces : 3 * pieces], refs[3 * pieces : 4 * pieces]
-    out_refs = refs[4 * pieces : 5 * pieces]
-    keys, values, queries, grads, queries_t, grads_t, dq, dk_t, dv_t = refs[5 * pieces :]
-    pair = pl.program_id(0)
+    out_refs = refs[-9 - pieces : -9]
+    keys, values, queries, grads, queries_t, grads_t, dq, dk_t, dv_t = refs[-9:]
+    pair = first + pl.program_id(0)
     size = in_refs[0].shape[1]
     count, padded = pieces * size, keys.shape[0]
     blocks = padded // block
@@ -587,19 +661,20 @@
         out_refs[i][2] = dv[at, :].astype(BF16)
 
 
-def attention_back(valid, parts, mixtures, grads, totals, block):
+def attention_back(valid, parts, mixtures, grads, totals, block, first, pairs, into, after):
     pieces = len(parts)
     _, size, width = parts[0].shape
-    pairs = width // LANES
     padded = padded_len(pieces * size, block)
-    triple = pl.BlockSpec((3, size, LANES), lambda h, _: (0, 0, h))
-    single = pl.BlockSpec((size, LANES), lambda h, _: (0, h))
+    triple = pl.BlockSpec((3, size, LANES), lambda h, _: (0, 0, first + h))
+    single = pl.BlockSpec((size, LANES), lambda h, _: (0, first + h))
+    in_specs = [triple] * pieces + [single] * 2 * pieces + [whole((size, LANES))] * pieces
+    aliases = {1 + len(in_specs) + i: i for i in range(len(into))}
     return pl.pallas_call(
-        functools.partial(attend_back_kernel, pieces=pieces, block=block, scale=HD**-0.5),
+        functools.partial(attend_back_kernel, pieces=pieces, block=block, scale=HD**-0.5, first=first),
         grid_spec=pltpu.PrefetchScalarGridSpec(
             num_scalar_prefetch=1,
             grid=(pairs,),
-            in_specs=[triple] * pieces + [single] * 2 * pieces + [whole((size, LANES))] * pieces,
+            in_specs=in_specs + [pl.BlockSpec(memory_space=pl.ANY)] * (len(into) + len(after)),
             out_specs=[triple] * pieces,
             scratch_shapes=[
                 pltpu.VMEM((padded, 2 * LANES), BF16),
@@ -614,12 +689,13 @@
             ],
         ),
         out_shape=[jax.ShapeDtypeStruct((3, size, width), BF16)] * pieces,
+        input_output_aliases=aliases,
         name="attend_back",
-        **params_for(30 * pairs * LANES * padded * padded, 16 * size * width * pieces, pairs * 2 * padded * padded),
-    )(valid, *parts, *mixtures, *grads, *totals)
-
-
-def merge_kernel(order, x_ref, own_ref, far_ref, table, own_w, far_w, middle_ref, branch_ref, normed_ref):
+        **params_for(30 * pairs * LANES * padded * padded, 16 * size * LANES * pairs * pieces, pairs * 2 * padded * padded, weight=LONG),
+    )(valid, *parts, *mixtures, *grads, *totals, *into, *after)
+
+
+def merge_kernel(place, x_ref, own_ref, far_ref, table, own_w, far_w, middle_ref, branch_ref, normed_ref):
     branch = dot(own_ref[...], own_w[...]) + dot(far_ref[...], far_w[...])
     branch += table[OUT_SHIFT : OUT_SHIFT + 1, :]
     middle = x_ref[...].astype(F32) + table[SCALE1 : SCALE1 + 1, :] * branch
@@ -637,7 +713,7 @@
     return -(-tokens // ROWS)
 
 
-def merge(order, x, own, far, table, weight):
+def merge(place, x, own, far, table, rest):
     tokens, width = x.shape
     half = width // 2
     wide = pl.BlockSpec((ROWS, width), lambda i, _: (i, 0))
@@ -652,8 +728,8 @@
                 narrow,
                 narrow,
                 whole(table.shape),
-                pl.BlockSpec((half, width), lambda i, order: (order[3], 0)),
-                pl.BlockSpec((half, width), lambda i, order: (order[0], 0)),
+                pl.BlockSpec((half, width), lambda i, place: (place[CORE], rest.shape[1] // width - 1)),
+                pl.BlockSpec((half, width), lambda i, place: (1 - place[CORE], rest.shape[1] // width - 1)),
             ],
             out_specs=[wide, wide, wide],
         ),
@@ -664,7 +740,7 @@
         ],
         name="merge",
         **params_for(2 * tokens * width * width, 14 * tokens * width + 2 * width * width),
-    )(order, x, own, far, table, weight, weight)
+    )(place, x, own, far, table, rest, rest)
 
 
 def gelu_and_slope(values):
@@ -677,83 +753,139 @@
     return values * phi, phi + values * bell * 0.3989422804014327
 
 
+def ungroup(grouped_ref, down):
+    width = down.shape[1]
+    groups = grouped_ref.shape[1] // width
+    each = grouped_ref.shape[0] // 2
+    for device in range(2):
+        for g in range(groups):
+            at = (device * groups + g) * each
+            down[at : at + each, :] = grouped_ref[device * each : (device + 1) * each, g * width : (g + 1) * width]
+
+
+def scaled_upstream(cotangent_ref, table):
+    return (cotangent_ref[...].astype(F32) * table[SCALE2 : SCALE2 + 1, :]).astype(BF16)
+
+
+def place_turned(place, block, target, k, chips):
+    half = block.shape[1] // 2
+    turned_block = block.T
+    first, second = turned_block[:half], turned_block[half:]
+    target[k * half : (k + 1) * half, :] = jnp.where(place[CORE] == 0, first, second)
+    target[(chips + k) * half : (chips + k + 1) * half, :] = jnp.where(place[CORE] == 0, second, first)
+
+
+def fill_turned(place, source_ref, target, chips):
+    wide = source_ref.shape[1] // chips
+    for k in range(chips):
+        at = pl.ds(pl.multiple_of(place[CHIPS + k] * wide, wide), wide)
+        place_turned(place, source_ref[:, at], target, k, chips)
+
+
+def split_rows(grad, mine_ref, other_ref):
+    chips, rows, _ = mine_ref.shape
+    for k in range(chips):
+        mine_ref[k] = grad[k * rows : (k + 1) * rows, :]
+        other_ref[k] = grad[(chips + k) * rows : (chips + k + 1) * rows, :]
+
+
+def group(grad, out_ref):
+    rows, columns = out_ref.shape[1], grad.shape[1]
+    for g in range(grad.shape[0] // rows):
+        out_ref[0, :, g * columns : (g + 1) * columns] = grad[g * rows : (g + 1) * rows, :]
+
+
 def mlp_kernel(
-    normed_ref, cotangent_ref, table, up_ref, shift_ref, down_ref,
-    branch_ref, delta_ref, grad_up_ref, grad_down_ref, grad_shift_ref,
-    upstream, upstream_t, normed_t,
+    place, normed_ref, cotangent_ref, table, up_ref, shift_ref, grouped_ref,
+    branch_ref, delta_ref, up_mine_ref, up_other_ref, down_mine_ref, down_other_ref, grad_shift_ref,
+    upstream, upstream_t, normed_t, down,
+    *, chips,
 ):
     @pl.when(pl.program_id(0) == 0)
     def _():
         scaled = (cotangent_ref[...].astype(F32) * table[SCALE2 : SCALE2 + 1, :]).astype(BF16)
         upstream[...] = scaled
         upstream_t[...] = turned(scaled)
-        normed_t[...] = turned(normed_ref[...])
+        fill_turned(place, normed_ref, normed_t, chips)
         branch_ref[...] = jnp.zeros_like(branch_ref)
         delta_ref[...] = jnp.zeros_like(delta_ref)
 
-    up, down = up_ref[...], down_ref[...]
-    hidden = dot(normed_ref[...], up) + shift_ref[...]
-    grad_active = dot(upstream[...], down, NT)
+    ungroup(grouped_ref, down)
+    hidden = dot(normed_ref[...], up_ref[...]) + shift_ref[...]
+    grad_active = dot(upstream[...], down[...], NT)
     active, slope = gelu_and_slope(hidden)
     active = active.astype(BF16)
     delta_hidden = (grad_active * slope).astype(BF16)
-    branch_ref[...] += dot(active, down)
-    delta_ref[...] += dot(delta_hidden, up, NT)
-    grad_up_ref[...] = dot(normed_t[...], delta_hidden).astype(BF16)
-    grad_down = dot(upstream_t[...], active).astype(BF16)
-    each = grad_down_ref.shape[2]
-    for i in range(grad_down_ref.shape[0]):
-        grad_down_ref[i] = grad_down[:, i * each : (i + 1) * each]
+    branch_ref[...] += dot(active, down[...])
+    delta_ref[...] += dot(delta_hidden, up_ref[...], NT)
+    split_rows(dot(normed_t[...], delta_hidden).astype(BF16), up_mine_ref, up_other_ref)
+    grad_down = dot(upstream_t[...], active)
+    each = grad_down.shape[1] // 2
+    first, second = grad_down[:, :each], grad_down[:, each:]
+    group(jnp.where(place[CORE] == 0, first, second).astype(BF16), down_mine_ref)
+    group(jnp.where(place[CORE] == 0, second, first).astype(BF16), down_other_ref)
     grad_shift_ref[...] = total_rows(delta_hidden.astype(F32))
 
 
-def mlp(normed, cotangent, table, up, up_shift, down, owners, block=512):
+def mlp(place, normed, cotangent, table, rest, up_shift, owners):
     tokens, width = normed.shape
-    hidden = up.shape[1]
-    each = hidden // owners
-    held = block // each
+    hidden = up_shift.shape[1]
+    rows = rest.shape[0] // owners
+    chips = owners // 2
+    block = hidden // chips
+    up_out = pl.BlockSpec((chips, rows, block), lambda j, place: (0, 0, place[CHIPS + j]))
+    down_out = pl.BlockSpec((1, rows, hidden), lambda j, _: (j, 0, 0))
+    sent = jax.ShapeDtypeStruct((chips, rows, hidden), BF16)
     return pl.pallas_call(
-        mlp_kernel,
-        grid=(hidden // block,),
-        in_specs=[
-            whole((tokens, width)),
-            whole((tokens, width)),
-            whole(table.shape),
-            pl.BlockSpec((width, block), lambda j: (0, j)),
-            pl.BlockSpec((1, block), lambda j: (0, j)),
-            pl.BlockSpec((block, width), lambda j: (j, 0)),
-        ],
-        out_specs=[
-            whole((tokens, width)),
-            whole((tokens, width)),
-            pl.BlockSpec((width, block), lambda j: (0, j)),
-            pl.BlockSpec((held, width, each), lambda j: (j, 0, 0)),
-            pl.BlockSpec((1, block), lambda j: (0, j)),
-        ],
+        functools.partial(mlp_kernel, chips=chips),
+        grid_spec=pltpu.PrefetchScalarGridSpec(
+            num_scalar_prefetch=1,
+            grid=(chips,),
+            in_specs=[
+                whole((tokens, width)),
+                whole((tokens, width)),
+                whole(table.shape),
+                pl.BlockSpec((width, block), lambda j, place: (0, place[CHIPS + j])),
+                pl.BlockSpec((1, block), lambda j, place: (0, place[CHIPS + j])),
+                pl.BlockSpec((2 * rows, hidden), lambda j, place: (place[CHIPS + j], 1)),
+            ],
+            out_specs=[
+                whole((tokens, width)),
+                whole((tokens, width)),
+                up_out,
+                up_out,
+                down_out,
+                down_out,
+                pl.BlockSpec((1, block), lambda j, place: (0, place[CHIPS + j])),
+            ],
+            scratch_shapes=[
+                pltpu.VMEM((tokens, width), BF16),
+                pltpu.VMEM((width, tokens), BF16),
+                pltpu.VMEM((width, tokens), BF16),
+                pltpu.VMEM((block, width), BF16),
+            ],
+        ),
         out_shape=[
             jax.ShapeDtypeStruct((tokens, width), F32),
             jax.ShapeDtypeStruct((tokens, width), F32),
-            jax.ShapeDtypeStruct((width, hidden), BF16),
-            jax.ShapeDtypeStruct((owners, width, each), BF16),
+            sent,
+            sent,
+            sent,
+            sent,
             jax.ShapeDtypeStruct((1, hidden), F32),
-        ],
-        scratch_shapes=[
-            pltpu.VMEM((tokens, width), BF16),
-            pltpu.VMEM((width, tokens), BF16),
-            pltpu.VMEM((width, tokens), BF16),
         ],
         name="mlp",
         **params_for(12 * tokens * width * hidden, 12 * tokens * width + 8 * width * hidden, 2 * tokens * hidden),
-    )(normed, cotangent, table, up, up_shift, down)
+    )(place, normed, cotangent, table, rest, up_shift, rest)
 
 
 SUM_ROWS = 8
 
 
 def unmerge_kernel(
-    order, middle_ref, branch1_ref, branch2_ref, delta_ref, cotangent_ref, own_ref, far_ref, table, own_w, far_w,
-    output_ref, delta_middle_ref, own_grad_ref, far_grad_ref, weight_ref, sums_ref,
-    delta1_all,
+    place, middle_ref, branch1_ref, branch2_ref, delta_ref, cotangent_ref, own_ref, far_ref, table, own_w, far_w,
+    output_ref, delta_middle_ref, own_grad_ref, far_grad_ref, mine_ref, other_ref, sums_ref,
+    delta1_all, mixture_t,
     *, tokens,
 ):
     step = pl.program_id(0)
@@ -795,16 +927,20 @@
 
     @pl.when(step == pl.num_programs(0) - 1)
     def _():
-        delta1_kept = delta1_all[:tokens, :]
-        half = own_ref.shape[1]
-        own_at = pl.multiple_of(order[3] * half, half)
-        far_at = pl.multiple_of(order[0] * half, half)
-        weight_ref[pl.ds(own_at, half), :] = dot(turned(own_ref[...]), delta1_kept).astype(BF16)
-        weight_ref[pl.ds(far_at, half), :] = dot(turned(far_ref[...]), delta1_kept).astype(BF16)
-
-
-def unmerge(order, middle, branch1, branch2, delta, cotangent, own, far, table, weight):
+        chips = mine_ref.shape[0]
+        wide = width // chips
+        for k in range(chips):
+            chip = place[CHIPS + k]
+            at = pl.ds(pl.multiple_of(lax.rem(chip, chips // 2) * wide, wide), wide)
+            mixed = jnp.where(chip // (chips // 2) == place[CORE], own_ref[:, at], far_ref[:, at])
+            place_turned(place, mixed, mixture_t, k, chips)
+        split_rows(dot(mixture_t[...], delta1_all[:tokens, :]).astype(BF16), mine_ref, other_ref)
+
+
+def unmerge(place, middle, branch1, branch2, delta, cotangent, own, far, table, rest, owners):
     tokens, width = middle.shape
+    chips = owners // 2
+    sent = (chips, width // owners, width)
     half = width // 2
     steps = row_steps(tokens)
     wide = pl.BlockSpec((ROWS, width), lambda i, _: (i, 0))
@@ -818,84 +954,51 @@
             + [whole((tokens, half))] * 2
             + [
                 whole(table.shape),
-                pl.BlockSpec((half, width), lambda i, order: (order[3], 0)),
-                pl.BlockSpec((half, width), lambda i, order: (order[0], 0)),
+                pl.BlockSpec((half, width), lambda i, place: (place[CORE], rest.shape[1] // width - 1)),
+                pl.BlockSpec((half, width), lambda i, place: (1 - place[CORE], rest.shape[1] // width - 1)),
             ],
-            out_specs=[wide, wide, narrow, narrow, whole((width, width)), whole((SUM_ROWS, width))],
-            scratch_shapes=[pltpu.VMEM((steps * ROWS, width), BF16)],
+            out_specs=[wide, wide, narrow, narrow, whole(sent), whole(sent), whole((SUM_ROWS, width))],
+            scratch_shapes=[pltpu.VMEM((steps * ROWS, width), BF16), pltpu.VMEM((width, tokens), BF16)],
         ),
         out_shape=[
             jax.ShapeDtypeStruct((tokens, width), BF16),
             jax.ShapeDtypeStruct((tokens, width), F32),
             jax.ShapeDtypeStruct((tokens, half), BF16),
             jax.ShapeDtypeStruct((tokens, half), BF16),
-            jax.ShapeDtypeStruct((width, width), BF16),
+            jax.ShapeDtypeStruct(sent, BF16),
+            jax.ShapeDtypeStruct(sent, BF16),
             jax.ShapeDtypeStruct((SUM_ROWS, width), F32),
         ],
         name="unmerge",
         **params_for(4 * tokens * width * width, 30 * tokens * width + 4 * width * width),
-    )(order, middle, branch1, branch2, delta, cotangent, own, far, table, weight, weight)
-
-
-def packed_grad_kernel(order, normed_ref, far_ref, own_ref, grad_ref, sums_ref, normed_t):
+    )(place, middle, branch1, branch2, delta, cotangent, own, far, table, rest, rest)
+
+
+def unproject_kernel(
+    place, x_ref, delta_middle_ref, table, normed_ref, own_ref, far_ref, weight_ref, middle_sums, up_sums, *refs, chips
+):
+    out_ref, mine_ref, other_ref, vectors_mine_ref, vectors_other_ref, delta, sums, normed_t = refs[-8:]
     step = pl.program_id(0)
+    width = x_ref.shape[1]
+    core = place[CORE]
 
     @pl.when(step == 0)
     def _():
-        normed_t[...] = turned(normed_ref[...])
-
-    block = jnp.where(step < 3, far_ref[0], own_ref[0])
-    grad_ref[...] = dot(normed_t[...], block).astype(BF16)
-    sums_ref[...] = jnp.broadcast_to(total_rows(block.astype(F32)), sums_ref.shape)
-
-
-def far_block(j, _):
-    return (jnp.minimum(j, 2), 0, 0)
-
-
-def own_block(j, _):
-    return (jnp.maximum(j - 3, 0), 0, 0)
-
-
-def packed_grad(order, normed, far, own):
-    tokens, width = normed.shape
-    half = width // 2
-    return pl.pallas_call(
-        packed_grad_kernel,
-        grid_spec=pltpu.PrefetchScalarGridSpec(
-            num_scalar_prefetch=1,
-            grid=(6,),
-            in_specs=[
-                whole((tokens, width)),
-                pl.BlockSpec((1, tokens, half), far_block),
-                pl.BlockSpec((1, tokens, half), own_block),
-            ],
-            out_specs=[
-                pl.BlockSpec((width, half), lambda j, order: (0, order[j])),
-                pl.BlockSpec((8, half), lambda j, order: (0, order[j])),
-            ],
-            scratch_shapes=[pltpu.VMEM((width, tokens), BF16)],
-        ),
-        out_shape=[
-            jax.ShapeDtypeStruct((width, 3 * width), BF16),
-            jax.ShapeDtypeStruct((8, 3 * width), F32),
-        ],
-        name="packed_grad",
-        **params_for(6 * tokens * width * width, 8 * tokens * width + 6 * width * width),
-    )(order, normed, far, own)
-
-
-def unproject_kernel(
-    order, x_ref, delta_middle_ref, table, far_ref, own_ref, weight_ref, out_ref, sums_ref, delta
-):
-    step = pl.program_id(0)
-
-    @pl.when(step == 0)
-    def _():
+        fill_turned(place, normed_ref, normed_t, chips)
         delta[...] = jnp.zeros_like(delta)
-
-    block = jnp.where(step < 3, far_ref[0], own_ref[0])
+        sums[...] = jnp.zeros_like(sums)
+
+    block = jnp.where(step < 3, own_ref[0], far_ref[0])
+    split_rows(dot(normed_t[...], block).astype(BF16), mine_ref, other_ref)
     delta[...] += dot(block, weight_ref[...], NT)
+    column_total = total_rows(block.astype(F32))
+    half = block.shape[1]
+    at = pl.ds(pl.multiple_of(jnp.where(step < 3, core, 1 - core) * half, half), half)
+    for kind, row in ((0, QUERY), (2, VALUE)):
+
+        @pl.when(lax.rem(step, 3) == kind)
+        def _():
+            sums[row : row + 1, at] = column_total
 
     @pl.when(step == pl.num_programs(0) - 1)
     def _():
@@ -904,16 +1007,44 @@
             x_ref[...].astype(F32), table[GAIN1 : GAIN1 + 1, :], delta_normed
         )
         out_ref[...] = (delta_middle_ref[...] + inner).astype(BF16)
-        sums_ref[...] = jnp.zeros_like(sums_ref)
-        sums_ref[0:1, :] = total_rows(gain_terms)
-        sums_ref[1:2, :] = total_rows(delta_normed)
-
-
-def unproject(order, x, delta_middle, table, far, own, weight):
+        rows = {
+            GAIN1: total_rows(gain_terms),
+            SHIFT1: total_rows(delta_normed),
+            OUT_SHIFT: middle_sums[5:6, :],
+            SCALE1: middle_sums[4:5, :],
+            GAIN2: middle_sums[2:3, :],
+            SHIFT2: middle_sums[3:4, :],
+            DOWN_SHIFT: middle_sums[1:2, :],
+            SCALE2: middle_sums[0:1, :],
+        }
+        for i, values in rows.items():
+            sums[i : i + 1, :] = values
+        each = up_sums.shape[1] // (2 * chips)
+        for out, side in ((vectors_mine_ref, core), (vectors_other_ref, 1 - core)):
+            out[...] = jnp.zeros_like(out)
+            for k in range(chips):
+                chip = place[CHIPS + k]
+                at = pl.ds(pl.multiple_of(chip * LANES, LANES), LANES)
+                out[k, : sums.shape[0], :] = sums[:, at].astype(BF16)
+                for r in range(each // LANES):
+                    at = pl.multiple_of((2 * chip + side) * each + r * LANES, LANES)
+                    row = up_sums[:, pl.ds(at, LANES)].astype(BF16)
+                    out[k, VECTORS + r : VECTORS + r + 1, :] = row
+
+
+def unproject(place, x, delta_middle, table, normed, own, far, weight, middle_sums, up_sums, owners, after):
     tokens, width = x.shape
     half = width // 2
+    chips = owners // 2
+    rows = width // owners
+    vectors = (chips, rows, LANES)
+
+    def column(j, place):
+        return 2 * lax.rem(j, 3) + jnp.where(j < 3, place[CORE], 1 - place[CORE])
+
+    sent = pl.BlockSpec((chips, rows, half), lambda j, place: (0, 0, column(j, place)))
     return pl.pallas_call(
-        unproject_kernel,
+        functools.partial(unproject_kernel, chips=chips),
         grid_spec=pltpu.PrefetchScalarGridSpec(
             num_scalar_prefetch=1,
             grid=(6,),
@@ -921,20 +1052,218 @@
                 whole((tokens, width)),
                 whole((tokens, width)),
                 whole(table.shape),
-                pl.BlockSpec((1, tokens, half), far_block),
-                pl.BlockSpec((1, tokens, half), own_block),
-                pl.BlockSpec((width, half), lambda j, order: (0, order[j])),
+                whole((tokens, width)),
+                pl.BlockSpec((1, tokens, half), lambda j, _: (jnp.minimum(j, 2), 0, 0)),
+                pl.BlockSpec((1, tokens, half), lambda j, _: (jnp.maximum(j - 3, 0), 0, 0)),
+                pl.BlockSpec((width, half), lambda j, place: (0, column(j, place))),
+                whole(middle_sums.shape),
+                whole(up_sums.shape),
+            ]
+            + [pl.BlockSpec(memory_space=pl.ANY)] * len(after),
+            out_specs=[whole((tokens, width)), sent, sent, whole(vectors), whole(vectors)],
+            scratch_shapes=[
+                pltpu.VMEM((tokens, width), F32),
+                pltpu.VMEM((16, width), F32),
+                pltpu.VMEM((width, tokens), BF16),
             ],
-            out_specs=[whole((tokens, width)), whole((SUM_ROWS, width))],
-            scratch_shapes=[pltpu.VMEM((tokens, width), F32)],
         ),
         out_shape=[
             jax.ShapeDtypeStruct((tokens, width), BF16),
-            jax.ShapeDtypeStruct((SUM_ROWS, width), F32),
+            jax.ShapeDtypeStruct((chips, rows, 3 * width), BF16),
+            jax.ShapeDtypeStruct((chips, rows, 3 * width), BF16),
+            jax.ShapeDtypeStruct(vectors, BF16),
+            jax.ShapeDtypeStruct(vectors, BF16),
         ],
         name="unproject",
-        **params_for(6 * tokens * width * width, 12 * tokens * width + 6 * width * width),
-    )(order, x, delta_middle, table, far, own, weight)
+        **params_for(12 * tokens * width * width, 18 * tokens * width + 12 * width * width, weight=SHORT),
+    )(place, x, delta_middle, table, normed, own, far, weight, middle_sums, up_sums, *after)
+
+
+def ring_of(chips):
+    return list(range(0, chips, 2)) + list(range(1, chips, 2))[::-1]
+
+
+def places(owners):
+    ring = ring_of(owners // 2)
+    rows = []
+    for f in range(owners):
+        chip, core = divmod(f, 2)
+        at = ring.index(chip)
+        columns = [1 - core, 3 - core, 5 - core, core, 2 + core, 4 + core]
+        rows.append(columns + [core] + ring[at:] + ring[:at])
+    return np.array(rows, np.int32)
+
+
+def ring_perm(chips, hop):
+    ring = ring_of(chips)
+    return [
+        (2 * ring[i] + core, 2 * ring[(i + hop) % chips] + core) for i in range(chips) for core in range(2)
+    ]
+
+
+def to_next(values, chips, hop):
+    return lax.ppermute(values, "fsdp", ring_perm(chips, hop))
+
+
+def ring_gather(piece, chips):
+    pieces = [None] * chips
+    pieces[0] = right = left = piece
+    for k in range(1, chips // 2 + 1):
+        pieces[-k] = right = to_next(right, chips, 1)
+        if k < chips - chips // 2:
+            pieces[k] = left = to_next(left, chips, -1)
+    return pieces
+
+
+def low_part(columns):
+    return columns // 2 if columns % (2 * LANES) == 0 else columns
+
+
+def ring_add_kernel(*refs, columns, mode, carried):
+    ways = 2 if mode in ("second", "next") else 1
+    shares = [refs[2 * len(columns) * d : 2 * len(columns) * (d + 1)] for d in range(ways)]
+    came = refs[2 * len(columns) * ways :]
+    outs = refs[len(refs) - carried - (1 if mode == "total" else 2) : len(refs) - carried]
+    start, low_start, high_start = 0, 0, 0
+    for i, each in enumerate(columns):
+        totals = [mine[2 * i][0].astype(F32) + mine[2 * i + 1][0].astype(F32) for mine in shares]
+        at = slice(start, start + each)
+        low = low_part(each)
+        low_at, high_at = slice(low_start, low_start + low), slice(high_start, high_start + each - low)
+        if mode == "first":
+            outs[0][:, low_at] = totals[0][:, :low].astype(BF16)
+            if low < each:
+                outs[1][:, high_at] = totals[0][:, low:].astype(BF16)
+        elif mode == "second":
+            outs[0][:, start : start + low] = (totals[0][:, :low] + came[0][:, low_at].astype(F32)).astype(BF16)
+            outs[1][:, start : start + low] = totals[1][:, :low].astype(BF16)
+            if low < each:
+                high = totals[1][:, low:] + came[1][:, high_at].astype(F32)
+                outs[0][:, start + low : start + each] = totals[0][:, low:].astype(BF16)
+                outs[1][:, start + low : start + each] = high.astype(BF16)
+        elif mode == "next":
+            for total, arrived, out in zip(totals, came, outs):
+                out[:, at] = (total + arrived[:, at].astype(F32)).astype(BF16)
+        else:
+            both_ways = came[0][:, at].astype(F32) + came[1][:, at].astype(F32)
+            outs[0][:, at] = (totals[0] + both_ways).astype(BF16)
+        start, low_start, high_start = at.stop, low_at.stop, high_at.stop
+
+
+class RingSum:
+    def __init__(self, *parts):
+        self.parts, self.chips = parts, parts[0][0].shape[0]
+        self.steps = self.chips // 2
+        self.step = 0
+        self.came = []
+
+    def add(self, mode, places, after=(), carry=()):
+        rows = self.parts[0][0].shape[1]
+        columns = [mine.shape[2] for mine, _ in self.parts]
+        total = sum(columns)
+        blocks = 2 if total > 4096 else 1
+        arrays, specs = [], []
+        for at in places:
+            for part, each in zip(self.parts, columns):
+                for array in part:
+                    arrays.append(array)
+                    specs.append(pl.BlockSpec((1, rows // blocks, each), lambda i, at=at: (at, i, 0)))
+        for came in self.came:
+            arrays.append(came)
+            specs.append(pl.BlockSpec((rows // blocks, came.shape[1]), lambda i: (i, 0)))
+        arrays += [*after, *carry]
+        anywhere = pl.BlockSpec(memory_space=pl.ANY)
+        specs += [anywhere] * (len(after) + len(carry))
+        low = sum(low_part(each) for each in columns)
+        out_columns = {"first": [low, total - low], "total": [total]}.get(mode, [total, total])
+        sums = len(out_columns)
+        outs = pl.pallas_call(
+            functools.partial(ring_add_kernel, columns=columns, mode=mode, carried=len(carry)),
+            grid=(blocks,),
+            in_specs=specs,
+            out_specs=[pl.BlockSpec((rows // blocks, out), lambda i: (i, 0)) for out in out_columns]
+            + [anywhere] * len(carry),
+            out_shape=[jax.ShapeDtypeStruct((rows, out), BF16) for out in out_columns]
+            + [jax.ShapeDtypeStruct(array.shape, array.dtype) for array in carry],
+            input_output_aliases={len(arrays) - len(carry) + i: sums + i for i in range(len(carry))},
+            name="ring_add",
+            **params_for(6 * rows * total, 16 * rows * total, weight=SHORT),
+        )(*arrays)
+        return outs[:sums], outs[sums:]
+
+    def sums(self, after=(), carry=()):
+        k = self.steps - self.step
+        if self.step == 0:
+            return self.add("first", [k], after, carry)
+        return self.add("second" if self.step == 1 else "next", [k, self.chips - k], after, carry)
+
+    def send(self, sums):
+        self.came = [to_next(sums[0], self.chips, 1), to_next(sums[1], self.chips, -1)]
+        self.step += 1
+
+    def total(self, carry=()):
+        assert self.step == self.steps
+        sums, carried = self.add("total", [0], (), carry)
+        return sums[0], carried
+
+
+def finish_rest_kernel(part_ref, came_ref, up_ref, down_ref, output_ref):
+    def total(at):
+        return part_ref[:, at].astype(F32) + came_ref[:, at].astype(F32)
+
+    rows, hidden = up_ref.shape
+    each, width = down_ref.shape
+    up_ref[...] = total(slice(0, hidden))
+    for g in range(0, width // rows, 2):
+        pair = [total(slice(hidden + each * h, hidden + each * (h + 1))) for h in (g, g + 1)]
+        down_ref[:, g * rows : (g + 2) * rows] = jnp.concatenate(pair, axis=0).T
+    output_ref[...] = total(slice(hidden + width // rows * each, None))
+
+
+def finish_rest(part, came, hidden, each, width):
+    in_vmem = pl.BlockSpec(memory_space=pltpu.VMEM)
+    rows = part.shape[0]
+    return pl.pallas_call(
+        finish_rest_kernel,
+        in_specs=[in_vmem] * 2,
+        out_specs=[in_vmem] * 3,
+        out_shape=[jax.ShapeDtypeStruct(shape, F32) for shape in ((rows, hidden), (each, width), (rows, width))],
+        name="finish_rest",
+        **params_for(part.size, 8 * part.size, weight=SHORT),
+    )(part, came)
+
+
+def finish_first_kernel(place, part_ref, came_ref, packed_ref, *vector_refs):
+    def total(rows, at):
+        return part_ref[rows, at].astype(F32) + came_ref[rows, at].astype(F32)
+
+    width = packed_ref.shape[1]
+    packed_ref[...] = total(slice(None), slice(0, width))
+    vectors = total(slice(0, 16), slice(width, width + LANES))
+    half = LANES // 2
+    mine = jnp.where(place[CORE] == 0, vectors[:, :half], vectors[:, half:])
+    for i in range(VECTORS):
+        vector_refs[i][...] = mine[i : i + 1, :].reshape(half)
+    count = vector_refs[VECTORS].shape[0]
+    vector_refs[VECTORS][...] = vectors[VECTORS : VECTORS + count // LANES, :].reshape(count)
+
+
+def finish_first(place, part, came, each):
+    in_vmem = pl.BlockSpec(memory_space=pltpu.VMEM)
+    rows, width = part.shape[0], part.shape[1] - LANES
+    shapes = [(rows, width)] + [(rows,)] * VECTORS + [(each,)]
+    return pl.pallas_call(
+        finish_first_kernel,
+        in_specs=[pl.BlockSpec(memory_space=pltpu.SMEM)] + [in_vmem] * 2,
+        out_specs=[in_vmem] * len(shapes),
+        out_shape=[jax.ShapeDtypeStruct(shape, F32) for shape in shapes],
+        name="finish_first",
+        **params_for(part.size, 8 * part.size, weight=SHORT),
+    )(place, part, came)
+
+
+def split_pairs(pairs):
+    return [pairs // 4, pairs // 2, pairs - pairs // 4 - pairs // 2] if pairs >= 4 else [pairs]
 
 
 def paired_body(
@@ -942,87 +1271,115 @@
     layer_scale1, norm2_gain, norm2_bias, up_weight, up_bias, down_weight, down_bias, layer_scale2, cotangent,
 ):
     owners = lax.axis_size("fsdp")
-    images, local_len, width = tokens.shape
-    core = lax.rem(lax.axis_index("fsdp"), 2)
-    regroup = [(f * 2 + s, (f - f % 2 + s) * 2 + f % 2) for f in range(owners) for s in range(2)]
+    chips = owners // 2
+    _, local_len, width = tokens.shape
+    me = lax.axis_index("fsdp")
+    core = lax.rem(me, 2)
+    place = lax.dynamic_index_in_dim(jnp.asarray(places(owners)), me, keepdims=False)
+    moves = [(f * 2 + s, (f - f % 2 + s) * 2 + f % 2) for f in range(owners) for s in range(2) if f % 2 != s]
     twin = [(f, f ^ 1) for f in range(owners)]
+    stays = core == lax.axis_index("seq")
+
+    def regroup_moves(values):
+        return lax.ppermute(values, ("fsdp", "seq"), moves)
 
     def regrouped(values):
-        return lax.ppermute(values, ("fsdp", "seq"), regroup)
+        return jnp.where(stays, values, regroup_moves(values))
 
     def to_twin(values):
         return lax.ppermute(values, "fsdp", twin)
 
-    x = regrouped(tokens.reshape(local_len, width))
-    valid_count = regrouped(lengths)
+    def across(values):
+        return lax.ppermute(values, "seq", [(0, 1), (1, 0)])
+
     vectors = (
         norm1_gain, norm1_bias, query_bias, value_bias, output_bias, layer_scale1, norm2_gain, norm2_bias,
         down_bias, layer_scale2,
     )
     rows = norm1_gain.shape[0]
-    small = jnp.concatenate(vectors + (up_bias,))
-    first_rows = packed_weight.shape[0]
-    small_block = jnp.zeros((first_rows * LANES,), BF16).at[: small.shape[0]].set(small)
-    first = jnp.concatenate([packed_weight, small_block.reshape(first_rows, LANES)], axis=1)
-    first_full = lax.all_gather(first, "fsdp", axis=0, tiled=True)
-    small_full = first_full[:, 3 * width :].reshape(owners, first_rows * LANES)
-    table = small_full[:, : 10 * rows].reshape(owners, 10, rows).transpose(1, 0, 2).reshape(10, width)
-    table = jnp.pad(table, ((0, 6), (0, 0))).astype(F32)
-    up_shift = small_full[:, 10 * rows : small.shape[0]].reshape(1, -1).astype(F32)
-    output_full = lax.all_gather(output_weight, "fsdp", axis=0, tiled=True)
-    up_full = lax.all_gather(up_weight, "fsdp", axis=0, tiled=True)
-    down_full = lax.all_gather(down_weight, "fsdp", axis=0, tiled=True)
-
-    order = jnp.stack([1 - core, 3 - core, 5 - core, core, 2 + core, 4 + core]).astype(jnp.int32)
+    hidden = up_weight.shape[1]
+    first, rest = pack(place, packed_weight, up_weight, down_weight, output_weight, vectors, up_bias)
+    own_pieces = ring_gather(first, chips)
+    far_pieces = [to_twin(piece) for piece in own_pieces]
+    x = regrouped(tokens.reshape(local_len, width))
+    valid_count = regrouped(lengths)
+    rest = lax.all_gather(rest, "fsdp", axis=0, tiled=True)
     starts = jnp.stack([core, 1 - core]) * local_len
     valid = jnp.clip(valid_count - starts, 0, local_len).astype(jnp.int32)
-
-    far_out, own_part, normed = project(order, x, table, first_full)
+    upstream = regrouped(cotangent.reshape(local_len, width))
+
+    far_out, own_part, normed, packed_full, table, up_shift = project(place, x, own_pieces, far_pieces, hidden)
     far_part = to_twin(far_out)
     parts = [own_part, far_part]
     (own_mix, far_mix_out), totals = attention(valid, parts, 352)
     far_mix = to_twin(far_mix_out)
-    middle, branch1, normed2 = merge(order, x, own_mix, far_mix, table, output_full)
-    upstream = regrouped(cotangent.reshape(local_len, width))
-    branch2, delta_normed2, grad_up, grad_down, grad_up_shift = mlp(
-        normed2, upstream, table, up_full, up_shift, down_full, owners
-    )
-    output, delta_middle, own_grad, far_grad_out, grad_output, sums2 = unmerge(
-        order, middle, branch1, branch2, delta_normed2, upstream, own_mix, far_mix, table, output_full
-    )
-    output = regrouped(output).reshape(tokens.shape)
+    middle, branch1, normed2 = merge(place, x, own_mix, far_mix, table, rest)
+
+    branch2, delta_normed2, up_mine, up_other, down_mine, down_other, up_sums = mlp(
+        place, normed2, upstream, table, rest, up_shift, owners
+    )
+    up_twin, down_twin = to_twin(up_other), to_twin(down_other)
+    output, delta_middle, own_grad, far_grad_out, output_mine, output_other, middle_sums = unmerge(
+        place, middle, branch1, branch2, delta_normed2, upstream, own_mix, far_mix, table, rest, owners
+    )
     far_grad = to_twin(far_grad_out)
-    own_delta, far_delta_out = attention_back(
-        valid, parts, [own_mix, far_mix_out], [own_grad, far_grad], totals, 352
-    )
+    output_twin = to_twin(output_other)
+    ring = RingSum((up_mine, up_twin), (down_mine, down_twin), (output_mine, output_twin))
+    output_sent = regroup_moves(output)
+    deltas = ()
+    grads = [own_grad, far_grad]
+    start = 0
+    for pairs in split_pairs(width // 2 // LANES):
+        sums, _ = ring.sums()
+        ring.send(sums)
+        after = [*sums, output_sent] if start else sums
+        deltas = attention_back(
+            valid, parts, [own_mix, far_mix_out], grads, totals, 352, start, pairs, deltas, after
+        )
+        start += pairs
+    own_delta, far_delta_out = deltas
+    sums, (far_delta_out,) = ring.sums(carry=[far_delta_out])
+    ring.send(sums)
     far_delta = to_twin(far_delta_out)
-    grad_packed, packed_sums = packed_grad(order, normed, far_delta, own_delta)
-    grad_x, sums1 = unproject(order, x, delta_middle, table, far_delta, own_delta, first_full)
-    grad_tokens = regrouped(grad_x).astype(F32).reshape(tokens.shape)
-
-    def owned(grad):
-        part = lax.psum_scatter(grad, "fsdp", scatter_dimension=0, tiled=True)
-        return part.astype(F32) + lax.ppermute(part, "seq", [(0, 1), (1, 0)]).astype(F32)
-
-    grad_up = owned(grad_up)
-    grad_down = owned(grad_down)[0].T
-    grad_output = owned(grad_output)
-    grad_packed = owned(grad_packed)
-    sums = jnp.concatenate(
-        [
-            sums1[0], sums1[1], packed_sums[0, :width], packed_sums[0, 2 * width :], sums2[5], sums2[4], sums2[2],
-            sums2[3], sums2[1], sums2[0], grad_up_shift[0],
-        ]
-    )
-    all_sums = lax.psum(sums, ("fsdp", "seq"))
-    me = lax.axis_index("fsdp")
-    mine = [lax.dynamic_slice(all_sums, (i * width + me * rows,), (rows,)) for i in range(10)]
+    grad_x, packed_mine, packed_other, vectors_mine, vectors_other = unproject(
+        place, x, delta_middle, table, normed, own_delta, far_delta, packed_full, middle_sums, up_sums, owners, []
+    )
+    output = jnp.where(stays, output, output_sent).reshape(tokens.shape)
+    rest_sum, (grad_x, packed_other, vectors_other) = ring.total(carry=[grad_x, packed_other, vectors_other])
+    vectors_twin, packed_twin = to_twin(vectors_other), to_twin(packed_other)
+    packed_ring = RingSum((packed_mine, packed_twin), (vectors_mine, vectors_twin))
+    grad_x_sent, rest_sent = regroup_moves(grad_x), across(rest_sum)
+    for after in ([], [], [grad_x_sent], [rest_sent]):
+        packed_ring.send(packed_ring.sums(after)[0])
+    grad_tokens = jnp.where(stays, grad_x, grad_x_sent).astype(F32).reshape(tokens.shape)
     each = up_bias.shape[0]
-    mine_up = lax.dynamic_slice(all_sums, (10 * width + me * each,), (each,))
+    grad_up, grad_down, grad_output = finish_rest(rest_sum, rest_sent, hidden, each, width)
+    first_sum, _ = packed_ring.total()
+    grad_packed, *mine = finish_first(place, first_sum, across(first_sum), each)
     return (
         output, grad_tokens, mine[0], mine[1], grad_packed, mine[2], mine[3], grad_output, mine[4], mine[5],
-        mine[6], mine[7], grad_up, mine_up, grad_down, mine[8], mine[9],
-    )
+        mine[6], mine[7], grad_up, mine[10], grad_down, mine[8], mine[9],
+    )
+
+
+def pairable(tokens, up_weight):
+    owners, chips = lax.axis_size("fsdp"), lax.axis_size("fsdp") // 2
+    width, hidden = up_weight.shape[0] * owners, up_weight.shape[1]
+    return (
+        lax.axis_size("seq") == 2
+        and tokens.shape[0] == 1
+        and tokens.shape[1] % 16 == 0
+        and owners == 2 * chips
+        and chips in (4, 8)
+        and width % (chips * LANES) == 0
+        and hidden % (owners * LANES) == 0
+        and H * HD == width
+    )
+
+
+def body(*args):
+    chosen = paired_body if pairable(args[0], args[12]) else general_body
+    return chosen(*args)
 
 
 def solution(mesh):
@@ -1065,6 +1422,4 @@
         P("fsdp"),
         P("fsdp"),
     )
-    paired = mesh.shape["seq"] == 2 and mesh.shape["fsdp"] % 2 == 0
-    chosen = paired_body if paired else general_body
-    return jax.shard_map(chosen, mesh=mesh, in_specs=in_specs, out_specs=out_specs, check_vma=False)
+    return jax.shard_map(body, mesh=mesh, in_specs=in_specs, out_specs=out_specs, check_vma=False)

time: 741 us -> 443 us (0.60)
  waiting for transfers between devices: 414 us -> 131 us
  blocking collectives: 50.7 us -> 0 us
  Pallas kernels: 182 us -> 226 us
    reduce_scatter x4 -> x0, waiting for transfers between devices: 198 us -> none  [owned(): part = lax.psum_scatter(grad, 'fsdp', scatter_dimension=0, tiled=True)]
    all_gather x4 -> x1, waiting for transfers between devices: 194 us -> 0.01 us  [paired_body(): rest = lax.all_gather(rest, 'fsdp', axis=0, tiled=True)]
    ppermute x9 -> x30, waiting for transfers between devices: 11.5 us -> 124 us  [the longest x23 113 us: to_next(): return lax.ppermute(values, 'fsdp', ring_perm(chips, hop))]
    psum x1 -> x0, blocking collectives: 50.7 us -> none  [paired_body(): all_sums = lax.psum(sums, ('fsdp', 'seq'))]
    pallas_call x4 -> x16, Pallas kernels: 86.4 us -> 124 us  [the longest x1 50.7 us: mlp(): pl.pallas_call(functools.partial(mlp_kernel, chips=chips), grid_spec=pltp...]
    concatenate x2 -> x0, local copies, waits for them, and re-layouts: 7.42 us -> none  [the longest x1 7.42 us: paired_body(): small = jnp.concatenate(vectors + (up_bias,))]
    pallas_call x1 -> x3, Pallas kernels: 45.9 us -> 52.1 us  [attention_back(): pl.pallas_call(functools.partial(attend_back_kernel, pieces=pieces, block...]
    ppermute x9 -> x30, starting transfers between devices: 34.3 us -> 36 us  [the longest x23 28.3 us: to_next(): return lax.ppermute(values, 'fsdp', ring_perm(chips, hop))]
  transfers between devices with their start and end apart: 21 -> 48, of which waited for: 9 -> 27; matrix products, arithmetic and copies ran while one was open for 2% -> 1% of each run, Pallas kernels for 16% -> 33%
where the time goes in v2:
time: 443 us; the launch traced here: 439 us
  Pallas kernels  226 us (51%)
  waiting for transfers between devices  131 us (30%)
  starting transfers between devices  44.9 us (10%)
  between operations  15.9 us (4%)
  local copies, waits for them, and re-layouts  14.5 us (3%)
  other arithmetic  6.05 us (1%)
    ppermute x23, waiting for transfers between devices, to_next(): return lax.ppermute(values, 'fsdp', ring_perm(chips, hop))  113 us
    pallas_call x3, Pallas kernels, attention_back(): pl.pallas_call(functools.partial(attend_back_kernel, pieces=pieces, block...  52.1 us
    pallas_call x1, Pallas kernels, mlp(): pl.pallas_call(functools.partial(mlp_kernel, chips=chips), grid_spec=pltp...  50.7 us
    pallas_call x10, Pallas kernels, add(): pl.pallas_call(functools.partial(ring_add_kernel, columns=columns, mode=m...  31.6 us
    pallas_call x1, Pallas kernels, attention(): pl.pallas_call(functools.partial(attend_kernel, pieces=pieces, block=bloc...  28.3 us
    ppermute x23, starting transfers between devices, to_next(): return lax.ppermute(values, 'fsdp', ring_perm(chips, hop))  28.3 us
    pallas_call x1, Pallas kernels, unproject(): pl.pallas_call(functools.partial(unproject_kernel, chips=chips), grid_spe...  19.5 us
    pallas_call x1, Pallas kernels, unmerge(): pl.pallas_call(functools.partial(unmerge_kernel, tokens=tokens), grid_spe...  14.5 us
  transfers between devices with their start and end apart: 48, of which 27 were waited for; matrix products, arithmetic and copies ran while one was open for 1% of the time, Pallas kernels for 33%

profile of v2, /device:TPU:0, one launch (start us, length us, event | category | flops | bytes accessed | tf_op | source)
XLA Modules:
  0.0 438.7 jit_solution(11985583154849549555)
XLA Ops:
  7.2 1.3 dynamic-slice_bitcast_fusion.place
  8.6 2.7 pack.1
  11.3 3.1 collective-permute-start.5
  15.2 12.3 %collective-permute-done.5.refs_7_ = bf16[64,3200]{1,0:T(8,128)(2,1)S(1)} collective-permute-done((bf16[64,3200]{1,0:T(8,128)(2,1)}, bf16[64,3200]{1,0:T(8,128)(2,1)S(1)}, u32[]{:S(2)}, u32[]{:S(2)}) %collective-permute-start.5) | collective-permute-done | bytes 409632 | tf_op jit(solution)/shard_map/ppermute | solution.py:1105
  27.4 2.4 collective-permute-start.6
  29.9 17.7 %collective-permute-done.6.refs_6_ = bf16[64,3200]{1,0:T(8,128)(2,1)} collective-permute-done((bf16[64,3200]{1,0:T(8,128)(2,1)S(1)}, bf16[64,3200]{1,0:T(8,128)(2,1)}, u32[]{:S(2)}, u32[]{:S(2)}) %collective-permute-start.6) | collective-permute-done | bytes 409632 | tf_op jit(solution)/shard_map/ppermute | solution.py:1105
  47.5 2.4 collective-permute-start.7
  50.5 17.4 %collective-permute-done.7.refs_5_ = bf16[64,3200]{1,0:T(8,128)(2,1)} collective-permute-done((bf16[64,3200]{1,0:T(8,128)(2,1)}, bf16[64,3200]{1,0:T(8,128)(2,1)}, u32[]{:S(2)}, u32[]{:S(2)}) %collective-permute-start.7) | collective-permute-done | bytes 409632 | tf_op jit(solution)/shard_map/ppermute | solution.py:1105
  67.9 2.5 collective-permute-start.8
  71.0 2.7 collective-permute-start.14
  73.8 13.5 %collective-permute-done.8.refs_4_ = bf16[64,3200]{1,0:T(8,128)(2,1)} collective-permute-done((bf16[64,3200]{1,0:T(8,128)(2,1)}, bf16[64,3200]{1,0:T(8,128)(2,1)}, u32[]{:S(2)}, u32[]{:S(2)}) %collective-permute-start.8) | collective-permute-done | bytes 409632 | tf_op jit(solution)/shard_map/ppermute | solution.py:1105
  87.4 1.2 broadcast_select_fusion.1.x_ref
  89.4 14.0 %project.1 = (bf16[3,688,512]{2,1,0:T(8,128)(2,1)}, bf16[3,688,512]{2,1,0:T(8,128)(2,1)}, bf16[688,1024]{1,0:T(8,128)(2,1)}, bf16[1024,3072]{1,0:T(8,128)(2,1)}, f32[16,1024]{1,0:T(8,128)}, /*index=5*/f32[1,4096]{1,0:T(1,128)}) custom-call(s32[15]{0:T(128)} %dynamic-slice_bitcast_fusion.place, bf16[688,1024]{1,0:T(8,128)(2,1)} %broadcast_select_fusion.1.x_ref, ...), custom_call_target="tpu_custom_call" | custom-call | flops 4328521728 | bytes 21037056 | tf_op jit(solution)/shard_map/project/pallas_call | solution.py:473
  103.6 1.2 collective-permute-start.1
  108.0 28.3 %attend.1 = (bf16[688,512]{1,0:T(8,128)(2,1)}, bf16[688,512]{1,0:T(8,128)(2,1)}, f32[688,128]{1,0:T(8,128)}, f32[688,128]{1,0:T(8,128)}) custom-call(s32[2]{0:T(128)} %fusion.1.valid, bf16[3,688,512]{2,1,0:T(8,128)(2,1)} %get-tuple-element.94.refs_0_, bf16[3,688,512]{2,1,0:T(8,128)(2,1)} %collective-permute-done.17.refs_1_), custom_call_target="tpu_custom_call" | custom-call | flops 16240345088 | bytes 5636096 | tf_op jit(solution)/shard_map/attend/pallas_call | solution.py:563
  136.3 3.7 collective-permute-start.18
  140.1 1.2 broadcast_select_fusion.cotangent_ref
  142.9 7.2 %merge.1 = (f32[688,1024]{1,0:T(8,128)}, f32[688,1024]{1,0:T(8,128)}, bf16[688,1024]{1,0:T(8,128)(2,1)}) custom-call(s32[15]{0:T(128)} %dynamic-slice_bitcast_fusion.place, bf16[688,1024]{1,0:T(8,128)(2,1)} %broadcast_select_fusion.1.x_ref, bf16[688,512]{1,0:T(8,128)(2,1)} %get-tuple-element.96.own_ref.refs_2_, bf16[688,512]{1,0:T(8,128)(2,1)} %copy-done.4, ...), custom_call_target="tpu_custom_call" | custom-call | flops 1442840576 | bytes 11960320 | tf_op jit(solution)/shard_map/merge/pallas_call | solution.py:721
  150.1 50.7 %mlp.1 = (f32[688,1024]{1,0:T(8,128)}, f32[688,1024]{1,0:T(8,128)}, bf16[8,64,4096]{2,1,0:T(8,128)(2,1)}, bf16[8,64,4096]{2,1,0:T(8,128)(2,1)}, bf16[8,64,4096]{...) custom-call(s32[15]{0:T(128)} %dynamic-slice_bitcast_fusion.place, ...), custom_call_target="tpu_custom_call" | custom-call | flops 34628173824 | bytes 42008576 | tf_op jit(solution)/shard_map/mlp/pallas_call | solution.py:839
  201.4 14.5 %unmerge.1 = (bf16[688,1024]{1,0:T(8,128)(2,1)}, f32[688,1024]{1,0:T(8,128)}, bf16[688,512]{1,0:T(8,128)(2,1)}, bf16[688,512]{1,0:T(8,128)(2,1)}, bf16[8,64,1024...) custom-call(s32[15]{0:T(128)} %dynamic-slice_bitcast_fusion.place, ...), custom_call_target="tpu_custom_call" | custom-call | flops 2885681152 | bytes 25329664 | tf_op jit(solution)/shard_map/unmerge/pallas_call | solution.py:948
  217.2 1.6 collective-permute-done.23.refs_5_.refs_11_
  219.8 2.5 ring_add.10
  222.3 2.5 collective-permute-start.24
  226.1 13.7 %attend_back.3 = (bf16[3,688,512]{2,1,0:T(8,128)(2,1)}, bf16[3,688,512]{2,1,0:T(8,128)(2,1)}) custom-call(s32[2]{0:T(128)} %fusion.1.valid, bf16[3,688,512]{2,1,0:T(8,128)(2,1)} %get-tuple-element.94.refs_0_, bf16[3,688,512]{2,1,0:T(8,128)(2,1)} %collective-permute-done.17.refs_1_, bf16[688,512]{1,0:T(8,128)(2,1)} %get-tuple-element.96.own_ref.refs_2_, ...), custom_call_target="tpu_custom_call" | custom-call | flops 121802588160 | bytes 45088768 | tf_op jit(solution)/shard_map/attend_back/pallas_call | solution.py:672
  239.8 1.5 collective-permute-done.25.refs_13_
  242.1 4.0 ring_add.11
  246.1 1.7 collective-permute-start.26
  248.4 1.1 copy-done.9
  249.5 24.6 %attend_back.4 = (bf16[3,688,512]{2,1,0:T(8,128)(2,1)}, bf16[3,688,512]{2,1,0:T(8,128)(2,1)}) custom-call(s32[2]{0:T(128)} %fusion.1.valid, bf16[3,688,512]{2,1,0:T(8,128)(2,1)} %get-tuple-element.94.refs_0_, bf16[3,688,512]{2,1,0:T(8,128)(2,1)} %collective-permute-done.17.refs_1_, ...), custom_call_target="tpu_custom_call", output_to_operand_aliasing={{0}: (9, {}), {1}: (10, {})} | custom-call | flops 243605176320 | bytes 90177536 | tf_op jit(solution)/shard_map/attend_back/pallas_call | solution.py:672
  274.3 1.6 collective-permute-done.27.refs_13_
  276.0 4.5 %ring_add.12 = (bf16[64,9216]{1,0:T(8,128)(2,1)}, bf16[64,9216]{1,0:T(8,128)(2,1)}) custom-call(bf16[8,64,4096]{2,1,0:T(8,128)(2,1)} %get-tuple-element.107.refs_0_.refs_6_, bf16[8,64,4096]{2,1,0:T(8,128)(2,1)} %collective-permute-done.21.refs_1_.refs_7_, bf16[8,64,4096]{2,1,0:T(8,128)(2,1)} %get-tuple-element.109.refs_2_.refs_8_, ...), custom_call_target="tpu_custom_call" | custom-call | flops 55296 | bytes 147456 | tf_op jit(solution)/shard_map/ring_add/pallas_call | solution.py:1180
  280.4 1.8 collective-permute-start.28
  282.7 13.8 %attend_back.5 = (bf16[3,688,512]{2,1,0:T(8,128)(2,1)}, bf16[3,688,512]{2,1,0:T(8,128)(2,1)}) custom-call(s32[2]{0:T(128)} %fusion.1.valid, bf16[3,688,512]{2,1,0:T(8,128)(2,1)} %get-tuple-element.94.refs_0_, bf16[3,688,512]{2,1,0:T(8,128)(2,1)} %collective-permute-done.17.refs_1_, ...), custom_call_target="tpu_custom_call", output_to_operand_aliasing={{0}: (9, {}), {1}: (10, {})} | custom-call | flops 121802588160 | bytes 45088768 | tf_op jit(solution)/shard_map/attend_back/pallas_call | solution.py:672
  296.4 11.0 %collective-permute-done.28.refs_12_ = bf16[64,9216]{1,0:T(8,128)(2,1)S(1)} collective-permute-done((bf16[64,9216]{1,0:T(8,128)(2,1)}, bf16[64,9216]{1,0:T(8,128)(2,1)S(1)}, u32[]{:S(2)}, u32[]{:S(2)}) %collective-permute-start.28) | collective-permute-done | bytes 1179680 | tf_op jit(solution)/shard_map/ppermute | solution.py:1105
  307.4 1.8 collective-permute-done.29.refs_13_
  310.2 4.5 %ring_add.13 = (bf16[64,9216]{1,0:T(8,128)(2,1)}, bf16[64,9216]{1,0:T(8,128)(2,1)}, bf16[3,688,512]{2,1,0:T(8,128)(2,1)}) custom-call(bf16[8,64,4096]{2,1,0:T(8,128)(2,1)} %get-tuple-element.107.refs_0_.refs_6_, bf16[8,64,4096]{2,1,0:T(8,128)(2,1)} %collective-permute-done.21.refs_1_.refs_7_, ...), custom_call_target="tpu_custom_call", output_to_operand_aliasing={{2}: (14, {})} | custom-call | flops 55296 | bytes 147456 | tf_op jit(solution)/shard_map/ring_add/pallas_call | solution.py:1180
  314.8 2.0 collective-permute-start.31
  317.1 2.1 collective-permute-done.33.far_ref
  319.2 1.3 copy-done.5
  320.4 19.5 %unproject.1 = (bf16[688,1024]{1,0:T(8,128)(2,1)}, bf16[8,64,3072]{2,1,0:T(8,128)(2,1)}, bf16[8,64,3072]{2,1,0:T(8,128)(2,1)}, bf16[8,64,128]{2,1,0:T(8,128)(2,1)}, bf16[8,64,128]{2,1,0:T(8,128)(2,1)}) custom-call(s32[15]{0:T(128)} %dynamic-slice_bitcast_fusion.place, bf16[688,1024]{1,0:T(8,128)(2,1)} %broadcast_select_fusion.1.x_ref, ...), custom_call_target="tpu_custom_call" | custom-call | flops 135266304 | bytes 394752 | tf_op jit(solution)/shard_map/unproject/pallas_call | solution.py:1046
  339.9 3.5 collective-permute-done.31.refs_6_
  343.4 2.0 collective-permute-done.32.refs_7_
  345.4 3.4 ring_add.14
  348.8 1.8 collective-permute-start.34
  350.6 2.3 collective-permute-start.43
  352.9 1.9 collective-permute-done.36.refs_3_.refs_7_
  356.6 2.0 ring_add.15
  358.5 1.7 collective-permute-start.37
  360.5 6.6 %collective-permute-done.38.refs_9_ = bf16[64,1536]{1,0:T(8,128)(2,1)S(1)} collective-permute-done((bf16[64,1536]{1,0:T(8,128)(2,1)}, bf16[64,1536]{1,0:T(8,128)(2,1)S(1)}, u32[]{:S(2)}, u32[]{:S(2)}) %collective-permute-start.38) | collective-permute-done | bytes 196640 | tf_op jit(solution)/shard_map/ppermute | solution.py:1105
  368.5 2.7 ring_add.16
  373.2 8.5 %collective-permute-done.39.refs_8_ = bf16[64,3200]{1,0:T(8,128)(2,1)S(1)} collective-permute-done((bf16[64,3200]{1,0:T(8,128)(2,1)}, bf16[64,3200]{1,0:T(8,128)(2,1)S(1)}, u32[]{:S(2)}, u32[]{:S(2)}) %collective-permute-start.39) | collective-permute-done | bytes 409632 | tf_op jit(solution)/shard_map/ppermute | solution.py:1105
  383.2 2.8 ring_add.17
  387.0 1.1 collective-permute-start.42
  388.1 6.5 %collective-permute-done.43.refs_10_.came_ref = bf16[64,9216]{1,0:T(8,128)(2,1)} collective-permute-done((bf16[64,9216]{1,0:T(8,128)(2,1)}, bf16[64,9216]{1,0:T(8,128)(2,1)}, u32[]{:S(2)}, u32[]{:S(2)}) %collective-permute-start.43) | collective-permute-done | bytes 1179680 | tf_op jit(solution)/shard_map/ppermute | solution.py:1293
  394.6 3.3 collective-permute-done.41.refs_8_
  397.9 1.3 collective-permute-done.42.refs_9_
  399.9 2.8 ring_add.18
  404.8 9.4 %collective-permute-done.44.refs_4_ = bf16[64,3200]{1,0:T(8,128)(2,1)S(1)} collective-permute-done((bf16[64,3200]{1,0:T(8,128)(2,1)}, bf16[64,3200]{1,0:T(8,128)(2,1)S(1)}, u32[]{:S(2)}, u32[]{:S(2)}) %collective-permute-start.44) | collective-permute-done | bytes 409632 | tf_op jit(solution)/shard_map/ppermute | solution.py:1105
  415.8 2.4 ring_add.19.part_ref
  418.2 1.2 select_bitcast_fusion
  419.5 3.5 finish_rest.1
  423.0 1.7 bitcast_convert_fusion
  424.7 3.9 collective-permute-done.46.came_ref
  429.4 2.2 finish_first.1
  (123 shorter events, 27.2 us)
Async XLA Ops:
  7.2 7.2 %copy-start.6 = (bf16[1,688,1024]{2,1,0:T(8,128)(2,1)S(1)}, bf16[1,688,1024]{2,1,0:T(8,128)(2,1)}, u32[]{:S(2)}) copy-start(bf16[1,688,1024]{2,1,0:T(8,128)(2,1)} %param.19) | copy-start | bytes 4227076
  7.2 134.9 %all-gather.2.cloned.1.call-start = ((), (), s32[]{:S(2)}) async-start(), calls=%async_computation | async-start | bytes 20054016 | tf_op jit(solution)/shard_map/all_gather | solution.py:1306
  11.3 16.1 %collective-permute-start.5 = (bf16[64,3200]{1,0:T(8,128)(2,1)}, bf16[64,3200]{1,0:T(8,128)(2,1)S(1)}, u32[]{:S(2)}, u32[]{:S(2)}) collective-permute-start(bf16[64,3200]{1,0:T(8,128)(2,1)} %get-tuple-element.93.refs_0_), channel_id=1, source_target_pairs={{0,8},{2,10},{8,16},{10,18},{16,24},{18,26},{24,28},{26,30},{28,20... | collective-permute-start | bytes 1228808 | tf_op jit(solution)/shard_map/ppermute | solution.py:1105
  14.4 59.4 %collective-permute-start = (bf16[688,1024]{1,0:T(8,128)(2,1)S(1)}, bf16[688,1024]{1,0:T(8,128)(2,1)S(1)}, u32[]{:S(2)}, u32[]{:S(2)}) collective-permute-start(bf16[688,1024]{1,0:T(8,128)(2,1)S(1)} %bitcast.15), channel_id=1, source_target_pairs={{1,2},{2,1},{5,6},{6,5},{9,10},{10,9},{13,14},{14,13},{17,18},{18,... | collective-permute-start | bytes 4227080 | tf_op jit(solution)/shard_map/ppermute | solution.py:1284
  15.1 14.7 %collective-permute-start.2 = (bf16[64,3200]{1,0:T(8,128)(2,1)}, bf16[64,3200]{1,0:T(8,128)(2,1)S(1)}, u32[]{:S(2)}, u32[]{:S(2)}) collective-permute-start(bf16[64,3200]{1,0:T(8,128)(2,1)} %get-tuple-element.93.refs_0_), channel_id=1, source_target_pairs={{0,4},{2,6},{8,0},{10,2},{16,8},{18,10},{24,16},{26,18},{28,24},{3... | collective-permute-start | bytes 1228808 | tf_op jit(solution)/shard_map/ppermute | solution.py:1105
  27.4 61.2 %copy-start.26 = (bf16[64,3200]{1,0:T(8,128)(2,1)}, bf16[64,3200]{1,0:T(8,128)(2,1)S(1)}, u32[]{:S(2)}) copy-start(bf16[64,3200]{1,0:T(8,128)(2,1)S(1)} %collective-permute-done.5.refs_7_) | copy-start | bytes 1228804
  27.4 20.1 %collective-permute-start.6 = (bf16[64,3200]{1,0:T(8,128)(2,1)S(1)}, bf16[64,3200]{1,0:T(8,128)(2,1)}, u32[]{:S(2)}, u32[]{:S(2)}) collective-permute-start(bf16[64,3200]{1,0:T(8,128)(2,1)S(1)} %collective-permute-done.5.refs_7_), channel_id=1, source_target_pairs={{0,8},{2,10},{8,16},{10,18},{16,24},{18,26},{24,28},{26,30},{28,20... | collective-permute-start | bytes 1228808 | tf_op jit(solution)/shard_map/ppermute | solution.py:1105
  29.8 20.2 %collective-permute-start.9 = (bf16[64,3200]{1,0:T(8,128)(2,1)}, bf16[64,3200]{1,0:T(8,128)(2,1)S(1)}, u32[]{:S(2)}, u32[]{:S(2)}) collective-permute-start(bf16[64,3200]{1,0:T(8,128)(2,1)} %get-tuple-element.93.refs_0_), channel_id=1, source_target_pairs={{0,2},{2,0},{4,6},{6,4},{8,10},{10,8},{12,14},{14,12},{16,18},{18,... | collective-permute-start | bytes 1228808 | tf_op jit(solution)/shard_map/ppermute | solution.py:1290
  29.8 44.0 %copy-start.27 = (bf16[64,3200]{1,0:T(8,128)(2,1)}, bf16[64,3200]{1,0:T(8,128)(2,1)S(1)}, u32[]{:S(2)}) copy-start(bf16[64,3200]{1,0:T(8,128)(2,1)S(1)} %collective-permute-done.2.refs_1_) | copy-start | bytes 1228804
  29.8 20.7 %collective-permute-start.3 = (bf16[64,3200]{1,0:T(8,128)(2,1)S(1)}, bf16[64,3200]{1,0:T(8,128)(2,1)}, u32[]{:S(2)}, u32[]{:S(2)}) collective-permute-start(bf16[64,3200]{1,0:T(8,128)(2,1)S(1)} %collective-permute-done.2.refs_1_), channel_id=1, source_target_pairs={{0,4},{2,6},{8,0},{10,2},{16,8},{18,10},{24,16},{26,18},{28,24},{3... | collective-permute-start | bytes 1228808 | tf_op jit(solution)/shard_map/ppermute | solution.py:1105
  47.5 20.4 %collective-permute-start.7 = (bf16[64,3200]{1,0:T(8,128)(2,1)}, bf16[64,3200]{1,0:T(8,128)(2,1)}, u32[]{:S(2)}, u32[]{:S(2)}) collective-permute-start(bf16[64,3200]{1,0:T(8,128)(2,1)} %collective-permute-done.6.refs_6_), channel_id=1, source_target_pairs={{0,8},{2,10},{8,16},{10,18},{16,24},{18,26},{24,28},{26,30},{28,20... | collective-permute-start | bytes 1228808 | tf_op jit(solution)/shard_map/ppermute | solution.py:1105
  50.0 20.4 %collective-permute-start.16 = (bf16[64,3200]{1,0:T(8,128)(2,1)S(1)}, bf16[64,3200]{1,0:T(8,128)(2,1)S(1)}, u32[]{:S(2)}, u32[]{:S(2)}) collective-permute-start(bf16[64,3200]{1,0:T(8,128)(2,1)S(1)} %collective-permute-done.5.refs_7_), channel_id=1, source_target_pairs={{0,2},{2,0},{4,6},{6,4},{8,10},{10,8},{12,14},{14,12},{16,18},{18,... | collective-permute-start | bytes 1228808 | tf_op jit(solution)/shard_map/ppermute | solution.py:1290
  50.0 23.9 %copy-start.28 = (bf16[64,3200]{1,0:T(8,128)(2,1)}, bf16[64,3200]{1,0:T(8,128)(2,1)S(1)}, u32[]{:S(2)}) copy-start(bf16[64,3200]{1,0:T(8,128)(2,1)S(1)} %collective-permute-done.9.refs_8_) | copy-start | bytes 1228804
  50.0 20.4 %collective-permute-start.10 = (bf16[64,3200]{1,0:T(8,128)(2,1)S(1)}, bf16[64,3200]{1,0:T(8,128)(2,1)S(1)}, u32[]{:S(2)}, u32[]{:S(2)}) collective-permute-start(bf16[64,3200]{1,0:T(8,128)(2,1)S(1)} %collective-permute-done.2.refs_1_), channel_id=1, source_target_pairs={{0,2},{2,0},{4,6},{6,4},{8,10},{10,8},{12,14},{14,12},{16,18},{18,... | collective-permute-start | bytes 1228808 | tf_op jit(solution)/shard_map/ppermute | solution.py:1290
  50.5 20.5 %collective-permute-start.4 = (bf16[64,3200]{1,0:T(8,128)(2,1)}, bf16[64,3200]{1,0:T(8,128)(2,1)}, u32[]{:S(2)}, u32[]{:S(2)}) collective-permute-start(bf16[64,3200]{1,0:T(8,128)(2,1)} %collective-permute-done.3.refs_2_), channel_id=1, source_target_pairs={{0,4},{2,6},{8,0},{10,2},{16,8},{18,10},{24,16},{26,18},{28,24},{3... | collective-permute-start | bytes 1228808 | tf_op jit(solution)/shard_map/ppermute | solution.py:1105
  67.9 19.4 %collective-permute-start.8 = (bf16[64,3200]{1,0:T(8,128)(2,1)}, bf16[64,3200]{1,0:T(8,128)(2,1)}, u32[]{:S(2)}, u32[]{:S(2)}) collective-permute-start(bf16[64,3200]{1,0:T(8,128)(2,1)} %collective-permute-done.7.refs_5_), channel_id=1, source_target_pairs={{0,8},{2,10},{8,16},{10,18},{16,24},{18,26},{24,28},{26,30},{28,20... | collective-permute-start | bytes 1228808 | tf_op jit(solution)/shard_map/ppermute | solution.py:1105
  70.4 16.9 %copy-start.29 = (bf16[64,3200]{1,0:T(8,128)(2,1)}, bf16[64,3200]{1,0:T(8,128)(2,1)S(1)}, u32[]{:S(2)}) copy-start(bf16[64,3200]{1,0:T(8,128)(2,1)S(1)} %collective-permute-done.16.refs_15_) | copy-start | bytes 1228804
  70.4 18.2 %collective-permute-start.15 = (bf16[64,3200]{1,0:T(8,128)(2,1)}, bf16[64,3200]{1,0:T(8,128)(2,1)}, u32[]{:S(2)}, u32[]{:S(2)}) collective-permute-start(bf16[64,3200]{1,0:T(8,128)(2,1)} %collective-permute-done.6.refs_6_), channel_id=1, source_target_pairs={{0,2},{2,0},{4,6},{6,4},{8,10},{10,8},{12,14},{14,12},{16,18},{18,... | collective-permute-start | bytes 1228808 | tf_op jit(solution)/shard_map/ppermute | solution.py:1290
  70.4 16.9 %copy-start.30 = (bf16[64,3200]{1,0:T(8,128)(2,1)}, bf16[64,3200]{1,0:T(8,128)(2,1)S(1)}, u32[]{:S(2)}) copy-start(bf16[64,3200]{1,0:T(8,128)(2,1)S(1)} %collective-permute-done.10.refs_9_) | copy-start | bytes 1228804
  70.4 18.2 %collective-permute-start.11 = (bf16[64,3200]{1,0:T(8,128)(2,1)}, bf16[64,3200]{1,0:T(8,128)(2,1)}, u32[]{:S(2)}, u32[]{:S(2)}) collective-permute-start(bf16[64,3200]{1,0:T(8,128)(2,1)} %collective-permute-done.3.refs_2_), channel_id=1, source_target_pairs={{0,2},{2,0},{4,6},{6,4},{8,10},{10,8},{12,14},{14,12},{16,18},{18,... | collective-permute-start | bytes 1228808 | tf_op jit(solution)/shard_map/ppermute | solution.py:1290
  71.0 17.6 %collective-permute-start.14 = (bf16[64,3200]{1,0:T(8,128)(2,1)}, bf16[64,3200]{1,0:T(8,128)(2,1)}, u32[]{:S(2)}, u32[]{:S(2)}) collective-permute-start(bf16[64,3200]{1,0:T(8,128)(2,1)} %collective-permute-done.7.refs_5_), channel_id=1, source_target_pairs={{0,2},{2,0},{4,6},{6,4},{8,10},{10,8},{12,14},{14,12},{16,18},{18,... | collective-permute-start | bytes 1228808 | tf_op jit(solution)/shard_map/ppermute | solution.py:1290
  73.8 14.8 %collective-permute-start.12 = (bf16[64,3200]{1,0:T(8,128)(2,1)}, bf16[64,3200]{1,0:T(8,128)(2,1)}, u32[]{:S(2)}, u32[]{:S(2)}) collective-permute-start(bf16[64,3200]{1,0:T(8,128)(2,1)} %collective-permute-done.4.refs_3_), channel_id=1, source_target_pairs={{0,2},{2,0},{4,6},{6,4},{8,10},{10,8},{12,14},{14,12},{16,18},{18,... | collective-permute-start | bytes 1228808 | tf_op jit(solution)/shard_map/ppermute | solution.py:1290
  87.3 2.1 collective-permute-start.13
  88.6 16.2 %copy-start.7 = (bf16[1,688,1024]{2,1,0:T(8,128)(2,1)S(1)}, bf16[1,688,1024]{2,1,0:T(8,128)(2,1)}, u32[]{:S(2)}) copy-start(bf16[1,688,1024]{2,1,0:T(8,128)(2,1)} %param.36) | copy-start | bytes 4227076
  103.5 4.5 %collective-permute-start.17 = (bf16[3,688,512]{2,1,0:T(8,128)(2,1)}, bf16[3,688,512]{2,1,0:T(8,128)(2,1)}, u32[]{:S(2)}, u32[]{:S(2)}) collective-permute-start(bf16[3,688,512]{2,1,0:T(8,128)(2,1)} %get-tuple-element.95), channel_id=1, source_target_pairs={{0,2},{2,0},{4,6},{6,4},{8,10},{10,8},{12,14},{14,12},{16,18},{18,... | collective-permute-start | bytes 6340616 | tf_op jit(solution)/shard_map/ppermute | solution.py:1290
  103.6 2.8 collective-permute-start.1
  104.8 35.3 %collective-permute-start.19 = (bf16[688,1024]{1,0:T(8,128)(2,1)S(1)}, bf16[688,1024]{1,0:T(8,128)(2,1)S(1)}, u32[]{:S(2)}, u32[]{:S(2)}) collective-permute-start(bf16[688,1024]{1,0:T(8,128)(2,1)S(1)} %bitcast.16), channel_id=1, source_target_pairs={{1,2},{2,1},{5,6},{6,5},{9,10},{10,9},{13,14},{14,13},{17,18},{18,... | collective-permute-start | bytes 4227080 | tf_op jit(solution)/shard_map/ppermute | solution.py:1284
  136.3 5.7 %collective-permute-start.18 = (bf16[688,512]{1,0:T(8,128)(2,1)}, bf16[688,512]{1,0:T(8,128)(2,1)S(1)}, u32[]{:S(2)}, u32[]{:S(2)}) collective-permute-start(bf16[688,512]{1,0:T(8,128)(2,1)} %get-tuple-element.97.refs_3_), channel_id=1, source_target_pairs={{0,2},{2,0},{4,6},{6,4},{8,10},{10,8},{12,14},{14,12},{16,18},{18,... | collective-permute-start | bytes 2113544 | tf_op jit(solution)/shard_map/ppermute | solution.py:1290
  200.8 18.0 %collective-permute-start.21 = (bf16[8,64,4096]{2,1,0:T(8,128)(2,1)}, bf16[8,64,4096]{2,1,0:T(8,128)(2,1)}, u32[]{:S(2)}, u32[]{:S(2)}) collective-permute-start(bf16[8,64,4096]{2,1,0:T(8,128)(2,1)} %get-tuple-element.108), channel_id=1, source_target_pairs={{0,2},{2,0},{4,6},{6,4},{8,10},{10,8},{12,14},{14,12},{16,18},{18,... | collective-permute-start | bytes 12582920 | tf_op jit(solution)/shard_map/ppermute | solution.py:1290
  201.3 17.6 %collective-permute-start.22 = (bf16[8,64,4096]{2,1,0:T(8,128)(2,1)}, bf16[8,64,4096]{2,1,0:T(8,128)(2,1)}, u32[]{:S(2)}, u32[]{:S(2)}) collective-permute-start(bf16[8,64,4096]{2,1,0:T(8,128)(2,1)} %get-tuple-element.110), channel_id=1, source_target_pairs={{0,2},{2,0},{4,6},{6,4},{8,10},{10,8},{12,14},{14,12},{16,18},{18,... | collective-permute-start | bytes 12582920 | tf_op jit(solution)/shard_map/ppermute | solution.py:1290
  215.9 2.9 collective-permute-start.23
  216.3 8.9 %collective-permute-start.30 = (bf16[688,512]{1,0:T(8,128)(2,1)}, bf16[688,512]{1,0:T(8,128)(2,1)S(1)}, u32[]{:S(2)}, u32[]{:S(2)}) collective-permute-start(bf16[688,512]{1,0:T(8,128)(2,1)} %get-tuple-element.120), channel_id=1, source_target_pairs={{0,2},{2,0},{4,6},{6,4},{8,10},{10,8},{12,14},{14,12},{16,18},{18,... | collective-permute-start | bytes 2113544 | tf_op jit(solution)/shard_map/ppermute | solution.py:1290
  216.5 31.9 %collective-permute-start.20 = (bf16[688,1024]{1,0:T(8,128)(2,1)}, bf16[688,1024]{1,0:T(8,128)(2,1)S(1)}, u32[]{:S(2)}, u32[]{:S(2)}) collective-permute-start(bf16[688,1024]{1,0:T(8,128)(2,1)} %get-tuple-element.106), channel_id=1, source_target_pairs={{1,2},{2,1},{5,6},{6,5},{9,10},{10,9},{13,14},{14,13},{17,18},{18,... | collective-permute-start | bytes 4227080 | tf_op jit(solution)/shard_map/ppermute | solution.py:1284
  222.3 17.5 %collective-permute-start.24 = (bf16[64,4608]{1,0:T(8,128)(2,1)}, bf16[64,4608]{1,0:T(8,128)(2,1)S(1)}, u32[]{:S(2)}, u32[]{:S(2)}) collective-permute-start(bf16[64,4608]{1,0:T(8,128)(2,1)} %get-tuple-element.113.refs_8_), channel_id=1, source_target_pairs={{0,8},{2,10},{8,16},{10,18},{16,24},{18,26},{24,28},{26,30},{28,20... | collective-permute-start | bytes 1769480 | tf_op jit(solution)/shard_map/ppermute | solution.py:1105
  224.8 16.5 %collective-permute-start.25 = (bf16[64,4608]{1,0:T(8,128)(2,1)}, bf16[64,4608]{1,0:T(8,128)(2,1)S(1)}, u32[]{:S(2)}, u32[]{:S(2)}) collective-permute-start(bf16[64,4608]{1,0:T(8,128)(2,1)} %get-tuple-element.114.refs_9_), channel_id=1, source_target_pairs={{0,4},{2,6},{8,0},{10,2},{16,8},{18,10},{24,16},{26,18},{28,24},{3... | collective-permute-start | bytes 1769480 | tf_op jit(solution)/shard_map/ppermute | solution.py:1105
  239.8 1.5 copy-start.14
  246.1 28.2 %collective-permute-start.26 = (bf16[64,9216]{1,0:T(8,128)(2,1)}, bf16[64,9216]{1,0:T(8,128)(2,1)}, u32[]{:S(2)}, u32[]{:S(2)}) collective-permute-start(bf16[64,9216]{1,0:T(8,128)(2,1)} %get-tuple-element.115.refs_10_), channel_id=1, source_target_pairs={{0,8},{2,10},{8,16},{10,18},{16,24},{18,26},{24,28},{26,30},{28,20... | collective-permute-start | bytes 3538952 | tf_op jit(solution)/shard_map/ppermute | solution.py:1105
  247.9 28.1 %collective-permute-start.27 = (bf16[64,9216]{1,0:T(8,128)(2,1)}, bf16[64,9216]{1,0:T(8,128)(2,1)}, u32[]{:S(2)}, u32[]{:S(2)}) collective-permute-start(bf16[64,9216]{1,0:T(8,128)(2,1)} %get-tuple-element.116.refs_11_), channel_id=1, source_target_pairs={{0,4},{2,6},{8,0},{10,2},{16,8},{18,10},{24,16},{26,18},{28,24},{3... | collective-permute-start | bytes 3538952 | tf_op jit(solution)/shard_map/ppermute | solution.py:1105
  280.4 27.0 %collective-permute-start.28 = (bf16[64,9216]{1,0:T(8,128)(2,1)}, bf16[64,9216]{1,0:T(8,128)(2,1)S(1)}, u32[]{:S(2)}, u32[]{:S(2)}) collective-permute-start(bf16[64,9216]{1,0:T(8,128)(2,1)} %get-tuple-element.117.refs_10_), channel_id=1, source_target_pairs={{0,8},{2,10},{8,16},{10,18},{16,24},{18,26},{24,28},{26,30},{28,20... | collective-permute-start | bytes 3538952 | tf_op jit(solution)/shard_map/ppermute | solution.py:1105
  282.2 27.0 %collective-permute-start.29 = (bf16[64,9216]{1,0:T(8,128)(2,1)}, bf16[64,9216]{1,0:T(8,128)(2,1)S(1)}, u32[]{:S(2)}, u32[]{:S(2)}) collective-permute-start(bf16[64,9216]{1,0:T(8,128)(2,1)} %get-tuple-element.118.refs_11_), channel_id=1, source_target_pairs={{0,4},{2,6},{8,0},{10,2},{16,8},{18,10},{24,16},{26,18},{28,24},{3... | collective-permute-start | bytes 3538952 | tf_op jit(solution)/shard_map/ppermute | solution.py:1105
  307.4 1.8 copy-start.12
  314.7 4.5 %collective-permute-start.33 = (bf16[3,688,512]{2,1,0:T(8,128)(2,1)}, bf16[3,688,512]{2,1,0:T(8,128)(2,1)S(1)}, u32[]{:S(2)}, u32[]{:S(2)}) collective-permute-start(bf16[3,688,512]{2,1,0:T(8,128)(2,1)} %get-tuple-element.133), channel_id=1, source_target_pairs={{0,2},{2,0},{4,6},{6,4},{8,10},{10,8},{12,14},{14,12},{16,18},{18,... | collective-permute-start | bytes 6340616 | tf_op jit(solution)/shard_map/ppermute | solution.py:1290
  314.8 28.6 %collective-permute-start.31 = (bf16[64,9216]{1,0:T(8,128)(2,1)}, bf16[64,9216]{1,0:T(8,128)(2,1)S(1)}, u32[]{:S(2)}, u32[]{:S(2)}) collective-permute-start(bf16[64,9216]{1,0:T(8,128)(2,1)} %get-tuple-element.128), channel_id=1, source_target_pairs={{0,8},{2,10},{8,16},{10,18},{16,24},{18,26},{24,28},{26,30},{28,20... | collective-permute-start | bytes 3538952 | tf_op jit(solution)/shard_map/ppermute | solution.py:1105
  316.8 28.6 %collective-permute-start.32 = (bf16[64,9216]{1,0:T(8,128)(2,1)}, bf16[64,9216]{1,0:T(8,128)(2,1)}, u32[]{:S(2)}, u32[]{:S(2)}) collective-permute-start(bf16[64,9216]{1,0:T(8,128)(2,1)} %get-tuple-element.129), channel_id=1, source_target_pairs={{0,4},{2,6},{8,0},{10,2},{16,8},{18,10},{24,16},{26,18},{28,24},{3... | collective-permute-start | bytes 3538952 | tf_op jit(solution)/shard_map/ppermute | solution.py:1105
  319.2 1.3 copy-start.5
  343.4 2.0 copy-start.11
  348.8 6.1 %collective-permute-start.35 = (bf16[8,64,3072]{2,1,0:T(8,128)(2,1)}, bf16[8,64,3072]{2,1,0:T(8,128)(2,1)S(1)}, u32[]{:S(2)}, u32[]{:S(2)}) collective-permute-start(bf16[8,64,3072]{2,1,0:T(8,128)(2,1)} %get-tuple-element.142), channel_id=1, source_target_pairs={{0,2},{2,0},{4,6},{6,4},{8,10},{10,8},{12,14},{14,12},{16,18},{18,... | collective-permute-start | bytes 9437192 | tf_op jit(solution)/shard_map/ppermute | solution.py:1290
  348.8 24.4 %collective-permute-start.34 = (bf16[688,1024]{1,0:T(8,128)(2,1)}, bf16[688,1024]{1,0:T(8,128)(2,1)}, u32[]{:S(2)}, u32[]{:S(2)}) collective-permute-start(bf16[688,1024]{1,0:T(8,128)(2,1)} %get-tuple-element.140), channel_id=1, source_target_pairs={{1,2},{2,1},{5,6},{6,5},{9,10},{10,9},{13,14},{14,13},{17,18},{18,... | collective-permute-start | bytes 4227080 | tf_op jit(solution)/shard_map/ppermute | solution.py:1284
  350.6 44.0 %collective-permute-start.43 = (bf16[64,9216]{1,0:T(8,128)(2,1)}, bf16[64,9216]{1,0:T(8,128)(2,1)}, u32[]{:S(2)}, u32[]{:S(2)}) collective-permute-start(bf16[64,9216]{1,0:T(8,128)(2,1)} %get-tuple-element.151.part_ref), channel_id=1, source_target_pairs={{0,1},{1,0},{2,3},{3,2},{4,5},{5,4},{6,7},{7,6},{8,9},{9,8},{10,11... | collective-permute-start | bytes 3538952 | tf_op jit(solution)/shard_map/ppermute | solution.py:1293
  352.9 1.9 collective-permute-start.36
  354.9 1.7 copy-start
  358.5 8.6 %collective-permute-start.37 = (bf16[64,1664]{1,0:T(8,128)(2,1)}, bf16[64,1664]{1,0:T(8,128)(2,1)S(1)}, u32[]{:S(2)}, u32[]{:S(2)}) collective-permute-start(bf16[64,1664]{1,0:T(8,128)(2,1)} %get-tuple-element.145), channel_id=1, source_target_pairs={{0,8},{2,10},{8,16},{10,18},{16,24},{18,26},{24,28},{26,30},{28,20... | collective-permute-start | bytes 638984 | tf_op jit(solution)/shard_map/ppermute | solution.py:1105
  360.3 6.9 %collective-permute-start.38 = (bf16[64,1536]{1,0:T(8,128)(2,1)}, bf16[64,1536]{1,0:T(8,128)(2,1)S(1)}, u32[]{:S(2)}, u32[]{:S(2)}) collective-permute-start(bf16[64,1536]{1,0:T(8,128)(2,1)} %get-tuple-element.146), channel_id=1, source_target_pairs={{0,4},{2,6},{8,0},{10,2},{16,8},{18,10},{24,16},{26,18},{28,24},{3... | collective-permute-start | bytes 589832 | tf_op jit(solution)/shard_map/ppermute | solution.py:1105
  371.1 10.6 %collective-permute-start.39 = (bf16[64,3200]{1,0:T(8,128)(2,1)}, bf16[64,3200]{1,0:T(8,128)(2,1)S(1)}, u32[]{:S(2)}, u32[]{:S(2)}) collective-permute-start(bf16[64,3200]{1,0:T(8,128)(2,1)} %get-tuple-element.147), channel_id=1, source_target_pairs={{0,8},{2,10},{8,16},{10,18},{16,24},{18,26},{24,28},{26,30},{28,20... | collective-permute-start | bytes 1228808 | tf_op jit(solution)/shard_map/ppermute | solution.py:1105
  372.1 10.3 %collective-permute-start.40 = (bf16[64,3200]{1,0:T(8,128)(2,1)}, bf16[64,3200]{1,0:T(8,128)(2,1)S(1)}, u32[]{:S(2)}, u32[]{:S(2)}) collective-permute-start(bf16[64,3200]{1,0:T(8,128)(2,1)} %get-tuple-element.148), channel_id=1, source_target_pairs={{0,4},{2,6},{8,0},{10,2},{16,8},{18,10},{24,16},{26,18},{28,24},{3... | collective-permute-start | bytes 1228808 | tf_op jit(solution)/shard_map/ppermute | solution.py:1105
  386.1 11.8 %collective-permute-start.41 = (bf16[64,3200]{1,0:T(8,128)(2,1)}, bf16[64,3200]{1,0:T(8,128)(2,1)S(1)}, u32[]{:S(2)}, u32[]{:S(2)}) collective-permute-start(bf16[64,3200]{1,0:T(8,128)(2,1)} %get-tuple-element.149), channel_id=1, source_target_pairs={{0,8},{2,10},{8,16},{10,18},{16,24},{18,26},{24,28},{26,30},{28,20... | collective-permute-start | bytes 1228808 | tf_op jit(solution)/shard_map/ppermute | solution.py:1105
  387.0 12.2 %collective-permute-start.42 = (bf16[64,3200]{1,0:T(8,128)(2,1)}, bf16[64,3200]{1,0:T(8,128)(2,1)S(1)}, u32[]{:S(2)}, u32[]{:S(2)}) collective-permute-start(bf16[64,3200]{1,0:T(8,128)(2,1)} %get-tuple-element.150), channel_id=1, source_target_pairs={{0,4},{2,6},{8,0},{10,2},{16,8},{18,10},{24,16},{26,18},{28,24},{3... | collective-permute-start | bytes 1228808 | tf_op jit(solution)/shard_map/ppermute | solution.py:1105
  397.9 1.3 copy-start.16
  402.8 11.4 %collective-permute-start.44 = (bf16[64,3200]{1,0:T(8,128)(2,1)}, bf16[64,3200]{1,0:T(8,128)(2,1)S(1)}, u32[]{:S(2)}, u32[]{:S(2)}) collective-permute-start(bf16[64,3200]{1,0:T(8,128)(2,1)} %get-tuple-element.152), channel_id=1, source_target_pairs={{0,8},{2,10},{8,16},{10,18},{16,24},{18,26},{24,28},{26,30},{28,20... | collective-permute-start | bytes 1228808 | tf_op jit(solution)/shard_map/ppermute | solution.py:1105
  403.8 14.4 %copy-start.8 = (bf16[688,1024]{1,0:T(8,128)(2,1)S(1)}, bf16[688,1024]{1,0:T(8,128)(2,1)}, u32[]{:S(2)}) copy-start(bf16[688,1024]{1,0:T(8,128)(2,1)} %get-tuple-element.106) | copy-start | bytes 4227076
  403.8 14.4 %copy-start.10 = (bf16[688,1024]{1,0:T(8,128)(2,1)S(1)}, bf16[688,1024]{1,0:T(8,128)(2,1)}, u32[]{:S(2)}) copy-start(bf16[688,1024]{1,0:T(8,128)(2,1)} %copy-done.9) | copy-start | bytes 4227076
  403.8 11.3 %collective-permute-start.45 = (bf16[64,3200]{1,0:T(8,128)(2,1)}, bf16[64,3200]{1,0:T(8,128)(2,1)S(1)}, u32[]{:S(2)}, u32[]{:S(2)}) collective-permute-start(bf16[64,3200]{1,0:T(8,128)(2,1)} %get-tuple-element.153), channel_id=1, source_target_pairs={{0,4},{2,6},{8,0},{10,2},{16,8},{18,10},{24,16},{26,18},{28,24},{3... | collective-permute-start | bytes 1228808 | tf_op jit(solution)/shard_map/ppermute | solution.py:1105
  418.2 10.4 %collective-permute-start.46 = (bf16[64,3200]{1,0:T(8,128)(2,1)}, bf16[64,3200]{1,0:T(8,128)(2,1)S(1)}, u32[]{:S(2)}, u32[]{:S(2)}) collective-permute-start(bf16[64,3200]{1,0:T(8,128)(2,1)} %ring_add.19.part_ref), channel_id=1, source_target_pairs={{0,1},{1,0},{2,3},{3,2},{4,5},{5,4},{6,7},{7,6},{8,9},{9,8},{10,11... | collective-permute-start | bytes 1228808 | tf_op jit(solution)/shard_map/ppermute | solution.py:1293
  419.5 3.5 copy-start.3
  (15 other events, 12.4 us)
Sparse Core Ops, SparseCore 0:
  11.4 129.0 all-gather.1

commit v3 on v2

--- a/solution.py
+++ b/solution.py
@@ -417,11 +417,10 @@
 
 
 def project_kernel(place, x_ref, *refs, chips):
-    own_refs, far_refs = refs[:chips], refs[chips : 2 * chips]
-    far_out_ref, own_ref, normed_ref, weight_ref, table_ref, up_ref = refs[2 * chips :]
+    own_refs, far_refs, own_vectors, far_vectors = (refs[chips * i : chips * (i + 1)] for i in range(4))
+    far_out_ref, own_ref, normed_ref, weight_ref, table_ref, up_ref = refs[4 * chips :]
     step = pl.program_id(0)
-    rows, block = own_refs[0].shape[0], weight_ref.shape[1]
-    packed = own_refs[0].shape[1] - LANES
+    rows = own_refs[0].shape[0]
     core = place[CORE]
 
     @pl.when(step == 0)
@@ -430,8 +429,8 @@
         each = up_ref.shape[1] // (2 * chips)
         for k in range(chips):
             chip = place[CHIPS + k]
-            own = own_refs[k][: table_ref.shape[0], packed:].astype(F32)
-            far = far_refs[k][: table_ref.shape[0], packed:].astype(F32)
+            own = own_vectors[k][...].astype(F32)
+            far = far_vectors[k][...].astype(F32)
             at = pl.ds(pl.multiple_of(chip * LANES, LANES), LANES)
             table_ref[:, at] = jnp.where(vector, own + far, 0.0)
             for part, side in ((own, core), (far, 1 - core)):
@@ -442,52 +441,47 @@
             x_ref[...].astype(F32), table_ref[GAIN1 : GAIN1 + 1, :], table_ref[SHIFT1 : SHIFT1 + 1, :]
         ).astype(BF16)
 
-    columns = pl.ds(pl.multiple_of(place[step] * block, block), block)
     for k in range(chips):
         start = 2 * place[CHIPS + k]
-        weight_ref[pl.ds(pl.multiple_of((start + core) * rows, rows), rows), :] = own_refs[k][:, columns]
-        weight_ref[pl.ds(pl.multiple_of((start + 1 - core) * rows, rows), rows), :] = far_refs[k][:, columns]
-    kind = lax.rem(step, 3)
-    side = pl.ds(pl.multiple_of(lax.rem(place[step], 2) * block, block), block)
+        weight_ref[pl.ds(pl.multiple_of((start + core) * rows, rows), rows), :] = own_refs[k][...]
+        weight_ref[pl.ds(pl.multiple_of((start + 1 - core) * rows, rows), rows), :] = far_refs[k][...]
     shift = jnp.where(
-        kind == 0,
-        table_ref[QUERY : QUERY + 1, side],
-        jnp.where(kind == 2, table_ref[VALUE : VALUE + 1, side], 0.0),
+        step == 0,
+        table_ref[QUERY : QUERY + 1, :],
+        jnp.where(step == 2, table_ref[VALUE : VALUE + 1, :], 0.0),
     )
     result = (dot(normed_ref[...], weight_ref[...]) + shift).astype(BF16)
-
-    @pl.when(step < 3)
-    def _():
-        far_out_ref[0] = result
-
-    @pl.when(step >= 3)
-    def _():
-        own_ref[0] = result
+    half = result.shape[1] // 2
+    low, high = result[:, :half], result[:, half:]
+    own_ref[0] = jnp.where(core == 0, low, high)
+    far_out_ref[0] = jnp.where(core == 0, high, low)
 
 
 def project(place, x, own_pieces, far_pieces, hidden):
     chips = len(own_pieces)
     tokens, width = x.shape
-    half = width // 2
-    piece = own_pieces[0].shape
+    rows = own_pieces[0].shape[0]
+    kind = pl.BlockSpec((1, tokens, width // 2), lambda j, _: (j, 0, 0))
     return pl.pallas_call(
         functools.partial(project_kernel, chips=chips),
         grid_spec=pltpu.PrefetchScalarGridSpec(
             num_scalar_prefetch=1,
-            grid=(6,),
-            in_specs=[whole((tokens, width))] + [whole(piece)] * 2 * chips,
+            grid=(3,),
+            in_specs=[whole((tokens, width))]
+            + [pl.BlockSpec((rows, width), lambda j, _: (0, j))] * 2 * chips
+            + [pl.BlockSpec((16, LANES), lambda j, _: (0, 3 * width // LANES))] * 2 * chips,
             out_specs=[
-                pl.BlockSpec((1, tokens, half), lambda j, _: (jnp.minimum(j, 2), 0, 0)),
-                pl.BlockSpec((1, tokens, half), lambda j, _: (jnp.maximum(j - 3, 0), 0, 0)),
+                kind,
+                kind,
                 whole((tokens, width)),
-                pl.BlockSpec((width, half), lambda j, place: (0, place[j])),
+                pl.BlockSpec((width, width), lambda j, _: (0, j)),
                 whole((16, width)),
                 whole((1, hidden)),
             ],
         ),
         out_shape=[
-            jax.ShapeDtypeStruct((3, tokens, half), BF16),
-            jax.ShapeDtypeStruct((3, tokens, half), BF16),
+            jax.ShapeDtypeStruct((3, tokens, width // 2), BF16),
+            jax.ShapeDtypeStruct((3, tokens, width // 2), BF16),
             jax.ShapeDtypeStruct((tokens, width), BF16),
             jax.ShapeDtypeStruct((width, 3 * width), BF16),
             jax.ShapeDtypeStruct((16, width), F32),
@@ -495,7 +489,7 @@
         ],
         name="project",
         **params_for(6 * tokens * width * width, 12 * tokens * width + 12 * width * width),
-    )(place, x, *own_pieces, *far_pieces)
+    )(place, x, *own_pieces, *far_pieces, *own_pieces, *far_pieces)
 
 
 def padded_len(count, block):
@@ -975,33 +969,41 @@
 
 
 def unproject_kernel(
-    place, x_ref, delta_middle_ref, table, normed_ref, own_ref, far_ref, weight_ref, middle_sums, up_sums, *refs, chips
+    place, x_hbm, delta_middle_hbm, table, normed_ref, own_ref, far_ref, weight_ref, middle_sums, up_sums, *refs, chips
 ):
-    out_ref, mine_ref, other_ref, vectors_mine_ref, vectors_other_ref, delta, sums, normed_t = refs[-8:]
+    (
+        out_ref, mine_ref, other_ref, vectors_mine_ref, vectors_other_ref,
+        delta, sums, normed_t, x_ref, delta_middle_ref, arrived,
+    ) = refs
     step = pl.program_id(0)
-    width = x_ref.shape[1]
     core = place[CORE]
+    copies = [
+        pltpu.make_async_copy(x_hbm, x_ref, arrived.at[0]),
+        pltpu.make_async_copy(delta_middle_hbm, delta_middle_ref, arrived.at[1]),
+    ]
 
     @pl.when(step == 0)
     def _():
+        for copy in copies:
+            copy.start()
         fill_turned(place, normed_ref, normed_t, chips)
         delta[...] = jnp.zeros_like(delta)
         sums[...] = jnp.zeros_like(sums)
 
-    block = jnp.where(step < 3, own_ref[0], far_ref[0])
+    own, far = own_ref[0], far_ref[0]
+    block = jnp.concatenate([jnp.where(core == 0, own, far), jnp.where(core == 0, far, own)], axis=1)
     split_rows(dot(normed_t[...], block).astype(BF16), mine_ref, other_ref)
     delta[...] += dot(block, weight_ref[...], NT)
-    column_total = total_rows(block.astype(F32))
-    half = block.shape[1]
-    at = pl.ds(pl.multiple_of(jnp.where(step < 3, core, 1 - core) * half, half), half)
     for kind, row in ((0, QUERY), (2, VALUE)):
 
-        @pl.when(lax.rem(step, 3) == kind)
+        @pl.when(step == kind)
         def _():
-            sums[row : row + 1, at] = column_total
+            sums[row : row + 1, :] = total_rows(block.astype(F32))
 
     @pl.when(step == pl.num_programs(0) - 1)
     def _():
+        for copy in copies:
+            copy.wait()
         delta_normed = delta[...]
         inner, gain_terms = normalize_back(
             x_ref[...].astype(F32), table[GAIN1 : GAIN1 + 1, :], delta_normed
@@ -1032,39 +1034,39 @@
                     out[k, VECTORS + r : VECTORS + r + 1, :] = row
 
 
-def unproject(place, x, delta_middle, table, normed, own, far, weight, middle_sums, up_sums, owners, after):
+def unproject(place, x, delta_middle, table, normed, own, far, weight, middle_sums, up_sums, owners):
     tokens, width = x.shape
     half = width // 2
     chips = owners // 2
     rows = width // owners
     vectors = (chips, rows, LANES)
-
-    def column(j, place):
-        return 2 * lax.rem(j, 3) + jnp.where(j < 3, place[CORE], 1 - place[CORE])
-
-    sent = pl.BlockSpec((chips, rows, half), lambda j, place: (0, 0, column(j, place)))
+    anywhere = pl.BlockSpec(memory_space=pl.ANY)
+    kind = pl.BlockSpec((1, tokens, half), lambda j, _: (j, 0, 0))
+    sent = pl.BlockSpec((chips, rows, width), lambda j, _: (0, 0, j))
     return pl.pallas_call(
         functools.partial(unproject_kernel, chips=chips),
         grid_spec=pltpu.PrefetchScalarGridSpec(
             num_scalar_prefetch=1,
-            grid=(6,),
+            grid=(3,),
             in_specs=[
-                whole((tokens, width)),
-                whole((tokens, width)),
+                anywhere,
+                anywhere,
                 whole(table.shape),
                 whole((tokens, width)),
-                pl.BlockSpec((1, tokens, half), lambda j, _: (jnp.minimum(j, 2), 0, 0)),
-                pl.BlockSpec((1, tokens, half), lambda j, _: (jnp.maximum(j - 3, 0), 0, 0)),
-                pl.BlockSpec((width, half), lambda j, place: (0, column(j, place))),
+                kind,
+                kind,
+                pl.BlockSpec((width, width), lambda j, _: (0, j)),
                 whole(middle_sums.shape),
                 whole(up_sums.shape),
-            ]
-            + [pl.BlockSpec(memory_space=pl.ANY)] * len(after),
+            ],
             out_specs=[whole((tokens, width)), sent, sent, whole(vectors), whole(vectors)],
             scratch_shapes=[
                 pltpu.VMEM((tokens, width), F32),
                 pltpu.VMEM((16, width), F32),
                 pltpu.VMEM((width, tokens), BF16),
+                pltpu.VMEM((tokens, width), BF16),
+                pltpu.VMEM((tokens, width), F32),
+                pltpu.SemaphoreType.DMA((2,)),
             ],
         ),
         out_shape=[
@@ -1076,7 +1078,7 @@
         ],
         name="unproject",
         **params_for(12 * tokens * width * width, 18 * tokens * width + 12 * width * width, weight=SHORT),
-    )(place, x, delta_middle, table, normed, own, far, weight, middle_sums, up_sums, *after)
+    )(place, x, delta_middle, table, normed, own, far, weight, middle_sums, up_sums)
 
 
 def ring_of(chips):
@@ -1152,22 +1154,24 @@
 
 class RingSum:
     def __init__(self, *parts):
-        self.parts, self.chips = parts, parts[0][0].shape[0]
+        self.parts, self.chips = [part[:2] for part in parts], parts[0][0].shape[0]
+        self.columns = [part[0].shape[2] // part[3] for part in parts]
+        self.blocks = [part[2] for part in parts]
         self.steps = self.chips // 2
         self.step = 0
         self.came = []
 
     def add(self, mode, places, after=(), carry=()):
         rows = self.parts[0][0].shape[1]
-        columns = [mine.shape[2] for mine, _ in self.parts]
+        columns = self.columns
         total = sum(columns)
         blocks = 2 if total > 4096 else 1
         arrays, specs = [], []
         for at in places:
-            for part, each in zip(self.parts, columns):
+            for part, each, block in zip(self.parts, columns, self.blocks):
                 for array in part:
                     arrays.append(array)
-                    specs.append(pl.BlockSpec((1, rows // blocks, each), lambda i, at=at: (at, i, 0)))
+                    specs.append(pl.BlockSpec((1, rows // blocks, each), lambda i, at=at, block=block: (at, i, block)))
         for came in self.came:
             arrays.append(came)
             specs.append(pl.BlockSpec((rows // blocks, came.shape[1]), lambda i: (i, 0)))
@@ -1207,7 +1211,20 @@
         return sums[0], carried
 
 
-def finish_rest_kernel(part_ref, came_ref, up_ref, down_ref, output_ref):
+def passed(arrays, after):
+    anywhere = pl.BlockSpec(memory_space=pl.ANY)
+    return pl.pallas_call(
+        lambda *refs: None,
+        in_specs=[anywhere] * (len(arrays) + len(after)),
+        out_specs=[anywhere] * len(arrays),
+        out_shape=[jax.ShapeDtypeStruct(array.shape, array.dtype) for array in arrays],
+        input_output_aliases={i: i for i in range(len(arrays))},
+        name="passed",
+        **params_for(1, 1),
+    )(*arrays, *after)
+
+
+def finish_rest_kernel(part_ref, came_ref, up_ref, down_ref):
     def total(at):
         return part_ref[:, at].astype(F32) + came_ref[:, at].astype(F32)
 
@@ -1217,7 +1234,6 @@
     for g in range(0, width // rows, 2):
         pair = [total(slice(hidden + each * h, hidden + each * (h + 1))) for h in (g, g + 1)]
         down_ref[:, g * rows : (g + 2) * rows] = jnp.concatenate(pair, axis=0).T
-    output_ref[...] = total(slice(hidden + width // rows * each, None))
 
 
 def finish_rest(part, came, hidden, each, width):
@@ -1226,20 +1242,22 @@
     return pl.pallas_call(
         finish_rest_kernel,
         in_specs=[in_vmem] * 2,
-        out_specs=[in_vmem] * 3,
-        out_shape=[jax.ShapeDtypeStruct(shape, F32) for shape in ((rows, hidden), (each, width), (rows, width))],
+        out_specs=[in_vmem] * 2,
+        out_shape=[jax.ShapeDtypeStruct(shape, F32) for shape in ((rows, hidden), (each, width))],
         name="finish_rest",
         **params_for(part.size, 8 * part.size, weight=SHORT),
     )(part, came)
 
 
-def finish_first_kernel(place, part_ref, came_ref, packed_ref, *vector_refs):
-    def total(rows, at):
-        return part_ref[rows, at].astype(F32) + came_ref[rows, at].astype(F32)
-
-    width = packed_ref.shape[1]
-    packed_ref[...] = total(slice(None), slice(0, width))
-    vectors = total(slice(0, 16), slice(width, width + LANES))
+def finish_first_kernel(place, *refs):
+    parts, came, (packed_ref, output_ref), vector_refs = refs[:2], refs[2:4], refs[4:6], refs[6:]
+    packed, out = packed_ref.shape[1] // 2, output_ref.shape[1] // 2
+    for i in range(2):
+        total = parts[i][...].astype(F32) + came[i][...].astype(F32)
+        packed_ref[:, packed * i : packed * (i + 1)] = total[:, :packed]
+        output_ref[:, out * i : out * (i + 1)] = total[:, packed : packed + out]
+        if i == 0:
+            vectors = total[:16, packed + out :]
     half = LANES // 2
     mine = jnp.where(place[CORE] == 0, vectors[:, :half], vectors[:, half:])
     for i in range(VECTORS):
@@ -1248,18 +1266,18 @@
     vector_refs[VECTORS][...] = vectors[VECTORS : VECTORS + count // LANES, :].reshape(count)
 
 
-def finish_first(place, part, came, each):
+def finish_first(place, parts, came, width, each):
     in_vmem = pl.BlockSpec(memory_space=pltpu.VMEM)
-    rows, width = part.shape[0], part.shape[1] - LANES
-    shapes = [(rows, width)] + [(rows,)] * VECTORS + [(each,)]
+    rows = parts[0].shape[0]
+    shapes = [(rows, 3 * width), (rows, width)] + [(rows,)] * VECTORS + [(each,)]
     return pl.pallas_call(
         finish_first_kernel,
-        in_specs=[pl.BlockSpec(memory_space=pltpu.SMEM)] + [in_vmem] * 2,
+        in_specs=[pl.BlockSpec(memory_space=pltpu.SMEM)] + [in_vmem] * 4,
         out_specs=[in_vmem] * len(shapes),
         out_shape=[jax.ShapeDtypeStruct(shape, F32) for shape in shapes],
         name="finish_first",
-        **params_for(part.size, 8 * part.size, weight=SHORT),
-    )(place, part, came)
+        **params_for(8 * rows * width, 32 * rows * width, weight=SHORT),
+    )(place, *parts, *came)
 
 
 def split_pairs(pairs):
@@ -1323,16 +1341,16 @@
         place, middle, branch1, branch2, delta_normed2, upstream, own_mix, far_mix, table, rest, owners
     )
     far_grad = to_twin(far_grad_out)
+    ring = RingSum((up_mine, up_twin, 0, 1), (down_mine, down_twin, 0, 1))
+    output_sent = regroup_moves(output)
     output_twin = to_twin(output_other)
-    ring = RingSum((up_mine, up_twin), (down_mine, down_twin), (output_mine, output_twin))
-    output_sent = regroup_moves(output)
     deltas = ()
     grads = [own_grad, far_grad]
     start = 0
     for pairs in split_pairs(width // 2 // LANES):
         sums, _ = ring.sums()
         ring.send(sums)
-        after = [*sums, output_sent] if start else sums
+        after = [*sums, output_sent, output_twin] if start else sums
         deltas = attention_back(
             valid, parts, [own_mix, far_mix_out], grads, totals, 352, start, pairs, deltas, after
         )
@@ -1342,20 +1360,32 @@
     ring.send(sums)
     far_delta = to_twin(far_delta_out)
     grad_x, packed_mine, packed_other, vectors_mine, vectors_other = unproject(
-        place, x, delta_middle, table, normed, own_delta, far_delta, packed_full, middle_sums, up_sums, owners, []
+        place, x, delta_middle, table, normed, own_delta, far_delta, packed_full, middle_sums, up_sums, owners
     )
     output = jnp.where(stays, output, output_sent).reshape(tokens.shape)
-    rest_sum, (grad_x, packed_other, vectors_other) = ring.total(carry=[grad_x, packed_other, vectors_other])
+    grad_x, packed_other, vectors_other = passed([grad_x, packed_other, vectors_other], ring.came)
     vectors_twin, packed_twin = to_twin(vectors_other), to_twin(packed_other)
-    packed_ring = RingSum((packed_mine, packed_twin), (vectors_mine, vectors_twin))
+    rest_sum, _ = ring.total()
+    rings = (
+        RingSum(
+            (packed_mine, packed_twin, 0, 2), (output_mine, output_twin, 0, 2), (vectors_mine, vectors_twin, 0, 1)
+        ),
+        RingSum((packed_mine, packed_twin, 1, 2), (output_mine, output_twin, 1, 2)),
+    )
     grad_x_sent, rest_sent = regroup_moves(grad_x), across(rest_sum)
-    for after in ([], [], [grad_x_sent], [rest_sent]):
-        packed_ring.send(packed_ring.sums(after)[0])
+    last = [rest_sum]
+    for step in range(rings[0].steps):
+        for half in rings:
+            after = [*last] + ([grad_x_sent] if step == 2 and half is rings[0] else [])
+            last, _ = half.sums(after)
+            half.send(last)
     grad_tokens = jnp.where(stays, grad_x, grad_x_sent).astype(F32).reshape(tokens.shape)
     each = up_bias.shape[0]
-    grad_up, grad_down, grad_output = finish_rest(rest_sum, rest_sent, hidden, each, width)
-    first_sum, _ = packed_ring.total()
-    grad_packed, *mine = finish_first(place, first_sum, across(first_sum), each)
+    grad_up, grad_down = finish_rest(rest_sum, rest_sent, hidden, each, width)
+    first_sums = [half.total()[0] for half in rings]
+    grad_packed, grad_output, *mine = finish_first(
+        place, first_sums, [across(half) for half in first_sums], width, each
+    )
     return (
         output, grad_tokens, mine[0], mine[1], grad_packed, mine[2], mine[3], grad_output, mine[4], mine[5],
         mine[6], mine[7], grad_up, mine[10], grad_down, mine[8], mine[9],

time: 443 us -> 426 us (0.962)
  waiting for transfers between devices: 131 us -> 98.1 us
  starting transfers between devices: 44.9 us -> 55.2 us
  Pallas kernels: 226 us -> 232 us
    ppermute x23 -> x31, waiting for transfers between devices: 113 us -> 86.6 us  [to_next(): return lax.ppermute(values, 'fsdp', ring_perm(chips, hop))]
    pallas_call x10 -> x15, Pallas kernels: 31.6 us -> 40 us  [add(): pl.pallas_call(functools.partial(ring_add_kernel, columns=columns, mode=m...]
    ppermute x23 -> x31, starting transfers between devices: 28.3 us -> 36.6 us  [to_next(): return lax.ppermute(values, 'fsdp', ring_perm(chips, hop))]
    ppermute x2 -> x3, waiting for transfers between devices: 10.4 us -> 6.65 us  [across(): return lax.ppermute(values, 'seq', [(0, 1), (1, 0)])]
    unnamed x62 -> x72, local copies, waits for them, and re-layouts: 13.2 us -> 13 us
  transfers between devices with their start and end apart: 48 -> 57, of which waited for: 27 -> 27; matrix products, arithmetic and copies ran while one was open for 1% -> 1% of each run, Pallas kernels for 33% -> 38%
where the time goes in v3:
time: 426 us; the launch traced here: 421 us
  Pallas kernels  232 us (54%)
  waiting for transfers between devices  98.1 us (23%)
  starting transfers between devices  55.2 us (13%)
  between operations  16.1 us (4%)
  local copies, waits for them, and re-layouts  14.3 us (3%)
  other arithmetic  6.06 us (1%)
    ppermute x31, waiting for transfers between devices, to_next(): return lax.ppermute(values, 'fsdp', ring_perm(chips, hop))  86.6 us
    pallas_call x3, Pallas kernels, attention_back(): pl.pallas_call(functools.partial(attend_back_kernel, pieces=pieces, block...  52 us
    pallas_call x1, Pallas kernels, mlp(): pl.pallas_call(functools.partial(mlp_kernel, chips=chips), grid_spec=pltp...  50.9 us
    pallas_call x15, Pallas kernels, add(): pl.pallas_call(functools.partial(ring_add_kernel, columns=columns, mode=m...  40 us
    ppermute x31, starting transfers between devices, to_next(): return lax.ppermute(values, 'fsdp', ring_perm(chips, hop))  36.6 us
    pallas_call x1, Pallas kernels, attention(): pl.pallas_call(functools.partial(attend_kernel, pieces=pieces, block=bloc...  28.3 us
    pallas_call x1, Pallas kernels, unproject(): pl.pallas_call(functools.partial(unproject_kernel, chips=chips), grid_spe...  18.2 us
    pallas_call x1, Pallas kernels, unmerge(): pl.pallas_call(functools.partial(unmerge_kernel, tokens=tokens), grid_spe...  14.5 us
  transfers between devices with their start and end apart: 57, of which 27 were waited for; matrix products, arithmetic and copies ran while one was open for 1% of the time, Pallas kernels for 38%

profile of v3, /device:TPU:0, one launch (start us, length us, event | category | flops | bytes accessed | tf_op | source)
XLA Modules:
  0.0 421.4 jit_solution(9345040249443546697)
XLA Ops:
  7.2 1.3 dynamic-slice_bitcast_fusion.place
  8.6 2.7 pack.1
  11.3 3.1 collective-permute-start.5
  15.2 12.3 %collective-permute-done.5.refs_7_.refs_23_ = bf16[64,3200]{1,0:T(8,128)(2,1)S(1)} collective-permute-done((bf16[64,3200]{1,0:T(8,128)(2,1)}, bf16[64,3200]{1,0:T(8,128)(2,1)S(1)}, u32[]{:S(2)}, u32[]{:S(2)}) %collective-permute-start.5) | collective-permute-done | bytes 409632 | tf_op jit(solution)/shard_map/ppermute | solution.py:1107
  27.4 2.4 collective-permute-start.6
  29.9 17.7 %collective-permute-done.6.refs_6_.refs_22_ = bf16[64,3200]{1,0:T(8,128)(2,1)} collective-permute-done((bf16[64,3200]{1,0:T(8,128)(2,1)S(1)}, bf16[64,3200]{1,0:T(8,128)(2,1)}, u32[]{:S(2)}, u32[]{:S(2)}) %collective-permute-start.6) | collective-permute-done | bytes 409632 | tf_op jit(solution)/shard_map/ppermute | solution.py:1107
  47.5 2.4 collective-permute-start.7
  50.5 17.4 %collective-permute-done.7.refs_5_.refs_21_ = bf16[64,3200]{1,0:T(8,128)(2,1)} collective-permute-done((bf16[64,3200]{1,0:T(8,128)(2,1)}, bf16[64,3200]{1,0:T(8,128)(2,1)}, u32[]{:S(2)}, u32[]{:S(2)}) %collective-permute-start.7) | collective-permute-done | bytes 409632 | tf_op jit(solution)/shard_map/ppermute | solution.py:1107
  67.9 2.5 collective-permute-start.8
  71.0 2.7 collective-permute-start.14
  73.8 13.5 %collective-permute-done.8.refs_4_.refs_20_ = bf16[64,3200]{1,0:T(8,128)(2,1)} collective-permute-done((bf16[64,3200]{1,0:T(8,128)(2,1)}, bf16[64,3200]{1,0:T(8,128)(2,1)}, u32[]{:S(2)}, u32[]{:S(2)}) %collective-permute-start.8) | collective-permute-done | bytes 409632 | tf_op jit(solution)/shard_map/ppermute | solution.py:1107
  87.3 1.2 broadcast_select_fusion.1.x_ref.x_hbm
  89.4 12.5 %project.1 = (bf16[3,688,512]{2,1,0:T(8,128)(2,1)}, bf16[3,688,512]{2,1,0:T(8,128)(2,1)}, bf16[688,1024]{1,0:T(8,128)(2,1)}, bf16[1024,3072]{1,0:T(8,128)(2,1)}, f32[16,1024]{1,0:T(8,128)}, /*index=5*/f32[1,4096]{1,0:T(1,128)}) custom-call(s32[15]{0:T(128)} %dynamic-slice_bitcast_fusion.place, bf16[688,1024]{1,0:T(8,128)(2,1)} %broadcast_select_fusion.1.x_ref.x_hbm, ...), custom_call_target="tpu_custom_call" | custom-call | flops 4328521728 | bytes 21037056 | tf_op jit(solution)/shard_map/project/pallas_call | solution.py:465
  106.5 28.3 %attend.1 = (bf16[688,512]{1,0:T(8,128)(2,1)}, bf16[688,512]{1,0:T(8,128)(2,1)}, f32[688,128]{1,0:T(8,128)}, f32[688,128]{1,0:T(8,128)}) custom-call(s32[2]{0:T(128)} %fusion.1.valid, bf16[3,688,512]{2,1,0:T(8,128)(2,1)} %get-tuple-element.101.refs_0_, bf16[3,688,512]{2,1,0:T(8,128)(2,1)} %collective-permute-done.17.refs_1_), custom_call_target="tpu_custom_call" | custom-call | flops 16240345088 | bytes 5636096 | tf_op jit(solution)/shard_map/attend/pallas_call | solution.py:557
  134.8 3.8 collective-permute-start.18
  138.6 1.3 broadcast_select_fusion.cotangent_ref
  141.5 7.1 %merge.1 = (f32[688,1024]{1,0:T(8,128)}, f32[688,1024]{1,0:T(8,128)}, bf16[688,1024]{1,0:T(8,128)(2,1)}) custom-call(s32[15]{0:T(128)} %dynamic-slice_bitcast_fusion.place, bf16[688,1024]{1,0:T(8,128)(2,1)} %broadcast_select_fusion.1.x_ref.x_hbm, bf16[688,512]{1,0:T(8,128)(2,1)} %get-tuple-element.103.own_ref.refs_2_, bf16[688,512]{1,0:T(8,128)(2,1)} %copy-done.6, ...), custom_call_target="tpu_custom_call" | custom-call | flops 1442840576 | bytes 11960320 | tf_op jit(solution)/shard_map/merge/pallas_call | solution.py:715
  148.6 50.9 %mlp.1 = (f32[688,1024]{1,0:T(8,128)}, f32[688,1024]{1,0:T(8,128)}, bf16[8,64,4096]{2,1,0:T(8,128)(2,1)}, bf16[8,64,4096]{2,1,0:T(8,128)(2,1)}, bf16[8,64,4096]{...) custom-call(s32[15]{0:T(128)} %dynamic-slice_bitcast_fusion.place, ...), custom_call_target="tpu_custom_call" | custom-call | flops 34628173824 | bytes 42008576 | tf_op jit(solution)/shard_map/mlp/pallas_call | solution.py:833
  200.1 14.5 %unmerge.1 = (bf16[688,1024]{1,0:T(8,128)(2,1)}, f32[688,1024]{1,0:T(8,128)}, bf16[688,512]{1,0:T(8,128)(2,1)}, bf16[688,512]{1,0:T(8,128)(2,1)}, bf16[8,64,1024...) custom-call(s32[15]{0:T(128)} %dynamic-slice_bitcast_fusion.place, ...), custom_call_target="tpu_custom_call" | custom-call | flops 2885681152 | bytes 25329664 | tf_op jit(solution)/shard_map/unmerge/pallas_call | solution.py:942
  216.0 2.4 ring_add.15
  218.4 2.5 collective-permute-start.24
  221.3 13.7 %attend_back.3 = (bf16[3,688,512]{2,1,0:T(8,128)(2,1)}, bf16[3,688,512]{2,1,0:T(8,128)(2,1)}) custom-call(s32[2]{0:T(128)} %fusion.1.valid, bf16[3,688,512]{2,1,0:T(8,128)(2,1)} %get-tuple-element.101.refs_0_, bf16[3,688,512]{2,1,0:T(8,128)(2,1)} %collective-permute-done.17.refs_1_, bf16[688,512]{1,0:T(8,128)(2,1)} %get-tuple-element.103.own_ref.refs_2_, ...), custom_call_target="tpu_custom_call" | custom-call | flops 121802588160 | bytes 45088768 | tf_op jit(solution)/shard_map/attend_back/pallas_call | solution.py:666
  236.7 3.7 ring_add.16
  240.3 2.0 collective-permute-start.27
  244.0 24.6 %attend_back.4 = (bf16[3,688,512]{2,1,0:T(8,128)(2,1)}, bf16[3,688,512]{2,1,0:T(8,128)(2,1)}) custom-call(s32[2]{0:T(128)} %fusion.1.valid, bf16[3,688,512]{2,1,0:T(8,128)(2,1)} %get-tuple-element.101.refs_0_, bf16[3,688,512]{2,1,0:T(8,128)(2,1)} %collective-permute-done.17.refs_1_, ...), custom_call_target="tpu_custom_call", output_to_operand_aliasing={{0}: (9, {}), {1}: (10, {})} | custom-call | flops 243605176320 | bytes 90177536 | tf_op jit(solution)/shard_map/attend_back/pallas_call | solution.py:666
  268.6 4.1 ring_add.17
  272.7 2.0 collective-permute-start.29
  274.9 13.7 %attend_back.5 = (bf16[3,688,512]{2,1,0:T(8,128)(2,1)}, bf16[3,688,512]{2,1,0:T(8,128)(2,1)}) custom-call(s32[2]{0:T(128)} %fusion.1.valid, bf16[3,688,512]{2,1,0:T(8,128)(2,1)} %get-tuple-element.101.refs_0_, bf16[3,688,512]{2,1,0:T(8,128)(2,1)} %collective-permute-done.17.refs_1_, ...), custom_call_target="tpu_custom_call", output_to_operand_aliasing={{0}: (9, {}), {1}: (10, {})} | custom-call | flops 121802588160 | bytes 45088768 | tf_op jit(solution)/shard_map/attend_back/pallas_call | solution.py:666
  288.7 9.5 %collective-permute-done.29.refs_8_ = bf16[64,8192]{1,0:T(8,128)(2,1)S(1)} collective-permute-done((bf16[64,8192]{1,0:T(8,128)(2,1)}, bf16[64,8192]{1,0:T(8,128)(2,1)S(1)}, u32[]{:S(2)}, u32[]{:S(2)}) %collective-permute-start.29) | collective-permute-done | bytes 1048608 | tf_op jit(solution)/shard_map/ppermute | solution.py:1107
  298.2 2.7 collective-permute-done.30.refs_9_
  301.9 4.1 ring_add.18
  308.5 2.1 collective-permute-done.31.far_ref
  310.6 18.2 %unproject.1 = (bf16[688,1024]{1,0:T(8,128)(2,1)}, bf16[8,64,3072]{2,1,0:T(8,128)(2,1)}, bf16[8,64,3072]{2,1,0:T(8,128)(2,1)}, bf16[8,64,128]{2,1,0:T(8,128)(2,1)}, bf16[8,64,128]{2,1,0:T(8,128)(2,1)}) custom-call(s32[15]{0:T(128)} %dynamic-slice_bitcast_fusion.place, bf16[688,1024]{1,0:T(8,128)(2,1)} %broadcast_select_fusion.1.x_ref.x_hbm, ...), custom_call_target="tpu_custom_call" | custom-call | flops 135266304 | bytes 394752 | tf_op jit(solution)/shard_map/unproject/pallas_call | solution.py:1046
  328.8 3.1 collective-permute-done.32.refs_3_.refs_4_
  331.9 1.3 collective-permute-done.33.refs_4_.refs_5_
  334.1 1.7 collective-permute-start.34
  336.6 3.2 ring_add.19.refs_6_.part_ref
  341.9 1.8 ring_add.20
  344.4 1.3 collective-permute-start.55
  345.7 1.3 collective-permute-start.37
  347.0 1.8 ring_add.21
  348.8 1.7 collective-permute-start.41
  352.5 2.4 ring_add.22
  357.6 2.3 ring_add.23
  359.9 1.6 collective-permute-start.45
  361.9 1.7 collective-permute-done.39.refs_12_
  365.0 2.5 ring_add.24
  367.5 1.3 collective-permute-start.43
  371.4 2.4 ring_add.25
  373.8 2.2 collective-permute-start.49
  378.3 2.5 ring_add.26
  380.8 1.7 collective-permute-start.47
  382.9 2.0 collective-permute-done.50.refs_9_
  384.9 2.4 ring_add.28
  387.3 1.4 collective-permute-start.51
  391.5 3.2 finish_rest.1
  394.9 1.4 collective-permute-done.52.refs_5_
  396.4 2.1 ring_add.29.refs_1_
  399.0 2.2 ring_add.27.refs_0_
  401.2 1.5 collective-permute-start.53
  402.7 1.7 bitcast_convert_fusion
  404.5 3.5 collective-permute-done.54.refs_3_
  407.9 3.2 collective-permute-done.53.refs_2_
  411.8 2.2 finish_first.1
  (157 shorter events, 37.4 us)
Async XLA Ops:
  7.2 7.2 %copy-start.7 = (bf16[1,688,1024]{2,1,0:T(8,128)(2,1)S(1)}, bf16[1,688,1024]{2,1,0:T(8,128)(2,1)}, u32[]{:S(2)}) copy-start(bf16[1,688,1024]{2,1,0:T(8,128)(2,1)} %param.19) | copy-start | bytes 4227076
  7.2 133.7 %all-gather.2.cloned.1.call-start = ((), (), s32[]{:S(2)}) async-start(), calls=%async_computation | async-start | bytes 20054016 | tf_op jit(solution)/shard_map/all_gather | solution.py:1324
  11.3 16.1 %collective-permute-start.5 = (bf16[64,3200]{1,0:T(8,128)(2,1)}, bf16[64,3200]{1,0:T(8,128)(2,1)S(1)}, u32[]{:S(2)}, u32[]{:S(2)}) collective-permute-start(bf16[64,3200]{1,0:T(8,128)(2,1)} %get-tuple-element.100.refs_0_.refs_16_), channel_id=1, source_target_pairs={{0,8},{2,10},{8,16},{10,18},{16,24},{18,26},{24,28},{26,30},{28,20... | collective-permute-start | bytes 1228808 | tf_op jit(solution)/shard_map/ppermute | solution.py:1107
  14.4 59.4 %collective-permute-start = (bf16[688,1024]{1,0:T(8,128)(2,1)S(1)}, bf16[688,1024]{1,0:T(8,128)(2,1)S(1)}, u32[]{:S(2)}, u32[]{:S(2)}) collective-permute-start(bf16[688,1024]{1,0:T(8,128)(2,1)S(1)} %bitcast.15), channel_id=1, source_target_pairs={{1,2},{2,1},{5,6},{6,5},{9,10},{10,9},{13,14},{14,13},{17,18},{18,... | collective-permute-start | bytes 4227080 | tf_op jit(solution)/shard_map/ppermute | solution.py:1302
  15.1 14.7 %collective-permute-start.2 = (bf16[64,3200]{1,0:T(8,128)(2,1)}, bf16[64,3200]{1,0:T(8,128)(2,1)S(1)}, u32[]{:S(2)}, u32[]{:S(2)}) collective-permute-start(bf16[64,3200]{1,0:T(8,128)(2,1)} %get-tuple-element.100.refs_0_.refs_16_), channel_id=1, source_target_pairs={{0,4},{2,6},{8,0},{10,2},{16,8},{18,10},{24,16},{26,18},{28,24},{3... | collective-permute-start | bytes 1228808 | tf_op jit(solution)/shard_map/ppermute | solution.py:1107
  27.4 61.2 %copy-start.31 = (bf16[64,3200]{1,0:T(8,128)(2,1)}, bf16[64,3200]{1,0:T(8,128)(2,1)S(1)}, u32[]{:S(2)}) copy-start(bf16[64,3200]{1,0:T(8,128)(2,1)S(1)} %collective-permute-done.5.refs_7_.refs_23_) | copy-start | bytes 1228804
  27.4 20.1 %collective-permute-start.6 = (bf16[64,3200]{1,0:T(8,128)(2,1)S(1)}, bf16[64,3200]{1,0:T(8,128)(2,1)}, u32[]{:S(2)}, u32[]{:S(2)}) collective-permute-start(bf16[64,3200]{1,0:T(8,128)(2,1)S(1)} %collective-permute-done.5.refs_7_.refs_23_), channel_id=1, source_target_pairs={{0,8},{2,10},{8,16},{10,18},{16,24},{18,26},{24,28},{26,30},{28,20... | collective-permute-start | bytes 1228808 | tf_op jit(solution)/shard_map/ppermute | solution.py:1107
  29.8 20.2 %collective-permute-start.9 = (bf16[64,3200]{1,0:T(8,128)(2,1)}, bf16[64,3200]{1,0:T(8,128)(2,1)S(1)}, u32[]{:S(2)}, u32[]{:S(2)}) collective-permute-start(bf16[64,3200]{1,0:T(8,128)(2,1)} %get-tuple-element.100.refs_0_.refs_16_), channel_id=1, source_target_pairs={{0,2},{2,0},{4,6},{6,4},{8,10},{10,8},{12,14},{14,12},{16,18},{18,... | collective-permute-start | bytes 1228808 | tf_op jit(solution)/shard_map/ppermute | solution.py:1308
  29.8 44.0 %copy-start.32 = (bf16[64,3200]{1,0:T(8,128)(2,1)}, bf16[64,3200]{1,0:T(8,128)(2,1)S(1)}, u32[]{:S(2)}) copy-start(bf16[64,3200]{1,0:T(8,128)(2,1)S(1)} %collective-permute-done.2.refs_1_.refs_17_) | copy-start | bytes 1228804
  29.8 20.7 %collective-permute-start.3 = (bf16[64,3200]{1,0:T(8,128)(2,1)S(1)}, bf16[64,3200]{1,0:T(8,128)(2,1)}, u32[]{:S(2)}, u32[]{:S(2)}) collective-permute-start(bf16[64,3200]{1,0:T(8,128)(2,1)S(1)} %collective-permute-done.2.refs_1_.refs_17_), channel_id=1, source_target_pairs={{0,4},{2,6},{8,0},{10,2},{16,8},{18,10},{24,16},{26,18},{28,24},{3... | collective-permute-start | bytes 1228808 | tf_op jit(solution)/shard_map/ppermute | solution.py:1107
  47.5 20.4 %collective-permute-start.7 = (bf16[64,3200]{1,0:T(8,128)(2,1)}, bf16[64,3200]{1,0:T(8,128)(2,1)}, u32[]{:S(2)}, u32[]{:S(2)}) collective-permute-start(bf16[64,3200]{1,0:T(8,128)(2,1)} %collective-permute-done.6.refs_6_.refs_22_), channel_id=1, source_target_pairs={{0,8},{2,10},{8,16},{10,18},{16,24},{18,26},{24,28},{26,30},{28,20... | collective-permute-start | bytes 1228808 | tf_op jit(solution)/shard_map/ppermute | solution.py:1107
  50.0 20.4 %collective-permute-start.16 = (bf16[64,3200]{1,0:T(8,128)(2,1)S(1)}, bf16[64,3200]{1,0:T(8,128)(2,1)S(1)}, u32[]{:S(2)}, u32[]{:S(2)}) collective-permute-start(bf16[64,3200]{1,0:T(8,128)(2,1)S(1)} %collective-permute-done.5.refs_7_.refs_23_), channel_id=1, source_target_pairs={{0,2},{2,0},{4,6},{6,4},{8,10},{10,8},{12,14},{14,12},{16,18},{18,... | collective-permute-start | bytes 1228808 | tf_op jit(solution)/shard_map/ppermute | solution.py:1308
  50.0 23.9 %copy-start.33 = (bf16[64,3200]{1,0:T(8,128)(2,1)}, bf16[64,3200]{1,0:T(8,128)(2,1)S(1)}, u32[]{:S(2)}) copy-start(bf16[64,3200]{1,0:T(8,128)(2,1)S(1)} %collective-permute-done.9.refs_8_.refs_24_) | copy-start | bytes 1228804
  50.0 20.4 %collective-permute-start.10 = (bf16[64,3200]{1,0:T(8,128)(2,1)S(1)}, bf16[64,3200]{1,0:T(8,128)(2,1)S(1)}, u32[]{:S(2)}, u32[]{:S(2)}) collective-permute-start(bf16[64,3200]{1,0:T(8,128)(2,1)S(1)} %collective-permute-done.2.refs_1_.refs_17_), channel_id=1, source_target_pairs={{0,2},{2,0},{4,6},{6,4},{8,10},{10,8},{12,14},{14,12},{16,18},{18,... | collective-permute-start | bytes 1228808 | tf_op jit(solution)/shard_map/ppermute | solution.py:1308
  50.5 20.5 %collective-permute-start.4 = (bf16[64,3200]{1,0:T(8,128)(2,1)}, bf16[64,3200]{1,0:T(8,128)(2,1)}, u32[]{:S(2)}, u32[]{:S(2)}) collective-permute-start(bf16[64,3200]{1,0:T(8,128)(2,1)} %collective-permute-done.3.refs_2_.refs_18_), channel_id=1, source_target_pairs={{0,4},{2,6},{8,0},{10,2},{16,8},{18,10},{24,16},{26,18},{28,24},{3... | collective-permute-start | bytes 1228808 | tf_op jit(solution)/shard_map/ppermute | solution.py:1107
  67.9 19.4 %collective-permute-start.8 = (bf16[64,3200]{1,0:T(8,128)(2,1)}, bf16[64,3200]{1,0:T(8,128)(2,1)}, u32[]{:S(2)}, u32[]{:S(2)}) collective-permute-start(bf16[64,3200]{1,0:T(8,128)(2,1)} %collective-permute-done.7.refs_5_.refs_21_), channel_id=1, source_target_pairs={{0,8},{2,10},{8,16},{10,18},{16,24},{18,26},{24,28},{26,30},{28,20... | collective-permute-start | bytes 1228808 | tf_op jit(solution)/shard_map/ppermute | solution.py:1107
  70.4 16.9 %copy-start.34 = (bf16[64,3200]{1,0:T(8,128)(2,1)}, bf16[64,3200]{1,0:T(8,128)(2,1)S(1)}, u32[]{:S(2)}) copy-start(bf16[64,3200]{1,0:T(8,128)(2,1)S(1)} %collective-permute-done.16.refs_15_.refs_31_) | copy-start | bytes 1228804
  70.4 18.2 %collective-permute-start.15 = (bf16[64,3200]{1,0:T(8,128)(2,1)}, bf16[64,3200]{1,0:T(8,128)(2,1)}, u32[]{:S(2)}, u32[]{:S(2)}) collective-permute-start(bf16[64,3200]{1,0:T(8,128)(2,1)} %collective-permute-done.6.refs_6_.refs_22_), channel_id=1, source_target_pairs={{0,2},{2,0},{4,6},{6,4},{8,10},{10,8},{12,14},{14,12},{16,18},{18,... | collective-permute-start | bytes 1228808 | tf_op jit(solution)/shard_map/ppermute | solution.py:1308
  70.4 16.9 %copy-start.35 = (bf16[64,3200]{1,0:T(8,128)(2,1)}, bf16[64,3200]{1,0:T(8,128)(2,1)S(1)}, u32[]{:S(2)}) copy-start(bf16[64,3200]{1,0:T(8,128)(2,1)S(1)} %collective-permute-done.10.refs_9_.refs_25_) | copy-start | bytes 1228804
  70.4 18.2 %collective-permute-start.11 = (bf16[64,3200]{1,0:T(8,128)(2,1)}, bf16[64,3200]{1,0:T(8,128)(2,1)}, u32[]{:S(2)}, u32[]{:S(2)}) collective-permute-start(bf16[64,3200]{1,0:T(8,128)(2,1)} %collective-permute-done.3.refs_2_.refs_18_), channel_id=1, source_target_pairs={{0,2},{2,0},{4,6},{6,4},{8,10},{10,8},{12,14},{14,12},{16,18},{18,... | collective-permute-start | bytes 1228808 | tf_op jit(solution)/shard_map/ppermute | solution.py:1308
  71.0 17.6 %collective-permute-start.14 = (bf16[64,3200]{1,0:T(8,128)(2,1)}, bf16[64,3200]{1,0:T(8,128)(2,1)}, u32[]{:S(2)}, u32[]{:S(2)}) collective-permute-start(bf16[64,3200]{1,0:T(8,128)(2,1)} %collective-permute-done.7.refs_5_.refs_21_), channel_id=1, source_target_pairs={{0,2},{2,0},{4,6},{6,4},{8,10},{10,8},{12,14},{14,12},{16,18},{18,... | collective-permute-start | bytes 1228808 | tf_op jit(solution)/shard_map/ppermute | solution.py:1308
  73.8 14.8 %collective-permute-start.12 = (bf16[64,3200]{1,0:T(8,128)(2,1)}, bf16[64,3200]{1,0:T(8,128)(2,1)}, u32[]{:S(2)}, u32[]{:S(2)}) collective-permute-start(bf16[64,3200]{1,0:T(8,128)(2,1)} %collective-permute-done.4.refs_3_.refs_19_), channel_id=1, source_target_pairs={{0,2},{2,0},{4,6},{6,4},{8,10},{10,8},{12,14},{14,12},{16,18},{18,... | collective-permute-start | bytes 1228808 | tf_op jit(solution)/shard_map/ppermute | solution.py:1308
  87.3 2.1 collective-permute-start.13
  88.6 14.6 %copy-start.8 = (bf16[1,688,1024]{2,1,0:T(8,128)(2,1)S(1)}, bf16[1,688,1024]{2,1,0:T(8,128)(2,1)}, u32[]{:S(2)}) copy-start(bf16[1,688,1024]{2,1,0:T(8,128)(2,1)} %param.36) | copy-start | bytes 4227076
  101.9 4.6 %collective-permute-start.17 = (bf16[3,688,512]{2,1,0:T(8,128)(2,1)}, bf16[3,688,512]{2,1,0:T(8,128)(2,1)}, u32[]{:S(2)}, u32[]{:S(2)}) collective-permute-start(bf16[3,688,512]{2,1,0:T(8,128)(2,1)} %get-tuple-element.102), channel_id=1, source_target_pairs={{0,2},{2,0},{4,6},{6,4},{8,10},{10,8},{12,14},{14,12},{16,18},{18,... | collective-permute-start | bytes 6340616 | tf_op jit(solution)/shard_map/ppermute | solution.py:1308
  102.0 2.8 collective-permute-start.1
  103.2 35.5 %collective-permute-start.19 = (bf16[688,1024]{1,0:T(8,128)(2,1)S(1)}, bf16[688,1024]{1,0:T(8,128)(2,1)S(1)}, u32[]{:S(2)}, u32[]{:S(2)}) collective-permute-start(bf16[688,1024]{1,0:T(8,128)(2,1)S(1)} %bitcast.16), channel_id=1, source_target_pairs={{1,2},{2,1},{5,6},{6,5},{9,10},{10,9},{13,14},{14,13},{17,18},{18,... | collective-permute-start | bytes 4227080 | tf_op jit(solution)/shard_map/ppermute | solution.py:1302
  134.8 5.8 %collective-permute-start.18 = (bf16[688,512]{1,0:T(8,128)(2,1)}, bf16[688,512]{1,0:T(8,128)(2,1)S(1)}, u32[]{:S(2)}, u32[]{:S(2)}) collective-permute-start(bf16[688,512]{1,0:T(8,128)(2,1)} %get-tuple-element.104.refs_3_), channel_id=1, source_target_pairs={{0,2},{2,0},{4,6},{6,4},{8,10},{10,8},{12,14},{14,12},{16,18},{18,... | collective-permute-start | bytes 2113544 | tf_op jit(solution)/shard_map/ppermute | solution.py:1308
  199.6 16.4 %collective-permute-start.22 = (bf16[8,64,4096]{2,1,0:T(8,128)(2,1)}, bf16[8,64,4096]{2,1,0:T(8,128)(2,1)}, u32[]{:S(2)}, u32[]{:S(2)}) collective-permute-start(bf16[8,64,4096]{2,1,0:T(8,128)(2,1)} %get-tuple-element.121), channel_id=1, source_target_pairs={{0,2},{2,0},{4,6},{6,4},{8,10},{10,8},{12,14},{14,12},{16,18},{18,... | collective-permute-start | bytes 12582920 | tf_op jit(solution)/shard_map/ppermute | solution.py:1308
  200.0 16.0 %collective-permute-start.23 = (bf16[8,64,4096]{2,1,0:T(8,128)(2,1)}, bf16[8,64,4096]{2,1,0:T(8,128)(2,1)}, u32[]{:S(2)}, u32[]{:S(2)}) collective-permute-start(bf16[8,64,4096]{2,1,0:T(8,128)(2,1)} %get-tuple-element.123), channel_id=1, source_target_pairs={{0,2},{2,0},{4,6},{6,4},{8,10},{10,8},{12,14},{14,12},{16,18},{18,... | collective-permute-start | bytes 12582920 | tf_op jit(solution)/shard_map/ppermute | solution.py:1308
  214.6 6.7 %collective-permute-start.21 = (bf16[688,512]{1,0:T(8,128)(2,1)}, bf16[688,512]{1,0:T(8,128)(2,1)}, u32[]{:S(2)}, u32[]{:S(2)}) collective-permute-start(bf16[688,512]{1,0:T(8,128)(2,1)} %get-tuple-element.117), channel_id=1, source_target_pairs={{0,2},{2,0},{4,6},{6,4},{8,10},{10,8},{12,14},{14,12},{16,18},{18,... | collective-permute-start | bytes 2113544 | tf_op jit(solution)/shard_map/ppermute | solution.py:1308
  215.1 27.5 %collective-permute-start.26 = (bf16[8,64,1024]{2,1,0:T(8,128)(2,1)}, bf16[8,64,1024]{2,1,0:T(8,128)(2,1)S(1)}, u32[]{:S(2)}, u32[]{:S(2)}) collective-permute-start(bf16[8,64,1024]{2,1,0:T(8,128)(2,1)} %get-tuple-element.130), channel_id=1, source_target_pairs={{0,2},{2,0},{4,6},{6,4},{8,10},{10,8},{12,14},{14,12},{16,18},{18,... | collective-permute-start | bytes 3145736 | tf_op jit(solution)/shard_map/ppermute | solution.py:1308
  215.2 27.4 %collective-permute-start.20 = (bf16[688,1024]{1,0:T(8,128)(2,1)}, bf16[688,1024]{1,0:T(8,128)(2,1)S(1)}, u32[]{:S(2)}, u32[]{:S(2)}) collective-permute-start(bf16[688,1024]{1,0:T(8,128)(2,1)} %get-tuple-element.113), channel_id=1, source_target_pairs={{1,2},{2,1},{5,6},{6,5},{9,10},{10,9},{13,14},{14,13},{17,18},{18,... | collective-permute-start | bytes 4227080 | tf_op jit(solution)/shard_map/ppermute | solution.py:1302
  218.4 16.7 %collective-permute-start.24 = (bf16[64,4096]{1,0:T(8,128)(2,1)}, bf16[64,4096]{1,0:T(8,128)(2,1)S(1)}, u32[]{:S(2)}, u32[]{:S(2)}) collective-permute-start(bf16[64,4096]{1,0:T(8,128)(2,1)} %get-tuple-element.124.refs_8_), channel_id=1, source_target_pairs={{0,8},{2,10},{8,16},{10,18},{16,24},{18,26},{24,28},{26,30},{28,20... | collective-permute-start | bytes 1572872 | tf_op jit(solution)/shard_map/ppermute | solution.py:1107
  220.9 14.2 %collective-permute-start.25 = (bf16[64,4096]{1,0:T(8,128)(2,1)}, bf16[64,4096]{1,0:T(8,128)(2,1)S(1)}, u32[]{:S(2)}, u32[]{:S(2)}) collective-permute-start(bf16[64,4096]{1,0:T(8,128)(2,1)} %get-tuple-element.125.refs_9_), channel_id=1, source_target_pairs={{0,4},{2,6},{8,0},{10,2},{16,8},{18,10},{24,16},{26,18},{28,24},{3... | collective-permute-start | bytes 1572872 | tf_op jit(solution)/shard_map/ppermute | solution.py:1107
  240.3 28.2 %collective-permute-start.27 = (bf16[64,8192]{1,0:T(8,128)(2,1)}, bf16[64,8192]{1,0:T(8,128)(2,1)}, u32[]{:S(2)}, u32[]{:S(2)}) collective-permute-start(bf16[64,8192]{1,0:T(8,128)(2,1)} %get-tuple-element.128.refs_10_), channel_id=1, source_target_pairs={{0,8},{2,10},{8,16},{10,18},{16,24},{18,26},{24,28},{26,30},{28,20... | collective-permute-start | bytes 3145736 | tf_op jit(solution)/shard_map/ppermute | solution.py:1107
  242.4 26.2 %collective-permute-start.28 = (bf16[64,8192]{1,0:T(8,128)(2,1)}, bf16[64,8192]{1,0:T(8,128)(2,1)}, u32[]{:S(2)}, u32[]{:S(2)}) collective-permute-start(bf16[64,8192]{1,0:T(8,128)(2,1)} %get-tuple-element.129.refs_11_), channel_id=1, source_target_pairs={{0,4},{2,6},{8,0},{10,2},{16,8},{18,10},{24,16},{26,18},{28,24},{3... | collective-permute-start | bytes 3145736 | tf_op jit(solution)/shard_map/ppermute | solution.py:1107
  272.7 25.5 %collective-permute-start.29 = (bf16[64,8192]{1,0:T(8,128)(2,1)}, bf16[64,8192]{1,0:T(8,128)(2,1)S(1)}, u32[]{:S(2)}, u32[]{:S(2)}) collective-permute-start(bf16[64,8192]{1,0:T(8,128)(2,1)} %get-tuple-element.133.refs_10_), channel_id=1, source_target_pairs={{0,8},{2,10},{8,16},{10,18},{16,24},{18,26},{24,28},{26,30},{28,20... | collective-permute-start | bytes 3145736 | tf_op jit(solution)/shard_map/ppermute | solution.py:1107
  274.7 26.2 %collective-permute-start.30 = (bf16[64,8192]{1,0:T(8,128)(2,1)}, bf16[64,8192]{1,0:T(8,128)(2,1)S(1)}, u32[]{:S(2)}, u32[]{:S(2)}) collective-permute-start(bf16[64,8192]{1,0:T(8,128)(2,1)} %get-tuple-element.134.refs_11_), channel_id=1, source_target_pairs={{0,4},{2,6},{8,0},{10,2},{16,8},{18,10},{24,16},{26,18},{28,24},{3... | collective-permute-start | bytes 3145736 | tf_op jit(solution)/shard_map/ppermute | solution.py:1107
  306.1 4.6 %collective-permute-start.31 = (bf16[3,688,512]{2,1,0:T(8,128)(2,1)}, bf16[3,688,512]{2,1,0:T(8,128)(2,1)}, u32[]{:S(2)}, u32[]{:S(2)}) collective-permute-start(bf16[3,688,512]{2,1,0:T(8,128)(2,1)} %get-tuple-element.137), channel_id=1, source_target_pairs={{0,2},{2,0},{4,6},{6,4},{8,10},{10,8},{12,14},{14,12},{16,18},{18,... | collective-permute-start | bytes 6340616 | tf_op jit(solution)/shard_map/ppermute | solution.py:1308
  306.2 25.7 %collective-permute-start.32 = (bf16[64,8192]{1,0:T(8,128)(2,1)}, bf16[64,8192]{1,0:T(8,128)(2,1)S(1)}, u32[]{:S(2)}, u32[]{:S(2)}) collective-permute-start(bf16[64,8192]{1,0:T(8,128)(2,1)} %get-tuple-element.144), channel_id=1, source_target_pairs={{0,8},{2,10},{8,16},{10,18},{16,24},{18,26},{24,28},{26,30},{28,20... | collective-permute-start | bytes 3145736 | tf_op jit(solution)/shard_map/ppermute | solution.py:1107
  307.3 25.8 %collective-permute-start.33 = (bf16[64,8192]{1,0:T(8,128)(2,1)}, bf16[64,8192]{1,0:T(8,128)(2,1)S(1)}, u32[]{:S(2)}, u32[]{:S(2)}) collective-permute-start(bf16[64,8192]{1,0:T(8,128)(2,1)} %get-tuple-element.145), channel_id=1, source_target_pairs={{0,4},{2,6},{8,0},{10,2},{16,8},{18,10},{24,16},{26,18},{28,24},{3... | collective-permute-start | bytes 3145736 | tf_op jit(solution)/shard_map/ppermute | solution.py:1107
  334.1 6.1 %collective-permute-start.35 = (bf16[8,64,3072]{2,1,0:T(8,128)(2,1)}, bf16[8,64,3072]{2,1,0:T(8,128)(2,1)S(1)}, u32[]{:S(2)}, u32[]{:S(2)}) collective-permute-start(bf16[8,64,3072]{2,1,0:T(8,128)(2,1)} %get-tuple-element.148), channel_id=1, source_target_pairs={{0,2},{2,0},{4,6},{6,4},{8,10},{10,8},{12,14},{14,12},{16,18},{18,... | collective-permute-start | bytes 9437192 | tf_op jit(solution)/shard_map/ppermute | solution.py:1308
  334.1 27.4 %collective-permute-start.34 = (bf16[688,1024]{1,0:T(8,128)(2,1)}, bf16[688,1024]{1,0:T(8,128)(2,1)}, u32[]{:S(2)}, u32[]{:S(2)}) collective-permute-start(bf16[688,1024]{1,0:T(8,128)(2,1)} %get-tuple-element.146), channel_id=1, source_target_pairs={{1,2},{2,1},{5,6},{6,5},{9,10},{10,9},{13,14},{14,13},{17,18},{18,... | collective-permute-start | bytes 4227080 | tf_op jit(solution)/shard_map/ppermute | solution.py:1302
  335.9 4.3 %collective-permute-start.36 = (bf16[8,64,128]{2,1,0:T(8,128)(2,1)}, bf16[8,64,128]{2,1,0:T(8,128)(2,1)S(1)}, u32[]{:S(2)}, u32[]{:S(2)}) collective-permute-start(bf16[8,64,128]{2,1,0:T(8,128)(2,1)} %get-tuple-element.151), channel_id=1, source_target_pairs={{0,2},{2,0},{4,6},{6,4},{8,10},{10,8},{12,14},{14,12},{16,18},{18,... | collective-permute-start | bytes 393224 | tf_op jit(solution)/shard_map/ppermute | solution.py:1308
  343.7 6.9 %collective-permute-start.38 = (bf16[64,1024]{1,0:T(8,128)(2,1)}, bf16[64,1024]{1,0:T(8,128)(2,1)S(1)}, u32[]{:S(2)}, u32[]{:S(2)}) collective-permute-start(bf16[64,1024]{1,0:T(8,128)(2,1)} %get-tuple-element.153.refs_5_), channel_id=1, source_target_pairs={{0,4},{2,6},{8,0},{10,2},{16,8},{18,10},{24,16},{26,18},{28,24},{3... | collective-permute-start | bytes 393224 | tf_op jit(solution)/shard_map/ppermute | solution.py:1107
  344.4 46.2 %collective-permute-start.55 = (bf16[64,8192]{1,0:T(8,128)(2,1)}, bf16[64,8192]{1,0:T(8,128)(2,1)S(1)}, u32[]{:S(2)}, u32[]{:S(2)}) collective-permute-start(bf16[64,8192]{1,0:T(8,128)(2,1)} %ring_add.19.refs_6_.part_ref), channel_id=1, source_target_pairs={{0,1},{1,0},{2,3},{3,2},{4,5},{5,4},{6,7},{7,6},{8,9},{9,8},{10,11... | collective-permute-start | bytes 3145736 | tf_op jit(solution)/shard_map/ppermute | solution.py:1311
  345.7 6.1 %collective-permute-start.37 = (bf16[64,1152]{1,0:T(8,128)(2,1)}, bf16[64,1152]{1,0:T(8,128)(2,1)S(1)}, u32[]{:S(2)}, u32[]{:S(2)}) collective-permute-start(bf16[64,1152]{1,0:T(8,128)(2,1)} %get-tuple-element.152.refs_4_), channel_id=1, source_target_pairs={{0,8},{2,10},{8,16},{10,18},{16,24},{18,26},{24,28},{26,30},{28,20... | collective-permute-start | bytes 442376 | tf_op jit(solution)/shard_map/ppermute | solution.py:1107
  348.8 7.1 %collective-permute-start.41 = (bf16[64,1024]{1,0:T(8,128)(2,1)}, bf16[64,1024]{1,0:T(8,128)(2,1)S(1)}, u32[]{:S(2)}, u32[]{:S(2)}) collective-permute-start(bf16[64,1024]{1,0:T(8,128)(2,1)} %get-tuple-element.154.refs_14_), channel_id=1, source_target_pairs={{0,8},{2,10},{8,16},{10,18},{16,24},{18,26},{24,28},{26,30},{28,20... | collective-permute-start | bytes 393224 | tf_op jit(solution)/shard_map/ppermute | solution.py:1107
  350.6 6.3 %collective-permute-start.42 = (bf16[64,1024]{1,0:T(8,128)(2,1)}, bf16[64,1024]{1,0:T(8,128)(2,1)S(1)}, u32[]{:S(2)}, u32[]{:S(2)}) collective-permute-start(bf16[64,1024]{1,0:T(8,128)(2,1)} %get-tuple-element.155.refs_15_), channel_id=1, source_target_pairs={{0,4},{2,6},{8,0},{10,2},{16,8},{18,10},{24,16},{26,18},{28,24},{3... | collective-permute-start | bytes 393224 | tf_op jit(solution)/shard_map/ppermute | solution.py:1107
  354.9 8.7 %collective-permute-start.39 = (bf16[64,2176]{1,0:T(8,128)(2,1)}, bf16[64,2176]{1,0:T(8,128)(2,1)S(1)}, u32[]{:S(2)}, u32[]{:S(2)}) collective-permute-start(bf16[64,2176]{1,0:T(8,128)(2,1)} %get-tuple-element.156.refs_10_), channel_id=1, source_target_pairs={{0,8},{2,10},{8,16},{10,18},{16,24},{18,26},{24,28},{26,30},{28,20... | collective-permute-start | bytes 835592 | tf_op jit(solution)/shard_map/ppermute | solution.py:1107
  356.0 7.7 %collective-permute-start.40 = (bf16[64,2176]{1,0:T(8,128)(2,1)}, bf16[64,2176]{1,0:T(8,128)(2,1)S(1)}, u32[]{:S(2)}, u32[]{:S(2)}) collective-permute-start(bf16[64,2176]{1,0:T(8,128)(2,1)} %get-tuple-element.157.refs_11_), channel_id=1, source_target_pairs={{0,4},{2,6},{8,0},{10,2},{16,8},{18,10},{24,16},{26,18},{28,24},{3... | collective-permute-start | bytes 835592 | tf_op jit(solution)/shard_map/ppermute | solution.py:1107
  359.9 9.7 %collective-permute-start.45 = (bf16[64,2048]{1,0:T(8,128)(2,1)}, bf16[64,2048]{1,0:T(8,128)(2,1)S(1)}, u32[]{:S(2)}, u32[]{:S(2)}) collective-permute-start(bf16[64,2048]{1,0:T(8,128)(2,1)} %get-tuple-element.158.refs_14_), channel_id=1, source_target_pairs={{0,8},{2,10},{8,16},{10,18},{16,24},{18,26},{24,28},{26,30},{28,20... | collective-permute-start | bytes 786440 | tf_op jit(solution)/shard_map/ppermute | solution.py:1107
  361.5 9.2 %collective-permute-start.46 = (bf16[64,2048]{1,0:T(8,128)(2,1)}, bf16[64,2048]{1,0:T(8,128)(2,1)S(1)}, u32[]{:S(2)}, u32[]{:S(2)}) collective-permute-start(bf16[64,2048]{1,0:T(8,128)(2,1)} %get-tuple-element.159.refs_15_), channel_id=1, source_target_pairs={{0,4},{2,6},{8,0},{10,2},{16,8},{18,10},{24,16},{26,18},{28,24},{3... | collective-permute-start | bytes 786440 | tf_op jit(solution)/shard_map/ppermute | solution.py:1107
  367.5 9.0 %collective-permute-start.43 = (bf16[64,2176]{1,0:T(8,128)(2,1)}, bf16[64,2176]{1,0:T(8,128)(2,1)S(1)}, u32[]{:S(2)}, u32[]{:S(2)}) collective-permute-start(bf16[64,2176]{1,0:T(8,128)(2,1)} %get-tuple-element.160.refs_10_), channel_id=1, source_target_pairs={{0,8},{2,10},{8,16},{10,18},{16,24},{18,26},{24,28},{26,30},{28,20... | collective-permute-start | bytes 835592 | tf_op jit(solution)/shard_map/ppermute | solution.py:1107
  368.9 8.7 %collective-permute-start.44 = (bf16[64,2176]{1,0:T(8,128)(2,1)}, bf16[64,2176]{1,0:T(8,128)(2,1)S(1)}, u32[]{:S(2)}, u32[]{:S(2)}) collective-permute-start(bf16[64,2176]{1,0:T(8,128)(2,1)} %get-tuple-element.161.refs_11_), channel_id=1, source_target_pairs={{0,4},{2,6},{8,0},{10,2},{16,8},{18,10},{24,16},{26,18},{28,24},{3... | collective-permute-start | bytes 835592 | tf_op jit(solution)/shard_map/ppermute | solution.py:1107
  373.8 9.1 %collective-permute-start.49 = (bf16[64,2048]{1,0:T(8,128)(2,1)}, bf16[64,2048]{1,0:T(8,128)(2,1)S(1)}, u32[]{:S(2)}, u32[]{:S(2)}) collective-permute-start(bf16[64,2048]{1,0:T(8,128)(2,1)} %get-tuple-element.162.refs_14_), channel_id=1, source_target_pairs={{0,8},{2,10},{8,16},{10,18},{16,24},{18,26},{24,28},{26,30},{28,20... | collective-permute-start | bytes 786440 | tf_op jit(solution)/shard_map/ppermute | solution.py:1107
  376.1 8.8 %collective-permute-start.50 = (bf16[64,2048]{1,0:T(8,128)(2,1)}, bf16[64,2048]{1,0:T(8,128)(2,1)}, u32[]{:S(2)}, u32[]{:S(2)}) collective-permute-start(bf16[64,2048]{1,0:T(8,128)(2,1)} %get-tuple-element.163.refs_15_), channel_id=1, source_target_pairs={{0,4},{2,6},{8,0},{10,2},{16,8},{18,10},{24,16},{26,18},{28,24},{3... | collective-permute-start | bytes 786440 | tf_op jit(solution)/shard_map/ppermute | solution.py:1107
  380.8 18.2 %collective-permute-start.47 = (bf16[64,2176]{1,0:T(8,128)(2,1)}, bf16[64,2176]{1,0:T(8,128)(2,1)}, u32[]{:S(2)}, u32[]{:S(2)}) collective-permute-start(bf16[64,2176]{1,0:T(8,128)(2,1)} %get-tuple-element.164.refs_10_), channel_id=1, source_target_pairs={{0,8},{2,10},{8,16},{10,18},{16,24},{18,26},{24,28},{26,30},{28,20... | collective-permute-start | bytes 835592 | tf_op jit(solution)/shard_map/ppermute | solution.py:1107
  382.5 16.5 %collective-permute-start.48 = (bf16[64,2176]{1,0:T(8,128)(2,1)}, bf16[64,2176]{1,0:T(8,128)(2,1)}, u32[]{:S(2)}, u32[]{:S(2)}) collective-permute-start(bf16[64,2176]{1,0:T(8,128)(2,1)} %get-tuple-element.165.refs_11_), channel_id=1, source_target_pairs={{0,4},{2,6},{8,0},{10,2},{16,8},{18,10},{24,16},{26,18},{28,24},{3... | collective-permute-start | bytes 835592 | tf_op jit(solution)/shard_map/ppermute | solution.py:1107
  387.3 7.6 %collective-permute-start.51 = (bf16[64,2048]{1,0:T(8,128)(2,1)}, bf16[64,2048]{1,0:T(8,128)(2,1)S(1)}, u32[]{:S(2)}, u32[]{:S(2)}) collective-permute-start(bf16[64,2048]{1,0:T(8,128)(2,1)} %get-tuple-element.166), channel_id=1, source_target_pairs={{0,8},{2,10},{8,16},{10,18},{16,24},{18,26},{24,28},{26,30},{28,20... | collective-permute-start | bytes 786440 | tf_op jit(solution)/shard_map/ppermute | solution.py:1107
  388.7 7.7 %collective-permute-start.52 = (bf16[64,2048]{1,0:T(8,128)(2,1)}, bf16[64,2048]{1,0:T(8,128)(2,1)}, u32[]{:S(2)}, u32[]{:S(2)}) collective-permute-start(bf16[64,2048]{1,0:T(8,128)(2,1)} %get-tuple-element.167), channel_id=1, source_target_pairs={{0,4},{2,6},{8,0},{10,2},{16,8},{18,10},{24,16},{26,18},{28,24},{3... | collective-permute-start | bytes 786440 | tf_op jit(solution)/shard_map/ppermute | solution.py:1107
  398.5 9.5 %collective-permute-start.54 = (bf16[64,2048]{1,0:T(8,128)(2,1)}, bf16[64,2048]{1,0:T(8,128)(2,1)S(1)}, u32[]{:S(2)}, u32[]{:S(2)}) collective-permute-start(bf16[64,2048]{1,0:T(8,128)(2,1)} %ring_add.29.refs_1_), channel_id=1, source_target_pairs={{0,1},{1,0},{2,3},{3,2},{4,5},{5,4},{6,7},{7,6},{8,9},{9,8},{10,11... | collective-permute-start | bytes 786440 | tf_op jit(solution)/shard_map/ppermute | solution.py:1311
  401.2 9.9 %collective-permute-start.53 = (bf16[64,2176]{1,0:T(8,128)(2,1)}, bf16[64,2176]{1,0:T(8,128)(2,1)S(1)}, u32[]{:S(2)}, u32[]{:S(2)}) collective-permute-start(bf16[64,2176]{1,0:T(8,128)(2,1)} %ring_add.27.refs_0_), channel_id=1, source_target_pairs={{0,1},{1,0},{2,3},{3,2},{4,5},{5,4},{6,7},{7,6},{8,9},{9,8},{10,11... | collective-permute-start | bytes 835592 | tf_op jit(solution)/shard_map/ppermute | solution.py:1311
  (29 other events, 47.8 us)
Sparse Core Ops, SparseCore 0:
  11.4 129.5 all-gather.1

commit v4 on v3

--- a/solution.py
+++ b/solution.py
@@ -313,6 +313,7 @@
 MASKED = -1e30
 LANES = 128
 VMEM_LIMIT = 60 * 2**20
+SMALL_VMEM = 8 * 2**20
 
 GAIN1, SHIFT1, QUERY, VALUE, OUT_SHIFT, SCALE1, GAIN2, SHIFT2, DOWN_SHIFT, SCALE2 = range(10)
 
@@ -339,10 +340,10 @@
 LONG, SHORT = 16.0, 1 / 64
 
 
-def params_for(flops, nbytes, transcendentals=0, weight=1.0):
+def params_for(flops, nbytes, transcendentals=0, weight=1.0, vmem=VMEM_LIMIT):
     flops, nbytes, transcendentals = (int(weight * count) for count in (flops, nbytes, transcendentals))
     return dict(
-        compiler_params=pltpu.CompilerParams(vmem_limit_bytes=VMEM_LIMIT),
+        compiler_params=pltpu.CompilerParams(vmem_limit_bytes=vmem),
         cost_estimate=pl.CostEstimate(
             flops=flops, bytes_accessed=nbytes, transcendentals=transcendentals
         ),
@@ -1191,7 +1192,7 @@
             + [jax.ShapeDtypeStruct(array.shape, array.dtype) for array in carry],
             input_output_aliases={len(arrays) - len(carry) + i: sums + i for i in range(len(carry))},
             name="ring_add",
-            **params_for(6 * rows * total, 16 * rows * total, weight=SHORT),
+            **params_for(6 * rows * total, 16 * rows * total, weight=SHORT, vmem=VMEM_LIMIT if blocks > 1 else SMALL_VMEM),
         )(*arrays)
         return outs[:sums], outs[sums:]
 
@@ -1205,9 +1206,9 @@
         self.came = [to_next(sums[0], self.chips, 1), to_next(sums[1], self.chips, -1)]
         self.step += 1
 
-    def total(self, carry=()):
+    def total(self, after=(), carry=()):
         assert self.step == self.steps
-        sums, carried = self.add("total", [0], (), carry)
+        sums, carried = self.add("total", [0], after, carry)
         return sums[0], carried
 
 
@@ -1220,7 +1221,7 @@
         out_shape=[jax.ShapeDtypeStruct(array.shape, array.dtype) for array in arrays],
         input_output_aliases={i: i for i in range(len(arrays))},
         name="passed",
-        **params_for(1, 1),
+        **params_for(1, 1, vmem=SMALL_VMEM),
     )(*arrays, *after)
 
 
@@ -1245,7 +1246,7 @@
         out_specs=[in_vmem] * 2,
         out_shape=[jax.ShapeDtypeStruct(shape, F32) for shape in ((rows, hidden), (each, width))],
         name="finish_rest",
-        **params_for(part.size, 8 * part.size, weight=SHORT),
+        **params_for(part.size, 8 * part.size, weight=SHORT, vmem=2 * SMALL_VMEM),
     )(part, came)
 
 
@@ -1276,7 +1277,7 @@
         out_specs=[in_vmem] * len(shapes),
         out_shape=[jax.ShapeDtypeStruct(shape, F32) for shape in shapes],
         name="finish_first",
-        **params_for(8 * rows * width, 32 * rows * width, weight=SHORT),
+        **params_for(8 * rows * width, 32 * rows * width, weight=SHORT, vmem=SMALL_VMEM),
     )(place, *parts, *came)
 
 
@@ -1382,7 +1383,8 @@
     grad_tokens = jnp.where(stays, grad_x, grad_x_sent).astype(F32).reshape(tokens.shape)
     each = up_bias.shape[0]
     grad_up, grad_down = finish_rest(rest_sum, rest_sent, hidden, each, width)
-    first_sums = [half.total()[0] for half in rings]
+    first_sum, _ = rings[0].total()
+    first_sums = [first_sum, rings[1].total([first_sum])[0]]
     grad_packed, grad_output, *mine = finish_first(
         place, first_sums, [across(half) for half in first_sums], width, each
     )

time: 426 us -> 416 us (0.977)
  Pallas kernels: 232 us -> 220 us
  local copies, waits for them, and re-layouts: 14.3 us -> 9.3 us
    pallas_call x15, Pallas kernels: 40 us -> 29.1 us  [add(): pl.pallas_call(functools.partial(ring_add_kernel, columns=columns, mode=m...]
    unnamed x72 -> x50, local copies, waits for them, and re-layouts: 13 us -> 7.99 us
    ppermute x31, waiting for transfers between devices: 86.6 us -> 91.3 us  [to_next(): return lax.ppermute(values, 'fsdp', ring_perm(chips, hop))]
  transfers between devices with their start and end apart: 57 -> 57, of which waited for: 27 -> 22; matrix products, arithmetic and copies ran while one was open for 1% -> 2% of each run, Pallas kernels for 38% -> 36%
where the time goes in v4:
time: 416 us; the launch traced here: 411 us
  Pallas kernels  220 us (53%)
  waiting for transfers between devices  102 us (25%)
  starting transfers between devices  56.9 us (14%)
  between operations  16.1 us (4%)
  local copies, waits for them, and re-layouts  9.3 us (2%)
  other arithmetic  7.4 us (2%)
    ppermute x31, waiting for transfers between devices, to_next(): return lax.ppermute(values, 'fsdp', ring_perm(chips, hop))  91.3 us
    pallas_call x3, Pallas kernels, attention_back(): pl.pallas_call(functools.partial(attend_back_kernel, pieces=pieces, block...  52.1 us
    pallas_call x1, Pallas kernels, mlp(): pl.pallas_call(functools.partial(mlp_kernel, chips=chips), grid_spec=pltp...  50.9 us
    ppermute x31, starting transfers between devices, to_next(): return lax.ppermute(values, 'fsdp', ring_perm(chips, hop))  36.9 us
    pallas_call x15, Pallas kernels, add(): pl.pallas_call(functools.partial(ring_add_kernel, columns=columns, mode=m...  29.1 us
    pallas_call x1, Pallas kernels, attention(): pl.pallas_call(functools.partial(attend_kernel, pieces=pieces, block=bloc...  28.3 us
    pallas_call x1, Pallas kernels, unproject(): pl.pallas_call(functools.partial(unproject_kernel, chips=chips), grid_spe...  18.2 us
    pallas_call x1, Pallas kernels, unmerge(): pl.pallas_call(functools.partial(unmerge_kernel, tokens=tokens), grid_spe...  14.5 us
  transfers between devices with their start and end apart: 57, of which 22 were waited for; matrix products, arithmetic and copies ran while one was open for 2% of the time, Pallas kernels for 36%

profile of v4, /device:TPU:0, one launch (start us, length us, event | category | flops | bytes accessed | tf_op | source)
XLA Modules:
  0.0 411.4 jit_solution(13132832220807661813)
XLA Ops:
  7.2 1.3 dynamic-slice_bitcast_fusion.place
  8.6 2.7 pack.1
  11.3 3.1 collective-permute-start.5
  15.2 12.3 %collective-permute-done.5.refs_7_.refs_23_ = bf16[64,3200]{1,0:T(8,128)(2,1)S(1)} collective-permute-done((bf16[64,3200]{1,0:T(8,128)(2,1)}, bf16[64,3200]{1,0:T(8,128)(2,1)S(1)}, u32[]{:S(2)}, u32[]{:S(2)}) %collective-permute-start.5) | collective-permute-done | bytes 409632 | tf_op jit(solution)/shard_map/ppermute | solution.py:1108
  27.4 2.4 collective-permute-start.6
  29.9 17.7 %collective-permute-done.6.refs_6_.refs_22_ = bf16[64,3200]{1,0:T(8,128)(2,1)} collective-permute-done((bf16[64,3200]{1,0:T(8,128)(2,1)S(1)}, bf16[64,3200]{1,0:T(8,128)(2,1)}, u32[]{:S(2)}, u32[]{:S(2)}) %collective-permute-start.6) | collective-permute-done | bytes 409632 | tf_op jit(solution)/shard_map/ppermute | solution.py:1108
  47.5 2.4 collective-permute-start.7
  50.5 17.4 %collective-permute-done.7.refs_5_.refs_21_ = bf16[64,3200]{1,0:T(8,128)(2,1)} collective-permute-done((bf16[64,3200]{1,0:T(8,128)(2,1)}, bf16[64,3200]{1,0:T(8,128)(2,1)}, u32[]{:S(2)}, u32[]{:S(2)}) %collective-permute-start.7) | collective-permute-done | bytes 409632 | tf_op jit(solution)/shard_map/ppermute | solution.py:1108
  67.9 2.5 collective-permute-start.8
  71.0 2.7 collective-permute-start.14
  73.8 13.5 %collective-permute-done.8.refs_4_.refs_20_ = bf16[64,3200]{1,0:T(8,128)(2,1)} collective-permute-done((bf16[64,3200]{1,0:T(8,128)(2,1)}, bf16[64,3200]{1,0:T(8,128)(2,1)}, u32[]{:S(2)}, u32[]{:S(2)}) %collective-permute-start.8) | collective-permute-done | bytes 409632 | tf_op jit(solution)/shard_map/ppermute | solution.py:1108
  87.3 1.2 broadcast_select_fusion.1.x_ref.x_hbm
  89.4 12.4 %project.1 = (bf16[3,688,512]{2,1,0:T(8,128)(2,1)}, bf16[3,688,512]{2,1,0:T(8,128)(2,1)}, bf16[688,1024]{1,0:T(8,128)(2,1)}, bf16[1024,3072]{1,0:T(8,128)(2,1)}, f32[16,1024]{1,0:T(8,128)}, /*index=5*/f32[1,4096]{1,0:T(1,128)}) custom-call(s32[15]{0:T(128)} %dynamic-slice_bitcast_fusion.place, bf16[688,1024]{1,0:T(8,128)(2,1)} %broadcast_select_fusion.1.x_ref.x_hbm, ...), custom_call_target="tpu_custom_call" | custom-call | flops 4328521728 | bytes 21037056 | tf_op jit(solution)/shard_map/project/pallas_call | solution.py:466
  102.0 1.2 collective-permute-start.1
  106.4 28.3 %attend.1 = (bf16[688,512]{1,0:T(8,128)(2,1)}, bf16[688,512]{1,0:T(8,128)(2,1)}, f32[688,128]{1,0:T(8,128)}, f32[688,128]{1,0:T(8,128)}) custom-call(s32[2]{0:T(128)} %fusion.1.valid, bf16[3,688,512]{2,1,0:T(8,128)(2,1)} %get-tuple-element.101.refs_0_, bf16[3,688,512]{2,1,0:T(8,128)(2,1)} %collective-permute-done.17.refs_1_), custom_call_target="tpu_custom_call" | custom-call | flops 16240345088 | bytes 5636096 | tf_op jit(solution)/shard_map/attend/pallas_call | solution.py:558
  134.7 3.8 collective-permute-start.18
  138.6 1.2 broadcast_select_fusion.cotangent_ref
  141.4 7.2 %merge.1 = (f32[688,1024]{1,0:T(8,128)}, f32[688,1024]{1,0:T(8,128)}, bf16[688,1024]{1,0:T(8,128)(2,1)}) custom-call(s32[15]{0:T(128)} %dynamic-slice_bitcast_fusion.place, bf16[688,1024]{1,0:T(8,128)(2,1)} %broadcast_select_fusion.1.x_ref.x_hbm, bf16[688,512]{1,0:T(8,128)(2,1)} %get-tuple-element.103.own_ref.refs_2_, bf16[688,512]{1,0:T(8,128)(2,1)} %copy-done.10, ...), custom_call_target="tpu_custom_call" | custom-call | flops 1442840576 | bytes 11960320 | tf_op jit(solution)/shard_map/merge/pallas_call | solution.py:716
  148.6 50.9 %mlp.1 = (f32[688,1024]{1,0:T(8,128)}, f32[688,1024]{1,0:T(8,128)}, bf16[8,64,4096]{2,1,0:T(8,128)(2,1)}, bf16[8,64,4096]{2,1,0:T(8,128)(2,1)}, bf16[8,64,4096]{...) custom-call(s32[15]{0:T(128)} %dynamic-slice_bitcast_fusion.place, ...), custom_call_target="tpu_custom_call" | custom-call | flops 34628173824 | bytes 42008576 | tf_op jit(solution)/shard_map/mlp/pallas_call | solution.py:834
  200.1 14.5 %unmerge.1 = (bf16[688,1024]{1,0:T(8,128)(2,1)}, f32[688,1024]{1,0:T(8,128)}, bf16[688,512]{1,0:T(8,128)(2,1)}, bf16[688,512]{1,0:T(8,128)(2,1)}, bf16[8,64,1024...) custom-call(s32[15]{0:T(128)} %dynamic-slice_bitcast_fusion.place, ...), custom_call_target="tpu_custom_call" | custom-call | flops 2885681152 | bytes 25329664 | tf_op jit(solution)/shard_map/unmerge/pallas_call | solution.py:943
  215.9 2.4 ring_add.15
  218.3 2.5 collective-permute-start.24
  221.3 13.7 %attend_back.3 = (bf16[3,688,512]{2,1,0:T(8,128)(2,1)}, bf16[3,688,512]{2,1,0:T(8,128)(2,1)}) custom-call(s32[2]{0:T(128)} %fusion.1.valid, bf16[3,688,512]{2,1,0:T(8,128)(2,1)} %get-tuple-element.101.refs_0_, bf16[3,688,512]{2,1,0:T(8,128)(2,1)} %collective-permute-done.17.refs_1_, bf16[688,512]{1,0:T(8,128)(2,1)} %get-tuple-element.103.own_ref.refs_2_, ...), custom_call_target="tpu_custom_call" | custom-call | flops 121802588160 | bytes 45088768 | tf_op jit(solution)/shard_map/attend_back/pallas_call | solution.py:667
  236.6 3.7 ring_add.16
  240.3 2.0 collective-permute-start.27
  244.0 24.6 %attend_back.4 = (bf16[3,688,512]{2,1,0:T(8,128)(2,1)}, bf16[3,688,512]{2,1,0:T(8,128)(2,1)}) custom-call(s32[2]{0:T(128)} %fusion.1.valid, bf16[3,688,512]{2,1,0:T(8,128)(2,1)} %get-tuple-element.101.refs_0_, bf16[3,688,512]{2,1,0:T(8,128)(2,1)} %collective-permute-done.17.refs_1_, ...), custom_call_target="tpu_custom_call", output_to_operand_aliasing={{0}: (9, {}), {1}: (10, {})} | custom-call | flops 243605176320 | bytes 90177536 | tf_op jit(solution)/shard_map/attend_back/pallas_call | solution.py:667
  268.6 4.1 ring_add.17
  272.7 2.0 collective-permute-start.29
  275.0 13.7 %attend_back.5 = (bf16[3,688,512]{2,1,0:T(8,128)(2,1)}, bf16[3,688,512]{2,1,0:T(8,128)(2,1)}) custom-call(s32[2]{0:T(128)} %fusion.1.valid, bf16[3,688,512]{2,1,0:T(8,128)(2,1)} %get-tuple-element.101.refs_0_, bf16[3,688,512]{2,1,0:T(8,128)(2,1)} %collective-permute-done.17.refs_1_, ...), custom_call_target="tpu_custom_call", output_to_operand_aliasing={{0}: (9, {}), {1}: (10, {})} | custom-call | flops 121802588160 | bytes 45088768 | tf_op jit(solution)/shard_map/attend_back/pallas_call | solution.py:667
  288.7 9.6 %collective-permute-done.29.refs_8_ = bf16[64,8192]{1,0:T(8,128)(2,1)S(1)} collective-permute-done((bf16[64,8192]{1,0:T(8,128)(2,1)}, bf16[64,8192]{1,0:T(8,128)(2,1)S(1)}, u32[]{:S(2)}, u32[]{:S(2)}) %collective-permute-start.29) | collective-permute-done | bytes 1048608 | tf_op jit(solution)/shard_map/ppermute | solution.py:1108
  298.3 2.7 collective-permute-done.30.refs_9_
  302.0 4.1 ring_add.18
  307.3 1.2 collective-permute-start.33
  308.5 2.1 collective-permute-done.31.far_ref
  310.7 18.2 %unproject.1 = (bf16[688,1024]{1,0:T(8,128)(2,1)}, bf16[8,64,3072]{2,1,0:T(8,128)(2,1)}, bf16[8,64,3072]{2,1,0:T(8,128)(2,1)}, bf16[8,64,128]{2,1,0:T(8,128)(2,1)}, bf16[8,64,128]{2,1,0:T(8,128)(2,1)}) custom-call(s32[15]{0:T(128)} %dynamic-slice_bitcast_fusion.place, bf16[688,1024]{1,0:T(8,128)(2,1)} %broadcast_select_fusion.1.x_ref.x_hbm, ...), custom_call_target="tpu_custom_call" | custom-call | flops 135266304 | bytes 394752 | tf_op jit(solution)/shard_map/unproject/pallas_call | solution.py:1047
  328.9 3.0 collective-permute-done.32.refs_3_.refs_4_
  331.9 1.2 collective-permute-done.33.refs_4_.refs_5_
  334.1 1.8 collective-permute-start.34
  336.6 3.3 ring_add.19.refs_6_.part_ref
  340.2 1.2 copy-done.1
  341.4 1.2 copy-done.4
  344.4 1.5 collective-permute-start.55
  345.9 1.2 collective-permute-start.37
  348.2 1.8 collective-permute-start.41
  350.2 2.4 collective-permute-done.37.refs_12_
  352.6 1.2 ring_add.22
  355.9 1.2 ring_add.23
  359.2 3.9 collective-permute-done.39.refs_12_
  363.1 1.2 ring_add.24
  364.4 1.3 collective-permute-start.43
  366.5 1.2 ring_add.25
  367.7 1.3 collective-permute-start.49
  369.8 4.1 collective-permute-done.43.refs_12_
  375.0 1.2 ring_add.26
  376.3 2.0 collective-permute-start.47
  379.5 1.1 collective-permute-done.50.refs_9_
  380.6 1.2 ring_add.28
  381.9 2.0 collective-permute-start.51
  383.9 1.2 select_bitcast_fusion
  385.2 2.9 finish_rest.1
  389.2 3.1 collective-permute-start.53
  393.6 3.1 bitcast_convert_fusion
  396.7 5.8 %collective-permute-done.54.refs_3_ = bf16[64,2048]{1,0:T(8,128)(2,1)S(1)} collective-permute-done((bf16[64,2048]{1,0:T(8,128)(2,1)S(1)}, bf16[64,2048]{1,0:T(8,128)(2,1)S(1)}, u32[]{:S(2)}, u32[]{:S(2)}) %collective-permute-start.54) | collective-permute-done | bytes 262176 | tf_op jit(solution)/shard_map/ppermute | solution.py:1312
  402.5 1.6 finish_first.1
  (135 shorter events, 30.1 us)
Async XLA Ops:
  7.2 133.7 %all-gather.2.cloned.1.call-start = ((), (), s32[]{:S(2)}) async-start(), calls=%async_computation | async-start | bytes 20054016 | tf_op jit(solution)/shard_map/all_gather | solution.py:1325
  11.3 16.1 %collective-permute-start.5 = (bf16[64,3200]{1,0:T(8,128)(2,1)}, bf16[64,3200]{1,0:T(8,128)(2,1)S(1)}, u32[]{:S(2)}, u32[]{:S(2)}) collective-permute-start(bf16[64,3200]{1,0:T(8,128)(2,1)} %get-tuple-element.100.refs_0_.refs_16_), channel_id=1, source_target_pairs={{0,8},{2,10},{8,16},{10,18},{16,24},{18,26},{24,28},{26,30},{28,20... | collective-permute-start | bytes 1228808 | tf_op jit(solution)/shard_map/ppermute | solution.py:1108
  14.3 59.4 %collective-permute-start = (bf16[688,1024]{1,0:T(8,128)(2,1)S(1)}, bf16[688,1024]{1,0:T(8,128)(2,1)S(1)}, u32[]{:S(2)}, u32[]{:S(2)}) collective-permute-start(bf16[688,1024]{1,0:T(8,128)(2,1)S(1)} %bitcast.15), channel_id=1, source_target_pairs={{1,2},{2,1},{5,6},{6,5},{9,10},{10,9},{13,14},{14,13},{17,18},{18,... | collective-permute-start | bytes 4227080 | tf_op jit(solution)/shard_map/ppermute | solution.py:1303
  15.1 14.7 %collective-permute-start.2 = (bf16[64,3200]{1,0:T(8,128)(2,1)}, bf16[64,3200]{1,0:T(8,128)(2,1)S(1)}, u32[]{:S(2)}, u32[]{:S(2)}) collective-permute-start(bf16[64,3200]{1,0:T(8,128)(2,1)} %get-tuple-element.100.refs_0_.refs_16_), channel_id=1, source_target_pairs={{0,4},{2,6},{8,0},{10,2},{16,8},{18,10},{24,16},{26,18},{28,24},{3... | collective-permute-start | bytes 1228808 | tf_op jit(solution)/shard_map/ppermute | solution.py:1108
  27.4 61.2 %copy-start.20 = (bf16[64,3200]{1,0:T(8,128)(2,1)}, bf16[64,3200]{1,0:T(8,128)(2,1)S(1)}, u32[]{:S(2)}) copy-start(bf16[64,3200]{1,0:T(8,128)(2,1)S(1)} %collective-permute-done.5.refs_7_.refs_23_) | copy-start | bytes 1228804
  27.4 20.1 %collective-permute-start.6 = (bf16[64,3200]{1,0:T(8,128)(2,1)S(1)}, bf16[64,3200]{1,0:T(8,128)(2,1)}, u32[]{:S(2)}, u32[]{:S(2)}) collective-permute-start(bf16[64,3200]{1,0:T(8,128)(2,1)S(1)} %collective-permute-done.5.refs_7_.refs_23_), channel_id=1, source_target_pairs={{0,8},{2,10},{8,16},{10,18},{16,24},{18,26},{24,28},{26,30},{28,20... | collective-permute-start | bytes 1228808 | tf_op jit(solution)/shard_map/ppermute | solution.py:1108
  29.8 20.2 %collective-permute-start.9 = (bf16[64,3200]{1,0:T(8,128)(2,1)}, bf16[64,3200]{1,0:T(8,128)(2,1)S(1)}, u32[]{:S(2)}, u32[]{:S(2)}) collective-permute-start(bf16[64,3200]{1,0:T(8,128)(2,1)} %get-tuple-element.100.refs_0_.refs_16_), channel_id=1, source_target_pairs={{0,2},{2,0},{4,6},{6,4},{8,10},{10,8},{12,14},{14,12},{16,18},{18,... | collective-permute-start | bytes 1228808 | tf_op jit(solution)/shard_map/ppermute | solution.py:1309
  29.8 44.0 %copy-start.21 = (bf16[64,3200]{1,0:T(8,128)(2,1)}, bf16[64,3200]{1,0:T(8,128)(2,1)S(1)}, u32[]{:S(2)}) copy-start(bf16[64,3200]{1,0:T(8,128)(2,1)S(1)} %collective-permute-done.2.refs_1_.refs_17_) | copy-start | bytes 1228804
  29.8 20.7 %collective-permute-start.3 = (bf16[64,3200]{1,0:T(8,128)(2,1)S(1)}, bf16[64,3200]{1,0:T(8,128)(2,1)}, u32[]{:S(2)}, u32[]{:S(2)}) collective-permute-start(bf16[64,3200]{1,0:T(8,128)(2,1)S(1)} %collective-permute-done.2.refs_1_.refs_17_), channel_id=1, source_target_pairs={{0,4},{2,6},{8,0},{10,2},{16,8},{18,10},{24,16},{26,18},{28,24},{3... | collective-permute-start | bytes 1228808 | tf_op jit(solution)/shard_map/ppermute | solution.py:1108
  47.5 20.4 %collective-permute-start.7 = (bf16[64,3200]{1,0:T(8,128)(2,1)}, bf16[64,3200]{1,0:T(8,128)(2,1)}, u32[]{:S(2)}, u32[]{:S(2)}) collective-permute-start(bf16[64,3200]{1,0:T(8,128)(2,1)} %collective-permute-done.6.refs_6_.refs_22_), channel_id=1, source_target_pairs={{0,8},{2,10},{8,16},{10,18},{16,24},{18,26},{24,28},{26,30},{28,20... | collective-permute-start | bytes 1228808 | tf_op jit(solution)/shard_map/ppermute | solution.py:1108
  50.0 20.4 %collective-permute-start.16 = (bf16[64,3200]{1,0:T(8,128)(2,1)S(1)}, bf16[64,3200]{1,0:T(8,128)(2,1)S(1)}, u32[]{:S(2)}, u32[]{:S(2)}) collective-permute-start(bf16[64,3200]{1,0:T(8,128)(2,1)S(1)} %collective-permute-done.5.refs_7_.refs_23_), channel_id=1, source_target_pairs={{0,2},{2,0},{4,6},{6,4},{8,10},{10,8},{12,14},{14,12},{16,18},{18,... | collective-permute-start | bytes 1228808 | tf_op jit(solution)/shard_map/ppermute | solution.py:1309
  50.0 23.9 %copy-start.22 = (bf16[64,3200]{1,0:T(8,128)(2,1)}, bf16[64,3200]{1,0:T(8,128)(2,1)S(1)}, u32[]{:S(2)}) copy-start(bf16[64,3200]{1,0:T(8,128)(2,1)S(1)} %collective-permute-done.9.refs_8_.refs_24_) | copy-start | bytes 1228804
  50.0 20.4 %collective-permute-start.10 = (bf16[64,3200]{1,0:T(8,128)(2,1)S(1)}, bf16[64,3200]{1,0:T(8,128)(2,1)S(1)}, u32[]{:S(2)}, u32[]{:S(2)}) collective-permute-start(bf16[64,3200]{1,0:T(8,128)(2,1)S(1)} %collective-permute-done.2.refs_1_.refs_17_), channel_id=1, source_target_pairs={{0,2},{2,0},{4,6},{6,4},{8,10},{10,8},{12,14},{14,12},{16,18},{18,... | collective-permute-start | bytes 1228808 | tf_op jit(solution)/shard_map/ppermute | solution.py:1309
  50.5 20.5 %collective-permute-start.4 = (bf16[64,3200]{1,0:T(8,128)(2,1)}, bf16[64,3200]{1,0:T(8,128)(2,1)}, u32[]{:S(2)}, u32[]{:S(2)}) collective-permute-start(bf16[64,3200]{1,0:T(8,128)(2,1)} %collective-permute-done.3.refs_2_.refs_18_), channel_id=1, source_target_pairs={{0,4},{2,6},{8,0},{10,2},{16,8},{18,10},{24,16},{26,18},{28,24},{3... | collective-permute-start | bytes 1228808 | tf_op jit(solution)/shard_map/ppermute | solution.py:1108
  67.9 19.4 %collective-permute-start.8 = (bf16[64,3200]{1,0:T(8,128)(2,1)}, bf16[64,3200]{1,0:T(8,128)(2,1)}, u32[]{:S(2)}, u32[]{:S(2)}) collective-permute-start(bf16[64,3200]{1,0:T(8,128)(2,1)} %collective-permute-done.7.refs_5_.refs_21_), channel_id=1, source_target_pairs={{0,8},{2,10},{8,16},{10,18},{16,24},{18,26},{24,28},{26,30},{28,20... | collective-permute-start | bytes 1228808 | tf_op jit(solution)/shard_map/ppermute | solution.py:1108
  70.4 16.9 %copy-start.23 = (bf16[64,3200]{1,0:T(8,128)(2,1)}, bf16[64,3200]{1,0:T(8,128)(2,1)S(1)}, u32[]{:S(2)}) copy-start(bf16[64,3200]{1,0:T(8,128)(2,1)S(1)} %collective-permute-done.16.refs_15_.refs_31_) | copy-start | bytes 1228804
  70.4 18.2 %collective-permute-start.15 = (bf16[64,3200]{1,0:T(8,128)(2,1)}, bf16[64,3200]{1,0:T(8,128)(2,1)}, u32[]{:S(2)}, u32[]{:S(2)}) collective-permute-start(bf16[64,3200]{1,0:T(8,128)(2,1)} %collective-permute-done.6.refs_6_.refs_22_), channel_id=1, source_target_pairs={{0,2},{2,0},{4,6},{6,4},{8,10},{10,8},{12,14},{14,12},{16,18},{18,... | collective-permute-start | bytes 1228808 | tf_op jit(solution)/shard_map/ppermute | solution.py:1309
  70.4 16.9 %copy-start.24 = (bf16[64,3200]{1,0:T(8,128)(2,1)}, bf16[64,3200]{1,0:T(8,128)(2,1)S(1)}, u32[]{:S(2)}) copy-start(bf16[64,3200]{1,0:T(8,128)(2,1)S(1)} %collective-permute-done.10.refs_9_.refs_25_) | copy-start | bytes 1228804
  70.4 18.2 %collective-permute-start.11 = (bf16[64,3200]{1,0:T(8,128)(2,1)}, bf16[64,3200]{1,0:T(8,128)(2,1)}, u32[]{:S(2)}, u32[]{:S(2)}) collective-permute-start(bf16[64,3200]{1,0:T(8,128)(2,1)} %collective-permute-done.3.refs_2_.refs_18_), channel_id=1, source_target_pairs={{0,2},{2,0},{4,6},{6,4},{8,10},{10,8},{12,14},{14,12},{16,18},{18,... | collective-permute-start | bytes 1228808 | tf_op jit(solution)/shard_map/ppermute | solution.py:1309
  71.0 17.6 %collective-permute-start.14 = (bf16[64,3200]{1,0:T(8,128)(2,1)}, bf16[64,3200]{1,0:T(8,128)(2,1)}, u32[]{:S(2)}, u32[]{:S(2)}) collective-permute-start(bf16[64,3200]{1,0:T(8,128)(2,1)} %collective-permute-done.7.refs_5_.refs_21_), channel_id=1, source_target_pairs={{0,2},{2,0},{4,6},{6,4},{8,10},{10,8},{12,14},{14,12},{16,18},{18,... | collective-permute-start | bytes 1228808 | tf_op jit(solution)/shard_map/ppermute | solution.py:1309
  73.7 14.8 %collective-permute-start.12 = (bf16[64,3200]{1,0:T(8,128)(2,1)}, bf16[64,3200]{1,0:T(8,128)(2,1)}, u32[]{:S(2)}, u32[]{:S(2)}) collective-permute-start(bf16[64,3200]{1,0:T(8,128)(2,1)} %collective-permute-done.4.refs_3_.refs_19_), channel_id=1, source_target_pairs={{0,2},{2,0},{4,6},{6,4},{8,10},{10,8},{12,14},{14,12},{16,18},{18,... | collective-permute-start | bytes 1228808 | tf_op jit(solution)/shard_map/ppermute | solution.py:1309
  87.3 2.1 collective-permute-start.13
  88.6 14.6 %copy-start.12 = (bf16[1,688,1024]{2,1,0:T(8,128)(2,1)S(1)}, bf16[1,688,1024]{2,1,0:T(8,128)(2,1)}, u32[]{:S(2)}) copy-start(bf16[1,688,1024]{2,1,0:T(8,128)(2,1)} %param.36) | copy-start | bytes 4227076
  101.8 4.6 %collective-permute-start.17 = (bf16[3,688,512]{2,1,0:T(8,128)(2,1)}, bf16[3,688,512]{2,1,0:T(8,128)(2,1)}, u32[]{:S(2)}, u32[]{:S(2)}) collective-permute-start(bf16[3,688,512]{2,1,0:T(8,128)(2,1)} %get-tuple-element.102), channel_id=1, source_target_pairs={{0,2},{2,0},{4,6},{6,4},{8,10},{10,8},{12,14},{14,12},{16,18},{18,... | collective-permute-start | bytes 6340616 | tf_op jit(solution)/shard_map/ppermute | solution.py:1309
  102.0 2.8 collective-permute-start.1
  103.1 35.4 %collective-permute-start.19 = (bf16[688,1024]{1,0:T(8,128)(2,1)S(1)}, bf16[688,1024]{1,0:T(8,128)(2,1)S(1)}, u32[]{:S(2)}, u32[]{:S(2)}) collective-permute-start(bf16[688,1024]{1,0:T(8,128)(2,1)S(1)} %bitcast.16), channel_id=1, source_target_pairs={{1,2},{2,1},{5,6},{6,5},{9,10},{10,9},{13,14},{14,13},{17,18},{18,... | collective-permute-start | bytes 4227080 | tf_op jit(solution)/shard_map/ppermute | solution.py:1303
  134.7 5.8 %collective-permute-start.18 = (bf16[688,512]{1,0:T(8,128)(2,1)}, bf16[688,512]{1,0:T(8,128)(2,1)S(1)}, u32[]{:S(2)}, u32[]{:S(2)}) collective-permute-start(bf16[688,512]{1,0:T(8,128)(2,1)} %get-tuple-element.104.refs_3_), channel_id=1, source_target_pairs={{0,2},{2,0},{4,6},{6,4},{8,10},{10,8},{12,14},{14,12},{16,18},{18,... | collective-permute-start | bytes 2113544 | tf_op jit(solution)/shard_map/ppermute | solution.py:1309
  199.5 16.4 %collective-permute-start.22 = (bf16[8,64,4096]{2,1,0:T(8,128)(2,1)}, bf16[8,64,4096]{2,1,0:T(8,128)(2,1)}, u32[]{:S(2)}, u32[]{:S(2)}) collective-permute-start(bf16[8,64,4096]{2,1,0:T(8,128)(2,1)} %get-tuple-element.121), channel_id=1, source_target_pairs={{0,2},{2,0},{4,6},{6,4},{8,10},{10,8},{12,14},{14,12},{16,18},{18,... | collective-permute-start | bytes 12582920 | tf_op jit(solution)/shard_map/ppermute | solution.py:1309
  199.9 16.0 %collective-permute-start.23 = (bf16[8,64,4096]{2,1,0:T(8,128)(2,1)}, bf16[8,64,4096]{2,1,0:T(8,128)(2,1)}, u32[]{:S(2)}, u32[]{:S(2)}) collective-permute-start(bf16[8,64,4096]{2,1,0:T(8,128)(2,1)} %get-tuple-element.123), channel_id=1, source_target_pairs={{0,2},{2,0},{4,6},{6,4},{8,10},{10,8},{12,14},{14,12},{16,18},{18,... | collective-permute-start | bytes 12582920 | tf_op jit(solution)/shard_map/ppermute | solution.py:1309
  214.6 6.8 %collective-permute-start.21 = (bf16[688,512]{1,0:T(8,128)(2,1)}, bf16[688,512]{1,0:T(8,128)(2,1)}, u32[]{:S(2)}, u32[]{:S(2)}) collective-permute-start(bf16[688,512]{1,0:T(8,128)(2,1)} %get-tuple-element.117), channel_id=1, source_target_pairs={{0,2},{2,0},{4,6},{6,4},{8,10},{10,8},{12,14},{14,12},{16,18},{18,... | collective-permute-start | bytes 2113544 | tf_op jit(solution)/shard_map/ppermute | solution.py:1309
  215.0 27.6 %collective-permute-start.26 = (bf16[8,64,1024]{2,1,0:T(8,128)(2,1)}, bf16[8,64,1024]{2,1,0:T(8,128)(2,1)S(1)}, u32[]{:S(2)}, u32[]{:S(2)}) collective-permute-start(bf16[8,64,1024]{2,1,0:T(8,128)(2,1)} %get-tuple-element.130), channel_id=1, source_target_pairs={{0,2},{2,0},{4,6},{6,4},{8,10},{10,8},{12,14},{14,12},{16,18},{18,... | collective-permute-start | bytes 3145736 | tf_op jit(solution)/shard_map/ppermute | solution.py:1309
  215.1 27.4 %collective-permute-start.20 = (bf16[688,1024]{1,0:T(8,128)(2,1)}, bf16[688,1024]{1,0:T(8,128)(2,1)S(1)}, u32[]{:S(2)}, u32[]{:S(2)}) collective-permute-start(bf16[688,1024]{1,0:T(8,128)(2,1)} %get-tuple-element.113), channel_id=1, source_target_pairs={{1,2},{2,1},{5,6},{6,5},{9,10},{10,9},{13,14},{14,13},{17,18},{18,... | collective-permute-start | bytes 4227080 | tf_op jit(solution)/shard_map/ppermute | solution.py:1303
  218.3 16.7 %collective-permute-start.24 = (bf16[64,4096]{1,0:T(8,128)(2,1)}, bf16[64,4096]{1,0:T(8,128)(2,1)S(1)}, u32[]{:S(2)}, u32[]{:S(2)}) collective-permute-start(bf16[64,4096]{1,0:T(8,128)(2,1)} %get-tuple-element.124.refs_8_), channel_id=1, source_target_pairs={{0,8},{2,10},{8,16},{10,18},{16,24},{18,26},{24,28},{26,30},{28,20... | collective-permute-start | bytes 1572872 | tf_op jit(solution)/shard_map/ppermute | solution.py:1108
  220.9 14.2 %collective-permute-start.25 = (bf16[64,4096]{1,0:T(8,128)(2,1)}, bf16[64,4096]{1,0:T(8,128)(2,1)S(1)}, u32[]{:S(2)}, u32[]{:S(2)}) collective-permute-start(bf16[64,4096]{1,0:T(8,128)(2,1)} %get-tuple-element.125.refs_9_), channel_id=1, source_target_pairs={{0,4},{2,6},{8,0},{10,2},{16,8},{18,10},{24,16},{26,18},{28,24},{3... | collective-permute-start | bytes 1572872 | tf_op jit(solution)/shard_map/ppermute | solution.py:1108
  240.3 28.3 %collective-permute-start.27 = (bf16[64,8192]{1,0:T(8,128)(2,1)}, bf16[64,8192]{1,0:T(8,128)(2,1)}, u32[]{:S(2)}, u32[]{:S(2)}) collective-permute-start(bf16[64,8192]{1,0:T(8,128)(2,1)} %get-tuple-element.128.refs_10_), channel_id=1, source_target_pairs={{0,8},{2,10},{8,16},{10,18},{16,24},{18,26},{24,28},{26,30},{28,20... | collective-permute-start | bytes 3145736 | tf_op jit(solution)/shard_map/ppermute | solution.py:1108
  242.4 26.2 %collective-permute-start.28 = (bf16[64,8192]{1,0:T(8,128)(2,1)}, bf16[64,8192]{1,0:T(8,128)(2,1)}, u32[]{:S(2)}, u32[]{:S(2)}) collective-permute-start(bf16[64,8192]{1,0:T(8,128)(2,1)} %get-tuple-element.129.refs_11_), channel_id=1, source_target_pairs={{0,4},{2,6},{8,0},{10,2},{16,8},{18,10},{24,16},{26,18},{28,24},{3... | collective-permute-start | bytes 3145736 | tf_op jit(solution)/shard_map/ppermute | solution.py:1108
  272.7 25.6 %collective-permute-start.29 = (bf16[64,8192]{1,0:T(8,128)(2,1)}, bf16[64,8192]{1,0:T(8,128)(2,1)S(1)}, u32[]{:S(2)}, u32[]{:S(2)}) collective-permute-start(bf16[64,8192]{1,0:T(8,128)(2,1)} %get-tuple-element.133.refs_10_), channel_id=1, source_target_pairs={{0,8},{2,10},{8,16},{10,18},{16,24},{18,26},{24,28},{26,30},{28,20... | collective-permute-start | bytes 3145736 | tf_op jit(solution)/shard_map/ppermute | solution.py:1108
  274.8 26.2 %collective-permute-start.30 = (bf16[64,8192]{1,0:T(8,128)(2,1)}, bf16[64,8192]{1,0:T(8,128)(2,1)S(1)}, u32[]{:S(2)}, u32[]{:S(2)}) collective-permute-start(bf16[64,8192]{1,0:T(8,128)(2,1)} %get-tuple-element.134.refs_11_), channel_id=1, source_target_pairs={{0,4},{2,6},{8,0},{10,2},{16,8},{18,10},{24,16},{26,18},{28,24},{3... | collective-permute-start | bytes 3145736 | tf_op jit(solution)/shard_map/ppermute | solution.py:1108
  306.1 4.6 %collective-permute-start.31 = (bf16[3,688,512]{2,1,0:T(8,128)(2,1)}, bf16[3,688,512]{2,1,0:T(8,128)(2,1)}, u32[]{:S(2)}, u32[]{:S(2)}) collective-permute-start(bf16[3,688,512]{2,1,0:T(8,128)(2,1)} %get-tuple-element.137), channel_id=1, source_target_pairs={{0,2},{2,0},{4,6},{6,4},{8,10},{10,8},{12,14},{14,12},{16,18},{18,... | collective-permute-start | bytes 6340616 | tf_op jit(solution)/shard_map/ppermute | solution.py:1309
  306.2 25.7 %collective-permute-start.32 = (bf16[64,8192]{1,0:T(8,128)(2,1)}, bf16[64,8192]{1,0:T(8,128)(2,1)S(1)}, u32[]{:S(2)}, u32[]{:S(2)}) collective-permute-start(bf16[64,8192]{1,0:T(8,128)(2,1)} %get-tuple-element.144), channel_id=1, source_target_pairs={{0,8},{2,10},{8,16},{10,18},{16,24},{18,26},{24,28},{26,30},{28,20... | collective-permute-start | bytes 3145736 | tf_op jit(solution)/shard_map/ppermute | solution.py:1108
  307.3 25.8 %collective-permute-start.33 = (bf16[64,8192]{1,0:T(8,128)(2,1)}, bf16[64,8192]{1,0:T(8,128)(2,1)S(1)}, u32[]{:S(2)}, u32[]{:S(2)}) collective-permute-start(bf16[64,8192]{1,0:T(8,128)(2,1)} %get-tuple-element.145), channel_id=1, source_target_pairs={{0,4},{2,6},{8,0},{10,2},{16,8},{18,10},{24,16},{26,18},{28,24},{3... | collective-permute-start | bytes 3145736 | tf_op jit(solution)/shard_map/ppermute | solution.py:1108
  334.1 6.1 %collective-permute-start.35 = (bf16[8,64,3072]{2,1,0:T(8,128)(2,1)}, bf16[8,64,3072]{2,1,0:T(8,128)(2,1)}, u32[]{:S(2)}, u32[]{:S(2)}) collective-permute-start(bf16[8,64,3072]{2,1,0:T(8,128)(2,1)} %get-tuple-element.148), channel_id=1, source_target_pairs={{0,2},{2,0},{4,6},{6,4},{8,10},{10,8},{12,14},{14,12},{16,18},{18,... | collective-permute-start | bytes 9437192 | tf_op jit(solution)/shard_map/ppermute | solution.py:1309
  334.1 24.0 %collective-permute-start.34 = (bf16[688,1024]{1,0:T(8,128)(2,1)}, bf16[688,1024]{1,0:T(8,128)(2,1)}, u32[]{:S(2)}, u32[]{:S(2)}) collective-permute-start(bf16[688,1024]{1,0:T(8,128)(2,1)} %get-tuple-element.146), channel_id=1, source_target_pairs={{1,2},{2,1},{5,6},{6,5},{9,10},{10,9},{13,14},{14,13},{17,18},{18,... | collective-permute-start | bytes 4227080 | tf_op jit(solution)/shard_map/ppermute | solution.py:1303
  335.8 4.3 %collective-permute-start.36 = (bf16[8,64,128]{2,1,0:T(8,128)(2,1)}, bf16[8,64,128]{2,1,0:T(8,128)(2,1)S(1)}, u32[]{:S(2)}, u32[]{:S(2)}) collective-permute-start(bf16[8,64,128]{2,1,0:T(8,128)(2,1)} %get-tuple-element.151), channel_id=1, source_target_pairs={{0,2},{2,0},{4,6},{6,4},{8,10},{10,8},{12,14},{14,12},{16,18},{18,... | collective-permute-start | bytes 393224 | tf_op jit(solution)/shard_map/ppermute | solution.py:1309
  343.6 6.3 %collective-permute-start.38 = (bf16[64,1024]{1,0:T(8,128)(2,1)S(1)}, bf16[64,1024]{1,0:T(8,128)(2,1)S(1)}, u32[]{:S(2)}, u32[]{:S(2)}) collective-permute-start(bf16[64,1024]{1,0:T(8,128)(2,1)S(1)} %get-tuple-element.153.refs_5_), channel_id=1, source_target_pairs={{0,4},{2,6},{8,0},{10,2},{16,8},{18,10},{24,16},{26,18},{28,24},{3... | collective-permute-start | bytes 393224 | tf_op jit(solution)/shard_map/ppermute | solution.py:1108
  344.4 40.7 %collective-permute-start.55 = (bf16[64,8192]{1,0:T(8,128)(2,1)}, bf16[64,8192]{1,0:T(8,128)(2,1)S(1)}, u32[]{:S(2)}, u32[]{:S(2)}) collective-permute-start(bf16[64,8192]{1,0:T(8,128)(2,1)} %ring_add.19.refs_6_.part_ref), channel_id=1, source_target_pairs={{0,1},{1,0},{2,3},{3,2},{4,5},{5,4},{6,7},{7,6},{8,9},{9,8},{10,11... | collective-permute-start | bytes 3145736 | tf_op jit(solution)/shard_map/ppermute | solution.py:1312
  345.9 6.7 %collective-permute-start.37 = (bf16[64,1152]{1,0:T(8,128)(2,1)S(1)}, bf16[64,1152]{1,0:T(8,128)(2,1)S(1)}, u32[]{:S(2)}, u32[]{:S(2)}) collective-permute-start(bf16[64,1152]{1,0:T(8,128)(2,1)S(1)} %get-tuple-element.152.refs_4_), channel_id=1, source_target_pairs={{0,8},{2,10},{8,16},{10,18},{16,24},{18,26},{24,28},{26,30},{28,20... | collective-permute-start | bytes 442376 | tf_op jit(solution)/shard_map/ppermute | solution.py:1108
  348.2 6.7 %collective-permute-start.41 = (bf16[64,1024]{1,0:T(8,128)(2,1)S(1)}, bf16[64,1024]{1,0:T(8,128)(2,1)S(1)}, u32[]{:S(2)}, u32[]{:S(2)}) collective-permute-start(bf16[64,1024]{1,0:T(8,128)(2,1)S(1)} %get-tuple-element.154.refs_14_), channel_id=1, source_target_pairs={{0,8},{2,10},{8,16},{10,18},{16,24},{18,26},{24,28},{26,30},{28,20... | collective-permute-start | bytes 393224 | tf_op jit(solution)/shard_map/ppermute | solution.py:1108
  350.0 6.0 %collective-permute-start.42 = (bf16[64,1024]{1,0:T(8,128)(2,1)S(1)}, bf16[64,1024]{1,0:T(8,128)(2,1)S(1)}, u32[]{:S(2)}, u32[]{:S(2)}) collective-permute-start(bf16[64,1024]{1,0:T(8,128)(2,1)S(1)} %get-tuple-element.155.refs_15_), channel_id=1, source_target_pairs={{0,4},{2,6},{8,0},{10,2},{16,8},{18,10},{24,16},{26,18},{28,24},{3... | collective-permute-start | bytes 393224 | tf_op jit(solution)/shard_map/ppermute | solution.py:1108
  353.8 9.3 %collective-permute-start.39 = (bf16[64,2176]{1,0:T(8,128)(2,1)S(1)}, bf16[64,2176]{1,0:T(8,128)(2,1)S(1)}, u32[]{:S(2)}, u32[]{:S(2)}) collective-permute-start(bf16[64,2176]{1,0:T(8,128)(2,1)S(1)} %get-tuple-element.156.refs_10_), channel_id=1, source_target_pairs={{0,8},{2,10},{8,16},{10,18},{16,24},{18,26},{24,28},{26,30},{28,20... | collective-permute-start | bytes 835592 | tf_op jit(solution)/shard_map/ppermute | solution.py:1108
  354.8 8.3 %collective-permute-start.40 = (bf16[64,2176]{1,0:T(8,128)(2,1)S(1)}, bf16[64,2176]{1,0:T(8,128)(2,1)S(1)}, u32[]{:S(2)}, u32[]{:S(2)}) collective-permute-start(bf16[64,2176]{1,0:T(8,128)(2,1)S(1)} %get-tuple-element.157.refs_11_), channel_id=1, source_target_pairs={{0,4},{2,6},{8,0},{10,2},{16,8},{18,10},{24,16},{26,18},{28,24},{3... | collective-permute-start | bytes 835592 | tf_op jit(solution)/shard_map/ppermute | solution.py:1108
  357.1 9.3 %collective-permute-start.45 = (bf16[64,2048]{1,0:T(8,128)(2,1)S(1)}, bf16[64,2048]{1,0:T(8,128)(2,1)S(1)}, u32[]{:S(2)}, u32[]{:S(2)}) collective-permute-start(bf16[64,2048]{1,0:T(8,128)(2,1)S(1)} %get-tuple-element.158.refs_14_), channel_id=1, source_target_pairs={{0,8},{2,10},{8,16},{10,18},{16,24},{18,26},{24,28},{26,30},{28,20... | collective-permute-start | bytes 786440 | tf_op jit(solution)/shard_map/ppermute | solution.py:1108
  358.1 8.4 %collective-permute-start.46 = (bf16[64,2048]{1,0:T(8,128)(2,1)S(1)}, bf16[64,2048]{1,0:T(8,128)(2,1)S(1)}, u32[]{:S(2)}, u32[]{:S(2)}) collective-permute-start(bf16[64,2048]{1,0:T(8,128)(2,1)S(1)} %get-tuple-element.159.refs_15_), channel_id=1, source_target_pairs={{0,4},{2,6},{8,0},{10,2},{16,8},{18,10},{24,16},{26,18},{28,24},{3... | collective-permute-start | bytes 786440 | tf_op jit(solution)/shard_map/ppermute | solution.py:1108
  364.4 9.5 %collective-permute-start.43 = (bf16[64,2176]{1,0:T(8,128)(2,1)S(1)}, bf16[64,2176]{1,0:T(8,128)(2,1)S(1)}, u32[]{:S(2)}, u32[]{:S(2)}) collective-permute-start(bf16[64,2176]{1,0:T(8,128)(2,1)S(1)} %get-tuple-element.160.refs_10_), channel_id=1, source_target_pairs={{0,8},{2,10},{8,16},{10,18},{16,24},{18,26},{24,28},{26,30},{28,20... | collective-permute-start | bytes 835592 | tf_op jit(solution)/shard_map/ppermute | solution.py:1108
  365.7 9.3 %collective-permute-start.44 = (bf16[64,2176]{1,0:T(8,128)(2,1)S(1)}, bf16[64,2176]{1,0:T(8,128)(2,1)S(1)}, u32[]{:S(2)}, u32[]{:S(2)}) collective-permute-start(bf16[64,2176]{1,0:T(8,128)(2,1)S(1)} %get-tuple-element.161.refs_11_), channel_id=1, source_target_pairs={{0,4},{2,6},{8,0},{10,2},{16,8},{18,10},{24,16},{26,18},{28,24},{3... | collective-permute-start | bytes 835592 | tf_op jit(solution)/shard_map/ppermute | solution.py:1108
  367.7 11.8 %collective-permute-start.49 = (bf16[64,2048]{1,0:T(8,128)(2,1)S(1)}, bf16[64,2048]{1,0:T(8,128)(2,1)S(1)}, u32[]{:S(2)}, u32[]{:S(2)}) collective-permute-start(bf16[64,2048]{1,0:T(8,128)(2,1)S(1)} %get-tuple-element.162.refs_14_), channel_id=1, source_target_pairs={{0,8},{2,10},{8,16},{10,18},{16,24},{18,26},{24,28},{26,30},{28,20... | collective-permute-start | bytes 786440 | tf_op jit(solution)/shard_map/ppermute | solution.py:1108
  369.0 11.6 %collective-permute-start.50 = (bf16[64,2048]{1,0:T(8,128)(2,1)S(1)}, bf16[64,2048]{1,0:T(8,128)(2,1)S(1)}, u32[]{:S(2)}, u32[]{:S(2)}) collective-permute-start(bf16[64,2048]{1,0:T(8,128)(2,1)S(1)} %get-tuple-element.163.refs_15_), channel_id=1, source_target_pairs={{0,4},{2,6},{8,0},{10,2},{16,8},{18,10},{24,16},{26,18},{28,24},{3... | collective-permute-start | bytes 786440 | tf_op jit(solution)/shard_map/ppermute | solution.py:1108
  376.3 11.8 %collective-permute-start.47 = (bf16[64,2176]{1,0:T(8,128)(2,1)S(1)}, bf16[64,2176]{1,0:T(8,128)(2,1)S(1)}, u32[]{:S(2)}, u32[]{:S(2)}) collective-permute-start(bf16[64,2176]{1,0:T(8,128)(2,1)S(1)} %get-tuple-element.164.refs_10_), channel_id=1, source_target_pairs={{0,8},{2,10},{8,16},{10,18},{16,24},{18,26},{24,28},{26,30},{28,20... | collective-permute-start | bytes 835592 | tf_op jit(solution)/shard_map/ppermute | solution.py:1108
  378.3 9.8 %collective-permute-start.48 = (bf16[64,2176]{1,0:T(8,128)(2,1)S(1)}, bf16[64,2176]{1,0:T(8,128)(2,1)S(1)}, u32[]{:S(2)}, u32[]{:S(2)}) collective-permute-start(bf16[64,2176]{1,0:T(8,128)(2,1)S(1)} %get-tuple-element.165.refs_11_), channel_id=1, source_target_pairs={{0,4},{2,6},{8,0},{10,2},{16,8},{18,10},{24,16},{26,18},{28,24},{3... | collective-permute-start | bytes 835592 | tf_op jit(solution)/shard_map/ppermute | solution.py:1108
  381.9 10.5 %collective-permute-start.51 = (bf16[64,2048]{1,0:T(8,128)(2,1)S(1)}, bf16[64,2048]{1,0:T(8,128)(2,1)S(1)}, u32[]{:S(2)}, u32[]{:S(2)}) collective-permute-start(bf16[64,2048]{1,0:T(8,128)(2,1)S(1)} %get-tuple-element.166), channel_id=1, source_target_pairs={{0,8},{2,10},{8,16},{10,18},{16,24},{18,26},{24,28},{26,30},{28,20... | collective-permute-start | bytes 786440 | tf_op jit(solution)/shard_map/ppermute | solution.py:1108
  383.9 8.4 %collective-permute-start.52 = (bf16[64,2048]{1,0:T(8,128)(2,1)S(1)}, bf16[64,2048]{1,0:T(8,128)(2,1)S(1)}, u32[]{:S(2)}, u32[]{:S(2)}) collective-permute-start(bf16[64,2048]{1,0:T(8,128)(2,1)S(1)} %get-tuple-element.167), channel_id=1, source_target_pairs={{0,4},{2,6},{8,0},{10,2},{16,8},{18,10},{24,16},{26,18},{28,24},{3... | collective-permute-start | bytes 786440 | tf_op jit(solution)/shard_map/ppermute | solution.py:1108
  389.2 13.3 %collective-permute-start.53 = (bf16[64,2176]{1,0:T(8,128)(2,1)S(1)}, bf16[64,2176]{1,0:T(8,128)(2,1)S(1)}, u32[]{:S(2)}, u32[]{:S(2)}) collective-permute-start(bf16[64,2176]{1,0:T(8,128)(2,1)S(1)} %ring_add.27.refs_6_.refs_0_), channel_id=1, source_target_pairs={{0,1},{1,0},{2,3},{3,2},{4,5},{5,4},{6,7},{7,6},{8,9},{9,8},{10,11... | collective-permute-start | bytes 835592 | tf_op jit(solution)/shard_map/ppermute | solution.py:1312
  393.4 9.1 %copy-start.9 = (s32[15]{0:T(128)S(1)}, s32[15]{0:T(128)}, u32[]{:S(2)}) copy-start(s32[15]{0:T(128)} %dynamic-slice_bitcast_fusion.place) | copy-start | bytes 184
  393.4 9.0 %collective-permute-start.54 = (bf16[64,2048]{1,0:T(8,128)(2,1)S(1)}, bf16[64,2048]{1,0:T(8,128)(2,1)S(1)}, u32[]{:S(2)}, u32[]{:S(2)}) collective-permute-start(bf16[64,2048]{1,0:T(8,128)(2,1)S(1)} %ring_add.29.refs_1_), channel_id=1, source_target_pairs={{0,1},{1,0},{2,3},{3,2},{4,5},{5,4},{6,7},{7,6},{8,9},{9,8},{10,11... | collective-permute-start | bytes 786440 | tf_op jit(solution)/shard_map/ppermute | solution.py:1312
  (18 other events, 47.9 us)
Sparse Core Ops, SparseCore 0:
  11.4 129.4 all-gather.1

commit v5 on v4

--- a/solution.py
+++ b/solution.py
@@ -377,19 +377,21 @@
 VECTORS = 10
 
 
-def pack_kernel(place, weight_ref, up_ref, down_ref, output_ref, *refs):
+def pack_kernel(weight_ref, up_ref, down_ref, output_ref, *refs):
     vector_refs, shift_ref = refs[:VECTORS], refs[VECTORS]
-    first_ref, rest_ref = refs[VECTORS + 1 :]
+    first_ref, rest_ref, laid = refs[VECTORS + 1 :]
     rows, width = weight_ref.shape
     first_ref[:, :width] = weight_ref[...]
-    first_ref[:, width:] = jnp.zeros((rows, LANES), BF16)
+    laid[...] = jnp.zeros_like(laid)
+    core = lax.rem(lax.axis_index("fsdp"), 2)
     for i, ref in enumerate(vector_refs):
         values = ref[...].astype(F32).reshape(1, -1)
         empty = jnp.zeros_like(values)
         first, second = jnp.concatenate([values, empty], 1), jnp.concatenate([empty, values], 1)
-        first_ref[i : i + 1, width:] = jnp.where(place[CORE] == 0, first, second).astype(BF16)
+        laid[i : i + 1, :] = jnp.where(core == 0, first, second)
     shift = shift_ref[...].astype(F32).reshape(-1, LANES)
-    first_ref[VECTORS : VECTORS + shift.shape[0], width:] = shift.astype(BF16)
+    laid[VECTORS : VECTORS + shift.shape[0], :] = shift
+    first_ref[:, width:] = laid[...].astype(BF16)
     at = 0
     for ref in (up_ref, down_ref, output_ref):
         for g in range(ref.shape[0] // rows):
@@ -397,21 +399,22 @@
             at += ref.shape[1]
 
 
-def pack(place, weight, up, down, output, vectors, up_shift):
+def pack(weight, up, down, output, vectors, up_shift):
     in_vmem = pl.BlockSpec(memory_space=pltpu.VMEM)
     rows, width = weight.shape
     others = (up.size + down.size + output.size) // rows
     return pl.pallas_call(
         pack_kernel,
-        in_specs=[pl.BlockSpec(memory_space=pltpu.SMEM)] + [in_vmem] * (VECTORS + 5),
+        in_specs=[in_vmem] * (VECTORS + 5),
         out_specs=[in_vmem, in_vmem],
         out_shape=[
             jax.ShapeDtypeStruct((rows, width + LANES), BF16),
             jax.ShapeDtypeStruct((rows, others), BF16),
         ],
+        scratch_shapes=[pltpu.VMEM((rows, LANES), F32)],
         name="pack",
         **params_for(0, 4 * rows * (width + others)),
-    )(place, weight, up, down, output, *vectors, up_shift)
+    )(weight, up, down, output, *vectors, up_shift)
 
 
 CORE, CHIPS = 6, 7
@@ -974,7 +977,7 @@
 ):
     (
         out_ref, mine_ref, other_ref, vectors_mine_ref, vectors_other_ref,
-        delta, sums, normed_t, x_ref, delta_middle_ref, arrived,
+        delta, sums, normed_t, x_ref, delta_middle_ref, laid, arrived,
     ) = refs
     step = pl.program_id(0)
     core = place[CORE]
@@ -1023,16 +1026,16 @@
         for i, values in rows.items():
             sums[i : i + 1, :] = values
         each = up_sums.shape[1] // (2 * chips)
+        laid[...] = jnp.zeros_like(laid)
         for out, side in ((vectors_mine_ref, core), (vectors_other_ref, 1 - core)):
-            out[...] = jnp.zeros_like(out)
             for k in range(chips):
                 chip = place[CHIPS + k]
                 at = pl.ds(pl.multiple_of(chip * LANES, LANES), LANES)
-                out[k, : sums.shape[0], :] = sums[:, at].astype(BF16)
+                laid[k, : sums.shape[0], :] = sums[:, at]
                 for r in range(each // LANES):
                     at = pl.multiple_of((2 * chip + side) * each + r * LANES, LANES)
-                    row = up_sums[:, pl.ds(at, LANES)].astype(BF16)
-                    out[k, VECTORS + r : VECTORS + r + 1, :] = row
+                    laid[k, VECTORS + r : VECTORS + r + 1, :] = up_sums[:, pl.ds(at, LANES)]
+            out[...] = laid[...].astype(BF16)
 
 
 def unproject(place, x, delta_middle, table, normed, own, far, weight, middle_sums, up_sums, owners):
@@ -1067,6 +1070,7 @@
                 pltpu.VMEM((width, tokens), BF16),
                 pltpu.VMEM((tokens, width), BF16),
                 pltpu.VMEM((tokens, width), F32),
+                pltpu.VMEM(vectors, F32),
                 pltpu.SemaphoreType.DMA((2,)),
             ],
         ),
@@ -1317,7 +1321,7 @@
     )
     rows = norm1_gain.shape[0]
     hidden = up_weight.shape[1]
-    first, rest = pack(place, packed_weight, up_weight, down_weight, output_weight, vectors, up_bias)
+    first, rest = pack(packed_weight, up_weight, down_weight, output_weight, vectors, up_bias)
     own_pieces = ring_gather(first, chips)
     far_pieces = [to_twin(piece) for piece in own_pieces]
     x = regrouped(tokens.reshape(local_len, width))

time: 416 us -> 416 us (level)
    unnamed x50 -> x48, local copies, waits for them, and re-layouts: 7.99 us -> 9.73 us
  transfers between devices with their start and end apart: 57 -> 57, of which waited for: 22 -> 20; matrix products, arithmetic and copies ran while one was open for 2% -> 2% of each run, Pallas kernels for 36% -> 36%
where the time goes in v5:
time: 416 us; the launch traced here: 411 us
  Pallas kernels  220 us (53%)
  waiting for transfers between devices  99.9 us (24%)
  starting transfers between devices  56.7 us (14%)
  between operations  16.1 us (4%)
  local copies, waits for them, and re-layouts  10.9 us (3%)
  other arithmetic  7.4 us (2%)
    ppermute x31, waiting for transfers between devices, to_next(): return lax.ppermute(values, 'fsdp', ring_perm(chips, hop))  91.1 us
    pallas_call x3, Pallas kernels, attention_back(): pl.pallas_call(functools.partial(attend_back_kernel, pieces=pieces, block...  52 us
    pallas_call x1, Pallas kernels, mlp(): pl.pallas_call(functools.partial(mlp_kernel, chips=chips), grid_spec=pltp...  50.9 us
    ppermute x31, starting transfers between devices, to_next(): return lax.ppermute(values, 'fsdp', ring_perm(chips, hop))  36.5 us
    pallas_call x15, Pallas kernels, add(): pl.pallas_call(functools.partial(ring_add_kernel, columns=columns, mode=m...  29.1 us
    pallas_call x1, Pallas kernels, attention(): pl.pallas_call(functools.partial(attend_kernel, pieces=pieces, block=bloc...  28.4 us
    pallas_call x1, Pallas kernels, unproject(): pl.pallas_call(functools.partial(unproject_kernel, chips=chips), grid_spe...  18.2 us
    pallas_call x1, Pallas kernels, unmerge(): pl.pallas_call(functools.partial(unmerge_kernel, tokens=tokens), grid_spe...  14.5 us
  transfers between devices with their start and end apart: 57, of which 20 were waited for; matrix products, arithmetic and copies ran while one was open for 2% of the time, Pallas kernels for 36%

profile of v5, /device:TPU:0, one launch (start us, length us, event | category | flops | bytes accessed | tf_op | source)
XLA Modules:
  0.0 411.2 jit_solution(979729915298333761)
XLA Ops:
  7.2 2.8 pack.1
  10.1 3.1 collective-permute-start.5
  13.9 12.3 %collective-permute-done.5.refs_7_.refs_23_ = bf16[64,3200]{1,0:T(8,128)(2,1)S(1)} collective-permute-done((bf16[64,3200]{1,0:T(8,128)(2,1)}, bf16[64,3200]{1,0:T(8,128)(2,1)S(1)}, u32[]{:S(2)}, u32[]{:S(2)}) %collective-permute-start.5) | collective-permute-done | bytes 409632 | tf_op jit(solution)/shard_map/ppermute | solution.py:1112
  26.2 2.4 collective-permute-start.6
  28.6 17.4 %collective-permute-done.6.refs_6_.refs_22_ = bf16[64,3200]{1,0:T(8,128)(2,1)S(1)} collective-permute-done((bf16[64,3200]{1,0:T(8,128)(2,1)S(1)}, bf16[64,3200]{1,0:T(8,128)(2,1)S(1)}, u32[]{:S(2)}, u32[]{:S(2)}) %collective-permute-start.6) | collective-permute-done | bytes 409632 | tf_op jit(solution)/shard_map/ppermute | solution.py:1112
  46.8 2.4 collective-permute-start.7
  49.7 17.2 %collective-permute-done.7.refs_5_.refs_21_ = bf16[64,3200]{1,0:T(8,128)(2,1)} collective-permute-done((bf16[64,3200]{1,0:T(8,128)(2,1)S(1)}, bf16[64,3200]{1,0:T(8,128)(2,1)}, u32[]{:S(2)}, u32[]{:S(2)}) %collective-permute-start.7) | collective-permute-done | bytes 409632 | tf_op jit(solution)/shard_map/ppermute | solution.py:1112
  67.0 2.4 collective-permute-start.8
  70.4 2.4 collective-permute-start.14
  72.8 13.6 %collective-permute-done.8.refs_4_.refs_20_ = bf16[64,3200]{1,0:T(8,128)(2,1)} collective-permute-done((bf16[64,3200]{1,0:T(8,128)(2,1)}, bf16[64,3200]{1,0:T(8,128)(2,1)}, u32[]{:S(2)}, u32[]{:S(2)}) %collective-permute-start.8) | collective-permute-done | bytes 409632 | tf_op jit(solution)/shard_map/ppermute | solution.py:1112
  86.4 1.2 dynamic-slice_bitcast_fusion.place
  87.6 1.2 broadcast_select_fusion.1.x_ref.x_hbm
  89.6 12.6 %project.1 = (bf16[3,688,512]{2,1,0:T(8,128)(2,1)}, bf16[3,688,512]{2,1,0:T(8,128)(2,1)}, bf16[688,1024]{1,0:T(8,128)(2,1)}, bf16[1024,3072]{1,0:T(8,128)(2,1)}, f32[16,1024]{1,0:T(8,128)}, /*index=5*/f32[1,4096]{1,0:T(1,128)}) custom-call(s32[15]{0:T(128)} %dynamic-slice_bitcast_fusion.place, bf16[688,1024]{1,0:T(8,128)(2,1)} %broadcast_select_fusion.1.x_ref.x_hbm, ...), custom_call_target="tpu_custom_call" | custom-call | flops 4328521728 | bytes 21037056 | tf_op jit(solution)/shard_map/project/pallas_call | solution.py:469
  106.9 28.4 %attend.1 = (bf16[688,512]{1,0:T(8,128)(2,1)}, bf16[688,512]{1,0:T(8,128)(2,1)}, f32[688,128]{1,0:T(8,128)}, f32[688,128]{1,0:T(8,128)}) custom-call(s32[2]{0:T(128)} %fusion.1.valid, bf16[3,688,512]{2,1,0:T(8,128)(2,1)} %get-tuple-element.101.refs_0_, bf16[3,688,512]{2,1,0:T(8,128)(2,1)} %collective-permute-done.17.refs_1_), custom_call_target="tpu_custom_call" | custom-call | flops 16240345088 | bytes 5636096 | tf_op jit(solution)/shard_map/attend/pallas_call | solution.py:561
  135.2 3.6 collective-permute-start.18
  138.8 1.2 broadcast_select_fusion.cotangent_ref
  141.7 7.2 %merge.1 = (f32[688,1024]{1,0:T(8,128)}, f32[688,1024]{1,0:T(8,128)}, bf16[688,1024]{1,0:T(8,128)(2,1)}) custom-call(s32[15]{0:T(128)} %dynamic-slice_bitcast_fusion.place, bf16[688,1024]{1,0:T(8,128)(2,1)} %broadcast_select_fusion.1.x_ref.x_hbm, bf16[688,512]{1,0:T(8,128)(2,1)} %get-tuple-element.103.own_ref.refs_2_, bf16[688,512]{1,0:T(8,128)(2,1)} %copy-done.10, ...), custom_call_target="tpu_custom_call" | custom-call | flops 1442840576 | bytes 11960320 | tf_op jit(solution)/shard_map/merge/pallas_call | solution.py:719
  148.8 50.9 %mlp.1 = (f32[688,1024]{1,0:T(8,128)}, f32[688,1024]{1,0:T(8,128)}, bf16[8,64,4096]{2,1,0:T(8,128)(2,1)}, bf16[8,64,4096]{2,1,0:T(8,128)(2,1)}, bf16[8,64,4096]{...) custom-call(s32[15]{0:T(128)} %dynamic-slice_bitcast_fusion.place, ...), custom_call_target="tpu_custom_call" | custom-call | flops 34628173824 | bytes 42008576 | tf_op jit(solution)/shard_map/mlp/pallas_call | solution.py:837
  200.4 14.5 %unmerge.1 = (bf16[688,1024]{1,0:T(8,128)(2,1)}, f32[688,1024]{1,0:T(8,128)}, bf16[688,512]{1,0:T(8,128)(2,1)}, bf16[688,512]{1,0:T(8,128)(2,1)}, bf16[8,64,1024...) custom-call(s32[15]{0:T(128)} %dynamic-slice_bitcast_fusion.place, ...), custom_call_target="tpu_custom_call" | custom-call | flops 2885681152 | bytes 25329664 | tf_op jit(solution)/shard_map/unmerge/pallas_call | solution.py:946
  216.2 2.4 ring_add.15
  218.6 2.3 collective-permute-start.24
  221.4 13.7 %attend_back.3 = (bf16[3,688,512]{2,1,0:T(8,128)(2,1)}, bf16[3,688,512]{2,1,0:T(8,128)(2,1)}) custom-call(s32[2]{0:T(128)} %fusion.1.valid, bf16[3,688,512]{2,1,0:T(8,128)(2,1)} %get-tuple-element.101.refs_0_, bf16[3,688,512]{2,1,0:T(8,128)(2,1)} %collective-permute-done.17.refs_1_, bf16[688,512]{1,0:T(8,128)(2,1)} %get-tuple-element.103.own_ref.refs_2_, ...), custom_call_target="tpu_custom_call" | custom-call | flops 121802588160 | bytes 45088768 | tf_op jit(solution)/shard_map/attend_back/pallas_call | solution.py:670
  236.7 3.7 ring_add.16
  240.4 2.0 collective-permute-start.27
  244.1 24.6 %attend_back.4 = (bf16[3,688,512]{2,1,0:T(8,128)(2,1)}, bf16[3,688,512]{2,1,0:T(8,128)(2,1)}) custom-call(s32[2]{0:T(128)} %fusion.1.valid, bf16[3,688,512]{2,1,0:T(8,128)(2,1)} %get-tuple-element.101.refs_0_, bf16[3,688,512]{2,1,0:T(8,128)(2,1)} %collective-permute-done.17.refs_1_, ...), custom_call_target="tpu_custom_call", output_to_operand_aliasing={{0}: (9, {}), {1}: (10, {})} | custom-call | flops 243605176320 | bytes 90177536 | tf_op jit(solution)/shard_map/attend_back/pallas_call | solution.py:670
  268.7 4.1 ring_add.17
  272.7 2.0 collective-permute-start.29
  275.0 13.7 %attend_back.5 = (bf16[3,688,512]{2,1,0:T(8,128)(2,1)}, bf16[3,688,512]{2,1,0:T(8,128)(2,1)}) custom-call(s32[2]{0:T(128)} %fusion.1.valid, bf16[3,688,512]{2,1,0:T(8,128)(2,1)} %get-tuple-element.101.refs_0_, bf16[3,688,512]{2,1,0:T(8,128)(2,1)} %collective-permute-done.17.refs_1_, ...), custom_call_target="tpu_custom_call", output_to_operand_aliasing={{0}: (9, {}), {1}: (10, {})} | custom-call | flops 121802588160 | bytes 45088768 | tf_op jit(solution)/shard_map/attend_back/pallas_call | solution.py:670
  288.7 9.2 %collective-permute-done.29.refs_8_ = bf16[64,8192]{1,0:T(8,128)(2,1)S(1)} collective-permute-done((bf16[64,8192]{1,0:T(8,128)(2,1)}, bf16[64,8192]{1,0:T(8,128)(2,1)S(1)}, u32[]{:S(2)}, u32[]{:S(2)}) %collective-permute-start.29) | collective-permute-done | bytes 1048608 | tf_op jit(solution)/shard_map/ppermute | solution.py:1112
  297.9 2.8 collective-permute-done.30.refs_9_
  301.7 4.1 ring_add.18
  306.2 1.4 collective-permute-start.32
  308.4 2.0 collective-permute-done.31.far_ref
  310.4 18.2 %unproject.1 = (bf16[688,1024]{1,0:T(8,128)(2,1)}, bf16[8,64,3072]{2,1,0:T(8,128)(2,1)}, bf16[8,64,3072]{2,1,0:T(8,128)(2,1)}, bf16[8,64,128]{2,1,0:T(8,128)(2,1)}, bf16[8,64,128]{2,1,0:T(8,128)(2,1)}) custom-call(s32[15]{0:T(128)} %dynamic-slice_bitcast_fusion.place, bf16[688,1024]{1,0:T(8,128)(2,1)} %broadcast_select_fusion.1.x_ref.x_hbm, ...), custom_call_target="tpu_custom_call" | custom-call | flops 135266304 | bytes 394752 | tf_op jit(solution)/shard_map/unproject/pallas_call | solution.py:1050
  328.6 3.0 collective-permute-done.32.refs_3_.refs_4_
  331.6 1.3 collective-permute-done.33.refs_4_.refs_5_
  333.9 1.8 collective-permute-start.34
  336.4 3.3 ring_add.19.refs_6_.part_ref
  339.9 1.2 copy-done.1
  341.2 1.2 copy-done.4
  344.2 1.5 collective-permute-start.55
  345.6 1.3 collective-permute-start.37
  347.9 1.8 collective-permute-start.41
  350.0 2.3 collective-permute-done.37.refs_12_
  352.3 1.2 ring_add.22
  355.6 1.2 ring_add.23
  358.9 4.0 collective-permute-done.39.refs_12_
  362.9 1.2 ring_add.24
  364.1 1.4 collective-permute-start.43
  366.2 1.2 ring_add.25
  367.4 1.4 collective-permute-start.49
  369.5 4.1 collective-permute-done.43.refs_12_
  373.6 1.2 collective-permute-done.44.refs_13_
  374.8 1.2 ring_add.26
  376.0 2.0 collective-permute-start.47
  379.2 1.2 collective-permute-done.50.refs_9_
  380.4 1.2 ring_add.28
  381.6 2.0 collective-permute-start.51
  383.7 1.2 select_bitcast_fusion
  385.0 2.9 finish_rest.1
  389.0 3.2 collective-permute-start.53
  393.5 3.1 bitcast_convert_fusion
  396.6 5.7 %collective-permute-done.54.refs_3_ = bf16[64,2048]{1,0:T(8,128)(2,1)S(1)} collective-permute-done((bf16[64,2048]{1,0:T(8,128)(2,1)S(1)}, bf16[64,2048]{1,0:T(8,128)(2,1)S(1)}, u32[]{:S(2)}, u32[]{:S(2)}) %collective-permute-start.54) | collective-permute-done | bytes 262176 | tf_op jit(solution)/shard_map/ppermute | solution.py:1316
  402.3 1.6 finish_first.1
  (133 shorter events, 30.9 us)
Async XLA Ops:
  7.2 5.9 %copy-start.11 = (bf16[1,688,1024]{2,1,0:T(8,128)(2,1)S(1)}, bf16[1,688,1024]{2,1,0:T(8,128)(2,1)}, u32[]{:S(2)}) copy-start(bf16[1,688,1024]{2,1,0:T(8,128)(2,1)} %param.19) | copy-start | bytes 4227076
  7.2 133.6 %all-gather.2.cloned.1.call-start = ((), (), s32[]{:S(2)}) async-start(), calls=%async_computation | async-start | bytes 20054016 | tf_op jit(solution)/shard_map/all_gather | solution.py:1329
  10.1 16.1 %collective-permute-start.5 = (bf16[64,3200]{1,0:T(8,128)(2,1)}, bf16[64,3200]{1,0:T(8,128)(2,1)S(1)}, u32[]{:S(2)}, u32[]{:S(2)}) collective-permute-start(bf16[64,3200]{1,0:T(8,128)(2,1)} %get-tuple-element.100.refs_0_.refs_16_), channel_id=1, source_target_pairs={{0,8},{2,10},{8,16},{10,18},{16,24},{18,26},{24,28},{26,30},{28,20... | collective-permute-start | bytes 1228808 | tf_op jit(solution)/shard_map/ppermute | solution.py:1112
  13.1 59.7 %collective-permute-start = (bf16[688,1024]{1,0:T(8,128)(2,1)S(1)}, bf16[688,1024]{1,0:T(8,128)(2,1)S(1)}, u32[]{:S(2)}, u32[]{:S(2)}) collective-permute-start(bf16[688,1024]{1,0:T(8,128)(2,1)S(1)} %bitcast.15), channel_id=1, source_target_pairs={{1,2},{2,1},{5,6},{6,5},{9,10},{10,9},{13,14},{14,13},{17,18},{18,... | collective-permute-start | bytes 4227080 | tf_op jit(solution)/shard_map/ppermute | solution.py:1307
  13.9 14.7 %collective-permute-start.2 = (bf16[64,3200]{1,0:T(8,128)(2,1)}, bf16[64,3200]{1,0:T(8,128)(2,1)}, u32[]{:S(2)}, u32[]{:S(2)}) collective-permute-start(bf16[64,3200]{1,0:T(8,128)(2,1)} %get-tuple-element.100.refs_0_.refs_16_), channel_id=1, source_target_pairs={{0,4},{2,6},{8,0},{10,2},{16,8},{18,10},{24,16},{26,18},{28,24},{3... | collective-permute-start | bytes 1228808 | tf_op jit(solution)/shard_map/ppermute | solution.py:1112
  26.2 62.6 %copy-start.20 = (bf16[64,3200]{1,0:T(8,128)(2,1)}, bf16[64,3200]{1,0:T(8,128)(2,1)S(1)}, u32[]{:S(2)}) copy-start(bf16[64,3200]{1,0:T(8,128)(2,1)S(1)} %collective-permute-done.5.refs_7_.refs_23_) | copy-start | bytes 1228804
  26.2 19.8 %collective-permute-start.6 = (bf16[64,3200]{1,0:T(8,128)(2,1)S(1)}, bf16[64,3200]{1,0:T(8,128)(2,1)S(1)}, u32[]{:S(2)}, u32[]{:S(2)}) collective-permute-start(bf16[64,3200]{1,0:T(8,128)(2,1)S(1)} %collective-permute-done.5.refs_7_.refs_23_), channel_id=1, source_target_pairs={{0,8},{2,10},{8,16},{10,18},{16,24},{18,26},{24,28},{26,30},{28,20... | collective-permute-start | bytes 1228808 | tf_op jit(solution)/shard_map/ppermute | solution.py:1112
  28.6 20.6 %collective-permute-start.9 = (bf16[64,3200]{1,0:T(8,128)(2,1)}, bf16[64,3200]{1,0:T(8,128)(2,1)S(1)}, u32[]{:S(2)}, u32[]{:S(2)}) collective-permute-start(bf16[64,3200]{1,0:T(8,128)(2,1)} %get-tuple-element.100.refs_0_.refs_16_), channel_id=1, source_target_pairs={{0,2},{2,0},{4,6},{6,4},{8,10},{10,8},{12,14},{14,12},{16,18},{18,... | collective-permute-start | bytes 1228808 | tf_op jit(solution)/shard_map/ppermute | solution.py:1313
  28.6 21.1 %collective-permute-start.3 = (bf16[64,3200]{1,0:T(8,128)(2,1)}, bf16[64,3200]{1,0:T(8,128)(2,1)}, u32[]{:S(2)}, u32[]{:S(2)}) collective-permute-start(bf16[64,3200]{1,0:T(8,128)(2,1)} %collective-permute-done.2.refs_1_.refs_17_), channel_id=1, source_target_pairs={{0,4},{2,6},{8,0},{10,2},{16,8},{18,10},{24,16},{26,18},{28,24},{3... | collective-permute-start | bytes 1228808 | tf_op jit(solution)/shard_map/ppermute | solution.py:1112
  46.8 20.2 %collective-permute-start.7 = (bf16[64,3200]{1,0:T(8,128)(2,1)S(1)}, bf16[64,3200]{1,0:T(8,128)(2,1)}, u32[]{:S(2)}, u32[]{:S(2)}) collective-permute-start(bf16[64,3200]{1,0:T(8,128)(2,1)S(1)} %collective-permute-done.6.refs_6_.refs_22_), channel_id=1, source_target_pairs={{0,8},{2,10},{8,16},{10,18},{16,24},{18,26},{24,28},{26,30},{28,20... | collective-permute-start | bytes 1228808 | tf_op jit(solution)/shard_map/ppermute | solution.py:1112
  49.2 20.2 %collective-permute-start.16 = (bf16[64,3200]{1,0:T(8,128)(2,1)S(1)}, bf16[64,3200]{1,0:T(8,128)(2,1)}, u32[]{:S(2)}, u32[]{:S(2)}) collective-permute-start(bf16[64,3200]{1,0:T(8,128)(2,1)S(1)} %collective-permute-done.5.refs_7_.refs_23_), channel_id=1, source_target_pairs={{0,2},{2,0},{4,6},{6,4},{8,10},{10,8},{12,14},{14,12},{16,18},{18,... | collective-permute-start | bytes 1228808 | tf_op jit(solution)/shard_map/ppermute | solution.py:1313
  49.2 17.7 %copy-start.22 = (bf16[64,3200]{1,0:T(8,128)(2,1)}, bf16[64,3200]{1,0:T(8,128)(2,1)S(1)}, u32[]{:S(2)}) copy-start(bf16[64,3200]{1,0:T(8,128)(2,1)S(1)} %collective-permute-done.9.refs_8_.refs_24_) | copy-start | bytes 1228804
  49.2 20.2 %collective-permute-start.10 = (bf16[64,3200]{1,0:T(8,128)(2,1)}, bf16[64,3200]{1,0:T(8,128)(2,1)}, u32[]{:S(2)}, u32[]{:S(2)}) collective-permute-start(bf16[64,3200]{1,0:T(8,128)(2,1)} %collective-permute-done.2.refs_1_.refs_17_), channel_id=1, source_target_pairs={{0,2},{2,0},{4,6},{6,4},{8,10},{10,8},{12,14},{14,12},{16,18},{18,... | collective-permute-start | bytes 1228808 | tf_op jit(solution)/shard_map/ppermute | solution.py:1313
  49.7 20.6 %collective-permute-start.4 = (bf16[64,3200]{1,0:T(8,128)(2,1)}, bf16[64,3200]{1,0:T(8,128)(2,1)}, u32[]{:S(2)}, u32[]{:S(2)}) collective-permute-start(bf16[64,3200]{1,0:T(8,128)(2,1)} %collective-permute-done.3.refs_2_.refs_18_), channel_id=1, source_target_pairs={{0,4},{2,6},{8,0},{10,2},{16,8},{18,10},{24,16},{26,18},{28,24},{3... | collective-permute-start | bytes 1228808 | tf_op jit(solution)/shard_map/ppermute | solution.py:1112
  67.0 19.4 %collective-permute-start.8 = (bf16[64,3200]{1,0:T(8,128)(2,1)}, bf16[64,3200]{1,0:T(8,128)(2,1)}, u32[]{:S(2)}, u32[]{:S(2)}) collective-permute-start(bf16[64,3200]{1,0:T(8,128)(2,1)} %collective-permute-done.7.refs_5_.refs_21_), channel_id=1, source_target_pairs={{0,8},{2,10},{8,16},{10,18},{16,24},{18,26},{24,28},{26,30},{28,20... | collective-permute-start | bytes 1228808 | tf_op jit(solution)/shard_map/ppermute | solution.py:1112
  69.4 19.4 %collective-permute-start.15 = (bf16[64,3200]{1,0:T(8,128)(2,1)}, bf16[64,3200]{1,0:T(8,128)(2,1)S(1)}, u32[]{:S(2)}, u32[]{:S(2)}) collective-permute-start(bf16[64,3200]{1,0:T(8,128)(2,1)} %copy-done.21), channel_id=1, source_target_pairs={{0,2},{2,0},{4,6},{6,4},{8,10},{10,8},{12,14},{14,12},{16,18},{18,... | collective-permute-start | bytes 1228808 | tf_op jit(solution)/shard_map/ppermute | solution.py:1313
  69.4 19.4 %collective-permute-start.11 = (bf16[64,3200]{1,0:T(8,128)(2,1)}, bf16[64,3200]{1,0:T(8,128)(2,1)}, u32[]{:S(2)}, u32[]{:S(2)}) collective-permute-start(bf16[64,3200]{1,0:T(8,128)(2,1)} %collective-permute-done.3.refs_2_.refs_18_), channel_id=1, source_target_pairs={{0,2},{2,0},{4,6},{6,4},{8,10},{10,8},{12,14},{14,12},{16,18},{18,... | collective-permute-start | bytes 1228808 | tf_op jit(solution)/shard_map/ppermute | solution.py:1313
  70.4 18.5 %collective-permute-start.14 = (bf16[64,3200]{1,0:T(8,128)(2,1)}, bf16[64,3200]{1,0:T(8,128)(2,1)}, u32[]{:S(2)}, u32[]{:S(2)}) collective-permute-start(bf16[64,3200]{1,0:T(8,128)(2,1)} %collective-permute-done.7.refs_5_.refs_21_), channel_id=1, source_target_pairs={{0,2},{2,0},{4,6},{6,4},{8,10},{10,8},{12,14},{14,12},{16,18},{18,... | collective-permute-start | bytes 1228808 | tf_op jit(solution)/shard_map/ppermute | solution.py:1313
  72.8 16.1 %collective-permute-start.12 = (bf16[64,3200]{1,0:T(8,128)(2,1)}, bf16[64,3200]{1,0:T(8,128)(2,1)}, u32[]{:S(2)}, u32[]{:S(2)}) collective-permute-start(bf16[64,3200]{1,0:T(8,128)(2,1)} %collective-permute-done.4.refs_3_.refs_19_), channel_id=1, source_target_pairs={{0,2},{2,0},{4,6},{6,4},{8,10},{10,8},{12,14},{14,12},{16,18},{18,... | collective-permute-start | bytes 1228808 | tf_op jit(solution)/shard_map/ppermute | solution.py:1313
  86.4 2.5 collective-permute-start.13
  88.8 15.1 %copy-start.12 = (bf16[1,688,1024]{2,1,0:T(8,128)(2,1)S(1)}, bf16[1,688,1024]{2,1,0:T(8,128)(2,1)}, u32[]{:S(2)}) copy-start(bf16[1,688,1024]{2,1,0:T(8,128)(2,1)} %param.36) | copy-start | bytes 4227076
  102.2 4.7 %collective-permute-start.17 = (bf16[3,688,512]{2,1,0:T(8,128)(2,1)}, bf16[3,688,512]{2,1,0:T(8,128)(2,1)}, u32[]{:S(2)}, u32[]{:S(2)}) collective-permute-start(bf16[3,688,512]{2,1,0:T(8,128)(2,1)} %get-tuple-element.102), channel_id=1, source_target_pairs={{0,2},{2,0},{4,6},{6,4},{8,10},{10,8},{12,14},{14,12},{16,18},{18,... | collective-permute-start | bytes 6340616 | tf_op jit(solution)/shard_map/ppermute | solution.py:1313
  102.7 2.8 collective-permute-start.1
  103.9 34.9 %collective-permute-start.19 = (bf16[688,1024]{1,0:T(8,128)(2,1)S(1)}, bf16[688,1024]{1,0:T(8,128)(2,1)S(1)}, u32[]{:S(2)}, u32[]{:S(2)}) collective-permute-start(bf16[688,1024]{1,0:T(8,128)(2,1)S(1)} %bitcast.16), channel_id=1, source_target_pairs={{1,2},{2,1},{5,6},{6,5},{9,10},{10,9},{13,14},{14,13},{17,18},{18,... | collective-permute-start | bytes 4227080 | tf_op jit(solution)/shard_map/ppermute | solution.py:1307
  135.2 5.6 %collective-permute-start.18 = (bf16[688,512]{1,0:T(8,128)(2,1)}, bf16[688,512]{1,0:T(8,128)(2,1)S(1)}, u32[]{:S(2)}, u32[]{:S(2)}) collective-permute-start(bf16[688,512]{1,0:T(8,128)(2,1)} %get-tuple-element.104.refs_3_), channel_id=1, source_target_pairs={{0,2},{2,0},{4,6},{6,4},{8,10},{10,8},{12,14},{14,12},{16,18},{18,... | collective-permute-start | bytes 2113544 | tf_op jit(solution)/shard_map/ppermute | solution.py:1313
  199.8 16.4 %collective-permute-start.22 = (bf16[8,64,4096]{2,1,0:T(8,128)(2,1)}, bf16[8,64,4096]{2,1,0:T(8,128)(2,1)}, u32[]{:S(2)}, u32[]{:S(2)}) collective-permute-start(bf16[8,64,4096]{2,1,0:T(8,128)(2,1)} %get-tuple-element.121), channel_id=1, source_target_pairs={{0,2},{2,0},{4,6},{6,4},{8,10},{10,8},{12,14},{14,12},{16,18},{18,... | collective-permute-start | bytes 12582920 | tf_op jit(solution)/shard_map/ppermute | solution.py:1313
  200.2 16.0 %collective-permute-start.23 = (bf16[8,64,4096]{2,1,0:T(8,128)(2,1)}, bf16[8,64,4096]{2,1,0:T(8,128)(2,1)}, u32[]{:S(2)}, u32[]{:S(2)}) collective-permute-start(bf16[8,64,4096]{2,1,0:T(8,128)(2,1)} %get-tuple-element.123), channel_id=1, source_target_pairs={{0,2},{2,0},{4,6},{6,4},{8,10},{10,8},{12,14},{14,12},{16,18},{18,... | collective-permute-start | bytes 12582920 | tf_op jit(solution)/shard_map/ppermute | solution.py:1313
  214.8 6.5 %collective-permute-start.21 = (bf16[688,512]{1,0:T(8,128)(2,1)}, bf16[688,512]{1,0:T(8,128)(2,1)}, u32[]{:S(2)}, u32[]{:S(2)}) collective-permute-start(bf16[688,512]{1,0:T(8,128)(2,1)} %get-tuple-element.117), channel_id=1, source_target_pairs={{0,2},{2,0},{4,6},{6,4},{8,10},{10,8},{12,14},{14,12},{16,18},{18,... | collective-permute-start | bytes 2113544 | tf_op jit(solution)/shard_map/ppermute | solution.py:1313
  215.3 27.3 %collective-permute-start.26 = (bf16[8,64,1024]{2,1,0:T(8,128)(2,1)}, bf16[8,64,1024]{2,1,0:T(8,128)(2,1)S(1)}, u32[]{:S(2)}, u32[]{:S(2)}) collective-permute-start(bf16[8,64,1024]{2,1,0:T(8,128)(2,1)} %get-tuple-element.130), channel_id=1, source_target_pairs={{0,2},{2,0},{4,6},{6,4},{8,10},{10,8},{12,14},{14,12},{16,18},{18,... | collective-permute-start | bytes 3145736 | tf_op jit(solution)/shard_map/ppermute | solution.py:1313
  215.4 27.2 %collective-permute-start.20 = (bf16[688,1024]{1,0:T(8,128)(2,1)}, bf16[688,1024]{1,0:T(8,128)(2,1)S(1)}, u32[]{:S(2)}, u32[]{:S(2)}) collective-permute-start(bf16[688,1024]{1,0:T(8,128)(2,1)} %get-tuple-element.113), channel_id=1, source_target_pairs={{1,2},{2,1},{5,6},{6,5},{9,10},{10,9},{13,14},{14,13},{17,18},{18,... | collective-permute-start | bytes 4227080 | tf_op jit(solution)/shard_map/ppermute | solution.py:1307
  218.6 16.5 %collective-permute-start.24 = (bf16[64,4096]{1,0:T(8,128)(2,1)}, bf16[64,4096]{1,0:T(8,128)(2,1)S(1)}, u32[]{:S(2)}, u32[]{:S(2)}) collective-permute-start(bf16[64,4096]{1,0:T(8,128)(2,1)} %get-tuple-element.124.refs_8_), channel_id=1, source_target_pairs={{0,8},{2,10},{8,16},{10,18},{16,24},{18,26},{24,28},{26,30},{28,20... | collective-permute-start | bytes 1572872 | tf_op jit(solution)/shard_map/ppermute | solution.py:1112
  220.9 14.2 %collective-permute-start.25 = (bf16[64,4096]{1,0:T(8,128)(2,1)}, bf16[64,4096]{1,0:T(8,128)(2,1)S(1)}, u32[]{:S(2)}, u32[]{:S(2)}) collective-permute-start(bf16[64,4096]{1,0:T(8,128)(2,1)} %get-tuple-element.125.refs_9_), channel_id=1, source_target_pairs={{0,4},{2,6},{8,0},{10,2},{16,8},{18,10},{24,16},{26,18},{28,24},{3... | collective-permute-start | bytes 1572872 | tf_op jit(solution)/shard_map/ppermute | solution.py:1112
  240.4 28.3 %collective-permute-start.27 = (bf16[64,8192]{1,0:T(8,128)(2,1)}, bf16[64,8192]{1,0:T(8,128)(2,1)}, u32[]{:S(2)}, u32[]{:S(2)}) collective-permute-start(bf16[64,8192]{1,0:T(8,128)(2,1)} %get-tuple-element.128.refs_10_), channel_id=1, source_target_pairs={{0,8},{2,10},{8,16},{10,18},{16,24},{18,26},{24,28},{26,30},{28,20... | collective-permute-start | bytes 3145736 | tf_op jit(solution)/shard_map/ppermute | solution.py:1112
  242.4 26.2 %collective-permute-start.28 = (bf16[64,8192]{1,0:T(8,128)(2,1)}, bf16[64,8192]{1,0:T(8,128)(2,1)}, u32[]{:S(2)}, u32[]{:S(2)}) collective-permute-start(bf16[64,8192]{1,0:T(8,128)(2,1)} %get-tuple-element.129.refs_11_), channel_id=1, source_target_pairs={{0,4},{2,6},{8,0},{10,2},{16,8},{18,10},{24,16},{26,18},{28,24},{3... | collective-permute-start | bytes 3145736 | tf_op jit(solution)/shard_map/ppermute | solution.py:1112
  272.7 25.2 %collective-permute-start.29 = (bf16[64,8192]{1,0:T(8,128)(2,1)}, bf16[64,8192]{1,0:T(8,128)(2,1)S(1)}, u32[]{:S(2)}, u32[]{:S(2)}) collective-permute-start(bf16[64,8192]{1,0:T(8,128)(2,1)} %get-tuple-element.133.refs_10_), channel_id=1, source_target_pairs={{0,8},{2,10},{8,16},{10,18},{16,24},{18,26},{24,28},{26,30},{28,20... | collective-permute-start | bytes 3145736 | tf_op jit(solution)/shard_map/ppermute | solution.py:1112
  274.8 25.9 %collective-permute-start.30 = (bf16[64,8192]{1,0:T(8,128)(2,1)}, bf16[64,8192]{1,0:T(8,128)(2,1)S(1)}, u32[]{:S(2)}, u32[]{:S(2)}) collective-permute-start(bf16[64,8192]{1,0:T(8,128)(2,1)} %get-tuple-element.134.refs_11_), channel_id=1, source_target_pairs={{0,4},{2,6},{8,0},{10,2},{16,8},{18,10},{24,16},{26,18},{28,24},{3... | collective-permute-start | bytes 3145736 | tf_op jit(solution)/shard_map/ppermute | solution.py:1112
  305.8 4.6 %collective-permute-start.31 = (bf16[3,688,512]{2,1,0:T(8,128)(2,1)}, bf16[3,688,512]{2,1,0:T(8,128)(2,1)}, u32[]{:S(2)}, u32[]{:S(2)}) collective-permute-start(bf16[3,688,512]{2,1,0:T(8,128)(2,1)} %get-tuple-element.137), channel_id=1, source_target_pairs={{0,2},{2,0},{4,6},{6,4},{8,10},{10,8},{12,14},{14,12},{16,18},{18,... | collective-permute-start | bytes 6340616 | tf_op jit(solution)/shard_map/ppermute | solution.py:1313
  306.2 25.5 %collective-permute-start.32 = (bf16[64,8192]{1,0:T(8,128)(2,1)}, bf16[64,8192]{1,0:T(8,128)(2,1)S(1)}, u32[]{:S(2)}, u32[]{:S(2)}) collective-permute-start(bf16[64,8192]{1,0:T(8,128)(2,1)} %get-tuple-element.144), channel_id=1, source_target_pairs={{0,8},{2,10},{8,16},{10,18},{16,24},{18,26},{24,28},{26,30},{28,20... | collective-permute-start | bytes 3145736 | tf_op jit(solution)/shard_map/ppermute | solution.py:1112
  307.6 25.3 %collective-permute-start.33 = (bf16[64,8192]{1,0:T(8,128)(2,1)}, bf16[64,8192]{1,0:T(8,128)(2,1)S(1)}, u32[]{:S(2)}, u32[]{:S(2)}) collective-permute-start(bf16[64,8192]{1,0:T(8,128)(2,1)} %get-tuple-element.145), channel_id=1, source_target_pairs={{0,4},{2,6},{8,0},{10,2},{16,8},{18,10},{24,16},{26,18},{28,24},{3... | collective-permute-start | bytes 3145736 | tf_op jit(solution)/shard_map/ppermute | solution.py:1112
  333.9 6.1 %collective-permute-start.35 = (bf16[8,64,3072]{2,1,0:T(8,128)(2,1)}, bf16[8,64,3072]{2,1,0:T(8,128)(2,1)}, u32[]{:S(2)}, u32[]{:S(2)}) collective-permute-start(bf16[8,64,3072]{2,1,0:T(8,128)(2,1)} %get-tuple-element.148), channel_id=1, source_target_pairs={{0,2},{2,0},{4,6},{6,4},{8,10},{10,8},{12,14},{14,12},{16,18},{18,... | collective-permute-start | bytes 9437192 | tf_op jit(solution)/shard_map/ppermute | solution.py:1313
  333.9 24.0 %collective-permute-start.34 = (bf16[688,1024]{1,0:T(8,128)(2,1)}, bf16[688,1024]{1,0:T(8,128)(2,1)}, u32[]{:S(2)}, u32[]{:S(2)}) collective-permute-start(bf16[688,1024]{1,0:T(8,128)(2,1)} %get-tuple-element.146), channel_id=1, source_target_pairs={{1,2},{2,1},{5,6},{6,5},{9,10},{10,9},{13,14},{14,13},{17,18},{18,... | collective-permute-start | bytes 4227080 | tf_op jit(solution)/shard_map/ppermute | solution.py:1307
  335.6 4.3 %collective-permute-start.36 = (bf16[8,64,128]{2,1,0:T(8,128)(2,1)}, bf16[8,64,128]{2,1,0:T(8,128)(2,1)S(1)}, u32[]{:S(2)}, u32[]{:S(2)}) collective-permute-start(bf16[8,64,128]{2,1,0:T(8,128)(2,1)} %get-tuple-element.151), channel_id=1, source_target_pairs={{0,2},{2,0},{4,6},{6,4},{8,10},{10,8},{12,14},{14,12},{16,18},{18,... | collective-permute-start | bytes 393224 | tf_op jit(solution)/shard_map/ppermute | solution.py:1313
  343.4 6.3 %collective-permute-start.38 = (bf16[64,1024]{1,0:T(8,128)(2,1)S(1)}, bf16[64,1024]{1,0:T(8,128)(2,1)S(1)}, u32[]{:S(2)}, u32[]{:S(2)}) collective-permute-start(bf16[64,1024]{1,0:T(8,128)(2,1)S(1)} %get-tuple-element.153.refs_5_), channel_id=1, source_target_pairs={{0,4},{2,6},{8,0},{10,2},{16,8},{18,10},{24,16},{26,18},{28,24},{3... | collective-permute-start | bytes 393224 | tf_op jit(solution)/shard_map/ppermute | solution.py:1112
  344.2 40.8 %collective-permute-start.55 = (bf16[64,8192]{1,0:T(8,128)(2,1)}, bf16[64,8192]{1,0:T(8,128)(2,1)S(1)}, u32[]{:S(2)}, u32[]{:S(2)}) collective-permute-start(bf16[64,8192]{1,0:T(8,128)(2,1)} %ring_add.19.refs_6_.part_ref), channel_id=1, source_target_pairs={{0,1},{1,0},{2,3},{3,2},{4,5},{5,4},{6,7},{7,6},{8,9},{9,8},{10,11... | collective-permute-start | bytes 3145736 | tf_op jit(solution)/shard_map/ppermute | solution.py:1316
  345.6 6.7 %collective-permute-start.37 = (bf16[64,1152]{1,0:T(8,128)(2,1)S(1)}, bf16[64,1152]{1,0:T(8,128)(2,1)S(1)}, u32[]{:S(2)}, u32[]{:S(2)}) collective-permute-start(bf16[64,1152]{1,0:T(8,128)(2,1)S(1)} %get-tuple-element.152.refs_4_), channel_id=1, source_target_pairs={{0,8},{2,10},{8,16},{10,18},{16,24},{18,26},{24,28},{26,30},{28,20... | collective-permute-start | bytes 442376 | tf_op jit(solution)/shard_map/ppermute | solution.py:1112
  347.9 6.7 %collective-permute-start.41 = (bf16[64,1024]{1,0:T(8,128)(2,1)S(1)}, bf16[64,1024]{1,0:T(8,128)(2,1)S(1)}, u32[]{:S(2)}, u32[]{:S(2)}) collective-permute-start(bf16[64,1024]{1,0:T(8,128)(2,1)S(1)} %get-tuple-element.154.refs_14_), channel_id=1, source_target_pairs={{0,8},{2,10},{8,16},{10,18},{16,24},{18,26},{24,28},{26,30},{28,20... | collective-permute-start | bytes 393224 | tf_op jit(solution)/shard_map/ppermute | solution.py:1112
  349.7 5.9 %collective-permute-start.42 = (bf16[64,1024]{1,0:T(8,128)(2,1)S(1)}, bf16[64,1024]{1,0:T(8,128)(2,1)S(1)}, u32[]{:S(2)}, u32[]{:S(2)}) collective-permute-start(bf16[64,1024]{1,0:T(8,128)(2,1)S(1)} %get-tuple-element.155.refs_15_), channel_id=1, source_target_pairs={{0,4},{2,6},{8,0},{10,2},{16,8},{18,10},{24,16},{26,18},{28,24},{3... | collective-permute-start | bytes 393224 | tf_op jit(solution)/shard_map/ppermute | solution.py:1112
  353.5 9.3 %collective-permute-start.39 = (bf16[64,2176]{1,0:T(8,128)(2,1)S(1)}, bf16[64,2176]{1,0:T(8,128)(2,1)S(1)}, u32[]{:S(2)}, u32[]{:S(2)}) collective-permute-start(bf16[64,2176]{1,0:T(8,128)(2,1)S(1)} %get-tuple-element.156.refs_10_), channel_id=1, source_target_pairs={{0,8},{2,10},{8,16},{10,18},{16,24},{18,26},{24,28},{26,30},{28,20... | collective-permute-start | bytes 835592 | tf_op jit(solution)/shard_map/ppermute | solution.py:1112
  354.6 8.3 %collective-permute-start.40 = (bf16[64,2176]{1,0:T(8,128)(2,1)S(1)}, bf16[64,2176]{1,0:T(8,128)(2,1)S(1)}, u32[]{:S(2)}, u32[]{:S(2)}) collective-permute-start(bf16[64,2176]{1,0:T(8,128)(2,1)S(1)} %get-tuple-element.157.refs_11_), channel_id=1, source_target_pairs={{0,4},{2,6},{8,0},{10,2},{16,8},{18,10},{24,16},{26,18},{28,24},{3... | collective-permute-start | bytes 835592 | tf_op jit(solution)/shard_map/ppermute | solution.py:1112
  356.8 9.4 %collective-permute-start.45 = (bf16[64,2048]{1,0:T(8,128)(2,1)S(1)}, bf16[64,2048]{1,0:T(8,128)(2,1)S(1)}, u32[]{:S(2)}, u32[]{:S(2)}) collective-permute-start(bf16[64,2048]{1,0:T(8,128)(2,1)S(1)} %get-tuple-element.158.refs_14_), channel_id=1, source_target_pairs={{0,8},{2,10},{8,16},{10,18},{16,24},{18,26},{24,28},{26,30},{28,20... | collective-permute-start | bytes 786440 | tf_op jit(solution)/shard_map/ppermute | solution.py:1112
  357.9 8.3 %collective-permute-start.46 = (bf16[64,2048]{1,0:T(8,128)(2,1)S(1)}, bf16[64,2048]{1,0:T(8,128)(2,1)S(1)}, u32[]{:S(2)}, u32[]{:S(2)}) collective-permute-start(bf16[64,2048]{1,0:T(8,128)(2,1)S(1)} %get-tuple-element.159.refs_15_), channel_id=1, source_target_pairs={{0,4},{2,6},{8,0},{10,2},{16,8},{18,10},{24,16},{26,18},{28,24},{3... | collective-permute-start | bytes 786440 | tf_op jit(solution)/shard_map/ppermute | solution.py:1112
  364.1 9.5 %collective-permute-start.43 = (bf16[64,2176]{1,0:T(8,128)(2,1)S(1)}, bf16[64,2176]{1,0:T(8,128)(2,1)S(1)}, u32[]{:S(2)}, u32[]{:S(2)}) collective-permute-start(bf16[64,2176]{1,0:T(8,128)(2,1)S(1)} %get-tuple-element.160.refs_10_), channel_id=1, source_target_pairs={{0,8},{2,10},{8,16},{10,18},{16,24},{18,26},{24,28},{26,30},{28,20... | collective-permute-start | bytes 835592 | tf_op jit(solution)/shard_map/ppermute | solution.py:1112
  365.5 9.3 %collective-permute-start.44 = (bf16[64,2176]{1,0:T(8,128)(2,1)S(1)}, bf16[64,2176]{1,0:T(8,128)(2,1)S(1)}, u32[]{:S(2)}, u32[]{:S(2)}) collective-permute-start(bf16[64,2176]{1,0:T(8,128)(2,1)S(1)} %get-tuple-element.161.refs_11_), channel_id=1, source_target_pairs={{0,4},{2,6},{8,0},{10,2},{16,8},{18,10},{24,16},{26,18},{28,24},{3... | collective-permute-start | bytes 835592 | tf_op jit(solution)/shard_map/ppermute | solution.py:1112
  367.4 11.8 %collective-permute-start.49 = (bf16[64,2048]{1,0:T(8,128)(2,1)S(1)}, bf16[64,2048]{1,0:T(8,128)(2,1)S(1)}, u32[]{:S(2)}, u32[]{:S(2)}) collective-permute-start(bf16[64,2048]{1,0:T(8,128)(2,1)S(1)} %get-tuple-element.162.refs_14_), channel_id=1, source_target_pairs={{0,8},{2,10},{8,16},{10,18},{16,24},{18,26},{24,28},{26,30},{28,20... | collective-permute-start | bytes 786440 | tf_op jit(solution)/shard_map/ppermute | solution.py:1112
  368.8 11.6 %collective-permute-start.50 = (bf16[64,2048]{1,0:T(8,128)(2,1)S(1)}, bf16[64,2048]{1,0:T(8,128)(2,1)S(1)}, u32[]{:S(2)}, u32[]{:S(2)}) collective-permute-start(bf16[64,2048]{1,0:T(8,128)(2,1)S(1)} %get-tuple-element.163.refs_15_), channel_id=1, source_target_pairs={{0,4},{2,6},{8,0},{10,2},{16,8},{18,10},{24,16},{26,18},{28,24},{3... | collective-permute-start | bytes 786440 | tf_op jit(solution)/shard_map/ppermute | solution.py:1112
  376.0 11.8 %collective-permute-start.47 = (bf16[64,2176]{1,0:T(8,128)(2,1)S(1)}, bf16[64,2176]{1,0:T(8,128)(2,1)S(1)}, u32[]{:S(2)}, u32[]{:S(2)}) collective-permute-start(bf16[64,2176]{1,0:T(8,128)(2,1)S(1)} %get-tuple-element.164.refs_10_), channel_id=1, source_target_pairs={{0,8},{2,10},{8,16},{10,18},{16,24},{18,26},{24,28},{26,30},{28,20... | collective-permute-start | bytes 835592 | tf_op jit(solution)/shard_map/ppermute | solution.py:1112
  378.1 5.6 %copy-start.13 = (bf16[688,1024]{1,0:T(8,128)(2,1)S(1)}, bf16[688,1024]{1,0:T(8,128)(2,1)}, u32[]{:S(2)}) copy-start(bf16[688,1024]{1,0:T(8,128)(2,1)} %get-tuple-element.113) | copy-start | bytes 4227076
  378.1 5.6 %copy-start.15 = (bf16[688,1024]{1,0:T(8,128)(2,1)S(1)}, bf16[688,1024]{1,0:T(8,128)(2,1)}, u32[]{:S(2)}) copy-start(bf16[688,1024]{1,0:T(8,128)(2,1)} %copy-done.14) | copy-start | bytes 4227076
  378.1 9.8 %collective-permute-start.48 = (bf16[64,2176]{1,0:T(8,128)(2,1)S(1)}, bf16[64,2176]{1,0:T(8,128)(2,1)S(1)}, u32[]{:S(2)}, u32[]{:S(2)}) collective-permute-start(bf16[64,2176]{1,0:T(8,128)(2,1)S(1)} %get-tuple-element.165.refs_11_), channel_id=1, source_target_pairs={{0,4},{2,6},{8,0},{10,2},{16,8},{18,10},{24,16},{26,18},{28,24},{3... | collective-permute-start | bytes 835592 | tf_op jit(solution)/shard_map/ppermute | solution.py:1112
  381.6 10.5 %collective-permute-start.51 = (bf16[64,2048]{1,0:T(8,128)(2,1)S(1)}, bf16[64,2048]{1,0:T(8,128)(2,1)S(1)}, u32[]{:S(2)}, u32[]{:S(2)}) collective-permute-start(bf16[64,2048]{1,0:T(8,128)(2,1)S(1)} %get-tuple-element.166), channel_id=1, source_target_pairs={{0,8},{2,10},{8,16},{10,18},{16,24},{18,26},{24,28},{26,30},{28,20... | collective-permute-start | bytes 786440 | tf_op jit(solution)/shard_map/ppermute | solution.py:1112
  383.7 8.5 %collective-permute-start.52 = (bf16[64,2048]{1,0:T(8,128)(2,1)S(1)}, bf16[64,2048]{1,0:T(8,128)(2,1)S(1)}, u32[]{:S(2)}, u32[]{:S(2)}) collective-permute-start(bf16[64,2048]{1,0:T(8,128)(2,1)S(1)} %get-tuple-element.167), channel_id=1, source_target_pairs={{0,4},{2,6},{8,0},{10,2},{16,8},{18,10},{24,16},{26,18},{28,24},{3... | collective-permute-start | bytes 786440 | tf_op jit(solution)/shard_map/ppermute | solution.py:1112
  389.0 13.3 %collective-permute-start.53 = (bf16[64,2176]{1,0:T(8,128)(2,1)S(1)}, bf16[64,2176]{1,0:T(8,128)(2,1)S(1)}, u32[]{:S(2)}, u32[]{:S(2)}) collective-permute-start(bf16[64,2176]{1,0:T(8,128)(2,1)S(1)} %ring_add.27.refs_6_.refs_0_), channel_id=1, source_target_pairs={{0,1},{1,0},{2,3},{3,2},{4,5},{5,4},{6,7},{7,6},{8,9},{9,8},{10,11... | collective-permute-start | bytes 835592 | tf_op jit(solution)/shard_map/ppermute | solution.py:1316
  393.3 9.1 %copy-start.9 = (s32[15]{0:T(128)S(1)}, s32[15]{0:T(128)}, u32[]{:S(2)}) copy-start(s32[15]{0:T(128)} %dynamic-slice_bitcast_fusion.place) | copy-start | bytes 184
  393.3 9.0 %collective-permute-start.54 = (bf16[64,2048]{1,0:T(8,128)(2,1)S(1)}, bf16[64,2048]{1,0:T(8,128)(2,1)S(1)}, u32[]{:S(2)}, u32[]{:S(2)}) collective-permute-start(bf16[64,2048]{1,0:T(8,128)(2,1)S(1)} %ring_add.29.refs_1_), channel_id=1, source_target_pairs={{0,1},{1,0},{2,3},{3,2},{4,5},{5,4},{6,7},{7,6},{8,9},{9,8},{10,11... | collective-permute-start | bytes 786440 | tf_op jit(solution)/shard_map/ppermute | solution.py:1316
  (17 other events, 31.1 us)
Sparse Core Ops, SparseCore 0:
  10.2 129.0 all-gather.1

commit v6 on v5

--- a/solution.py
+++ b/solution.py
@@ -1286,7 +1286,7 @@
 
 
 def split_pairs(pairs):
-    return [pairs // 4, pairs // 2, pairs - pairs // 4 - pairs // 2] if pairs >= 4 else [pairs]
+    return [pairs // 4, pairs // 4, pairs - 2 * (pairs // 4)] if pairs >= 4 else [pairs]
 
 
 def paired_body(

time: 416 us -> 415 us (level)
    unnamed x48 -> x46, local copies, waits for them, and re-layouts: 9.73 us -> 8.79 us
  transfers between devices with their start and end apart: 57 -> 57, of which waited for: 20 -> 21; matrix products, arithmetic and copies ran while one was open for 2% -> 2% of each run, Pallas kernels for 36% -> 37%
where the time goes in v6:
time: 415 us; the launch traced here: 409 us
  Pallas kernels  220 us (53%)
  waiting for transfers between devices  99.6 us (24%)
  starting transfers between devices  56.3 us (14%)
  between operations  16.1 us (4%)
  local copies, waits for them, and re-layouts  9.99 us (2%)
  other arithmetic  7.41 us (2%)
    ppermute x31, waiting for transfers between devices, to_next(): return lax.ppermute(values, 'fsdp', ring_perm(chips, hop))  90.5 us
    pallas_call x3, Pallas kernels, attention_back(): pl.pallas_call(functools.partial(attend_back_kernel, pieces=pieces, block...  52 us
    pallas_call x1, Pallas kernels, mlp(): pl.pallas_call(functools.partial(mlp_kernel, chips=chips), grid_spec=pltp...  50.8 us
    ppermute x31, starting transfers between devices, to_next(): return lax.ppermute(values, 'fsdp', ring_perm(chips, hop))  36.6 us
    pallas_call x15, Pallas kernels, add(): pl.pallas_call(functools.partial(ring_add_kernel, columns=columns, mode=m...  29.1 us
    pallas_call x1, Pallas kernels, attention(): pl.pallas_call(functools.partial(attend_kernel, pieces=pieces, block=bloc...  28.4 us
    pallas_call x1, Pallas kernels, unproject(): pl.pallas_call(functools.partial(unproject_kernel, chips=chips), grid_spe...  18.3 us
    pallas_call x1, Pallas kernels, unmerge(): pl.pallas_call(functools.partial(unmerge_kernel, tokens=tokens), grid_spe...  14.5 us
  transfers between devices with their start and end apart: 57, of which 21 were waited for; matrix products, arithmetic and copies ran while one was open for 2% of the time, Pallas kernels for 37%

profile of v6, /device:TPU:0, one launch (start us, length us, event | category | flops | bytes accessed | tf_op | source)
XLA Modules:
  0.0 409.5 jit_solution(8458675068400487897)
XLA Ops:
  7.2 2.8 pack.1
  10.1 3.1 collective-permute-start.5
  13.9 12.3 %collective-permute-done.5.refs_7_.refs_23_ = bf16[64,3200]{1,0:T(8,128)(2,1)S(1)} collective-permute-done((bf16[64,3200]{1,0:T(8,128)(2,1)}, bf16[64,3200]{1,0:T(8,128)(2,1)S(1)}, u32[]{:S(2)}, u32[]{:S(2)}) %collective-permute-start.5) | collective-permute-done | bytes 409632 | tf_op jit(solution)/shard_map/ppermute | solution.py:1112
  26.2 2.4 collective-permute-start.6
  28.6 17.4 %collective-permute-done.6.refs_6_.refs_22_ = bf16[64,3200]{1,0:T(8,128)(2,1)S(1)} collective-permute-done((bf16[64,3200]{1,0:T(8,128)(2,1)S(1)}, bf16[64,3200]{1,0:T(8,128)(2,1)S(1)}, u32[]{:S(2)}, u32[]{:S(2)}) %collective-permute-start.6) | collective-permute-done | bytes 409632 | tf_op jit(solution)/shard_map/ppermute | solution.py:1112
  46.8 2.4 collective-permute-start.7
  49.7 17.2 %collective-permute-done.7.refs_5_.refs_21_ = bf16[64,3200]{1,0:T(8,128)(2,1)} collective-permute-done((bf16[64,3200]{1,0:T(8,128)(2,1)S(1)}, bf16[64,3200]{1,0:T(8,128)(2,1)}, u32[]{:S(2)}, u32[]{:S(2)}) %collective-permute-start.7) | collective-permute-done | bytes 409632 | tf_op jit(solution)/shard_map/ppermute | solution.py:1112
  67.0 2.4 collective-permute-start.8
  70.4 2.4 collective-permute-start.14
  72.8 13.6 %collective-permute-done.8.refs_4_.refs_20_ = bf16[64,3200]{1,0:T(8,128)(2,1)} collective-permute-done((bf16[64,3200]{1,0:T(8,128)(2,1)}, bf16[64,3200]{1,0:T(8,128)(2,1)}, u32[]{:S(2)}, u32[]{:S(2)}) %collective-permute-start.8) | collective-permute-done | bytes 409632 | tf_op jit(solution)/shard_map/ppermute | solution.py:1112
  86.4 1.2 dynamic-slice_bitcast_fusion.place
  87.6 1.2 broadcast_select_fusion.1.x_ref.x_hbm
  89.6 12.5 %project.1 = (bf16[3,688,512]{2,1,0:T(8,128)(2,1)}, bf16[3,688,512]{2,1,0:T(8,128)(2,1)}, bf16[688,1024]{1,0:T(8,128)(2,1)}, bf16[1024,3072]{1,0:T(8,128)(2,1)}, f32[16,1024]{1,0:T(8,128)}, /*index=5*/f32[1,4096]{1,0:T(1,128)}) custom-call(s32[15]{0:T(128)} %dynamic-slice_bitcast_fusion.place, bf16[688,1024]{1,0:T(8,128)(2,1)} %broadcast_select_fusion.1.x_ref.x_hbm, ...), custom_call_target="tpu_custom_call" | custom-call | flops 4328521728 | bytes 21037056 | tf_op jit(solution)/shard_map/project/pallas_call | solution.py:469
  106.7 28.4 %attend.1 = (bf16[688,512]{1,0:T(8,128)(2,1)}, bf16[688,512]{1,0:T(8,128)(2,1)}, f32[688,128]{1,0:T(8,128)}, f32[688,128]{1,0:T(8,128)}) custom-call(s32[2]{0:T(128)} %fusion.1.valid, bf16[3,688,512]{2,1,0:T(8,128)(2,1)} %get-tuple-element.101.refs_0_, bf16[3,688,512]{2,1,0:T(8,128)(2,1)} %collective-permute-done.17.refs_1_), custom_call_target="tpu_custom_call" | custom-call | flops 16240345088 | bytes 5636096 | tf_op jit(solution)/shard_map/attend/pallas_call | solution.py:561
  135.1 3.6 collective-permute-start.18
  138.8 1.2 broadcast_select_fusion.cotangent_ref
  141.6 7.2 %merge.1 = (f32[688,1024]{1,0:T(8,128)}, f32[688,1024]{1,0:T(8,128)}, bf16[688,1024]{1,0:T(8,128)(2,1)}) custom-call(s32[15]{0:T(128)} %dynamic-slice_bitcast_fusion.place, bf16[688,1024]{1,0:T(8,128)(2,1)} %broadcast_select_fusion.1.x_ref.x_hbm, bf16[688,512]{1,0:T(8,128)(2,1)} %get-tuple-element.103.own_ref.refs_2_, bf16[688,512]{1,0:T(8,128)(2,1)} %copy-done.10, ...), custom_call_target="tpu_custom_call" | custom-call | flops 1442840576 | bytes 11960320 | tf_op jit(solution)/shard_map/merge/pallas_call | solution.py:719
  148.8 50.8 %mlp.1 = (f32[688,1024]{1,0:T(8,128)}, f32[688,1024]{1,0:T(8,128)}, bf16[8,64,4096]{2,1,0:T(8,128)(2,1)}, bf16[8,64,4096]{2,1,0:T(8,128)(2,1)}, bf16[8,64,4096]{...) custom-call(s32[15]{0:T(128)} %dynamic-slice_bitcast_fusion.place, ...), custom_call_target="tpu_custom_call" | custom-call | flops 34628173824 | bytes 42008576 | tf_op jit(solution)/shard_map/mlp/pallas_call | solution.py:837
  200.2 14.5 %unmerge.1 = (bf16[688,1024]{1,0:T(8,128)(2,1)}, f32[688,1024]{1,0:T(8,128)}, bf16[688,512]{1,0:T(8,128)(2,1)}, bf16[688,512]{1,0:T(8,128)(2,1)}, bf16[8,64,1024...) custom-call(s32[15]{0:T(128)} %dynamic-slice_bitcast_fusion.place, ...), custom_call_target="tpu_custom_call" | custom-call | flops 2885681152 | bytes 25329664 | tf_op jit(solution)/shard_map/unmerge/pallas_call | solution.py:946
  216.0 2.4 ring_add.15
  218.4 2.4 collective-permute-start.24
  221.3 13.7 %attend_back.3 = (bf16[3,688,512]{2,1,0:T(8,128)(2,1)}, bf16[3,688,512]{2,1,0:T(8,128)(2,1)}) custom-call(s32[2]{0:T(128)} %fusion.1.valid, bf16[3,688,512]{2,1,0:T(8,128)(2,1)} %get-tuple-element.101.refs_0_, bf16[3,688,512]{2,1,0:T(8,128)(2,1)} %collective-permute-done.17.refs_1_, bf16[688,512]{1,0:T(8,128)(2,1)} %get-tuple-element.103.own_ref.refs_2_, ...), custom_call_target="tpu_custom_call" | custom-call | flops 121802588160 | bytes 45088768 | tf_op jit(solution)/shard_map/attend_back/pallas_call | solution.py:670
  236.6 3.7 ring_add.16
  240.3 2.0 collective-permute-start.27
  244.0 13.8 %attend_back.4 = (bf16[3,688,512]{2,1,0:T(8,128)(2,1)}, bf16[3,688,512]{2,1,0:T(8,128)(2,1)}) custom-call(s32[2]{0:T(128)} %fusion.1.valid, bf16[3,688,512]{2,1,0:T(8,128)(2,1)} %get-tuple-element.101.refs_0_, bf16[3,688,512]{2,1,0:T(8,128)(2,1)} %collective-permute-done.17.refs_1_, ...), custom_call_target="tpu_custom_call", output_to_operand_aliasing={{0}: (9, {}), {1}: (10, {})} | custom-call | flops 121802588160 | bytes 45088768 | tf_op jit(solution)/shard_map/attend_back/pallas_call | solution.py:670
  257.7 7.2 %collective-permute-done.27.refs_8_ = bf16[64,8192]{1,0:T(8,128)(2,1)S(1)} collective-permute-done((bf16[64,8192]{1,0:T(8,128)(2,1)}, bf16[64,8192]{1,0:T(8,128)(2,1)S(1)}, u32[]{:S(2)}, u32[]{:S(2)}) %collective-permute-start.27) | collective-permute-done | bytes 1048608 | tf_op jit(solution)/shard_map/ppermute | solution.py:1112
  264.9 2.9 collective-permute-done.28.refs_9_
  267.7 4.1 ring_add.17
  271.8 1.3 collective-permute-start.29
  274.1 24.6 %attend_back.5 = (bf16[3,688,512]{2,1,0:T(8,128)(2,1)}, bf16[3,688,512]{2,1,0:T(8,128)(2,1)}) custom-call(s32[2]{0:T(128)} %fusion.1.valid, bf16[3,688,512]{2,1,0:T(8,128)(2,1)} %get-tuple-element.101.refs_0_, bf16[3,688,512]{2,1,0:T(8,128)(2,1)} %collective-permute-done.17.refs_1_, ...), custom_call_target="tpu_custom_call", output_to_operand_aliasing={{0}: (9, {}), {1}: (10, {})} | custom-call | flops 243605176320 | bytes 90177536 | tf_op jit(solution)/shard_map/attend_back/pallas_call | solution.py:670
  299.6 4.1 ring_add.18
  303.7 1.7 collective-permute-start.32
  306.0 2.2 collective-permute-done.31.far_ref
  308.2 18.3 %unproject.1 = (bf16[688,1024]{1,0:T(8,128)(2,1)}, bf16[8,64,3072]{2,1,0:T(8,128)(2,1)}, bf16[8,64,3072]{2,1,0:T(8,128)(2,1)}, bf16[8,64,128]{2,1,0:T(8,128)(2,1)}, bf16[8,64,128]{2,1,0:T(8,128)(2,1)}) custom-call(s32[15]{0:T(128)} %dynamic-slice_bitcast_fusion.place, bf16[688,1024]{1,0:T(8,128)(2,1)} %broadcast_select_fusion.1.x_ref.x_hbm, ...), custom_call_target="tpu_custom_call" | custom-call | flops 135266304 | bytes 394752 | tf_op jit(solution)/shard_map/unproject/pallas_call | solution.py:1050
  326.5 2.9 collective-permute-done.32.refs_3_.refs_4_
  329.5 1.6 collective-permute-done.33.refs_4_.refs_5_
  332.0 1.8 collective-permute-start.34
  334.6 3.3 ring_add.19.refs_6_.part_ref
  338.1 1.2 copy-done.1
  339.3 1.2 copy-done.4
  342.0 1.5 collective-permute-start.55
  343.5 1.6 collective-permute-start.37
  346.1 1.6 collective-permute-start.41
  348.2 1.6 collective-permute-done.37.refs_12_
  351.1 1.8 collective-permute-start.39
  354.3 1.8 collective-permute-start.45
  356.4 4.3 %collective-permute-done.39.refs_12_ = bf16[64,2176]{1,0:T(8,128)(2,1)S(1)} collective-permute-done((bf16[64,2176]{1,0:T(8,128)(2,1)S(1)}, bf16[64,2176]{1,0:T(8,128)(2,1)S(1)}, u32[]{:S(2)}, u32[]{:S(2)}) %collective-permute-start.39) | collective-permute-done | bytes 278560 | tf_op jit(solution)/shard_map/ppermute | solution.py:1112
  360.7 1.2 ring_add.24
  361.9 1.7 collective-permute-start.43
  364.0 1.2 ring_add.25
  365.3 1.7 collective-permute-start.49
  367.3 4.1 %collective-permute-done.43.refs_12_ = bf16[64,2176]{1,0:T(8,128)(2,1)S(1)} collective-permute-done((bf16[64,2176]{1,0:T(8,128)(2,1)S(1)}, bf16[64,2176]{1,0:T(8,128)(2,1)S(1)}, u32[]{:S(2)}, u32[]{:S(2)}) %collective-permute-start.43) | collective-permute-done | bytes 278560 | tf_op jit(solution)/shard_map/ppermute | solution.py:1112
  371.4 1.8 collective-permute-done.44.refs_13_
  373.2 1.2 ring_add.26
  374.5 1.6 collective-permute-start.47
  377.1 1.8 collective-permute-done.50.refs_9_
  378.9 1.2 ring_add.28
  380.1 1.6 collective-permute-start.51
  382.2 1.2 select_bitcast_fusion
  383.4 2.9 finish_rest.1
  387.4 3.1 collective-permute-start.53
  391.7 3.1 bitcast_convert_fusion
  394.8 5.7 %collective-permute-done.54.refs_3_ = bf16[64,2048]{1,0:T(8,128)(2,1)S(1)} collective-permute-done((bf16[64,2048]{1,0:T(8,128)(2,1)S(1)}, bf16[64,2048]{1,0:T(8,128)(2,1)S(1)}, u32[]{:S(2)}, u32[]{:S(2)}) %collective-permute-start.54) | collective-permute-done | bytes 262176 | tf_op jit(solution)/shard_map/ppermute | solution.py:1316
  400.6 1.6 finish_first.1
  (131 shorter events, 29.2 us)
Async XLA Ops:
  7.2 5.9 %copy-start.11 = (bf16[1,688,1024]{2,1,0:T(8,128)(2,1)S(1)}, bf16[1,688,1024]{2,1,0:T(8,128)(2,1)}, u32[]{:S(2)}) copy-start(bf16[1,688,1024]{2,1,0:T(8,128)(2,1)} %param.19) | copy-start | bytes 4227076
  7.2 133.6 %all-gather.2.cloned.1.call-start = ((), (), s32[]{:S(2)}) async-start(), calls=%async_computation | async-start | bytes 20054016 | tf_op jit(solution)/shard_map/all_gather | solution.py:1329
  10.1 16.1 %collective-permute-start.5 = (bf16[64,3200]{1,0:T(8,128)(2,1)}, bf16[64,3200]{1,0:T(8,128)(2,1)S(1)}, u32[]{:S(2)}, u32[]{:S(2)}) collective-permute-start(bf16[64,3200]{1,0:T(8,128)(2,1)} %get-tuple-element.100.refs_0_.refs_16_), channel_id=1, source_target_pairs={{0,8},{2,10},{8,16},{10,18},{16,24},{18,26},{24,28},{26,30},{28,20... | collective-permute-start | bytes 1228808 | tf_op jit(solution)/shard_map/ppermute | solution.py:1112
  13.1 59.7 %collective-permute-start = (bf16[688,1024]{1,0:T(8,128)(2,1)S(1)}, bf16[688,1024]{1,0:T(8,128)(2,1)S(1)}, u32[]{:S(2)}, u32[]{:S(2)}) collective-permute-start(bf16[688,1024]{1,0:T(8,128)(2,1)S(1)} %bitcast.15), channel_id=1, source_target_pairs={{1,2},{2,1},{5,6},{6,5},{9,10},{10,9},{13,14},{14,13},{17,18},{18,... | collective-permute-start | bytes 4227080 | tf_op jit(solution)/shard_map/ppermute | solution.py:1307
  13.9 14.7 %collective-permute-start.2 = (bf16[64,3200]{1,0:T(8,128)(2,1)}, bf16[64,3200]{1,0:T(8,128)(2,1)}, u32[]{:S(2)}, u32[]{:S(2)}) collective-permute-start(bf16[64,3200]{1,0:T(8,128)(2,1)} %get-tuple-element.100.refs_0_.refs_16_), channel_id=1, source_target_pairs={{0,4},{2,6},{8,0},{10,2},{16,8},{18,10},{24,16},{26,18},{28,24},{3... | collective-permute-start | bytes 1228808 | tf_op jit(solution)/shard_map/ppermute | solution.py:1112
  26.2 62.6 %copy-start.19 = (bf16[64,3200]{1,0:T(8,128)(2,1)}, bf16[64,3200]{1,0:T(8,128)(2,1)S(1)}, u32[]{:S(2)}) copy-start(bf16[64,3200]{1,0:T(8,128)(2,1)S(1)} %collective-permute-done.5.refs_7_.refs_23_) | copy-start | bytes 1228804
  26.2 19.8 %collective-permute-start.6 = (bf16[64,3200]{1,0:T(8,128)(2,1)S(1)}, bf16[64,3200]{1,0:T(8,128)(2,1)S(1)}, u32[]{:S(2)}, u32[]{:S(2)}) collective-permute-start(bf16[64,3200]{1,0:T(8,128)(2,1)S(1)} %collective-permute-done.5.refs_7_.refs_23_), channel_id=1, source_target_pairs={{0,8},{2,10},{8,16},{10,18},{16,24},{18,26},{24,28},{26,30},{28,20... | collective-permute-start | bytes 1228808 | tf_op jit(solution)/shard_map/ppermute | solution.py:1112
  28.6 20.6 %collective-permute-start.9 = (bf16[64,3200]{1,0:T(8,128)(2,1)}, bf16[64,3200]{1,0:T(8,128)(2,1)S(1)}, u32[]{:S(2)}, u32[]{:S(2)}) collective-permute-start(bf16[64,3200]{1,0:T(8,128)(2,1)} %get-tuple-element.100.refs_0_.refs_16_), channel_id=1, source_target_pairs={{0,2},{2,0},{4,6},{6,4},{8,10},{10,8},{12,14},{14,12},{16,18},{18,... | collective-permute-start | bytes 1228808 | tf_op jit(solution)/shard_map/ppermute | solution.py:1313
  28.6 21.1 %collective-permute-start.3 = (bf16[64,3200]{1,0:T(8,128)(2,1)}, bf16[64,3200]{1,0:T(8,128)(2,1)}, u32[]{:S(2)}, u32[]{:S(2)}) collective-permute-start(bf16[64,3200]{1,0:T(8,128)(2,1)} %collective-permute-done.2.refs_1_.refs_17_), channel_id=1, source_target_pairs={{0,4},{2,6},{8,0},{10,2},{16,8},{18,10},{24,16},{26,18},{28,24},{3... | collective-permute-start | bytes 1228808 | tf_op jit(solution)/shard_map/ppermute | solution.py:1112
  46.8 20.2 %collective-permute-start.7 = (bf16[64,3200]{1,0:T(8,128)(2,1)S(1)}, bf16[64,3200]{1,0:T(8,128)(2,1)}, u32[]{:S(2)}, u32[]{:S(2)}) collective-permute-start(bf16[64,3200]{1,0:T(8,128)(2,1)S(1)} %collective-permute-done.6.refs_6_.refs_22_), channel_id=1, source_target_pairs={{0,8},{2,10},{8,16},{10,18},{16,24},{18,26},{24,28},{26,30},{28,20... | collective-permute-start | bytes 1228808 | tf_op jit(solution)/shard_map/ppermute | solution.py:1112
  49.2 20.2 %collective-permute-start.16 = (bf16[64,3200]{1,0:T(8,128)(2,1)S(1)}, bf16[64,3200]{1,0:T(8,128)(2,1)}, u32[]{:S(2)}, u32[]{:S(2)}) collective-permute-start(bf16[64,3200]{1,0:T(8,128)(2,1)S(1)} %collective-permute-done.5.refs_7_.refs_23_), channel_id=1, source_target_pairs={{0,2},{2,0},{4,6},{6,4},{8,10},{10,8},{12,14},{14,12},{16,18},{18,... | collective-permute-start | bytes 1228808 | tf_op jit(solution)/shard_map/ppermute | solution.py:1313
  49.2 17.7 %copy-start.21 = (bf16[64,3200]{1,0:T(8,128)(2,1)}, bf16[64,3200]{1,0:T(8,128)(2,1)S(1)}, u32[]{:S(2)}) copy-start(bf16[64,3200]{1,0:T(8,128)(2,1)S(1)} %collective-permute-done.9.refs_8_.refs_24_) | copy-start | bytes 1228804
  49.2 20.2 %collective-permute-start.10 = (bf16[64,3200]{1,0:T(8,128)(2,1)}, bf16[64,3200]{1,0:T(8,128)(2,1)}, u32[]{:S(2)}, u32[]{:S(2)}) collective-permute-start(bf16[64,3200]{1,0:T(8,128)(2,1)} %collective-permute-done.2.refs_1_.refs_17_), channel_id=1, source_target_pairs={{0,2},{2,0},{4,6},{6,4},{8,10},{10,8},{12,14},{14,12},{16,18},{18,... | collective-permute-start | bytes 1228808 | tf_op jit(solution)/shard_map/ppermute | solution.py:1313
  49.7 20.6 %collective-permute-start.4 = (bf16[64,3200]{1,0:T(8,128)(2,1)}, bf16[64,3200]{1,0:T(8,128)(2,1)}, u32[]{:S(2)}, u32[]{:S(2)}) collective-permute-start(bf16[64,3200]{1,0:T(8,128)(2,1)} %collective-permute-done.3.refs_2_.refs_18_), channel_id=1, source_target_pairs={{0,4},{2,6},{8,0},{10,2},{16,8},{18,10},{24,16},{26,18},{28,24},{3... | collective-permute-start | bytes 1228808 | tf_op jit(solution)/shard_map/ppermute | solution.py:1112
  67.0 19.4 %collective-permute-start.8 = (bf16[64,3200]{1,0:T(8,128)(2,1)}, bf16[64,3200]{1,0:T(8,128)(2,1)}, u32[]{:S(2)}, u32[]{:S(2)}) collective-permute-start(bf16[64,3200]{1,0:T(8,128)(2,1)} %collective-permute-done.7.refs_5_.refs_21_), channel_id=1, source_target_pairs={{0,8},{2,10},{8,16},{10,18},{16,24},{18,26},{24,28},{26,30},{28,20... | collective-permute-start | bytes 1228808 | tf_op jit(solution)/shard_map/ppermute | solution.py:1112
  69.4 19.4 %collective-permute-start.15 = (bf16[64,3200]{1,0:T(8,128)(2,1)}, bf16[64,3200]{1,0:T(8,128)(2,1)S(1)}, u32[]{:S(2)}, u32[]{:S(2)}) collective-permute-start(bf16[64,3200]{1,0:T(8,128)(2,1)} %copy-done.20), channel_id=1, source_target_pairs={{0,2},{2,0},{4,6},{6,4},{8,10},{10,8},{12,14},{14,12},{16,18},{18,... | collective-permute-start | bytes 1228808 | tf_op jit(solution)/shard_map/ppermute | solution.py:1313
  69.4 19.4 %collective-permute-start.11 = (bf16[64,3200]{1,0:T(8,128)(2,1)}, bf16[64,3200]{1,0:T(8,128)(2,1)}, u32[]{:S(2)}, u32[]{:S(2)}) collective-permute-start(bf16[64,3200]{1,0:T(8,128)(2,1)} %collective-permute-done.3.refs_2_.refs_18_), channel_id=1, source_target_pairs={{0,2},{2,0},{4,6},{6,4},{8,10},{10,8},{12,14},{14,12},{16,18},{18,... | collective-permute-start | bytes 1228808 | tf_op jit(solution)/shard_map/ppermute | solution.py:1313
  70.4 18.5 %collective-permute-start.14 = (bf16[64,3200]{1,0:T(8,128)(2,1)}, bf16[64,3200]{1,0:T(8,128)(2,1)}, u32[]{:S(2)}, u32[]{:S(2)}) collective-permute-start(bf16[64,3200]{1,0:T(8,128)(2,1)} %collective-permute-done.7.refs_5_.refs_21_), channel_id=1, source_target_pairs={{0,2},{2,0},{4,6},{6,4},{8,10},{10,8},{12,14},{14,12},{16,18},{18,... | collective-permute-start | bytes 1228808 | tf_op jit(solution)/shard_map/ppermute | solution.py:1313
  72.8 16.1 %collective-permute-start.12 = (bf16[64,3200]{1,0:T(8,128)(2,1)}, bf16[64,3200]{1,0:T(8,128)(2,1)}, u32[]{:S(2)}, u32[]{:S(2)}) collective-permute-start(bf16[64,3200]{1,0:T(8,128)(2,1)} %collective-permute-done.4.refs_3_.refs_19_), channel_id=1, source_target_pairs={{0,2},{2,0},{4,6},{6,4},{8,10},{10,8},{12,14},{14,12},{16,18},{18,... | collective-permute-start | bytes 1228808 | tf_op jit(solution)/shard_map/ppermute | solution.py:1313
  86.4 2.5 collective-permute-start.13
  88.8 15.0 %copy-start.12 = (bf16[1,688,1024]{2,1,0:T(8,128)(2,1)S(1)}, bf16[1,688,1024]{2,1,0:T(8,128)(2,1)}, u32[]{:S(2)}) copy-start(bf16[1,688,1024]{2,1,0:T(8,128)(2,1)} %param.36) | copy-start | bytes 4227076
  102.1 4.7 %collective-permute-start.17 = (bf16[3,688,512]{2,1,0:T(8,128)(2,1)}, bf16[3,688,512]{2,1,0:T(8,128)(2,1)}, u32[]{:S(2)}, u32[]{:S(2)}) collective-permute-start(bf16[3,688,512]{2,1,0:T(8,128)(2,1)} %get-tuple-element.102), channel_id=1, source_target_pairs={{0,2},{2,0},{4,6},{6,4},{8,10},{10,8},{12,14},{14,12},{16,18},{18,... | collective-permute-start | bytes 6340616 | tf_op jit(solution)/shard_map/ppermute | solution.py:1313
  102.6 2.8 collective-permute-start.1
  103.8 35.0 %collective-permute-start.19 = (bf16[688,1024]{1,0:T(8,128)(2,1)S(1)}, bf16[688,1024]{1,0:T(8,128)(2,1)S(1)}, u32[]{:S(2)}, u32[]{:S(2)}) collective-permute-start(bf16[688,1024]{1,0:T(8,128)(2,1)S(1)} %bitcast.16), channel_id=1, source_target_pairs={{1,2},{2,1},{5,6},{6,5},{9,10},{10,9},{13,14},{14,13},{17,18},{18,... | collective-permute-start | bytes 4227080 | tf_op jit(solution)/shard_map/ppermute | solution.py:1307
  135.1 5.7 %collective-permute-start.18 = (bf16[688,512]{1,0:T(8,128)(2,1)}, bf16[688,512]{1,0:T(8,128)(2,1)S(1)}, u32[]{:S(2)}, u32[]{:S(2)}) collective-permute-start(bf16[688,512]{1,0:T(8,128)(2,1)} %get-tuple-element.104.refs_3_), channel_id=1, source_target_pairs={{0,2},{2,0},{4,6},{6,4},{8,10},{10,8},{12,14},{14,12},{16,18},{18,... | collective-permute-start | bytes 2113544 | tf_op jit(solution)/shard_map/ppermute | solution.py:1313
  199.6 16.4 %collective-permute-start.22 = (bf16[8,64,4096]{2,1,0:T(8,128)(2,1)}, bf16[8,64,4096]{2,1,0:T(8,128)(2,1)}, u32[]{:S(2)}, u32[]{:S(2)}) collective-permute-start(bf16[8,64,4096]{2,1,0:T(8,128)(2,1)} %get-tuple-element.121), channel_id=1, source_target_pairs={{0,2},{2,0},{4,6},{6,4},{8,10},{10,8},{12,14},{14,12},{16,18},{18,... | collective-permute-start | bytes 12582920 | tf_op jit(solution)/shard_map/ppermute | solution.py:1313
  200.0 16.0 %collective-permute-start.23 = (bf16[8,64,4096]{2,1,0:T(8,128)(2,1)}, bf16[8,64,4096]{2,1,0:T(8,128)(2,1)}, u32[]{:S(2)}, u32[]{:S(2)}) collective-permute-start(bf16[8,64,4096]{2,1,0:T(8,128)(2,1)} %get-tuple-element.123), channel_id=1, source_target_pairs={{0,2},{2,0},{4,6},{6,4},{8,10},{10,8},{12,14},{14,12},{16,18},{18,... | collective-permute-start | bytes 12582920 | tf_op jit(solution)/shard_map/ppermute | solution.py:1313
  214.7 6.6 %collective-permute-start.21 = (bf16[688,512]{1,0:T(8,128)(2,1)}, bf16[688,512]{1,0:T(8,128)(2,1)}, u32[]{:S(2)}, u32[]{:S(2)}) collective-permute-start(bf16[688,512]{1,0:T(8,128)(2,1)} %get-tuple-element.117), channel_id=1, source_target_pairs={{0,2},{2,0},{4,6},{6,4},{8,10},{10,8},{12,14},{14,12},{16,18},{18,... | collective-permute-start | bytes 2113544 | tf_op jit(solution)/shard_map/ppermute | solution.py:1313
  215.1 27.4 %collective-permute-start.26 = (bf16[8,64,1024]{2,1,0:T(8,128)(2,1)}, bf16[8,64,1024]{2,1,0:T(8,128)(2,1)S(1)}, u32[]{:S(2)}, u32[]{:S(2)}) collective-permute-start(bf16[8,64,1024]{2,1,0:T(8,128)(2,1)} %get-tuple-element.130), channel_id=1, source_target_pairs={{0,2},{2,0},{4,6},{6,4},{8,10},{10,8},{12,14},{14,12},{16,18},{18,... | collective-permute-start | bytes 3145736 | tf_op jit(solution)/shard_map/ppermute | solution.py:1313
  215.3 27.3 %collective-permute-start.20 = (bf16[688,1024]{1,0:T(8,128)(2,1)}, bf16[688,1024]{1,0:T(8,128)(2,1)S(1)}, u32[]{:S(2)}, u32[]{:S(2)}) collective-permute-start(bf16[688,1024]{1,0:T(8,128)(2,1)} %get-tuple-element.113), channel_id=1, source_target_pairs={{1,2},{2,1},{5,6},{6,5},{9,10},{10,9},{13,14},{14,13},{17,18},{18,... | collective-permute-start | bytes 4227080 | tf_op jit(solution)/shard_map/ppermute | solution.py:1307
  218.4 16.6 %collective-permute-start.24 = (bf16[64,4096]{1,0:T(8,128)(2,1)}, bf16[64,4096]{1,0:T(8,128)(2,1)S(1)}, u32[]{:S(2)}, u32[]{:S(2)}) collective-permute-start(bf16[64,4096]{1,0:T(8,128)(2,1)} %get-tuple-element.124.refs_8_), channel_id=1, source_target_pairs={{0,8},{2,10},{8,16},{10,18},{16,24},{18,26},{24,28},{26,30},{28,20... | collective-permute-start | bytes 1572872 | tf_op jit(solution)/shard_map/ppermute | solution.py:1112
  220.8 14.2 %collective-permute-start.25 = (bf16[64,4096]{1,0:T(8,128)(2,1)}, bf16[64,4096]{1,0:T(8,128)(2,1)S(1)}, u32[]{:S(2)}, u32[]{:S(2)}) collective-permute-start(bf16[64,4096]{1,0:T(8,128)(2,1)} %get-tuple-element.125.refs_9_), channel_id=1, source_target_pairs={{0,4},{2,6},{8,0},{10,2},{16,8},{18,10},{24,16},{26,18},{28,24},{3... | collective-permute-start | bytes 1572872 | tf_op jit(solution)/shard_map/ppermute | solution.py:1112
  240.3 24.6 %collective-permute-start.27 = (bf16[64,8192]{1,0:T(8,128)(2,1)}, bf16[64,8192]{1,0:T(8,128)(2,1)S(1)}, u32[]{:S(2)}, u32[]{:S(2)}) collective-permute-start(bf16[64,8192]{1,0:T(8,128)(2,1)} %get-tuple-element.128.refs_10_), channel_id=1, source_target_pairs={{0,8},{2,10},{8,16},{10,18},{16,24},{18,26},{24,28},{26,30},{28,20... | collective-permute-start | bytes 3145736 | tf_op jit(solution)/shard_map/ppermute | solution.py:1112
  242.3 25.4 %collective-permute-start.28 = (bf16[64,8192]{1,0:T(8,128)(2,1)}, bf16[64,8192]{1,0:T(8,128)(2,1)}, u32[]{:S(2)}, u32[]{:S(2)}) collective-permute-start(bf16[64,8192]{1,0:T(8,128)(2,1)} %get-tuple-element.129.refs_11_), channel_id=1, source_target_pairs={{0,4},{2,6},{8,0},{10,2},{16,8},{18,10},{24,16},{26,18},{28,24},{3... | collective-permute-start | bytes 3145736 | tf_op jit(solution)/shard_map/ppermute | solution.py:1112
  271.8 26.8 %collective-permute-start.29 = (bf16[64,8192]{1,0:T(8,128)(2,1)}, bf16[64,8192]{1,0:T(8,128)(2,1)}, u32[]{:S(2)}, u32[]{:S(2)}) collective-permute-start(bf16[64,8192]{1,0:T(8,128)(2,1)} %get-tuple-element.133.refs_10_), channel_id=1, source_target_pairs={{0,8},{2,10},{8,16},{10,18},{16,24},{18,26},{24,28},{26,30},{28,20... | collective-permute-start | bytes 3145736 | tf_op jit(solution)/shard_map/ppermute | solution.py:1112
  273.1 26.4 %collective-permute-start.30 = (bf16[64,8192]{1,0:T(8,128)(2,1)}, bf16[64,8192]{1,0:T(8,128)(2,1)}, u32[]{:S(2)}, u32[]{:S(2)}) collective-permute-start(bf16[64,8192]{1,0:T(8,128)(2,1)} %get-tuple-element.134.refs_11_), channel_id=1, source_target_pairs={{0,4},{2,6},{8,0},{10,2},{16,8},{18,10},{24,16},{26,18},{28,24},{3... | collective-permute-start | bytes 3145736 | tf_op jit(solution)/shard_map/ppermute | solution.py:1112
  303.6 4.6 %collective-permute-start.31 = (bf16[3,688,512]{2,1,0:T(8,128)(2,1)}, bf16[3,688,512]{2,1,0:T(8,128)(2,1)}, u32[]{:S(2)}, u32[]{:S(2)}) collective-permute-start(bf16[3,688,512]{2,1,0:T(8,128)(2,1)} %get-tuple-element.137), channel_id=1, source_target_pairs={{0,2},{2,0},{4,6},{6,4},{8,10},{10,8},{12,14},{14,12},{16,18},{18,... | collective-permute-start | bytes 6340616 | tf_op jit(solution)/shard_map/ppermute | solution.py:1313
  303.7 25.8 %collective-permute-start.32 = (bf16[64,8192]{1,0:T(8,128)(2,1)}, bf16[64,8192]{1,0:T(8,128)(2,1)S(1)}, u32[]{:S(2)}, u32[]{:S(2)}) collective-permute-start(bf16[64,8192]{1,0:T(8,128)(2,1)} %get-tuple-element.144), channel_id=1, source_target_pairs={{0,8},{2,10},{8,16},{10,18},{16,24},{18,26},{24,28},{26,30},{28,20... | collective-permute-start | bytes 3145736 | tf_op jit(solution)/shard_map/ppermute | solution.py:1112
  305.4 25.7 %collective-permute-start.33 = (bf16[64,8192]{1,0:T(8,128)(2,1)}, bf16[64,8192]{1,0:T(8,128)(2,1)S(1)}, u32[]{:S(2)}, u32[]{:S(2)}) collective-permute-start(bf16[64,8192]{1,0:T(8,128)(2,1)} %get-tuple-element.145), channel_id=1, source_target_pairs={{0,4},{2,6},{8,0},{10,2},{16,8},{18,10},{24,16},{26,18},{28,24},{3... | collective-permute-start | bytes 3145736 | tf_op jit(solution)/shard_map/ppermute | solution.py:1112
  332.0 6.1 %collective-permute-start.35 = (bf16[8,64,3072]{2,1,0:T(8,128)(2,1)}, bf16[8,64,3072]{2,1,0:T(8,128)(2,1)}, u32[]{:S(2)}, u32[]{:S(2)}) collective-permute-start(bf16[8,64,3072]{2,1,0:T(8,128)(2,1)} %get-tuple-element.148), channel_id=1, source_target_pairs={{0,2},{2,0},{4,6},{6,4},{8,10},{10,8},{12,14},{14,12},{16,18},{18,... | collective-permute-start | bytes 9437192 | tf_op jit(solution)/shard_map/ppermute | solution.py:1313
  332.0 24.1 %collective-permute-start.34 = (bf16[688,1024]{1,0:T(8,128)(2,1)}, bf16[688,1024]{1,0:T(8,128)(2,1)}, u32[]{:S(2)}, u32[]{:S(2)}) collective-permute-start(bf16[688,1024]{1,0:T(8,128)(2,1)} %get-tuple-element.146), channel_id=1, source_target_pairs={{1,2},{2,1},{5,6},{6,5},{9,10},{10,9},{13,14},{14,13},{17,18},{18,... | collective-permute-start | bytes 4227080 | tf_op jit(solution)/shard_map/ppermute | solution.py:1307
  333.8 4.3 %collective-permute-start.36 = (bf16[8,64,128]{2,1,0:T(8,128)(2,1)}, bf16[8,64,128]{2,1,0:T(8,128)(2,1)S(1)}, u32[]{:S(2)}, u32[]{:S(2)}) collective-permute-start(bf16[8,64,128]{2,1,0:T(8,128)(2,1)} %get-tuple-element.151), channel_id=1, source_target_pairs={{0,2},{2,0},{4,6},{6,4},{8,10},{10,8},{12,14},{14,12},{16,18},{18,... | collective-permute-start | bytes 393224 | tf_op jit(solution)/shard_map/ppermute | solution.py:1313
  341.6 6.2 %collective-permute-start.38 = (bf16[64,1024]{1,0:T(8,128)(2,1)S(1)}, bf16[64,1024]{1,0:T(8,128)(2,1)S(1)}, u32[]{:S(2)}, u32[]{:S(2)}) collective-permute-start(bf16[64,1024]{1,0:T(8,128)(2,1)S(1)} %get-tuple-element.153.refs_5_), channel_id=1, source_target_pairs={{0,4},{2,6},{8,0},{10,2},{16,8},{18,10},{24,16},{26,18},{28,24},{3... | collective-permute-start | bytes 393224 | tf_op jit(solution)/shard_map/ppermute | solution.py:1112
  342.0 41.4 %collective-permute-start.55 = (bf16[64,8192]{1,0:T(8,128)(2,1)}, bf16[64,8192]{1,0:T(8,128)(2,1)S(1)}, u32[]{:S(2)}, u32[]{:S(2)}) collective-permute-start(bf16[64,8192]{1,0:T(8,128)(2,1)} %ring_add.19.refs_6_.part_ref), channel_id=1, source_target_pairs={{0,1},{1,0},{2,3},{3,2},{4,5},{5,4},{6,7},{7,6},{8,9},{9,8},{10,11... | collective-permute-start | bytes 3145736 | tf_op jit(solution)/shard_map/ppermute | solution.py:1316
  343.5 6.4 %collective-permute-start.37 = (bf16[64,1152]{1,0:T(8,128)(2,1)S(1)}, bf16[64,1152]{1,0:T(8,128)(2,1)S(1)}, u32[]{:S(2)}, u32[]{:S(2)}) collective-permute-start(bf16[64,1152]{1,0:T(8,128)(2,1)S(1)} %get-tuple-element.152.refs_4_), channel_id=1, source_target_pairs={{0,8},{2,10},{8,16},{10,18},{16,24},{18,26},{24,28},{26,30},{28,20... | collective-permute-start | bytes 442376 | tf_op jit(solution)/shard_map/ppermute | solution.py:1112
  346.1 6.7 %collective-permute-start.41 = (bf16[64,1024]{1,0:T(8,128)(2,1)S(1)}, bf16[64,1024]{1,0:T(8,128)(2,1)S(1)}, u32[]{:S(2)}, u32[]{:S(2)}) collective-permute-start(bf16[64,1024]{1,0:T(8,128)(2,1)S(1)} %get-tuple-element.154.refs_14_), channel_id=1, source_target_pairs={{0,8},{2,10},{8,16},{10,18},{16,24},{18,26},{24,28},{26,30},{28,20... | collective-permute-start | bytes 393224 | tf_op jit(solution)/shard_map/ppermute | solution.py:1112
  347.7 5.4 %collective-permute-start.42 = (bf16[64,1024]{1,0:T(8,128)(2,1)S(1)}, bf16[64,1024]{1,0:T(8,128)(2,1)S(1)}, u32[]{:S(2)}, u32[]{:S(2)}) collective-permute-start(bf16[64,1024]{1,0:T(8,128)(2,1)S(1)} %get-tuple-element.155.refs_15_), channel_id=1, source_target_pairs={{0,4},{2,6},{8,0},{10,2},{16,8},{18,10},{24,16},{26,18},{28,24},{3... | collective-permute-start | bytes 393224 | tf_op jit(solution)/shard_map/ppermute | solution.py:1112
  351.1 9.6 %collective-permute-start.39 = (bf16[64,2176]{1,0:T(8,128)(2,1)S(1)}, bf16[64,2176]{1,0:T(8,128)(2,1)S(1)}, u32[]{:S(2)}, u32[]{:S(2)}) collective-permute-start(bf16[64,2176]{1,0:T(8,128)(2,1)S(1)} %get-tuple-element.156.refs_10_), channel_id=1, source_target_pairs={{0,8},{2,10},{8,16},{10,18},{16,24},{18,26},{24,28},{26,30},{28,20... | collective-permute-start | bytes 835592 | tf_op jit(solution)/shard_map/ppermute | solution.py:1112
  352.9 7.8 %collective-permute-start.40 = (bf16[64,2176]{1,0:T(8,128)(2,1)S(1)}, bf16[64,2176]{1,0:T(8,128)(2,1)S(1)}, u32[]{:S(2)}, u32[]{:S(2)}) collective-permute-start(bf16[64,2176]{1,0:T(8,128)(2,1)S(1)} %get-tuple-element.157.refs_11_), channel_id=1, source_target_pairs={{0,4},{2,6},{8,0},{10,2},{16,8},{18,10},{24,16},{26,18},{28,24},{3... | collective-permute-start | bytes 835592 | tf_op jit(solution)/shard_map/ppermute | solution.py:1112
  354.3 9.7 %collective-permute-start.45 = (bf16[64,2048]{1,0:T(8,128)(2,1)S(1)}, bf16[64,2048]{1,0:T(8,128)(2,1)S(1)}, u32[]{:S(2)}, u32[]{:S(2)}) collective-permute-start(bf16[64,2048]{1,0:T(8,128)(2,1)S(1)} %get-tuple-element.158.refs_14_), channel_id=1, source_target_pairs={{0,8},{2,10},{8,16},{10,18},{16,24},{18,26},{24,28},{26,30},{28,20... | collective-permute-start | bytes 786440 | tf_op jit(solution)/shard_map/ppermute | solution.py:1112
  356.1 7.9 %collective-permute-start.46 = (bf16[64,2048]{1,0:T(8,128)(2,1)S(1)}, bf16[64,2048]{1,0:T(8,128)(2,1)S(1)}, u32[]{:S(2)}, u32[]{:S(2)}) collective-permute-start(bf16[64,2048]{1,0:T(8,128)(2,1)S(1)} %get-tuple-element.159.refs_15_), channel_id=1, source_target_pairs={{0,4},{2,6},{8,0},{10,2},{16,8},{18,10},{24,16},{26,18},{28,24},{3... | collective-permute-start | bytes 786440 | tf_op jit(solution)/shard_map/ppermute | solution.py:1112
  361.9 9.5 %collective-permute-start.43 = (bf16[64,2176]{1,0:T(8,128)(2,1)S(1)}, bf16[64,2176]{1,0:T(8,128)(2,1)S(1)}, u32[]{:S(2)}, u32[]{:S(2)}) collective-permute-start(bf16[64,2176]{1,0:T(8,128)(2,1)S(1)} %get-tuple-element.160.refs_10_), channel_id=1, source_target_pairs={{0,8},{2,10},{8,16},{10,18},{16,24},{18,26},{24,28},{26,30},{28,20... | collective-permute-start | bytes 835592 | tf_op jit(solution)/shard_map/ppermute | solution.py:1112
  363.6 9.6 %collective-permute-start.44 = (bf16[64,2176]{1,0:T(8,128)(2,1)S(1)}, bf16[64,2176]{1,0:T(8,128)(2,1)S(1)}, u32[]{:S(2)}, u32[]{:S(2)}) collective-permute-start(bf16[64,2176]{1,0:T(8,128)(2,1)S(1)} %get-tuple-element.161.refs_11_), channel_id=1, source_target_pairs={{0,4},{2,6},{8,0},{10,2},{16,8},{18,10},{24,16},{26,18},{28,24},{3... | collective-permute-start | bytes 835592 | tf_op jit(solution)/shard_map/ppermute | solution.py:1112
  365.3 11.8 %collective-permute-start.49 = (bf16[64,2048]{1,0:T(8,128)(2,1)S(1)}, bf16[64,2048]{1,0:T(8,128)(2,1)S(1)}, u32[]{:S(2)}, u32[]{:S(2)}) collective-permute-start(bf16[64,2048]{1,0:T(8,128)(2,1)S(1)} %get-tuple-element.162.refs_14_), channel_id=1, source_target_pairs={{0,8},{2,10},{8,16},{10,18},{16,24},{18,26},{24,28},{26,30},{28,20... | collective-permute-start | bytes 786440 | tf_op jit(solution)/shard_map/ppermute | solution.py:1112
  367.0 11.9 %collective-permute-start.50 = (bf16[64,2048]{1,0:T(8,128)(2,1)S(1)}, bf16[64,2048]{1,0:T(8,128)(2,1)S(1)}, u32[]{:S(2)}, u32[]{:S(2)}) collective-permute-start(bf16[64,2048]{1,0:T(8,128)(2,1)S(1)} %get-tuple-element.163.refs_15_), channel_id=1, source_target_pairs={{0,4},{2,6},{8,0},{10,2},{16,8},{18,10},{24,16},{26,18},{28,24},{3... | collective-permute-start | bytes 786440 | tf_op jit(solution)/shard_map/ppermute | solution.py:1112
  374.5 11.8 %collective-permute-start.47 = (bf16[64,2176]{1,0:T(8,128)(2,1)S(1)}, bf16[64,2176]{1,0:T(8,128)(2,1)S(1)}, u32[]{:S(2)}, u32[]{:S(2)}) collective-permute-start(bf16[64,2176]{1,0:T(8,128)(2,1)S(1)} %get-tuple-element.164.refs_10_), channel_id=1, source_target_pairs={{0,8},{2,10},{8,16},{10,18},{16,24},{18,26},{24,28},{26,30},{28,20... | collective-permute-start | bytes 835592 | tf_op jit(solution)/shard_map/ppermute | solution.py:1112
  376.1 6.1 %copy-start.13 = (bf16[688,1024]{1,0:T(8,128)(2,1)S(1)}, bf16[688,1024]{1,0:T(8,128)(2,1)}, u32[]{:S(2)}) copy-start(bf16[688,1024]{1,0:T(8,128)(2,1)} %get-tuple-element.113) | copy-start | bytes 4227076
  376.1 6.1 %copy-start.15 = (bf16[688,1024]{1,0:T(8,128)(2,1)S(1)}, bf16[688,1024]{1,0:T(8,128)(2,1)}, u32[]{:S(2)}) copy-start(bf16[688,1024]{1,0:T(8,128)(2,1)} %copy-done.14) | copy-start | bytes 4227076
  376.1 10.2 %collective-permute-start.48 = (bf16[64,2176]{1,0:T(8,128)(2,1)S(1)}, bf16[64,2176]{1,0:T(8,128)(2,1)S(1)}, u32[]{:S(2)}, u32[]{:S(2)}) collective-permute-start(bf16[64,2176]{1,0:T(8,128)(2,1)S(1)} %get-tuple-element.165.refs_11_), channel_id=1, source_target_pairs={{0,4},{2,6},{8,0},{10,2},{16,8},{18,10},{24,16},{26,18},{28,24},{3... | collective-permute-start | bytes 835592 | tf_op jit(solution)/shard_map/ppermute | solution.py:1112
  380.1 10.5 %collective-permute-start.51 = (bf16[64,2048]{1,0:T(8,128)(2,1)S(1)}, bf16[64,2048]{1,0:T(8,128)(2,1)S(1)}, u32[]{:S(2)}, u32[]{:S(2)}) collective-permute-start(bf16[64,2048]{1,0:T(8,128)(2,1)S(1)} %get-tuple-element.166), channel_id=1, source_target_pairs={{0,8},{2,10},{8,16},{10,18},{16,24},{18,26},{24,28},{26,30},{28,20... | collective-permute-start | bytes 786440 | tf_op jit(solution)/shard_map/ppermute | solution.py:1112
  381.7 8.8 %collective-permute-start.52 = (bf16[64,2048]{1,0:T(8,128)(2,1)S(1)}, bf16[64,2048]{1,0:T(8,128)(2,1)S(1)}, u32[]{:S(2)}, u32[]{:S(2)}) collective-permute-start(bf16[64,2048]{1,0:T(8,128)(2,1)S(1)} %get-tuple-element.167), channel_id=1, source_target_pairs={{0,4},{2,6},{8,0},{10,2},{16,8},{18,10},{24,16},{26,18},{28,24},{3... | collective-permute-start | bytes 786440 | tf_op jit(solution)/shard_map/ppermute | solution.py:1112
  387.4 13.1 %collective-permute-start.53 = (bf16[64,2176]{1,0:T(8,128)(2,1)S(1)}, bf16[64,2176]{1,0:T(8,128)(2,1)S(1)}, u32[]{:S(2)}, u32[]{:S(2)}) collective-permute-start(bf16[64,2176]{1,0:T(8,128)(2,1)S(1)} %ring_add.27.refs_6_.refs_0_), channel_id=1, source_target_pairs={{0,1},{1,0},{2,3},{3,2},{4,5},{5,4},{6,7},{7,6},{8,9},{9,8},{10,11... | collective-permute-start | bytes 835592 | tf_op jit(solution)/shard_map/ppermute | solution.py:1316
  391.6 9.0 %copy-start.9 = (s32[15]{0:T(128)S(1)}, s32[15]{0:T(128)}, u32[]{:S(2)}) copy-start(s32[15]{0:T(128)} %dynamic-slice_bitcast_fusion.place) | copy-start | bytes 184
  391.6 8.9 %collective-permute-start.54 = (bf16[64,2048]{1,0:T(8,128)(2,1)S(1)}, bf16[64,2048]{1,0:T(8,128)(2,1)S(1)}, u32[]{:S(2)}, u32[]{:S(2)}) collective-permute-start(bf16[64,2048]{1,0:T(8,128)(2,1)S(1)} %ring_add.29.refs_1_), channel_id=1, source_target_pairs={{0,1},{1,0},{2,3},{3,2},{4,5},{5,4},{6,7},{7,6},{8,9},{9,8},{10,11... | collective-permute-start | bytes 786440 | tf_op jit(solution)/shard_map/ppermute | solution.py:1316
  (16 other events, 31.4 us)
Sparse Core Ops, SparseCore 0:
  10.2 129.0 all-gather.1

commit v7 on v6

--- a/solution.py
+++ b/solution.py
@@ -311,6 +311,7 @@
 NT = (((1,), (1,)), ((), ()))
 NN = (((1,), (0,)), ((), ()))
 MASKED = -1e30
+LOG2E = 1.4426950408889634
 LANES = 128
 VMEM_LIMIT = 60 * 2**20
 SMALL_VMEM = 8 * 2**20
@@ -517,7 +518,7 @@
         values[at, LANES:] = jnp.where(lane == 0, 1.0, 0.0).astype(BF16)
         for j in range(2):
             mine = lane // HD == j
-            queries[j, at, :LANES] = jnp.where(mine, in_refs[i][0].astype(F32) * scale, 0.0).astype(BF16)
+            queries[j, at, :LANES] = jnp.where(mine, in_refs[i][0].astype(F32) * (scale * LOG2E), 0.0).astype(BF16)
             queries[j, at, LANES:] = jnp.where(lane == 0, 1.0, 0.0).astype(BF16)
     if padded > count:
         rest = pl.ds(count, padded - count)
@@ -540,11 +541,11 @@
         for j in range(2):
             scores = dot(queries[j, at, :], keys[...], NT)
             largest = jnp.max(scores, axis=1, keepdims=True)
-            weights = jnp.exp(scores - largest).astype(BF16)
+            weights = jnp.exp2(scores - largest).astype(BF16)
             result = dot(weights, values[...])
             total = result[:, LANES : LANES + 1]
             results.append(result[:, :LANES] * (1.0 / total))
-            logs += jnp.where(block_lane == 2 * pair + j, largest + jnp.log(total), 0.0)
+            logs += jnp.where(block_lane == 2 * pair + j, largest + LOG2E * jnp.log(total), 0.0)
         mixed[at, :] = jnp.where(block_lane < HD, results[0], results[1])
         totals[at, :] = logs
     for i in range(pieces):
@@ -621,7 +622,7 @@
         for i in range(pieces):
             at = pl.ds(i * size, size)
             grad = jnp.where(mine, grad_refs[i][...].astype(F32), 0.0)
-            queries[j, at, :LANES] = jnp.where(mine, in_refs[i][0].astype(F32) * scale, 0.0).astype(BF16)
+            queries[j, at, :LANES] = jnp.where(mine, in_refs[i][0].astype(F32) * (scale * LOG2E), 0.0).astype(BF16)
             grads[j, at, :LANES] = grad.astype(BF16)
             log_total = jnp.sum(
                 jnp.where(lane == 2 * pair + j, total_refs[i][...], 0.0), axis=1, keepdims=True
@@ -645,7 +646,7 @@
         results = []
         for j in range(2):
             mine = pl.ds(j * HD, HD)
-            probs = jnp.exp(dot(queries[j, at, :], keys[...], NT))
+            probs = jnp.exp2(dot(queries[j, at, :], keys[...], NT))
             grad_scores = (probs * dot(grads[j, at, :], values[...], NT)).astype(BF16)
             results.append(dot(grad_scores, keys[:, :LANES]) * scale)
             dv_t[mine, :] += dot(grads_t[b, mine, :], probs.astype(BF16))

time: 415 us -> 414 us (level)
  transfers between devices with their start and end apart: 57 -> 57, of which waited for: 21 -> 21; matrix products, arithmetic and copies ran while one was open for 2% -> 2% of each run, Pallas kernels for 37% -> 36%
where the time goes in v7:
time: 414 us; the launch traced here: 408 us
  Pallas kernels  219 us (53%)
  waiting for transfers between devices  100 us (24%)
  starting transfers between devices  56 us (14%)
  between operations  16.1 us (4%)
  local copies, waits for them, and re-layouts  9.99 us (2%)
  other arithmetic  7.41 us (2%)
    ppermute x31, waiting for transfers between devices, to_next(): return lax.ppermute(values, 'fsdp', ring_perm(chips, hop))  91 us
    pallas_call x3, Pallas kernels, attention_back(): pl.pallas_call(functools.partial(attend_back_kernel, pieces=pieces, block...  51.4 us
    pallas_call x1, Pallas kernels, mlp(): pl.pallas_call(functools.partial(mlp_kernel, chips=chips), grid_spec=pltp...  50.8 us
    ppermute x31, starting transfers between devices, to_next(): return lax.ppermute(values, 'fsdp', ring_perm(chips, hop))  36.5 us
    pallas_call x15, Pallas kernels, add(): pl.pallas_call(functools.partial(ring_add_kernel, columns=columns, mode=m...  29.1 us
    pallas_call x1, Pallas kernels, attention(): pl.pallas_call(functools.partial(attend_kernel, pieces=pieces, block=bloc...  27.6 us
    pallas_call x1, Pallas kernels, unproject(): pl.pallas_call(functools.partial(unproject_kernel, chips=chips), grid_spe...  18.3 us
    pallas_call x1, Pallas kernels, unmerge(): pl.pallas_call(functools.partial(unmerge_kernel, tokens=tokens), grid_spe...  14.5 us
  transfers between devices with their start and end apart: 57, of which 21 were waited for; matrix products, arithmetic and copies ran while one was open for 2% of the time, Pallas kernels for 36%

profile of v7, /device:TPU:0, one launch (start us, length us, event | category | flops | bytes accessed | tf_op | source)
XLA Modules:
  0.0 408.5 jit_solution(10067518175204249805)
XLA Ops:
  7.2 2.8 pack.1
  10.1 3.1 collective-permute-start.5
  13.9 12.3 %collective-permute-done.5.refs_7_.refs_23_ = bf16[64,3200]{1,0:T(8,128)(2,1)S(1)} collective-permute-done((bf16[64,3200]{1,0:T(8,128)(2,1)}, bf16[64,3200]{1,0:T(8,128)(2,1)S(1)}, u32[]{:S(2)}, u32[]{:S(2)}) %collective-permute-start.5) | collective-permute-done | bytes 409632 | tf_op jit(solution)/shard_map/ppermute | solution.py:1113
  26.2 2.4 collective-permute-start.6
  28.6 17.4 %collective-permute-done.6.refs_6_.refs_22_ = bf16[64,3200]{1,0:T(8,128)(2,1)S(1)} collective-permute-done((bf16[64,3200]{1,0:T(8,128)(2,1)S(1)}, bf16[64,3200]{1,0:T(8,128)(2,1)S(1)}, u32[]{:S(2)}, u32[]{:S(2)}) %collective-permute-start.6) | collective-permute-done | bytes 409632 | tf_op jit(solution)/shard_map/ppermute | solution.py:1113
  46.8 2.4 collective-permute-start.7
  49.7 17.2 %collective-permute-done.7.refs_5_.refs_21_ = bf16[64,3200]{1,0:T(8,128)(2,1)} collective-permute-done((bf16[64,3200]{1,0:T(8,128)(2,1)S(1)}, bf16[64,3200]{1,0:T(8,128)(2,1)}, u32[]{:S(2)}, u32[]{:S(2)}) %collective-permute-start.7) | collective-permute-done | bytes 409632 | tf_op jit(solution)/shard_map/ppermute | solution.py:1113
  67.0 2.4 collective-permute-start.8
  70.4 2.4 collective-permute-start.14
  72.8 13.6 %collective-permute-done.8.refs_4_.refs_20_ = bf16[64,3200]{1,0:T(8,128)(2,1)} collective-permute-done((bf16[64,3200]{1,0:T(8,128)(2,1)}, bf16[64,3200]{1,0:T(8,128)(2,1)}, u32[]{:S(2)}, u32[]{:S(2)}) %collective-permute-start.8) | collective-permute-done | bytes 409632 | tf_op jit(solution)/shard_map/ppermute | solution.py:1113
  87.6 1.2 broadcast_select_fusion.1.x_ref.x_hbm
  89.6 12.5 %project.1 = (bf16[3,688,512]{2,1,0:T(8,128)(2,1)}, bf16[3,688,512]{2,1,0:T(8,128)(2,1)}, bf16[688,1024]{1,0:T(8,128)(2,1)}, bf16[1024,3072]{1,0:T(8,128)(2,1)}, f32[16,1024]{1,0:T(8,128)}, /*index=5*/f32[1,4096]{1,0:T(1,128)}) custom-call(s32[15]{0:T(128)} %dynamic-slice_bitcast_fusion.place, bf16[688,1024]{1,0:T(8,128)(2,1)} %broadcast_select_fusion.1.x_ref.x_hbm, ...), custom_call_target="tpu_custom_call" | custom-call | flops 4328521728 | bytes 21037056 | tf_op jit(solution)/shard_map/project/pallas_call | solution.py:470
  106.7 27.6 %attend.1 = (bf16[688,512]{1,0:T(8,128)(2,1)}, bf16[688,512]{1,0:T(8,128)(2,1)}, f32[688,128]{1,0:T(8,128)}, f32[688,128]{1,0:T(8,128)}) custom-call(s32[2]{0:T(128)} %fusion.1.valid, bf16[3,688,512]{2,1,0:T(8,128)(2,1)} %get-tuple-element.101.refs_0_, bf16[3,688,512]{2,1,0:T(8,128)(2,1)} %collective-permute-done.17.refs_1_), custom_call_target="tpu_custom_call" | custom-call | flops 16240345088 | bytes 5636096 | tf_op jit(solution)/shard_map/attend/pallas_call | solution.py:562
  134.4 3.6 collective-permute-start.18
  138.0 1.2 broadcast_select_fusion.cotangent_ref
  141.1 7.2 %merge.1 = (f32[688,1024]{1,0:T(8,128)}, f32[688,1024]{1,0:T(8,128)}, bf16[688,1024]{1,0:T(8,128)(2,1)}) custom-call(s32[15]{0:T(128)} %dynamic-slice_bitcast_fusion.place, bf16[688,1024]{1,0:T(8,128)(2,1)} %broadcast_select_fusion.1.x_ref.x_hbm, bf16[688,512]{1,0:T(8,128)(2,1)} %get-tuple-element.103.own_ref.refs_2_, bf16[688,512]{1,0:T(8,128)(2,1)} %copy-done.10, ...), custom_call_target="tpu_custom_call" | custom-call | flops 1442840576 | bytes 11960320 | tf_op jit(solution)/shard_map/merge/pallas_call | solution.py:720
  148.2 50.8 %mlp.1 = (f32[688,1024]{1,0:T(8,128)}, f32[688,1024]{1,0:T(8,128)}, bf16[8,64,4096]{2,1,0:T(8,128)(2,1)}, bf16[8,64,4096]{2,1,0:T(8,128)(2,1)}, bf16[8,64,4096]{...) custom-call(s32[15]{0:T(128)} %dynamic-slice_bitcast_fusion.place, ...), custom_call_target="tpu_custom_call" | custom-call | flops 34628173824 | bytes 42008576 | tf_op jit(solution)/shard_map/mlp/pallas_call | solution.py:838
  199.6 14.5 %unmerge.1 = (bf16[688,1024]{1,0:T(8,128)(2,1)}, f32[688,1024]{1,0:T(8,128)}, bf16[688,512]{1,0:T(8,128)(2,1)}, bf16[688,512]{1,0:T(8,128)(2,1)}, bf16[8,64,1024...) custom-call(s32[15]{0:T(128)} %dynamic-slice_bitcast_fusion.place, ...), custom_call_target="tpu_custom_call" | custom-call | flops 2885681152 | bytes 25329664 | tf_op jit(solution)/shard_map/unmerge/pallas_call | solution.py:947
  215.4 2.4 ring_add.15
  217.8 2.2 collective-permute-start.24
  220.5 13.6 %attend_back.3 = (bf16[3,688,512]{2,1,0:T(8,128)(2,1)}, bf16[3,688,512]{2,1,0:T(8,128)(2,1)}) custom-call(s32[2]{0:T(128)} %fusion.1.valid, bf16[3,688,512]{2,1,0:T(8,128)(2,1)} %get-tuple-element.101.refs_0_, bf16[3,688,512]{2,1,0:T(8,128)(2,1)} %collective-permute-done.17.refs_1_, bf16[688,512]{1,0:T(8,128)(2,1)} %get-tuple-element.103.own_ref.refs_2_, ...), custom_call_target="tpu_custom_call" | custom-call | flops 121802588160 | bytes 45088768 | tf_op jit(solution)/shard_map/attend_back/pallas_call | solution.py:671
  235.7 3.7 ring_add.16
  239.4 2.0 collective-permute-start.27
  243.1 13.6 %attend_back.4 = (bf16[3,688,512]{2,1,0:T(8,128)(2,1)}, bf16[3,688,512]{2,1,0:T(8,128)(2,1)}) custom-call(s32[2]{0:T(128)} %fusion.1.valid, bf16[3,688,512]{2,1,0:T(8,128)(2,1)} %get-tuple-element.101.refs_0_, bf16[3,688,512]{2,1,0:T(8,128)(2,1)} %collective-permute-done.17.refs_1_, ...), custom_call_target="tpu_custom_call", output_to_operand_aliasing={{0}: (9, {}), {1}: (10, {})} | custom-call | flops 121802588160 | bytes 45088768 | tf_op jit(solution)/shard_map/attend_back/pallas_call | solution.py:671
  256.7 7.3 %collective-permute-done.27.refs_8_ = bf16[64,8192]{1,0:T(8,128)(2,1)S(1)} collective-permute-done((bf16[64,8192]{1,0:T(8,128)(2,1)}, bf16[64,8192]{1,0:T(8,128)(2,1)S(1)}, u32[]{:S(2)}, u32[]{:S(2)}) %collective-permute-start.27) | collective-permute-done | bytes 1048608 | tf_op jit(solution)/shard_map/ppermute | solution.py:1113
  264.0 2.9 collective-permute-done.28.refs_9_
  266.8 4.1 ring_add.17
  270.9 1.3 collective-permute-start.29
  273.2 24.2 %attend_back.5 = (bf16[3,688,512]{2,1,0:T(8,128)(2,1)}, bf16[3,688,512]{2,1,0:T(8,128)(2,1)}) custom-call(s32[2]{0:T(128)} %fusion.1.valid, bf16[3,688,512]{2,1,0:T(8,128)(2,1)} %get-tuple-element.101.refs_0_, bf16[3,688,512]{2,1,0:T(8,128)(2,1)} %collective-permute-done.17.refs_1_, ...), custom_call_target="tpu_custom_call", output_to_operand_aliasing={{0}: (9, {}), {1}: (10, {})} | custom-call | flops 243605176320 | bytes 90177536 | tf_op jit(solution)/shard_map/attend_back/pallas_call | solution.py:671
  297.4 1.3 collective-permute-done.30.refs_9_
  298.7 4.1 ring_add.18
  302.8 1.7 collective-permute-start.32
  305.1 2.2 collective-permute-done.31.far_ref
  307.3 18.3 %unproject.1 = (bf16[688,1024]{1,0:T(8,128)(2,1)}, bf16[8,64,3072]{2,1,0:T(8,128)(2,1)}, bf16[8,64,3072]{2,1,0:T(8,128)(2,1)}, bf16[8,64,128]{2,1,0:T(8,128)(2,1)}, bf16[8,64,128]{2,1,0:T(8,128)(2,1)}) custom-call(s32[15]{0:T(128)} %dynamic-slice_bitcast_fusion.place, bf16[688,1024]{1,0:T(8,128)(2,1)} %broadcast_select_fusion.1.x_ref.x_hbm, ...), custom_call_target="tpu_custom_call" | custom-call | flops 135266304 | bytes 394752 | tf_op jit(solution)/shard_map/unproject/pallas_call | solution.py:1051
  325.7 2.9 collective-permute-done.32.refs_3_.refs_4_
  328.6 1.6 collective-permute-done.33.refs_4_.refs_5_
  331.1 1.8 collective-permute-start.34
  333.6 3.3 ring_add.19.refs_6_.part_ref
  337.2 1.2 copy-done.1
  338.4 1.2 copy-done.4
  341.1 1.5 collective-permute-start.55
  342.6 1.6 collective-permute-start.37
  345.2 1.6 collective-permute-start.41
  347.3 1.7 collective-permute-done.37.refs_12_
  350.2 1.8 collective-permute-start.39
  353.5 1.8 collective-permute-start.45
  355.5 4.3 %collective-permute-done.39.refs_12_ = bf16[64,2176]{1,0:T(8,128)(2,1)S(1)} collective-permute-done((bf16[64,2176]{1,0:T(8,128)(2,1)S(1)}, bf16[64,2176]{1,0:T(8,128)(2,1)S(1)}, u32[]{:S(2)}, u32[]{:S(2)}) %collective-permute-start.39) | collective-permute-done | bytes 278560 | tf_op jit(solution)/shard_map/ppermute | solution.py:1113
  359.8 1.2 ring_add.24
  361.1 1.7 collective-permute-start.43
  363.2 1.2 ring_add.25
  364.4 1.7 collective-permute-start.49
  366.5 4.1 %collective-permute-done.43.refs_12_ = bf16[64,2176]{1,0:T(8,128)(2,1)S(1)} collective-permute-done((bf16[64,2176]{1,0:T(8,128)(2,1)S(1)}, bf16[64,2176]{1,0:T(8,128)(2,1)S(1)}, u32[]{:S(2)}, u32[]{:S(2)}) %collective-permute-start.43) | collective-permute-done | bytes 278560 | tf_op jit(solution)/shard_map/ppermute | solution.py:1113
  370.6 1.8 collective-permute-done.44.refs_13_
  372.3 1.2 ring_add.26
  373.6 1.6 collective-permute-start.47
  376.2 1.8 collective-permute-done.50.refs_9_
  378.0 1.2 ring_add.28
  379.2 1.6 collective-permute-start.51
  381.3 1.2 select_bitcast_fusion
  382.5 2.9 finish_rest.1
  386.5 2.9 collective-permute-start.53
  390.7 3.1 bitcast_convert_fusion
  393.8 5.8 %collective-permute-done.54.refs_3_ = bf16[64,2048]{1,0:T(8,128)(2,1)S(1)} collective-permute-done((bf16[64,2048]{1,0:T(8,128)(2,1)S(1)}, bf16[64,2048]{1,0:T(8,128)(2,1)S(1)}, u32[]{:S(2)}, u32[]{:S(2)}) %collective-permute-start.54) | collective-permute-done | bytes 262176 | tf_op jit(solution)/shard_map/ppermute | solution.py:1317
  399.6 1.6 finish_first.1
  (131 shorter events, 29.9 us)
Async XLA Ops:
  7.2 5.9 %copy-start.11 = (bf16[1,688,1024]{2,1,0:T(8,128)(2,1)S(1)}, bf16[1,688,1024]{2,1,0:T(8,128)(2,1)}, u32[]{:S(2)}) copy-start(bf16[1,688,1024]{2,1,0:T(8,128)(2,1)} %param.19) | copy-start | bytes 4227076
  7.2 133.0 %all-gather.2.cloned.1.call-start = ((), (), s32[]{:S(2)}) async-start(), calls=%async_computation | async-start | bytes 20054016 | tf_op jit(solution)/shard_map/all_gather | solution.py:1330
  10.1 16.1 %collective-permute-start.5 = (bf16[64,3200]{1,0:T(8,128)(2,1)}, bf16[64,3200]{1,0:T(8,128)(2,1)S(1)}, u32[]{:S(2)}, u32[]{:S(2)}) collective-permute-start(bf16[64,3200]{1,0:T(8,128)(2,1)} %get-tuple-element.100.refs_0_.refs_16_), channel_id=1, source_target_pairs={{0,8},{2,10},{8,16},{10,18},{16,24},{18,26},{24,28},{26,30},{28,20... | collective-permute-start | bytes 1228808 | tf_op jit(solution)/shard_map/ppermute | solution.py:1113
  13.1 59.7 %collective-permute-start = (bf16[688,1024]{1,0:T(8,128)(2,1)S(1)}, bf16[688,1024]{1,0:T(8,128)(2,1)S(1)}, u32[]{:S(2)}, u32[]{:S(2)}) collective-permute-start(bf16[688,1024]{1,0:T(8,128)(2,1)S(1)} %bitcast.15), channel_id=1, source_target_pairs={{1,2},{2,1},{5,6},{6,5},{9,10},{10,9},{13,14},{14,13},{17,18},{18,... | collective-permute-start | bytes 4227080 | tf_op jit(solution)/shard_map/ppermute | solution.py:1308
  13.9 14.7 %collective-permute-start.2 = (bf16[64,3200]{1,0:T(8,128)(2,1)}, bf16[64,3200]{1,0:T(8,128)(2,1)}, u32[]{:S(2)}, u32[]{:S(2)}) collective-permute-start(bf16[64,3200]{1,0:T(8,128)(2,1)} %get-tuple-element.100.refs_0_.refs_16_), channel_id=1, source_target_pairs={{0,4},{2,6},{8,0},{10,2},{16,8},{18,10},{24,16},{26,18},{28,24},{3... | collective-permute-start | bytes 1228808 | tf_op jit(solution)/shard_map/ppermute | solution.py:1113
  26.2 62.6 %copy-start.19 = (bf16[64,3200]{1,0:T(8,128)(2,1)}, bf16[64,3200]{1,0:T(8,128)(2,1)S(1)}, u32[]{:S(2)}) copy-start(bf16[64,3200]{1,0:T(8,128)(2,1)S(1)} %collective-permute-done.5.refs_7_.refs_23_) | copy-start | bytes 1228804
  26.2 19.8 %collective-permute-start.6 = (bf16[64,3200]{1,0:T(8,128)(2,1)S(1)}, bf16[64,3200]{1,0:T(8,128)(2,1)S(1)}, u32[]{:S(2)}, u32[]{:S(2)}) collective-permute-start(bf16[64,3200]{1,0:T(8,128)(2,1)S(1)} %collective-permute-done.5.refs_7_.refs_23_), channel_id=1, source_target_pairs={{0,8},{2,10},{8,16},{10,18},{16,24},{18,26},{24,28},{26,30},{28,20... | collective-permute-start | bytes 1228808 | tf_op jit(solution)/shard_map/ppermute | solution.py:1113
  28.6 20.6 %collective-permute-start.9 = (bf16[64,3200]{1,0:T(8,128)(2,1)}, bf16[64,3200]{1,0:T(8,128)(2,1)S(1)}, u32[]{:S(2)}, u32[]{:S(2)}) collective-permute-start(bf16[64,3200]{1,0:T(8,128)(2,1)} %get-tuple-element.100.refs_0_.refs_16_), channel_id=1, source_target_pairs={{0,2},{2,0},{4,6},{6,4},{8,10},{10,8},{12,14},{14,12},{16,18},{18,... | collective-permute-start | bytes 1228808 | tf_op jit(solution)/shard_map/ppermute | solution.py:1314
  28.6 21.1 %collective-permute-start.3 = (bf16[64,3200]{1,0:T(8,128)(2,1)}, bf16[64,3200]{1,0:T(8,128)(2,1)}, u32[]{:S(2)}, u32[]{:S(2)}) collective-permute-start(bf16[64,3200]{1,0:T(8,128)(2,1)} %collective-permute-done.2.refs_1_.refs_17_), channel_id=1, source_target_pairs={{0,4},{2,6},{8,0},{10,2},{16,8},{18,10},{24,16},{26,18},{28,24},{3... | collective-permute-start | bytes 1228808 | tf_op jit(solution)/shard_map/ppermute | solution.py:1113
  46.8 20.2 %collective-permute-start.7 = (bf16[64,3200]{1,0:T(8,128)(2,1)S(1)}, bf16[64,3200]{1,0:T(8,128)(2,1)}, u32[]{:S(2)}, u32[]{:S(2)}) collective-permute-start(bf16[64,3200]{1,0:T(8,128)(2,1)S(1)} %collective-permute-done.6.refs_6_.refs_22_), channel_id=1, source_target_pairs={{0,8},{2,10},{8,16},{10,18},{16,24},{18,26},{24,28},{26,30},{28,20... | collective-permute-start | bytes 1228808 | tf_op jit(solution)/shard_map/ppermute | solution.py:1113
  49.2 20.2 %collective-permute-start.16 = (bf16[64,3200]{1,0:T(8,128)(2,1)S(1)}, bf16[64,3200]{1,0:T(8,128)(2,1)}, u32[]{:S(2)}, u32[]{:S(2)}) collective-permute-start(bf16[64,3200]{1,0:T(8,128)(2,1)S(1)} %collective-permute-done.5.refs_7_.refs_23_), channel_id=1, source_target_pairs={{0,2},{2,0},{4,6},{6,4},{8,10},{10,8},{12,14},{14,12},{16,18},{18,... | collective-permute-start | bytes 1228808 | tf_op jit(solution)/shard_map/ppermute | solution.py:1314
  49.2 17.7 %copy-start.21 = (bf16[64,3200]{1,0:T(8,128)(2,1)}, bf16[64,3200]{1,0:T(8,128)(2,1)S(1)}, u32[]{:S(2)}) copy-start(bf16[64,3200]{1,0:T(8,128)(2,1)S(1)} %collective-permute-done.9.refs_8_.refs_24_) | copy-start | bytes 1228804
  49.2 20.2 %collective-permute-start.10 = (bf16[64,3200]{1,0:T(8,128)(2,1)}, bf16[64,3200]{1,0:T(8,128)(2,1)}, u32[]{:S(2)}, u32[]{:S(2)}) collective-permute-start(bf16[64,3200]{1,0:T(8,128)(2,1)} %collective-permute-done.2.refs_1_.refs_17_), channel_id=1, source_target_pairs={{0,2},{2,0},{4,6},{6,4},{8,10},{10,8},{12,14},{14,12},{16,18},{18,... | collective-permute-start | bytes 1228808 | tf_op jit(solution)/shard_map/ppermute | solution.py:1314
  49.7 20.6 %collective-permute-start.4 = (bf16[64,3200]{1,0:T(8,128)(2,1)}, bf16[64,3200]{1,0:T(8,128)(2,1)}, u32[]{:S(2)}, u32[]{:S(2)}) collective-permute-start(bf16[64,3200]{1,0:T(8,128)(2,1)} %collective-permute-done.3.refs_2_.refs_18_), channel_id=1, source_target_pairs={{0,4},{2,6},{8,0},{10,2},{16,8},{18,10},{24,16},{26,18},{28,24},{3... | collective-permute-start | bytes 1228808 | tf_op jit(solution)/shard_map/ppermute | solution.py:1113
  67.0 19.4 %collective-permute-start.8 = (bf16[64,3200]{1,0:T(8,128)(2,1)}, bf16[64,3200]{1,0:T(8,128)(2,1)}, u32[]{:S(2)}, u32[]{:S(2)}) collective-permute-start(bf16[64,3200]{1,0:T(8,128)(2,1)} %collective-permute-done.7.refs_5_.refs_21_), channel_id=1, source_target_pairs={{0,8},{2,10},{8,16},{10,18},{16,24},{18,26},{24,28},{26,30},{28,20... | collective-permute-start | bytes 1228808 | tf_op jit(solution)/shard_map/ppermute | solution.py:1113
  69.4 19.4 %collective-permute-start.15 = (bf16[64,3200]{1,0:T(8,128)(2,1)}, bf16[64,3200]{1,0:T(8,128)(2,1)S(1)}, u32[]{:S(2)}, u32[]{:S(2)}) collective-permute-start(bf16[64,3200]{1,0:T(8,128)(2,1)} %copy-done.20), channel_id=1, source_target_pairs={{0,2},{2,0},{4,6},{6,4},{8,10},{10,8},{12,14},{14,12},{16,18},{18,... | collective-permute-start | bytes 1228808 | tf_op jit(solution)/shard_map/ppermute | solution.py:1314
  69.4 19.4 %collective-permute-start.11 = (bf16[64,3200]{1,0:T(8,128)(2,1)}, bf16[64,3200]{1,0:T(8,128)(2,1)}, u32[]{:S(2)}, u32[]{:S(2)}) collective-permute-start(bf16[64,3200]{1,0:T(8,128)(2,1)} %collective-permute-done.3.refs_2_.refs_18_), channel_id=1, source_target_pairs={{0,2},{2,0},{4,6},{6,4},{8,10},{10,8},{12,14},{14,12},{16,18},{18,... | collective-permute-start | bytes 1228808 | tf_op jit(solution)/shard_map/ppermute | solution.py:1314
  70.4 18.5 %collective-permute-start.14 = (bf16[64,3200]{1,0:T(8,128)(2,1)}, bf16[64,3200]{1,0:T(8,128)(2,1)}, u32[]{:S(2)}, u32[]{:S(2)}) collective-permute-start(bf16[64,3200]{1,0:T(8,128)(2,1)} %collective-permute-done.7.refs_5_.refs_21_), channel_id=1, source_target_pairs={{0,2},{2,0},{4,6},{6,4},{8,10},{10,8},{12,14},{14,12},{16,18},{18,... | collective-permute-start | bytes 1228808 | tf_op jit(solution)/shard_map/ppermute | solution.py:1314
  72.8 16.1 %collective-permute-start.12 = (bf16[64,3200]{1,0:T(8,128)(2,1)}, bf16[64,3200]{1,0:T(8,128)(2,1)}, u32[]{:S(2)}, u32[]{:S(2)}) collective-permute-start(bf16[64,3200]{1,0:T(8,128)(2,1)} %collective-permute-done.4.refs_3_.refs_19_), channel_id=1, source_target_pairs={{0,2},{2,0},{4,6},{6,4},{8,10},{10,8},{12,14},{14,12},{16,18},{18,... | collective-permute-start | bytes 1228808 | tf_op jit(solution)/shard_map/ppermute | solution.py:1314
  86.4 2.5 collective-permute-start.13
  88.8 15.0 %copy-start.12 = (bf16[1,688,1024]{2,1,0:T(8,128)(2,1)S(1)}, bf16[1,688,1024]{2,1,0:T(8,128)(2,1)}, u32[]{:S(2)}) copy-start(bf16[1,688,1024]{2,1,0:T(8,128)(2,1)} %param.36) | copy-start | bytes 4227076
  102.1 4.7 %collective-permute-start.17 = (bf16[3,688,512]{2,1,0:T(8,128)(2,1)}, bf16[3,688,512]{2,1,0:T(8,128)(2,1)}, u32[]{:S(2)}, u32[]{:S(2)}) collective-permute-start(bf16[3,688,512]{2,1,0:T(8,128)(2,1)} %get-tuple-element.102), channel_id=1, source_target_pairs={{0,2},{2,0},{4,6},{6,4},{8,10},{10,8},{12,14},{14,12},{16,18},{18,... | collective-permute-start | bytes 6340616 | tf_op jit(solution)/shard_map/ppermute | solution.py:1314
  102.6 2.8 collective-permute-start.1
  103.8 34.2 %collective-permute-start.19 = (bf16[688,1024]{1,0:T(8,128)(2,1)S(1)}, bf16[688,1024]{1,0:T(8,128)(2,1)S(1)}, u32[]{:S(2)}, u32[]{:S(2)}) collective-permute-start(bf16[688,1024]{1,0:T(8,128)(2,1)S(1)} %bitcast.16), channel_id=1, source_target_pairs={{1,2},{2,1},{5,6},{6,5},{9,10},{10,9},{13,14},{14,13},{17,18},{18,... | collective-permute-start | bytes 4227080 | tf_op jit(solution)/shard_map/ppermute | solution.py:1308
  134.4 5.8 %collective-permute-start.18 = (bf16[688,512]{1,0:T(8,128)(2,1)}, bf16[688,512]{1,0:T(8,128)(2,1)S(1)}, u32[]{:S(2)}, u32[]{:S(2)}) collective-permute-start(bf16[688,512]{1,0:T(8,128)(2,1)} %get-tuple-element.104.refs_3_), channel_id=1, source_target_pairs={{0,2},{2,0},{4,6},{6,4},{8,10},{10,8},{12,14},{14,12},{16,18},{18,... | collective-permute-start | bytes 2113544 | tf_op jit(solution)/shard_map/ppermute | solution.py:1314
  199.0 16.4 %collective-permute-start.22 = (bf16[8,64,4096]{2,1,0:T(8,128)(2,1)}, bf16[8,64,4096]{2,1,0:T(8,128)(2,1)}, u32[]{:S(2)}, u32[]{:S(2)}) collective-permute-start(bf16[8,64,4096]{2,1,0:T(8,128)(2,1)} %get-tuple-element.121), channel_id=1, source_target_pairs={{0,2},{2,0},{4,6},{6,4},{8,10},{10,8},{12,14},{14,12},{16,18},{18,... | collective-permute-start | bytes 12582920 | tf_op jit(solution)/shard_map/ppermute | solution.py:1314
  199.5 16.0 %collective-permute-start.23 = (bf16[8,64,4096]{2,1,0:T(8,128)(2,1)}, bf16[8,64,4096]{2,1,0:T(8,128)(2,1)}, u32[]{:S(2)}, u32[]{:S(2)}) collective-permute-start(bf16[8,64,4096]{2,1,0:T(8,128)(2,1)} %get-tuple-element.123), channel_id=1, source_target_pairs={{0,2},{2,0},{4,6},{6,4},{8,10},{10,8},{12,14},{14,12},{16,18},{18,... | collective-permute-start | bytes 12582920 | tf_op jit(solution)/shard_map/ppermute | solution.py:1314
  214.1 6.4 %collective-permute-start.21 = (bf16[688,512]{1,0:T(8,128)(2,1)}, bf16[688,512]{1,0:T(8,128)(2,1)}, u32[]{:S(2)}, u32[]{:S(2)}) collective-permute-start(bf16[688,512]{1,0:T(8,128)(2,1)} %get-tuple-element.117), channel_id=1, source_target_pairs={{0,2},{2,0},{4,6},{6,4},{8,10},{10,8},{12,14},{14,12},{16,18},{18,... | collective-permute-start | bytes 2113544 | tf_op jit(solution)/shard_map/ppermute | solution.py:1314
  214.6 27.1 %collective-permute-start.26 = (bf16[8,64,1024]{2,1,0:T(8,128)(2,1)}, bf16[8,64,1024]{2,1,0:T(8,128)(2,1)S(1)}, u32[]{:S(2)}, u32[]{:S(2)}) collective-permute-start(bf16[8,64,1024]{2,1,0:T(8,128)(2,1)} %get-tuple-element.130), channel_id=1, source_target_pairs={{0,2},{2,0},{4,6},{6,4},{8,10},{10,8},{12,14},{14,12},{16,18},{18,... | collective-permute-start | bytes 3145736 | tf_op jit(solution)/shard_map/ppermute | solution.py:1314
  214.7 26.9 %collective-permute-start.20 = (bf16[688,1024]{1,0:T(8,128)(2,1)}, bf16[688,1024]{1,0:T(8,128)(2,1)S(1)}, u32[]{:S(2)}, u32[]{:S(2)}) collective-permute-start(bf16[688,1024]{1,0:T(8,128)(2,1)} %get-tuple-element.113), channel_id=1, source_target_pairs={{1,2},{2,1},{5,6},{6,5},{9,10},{10,9},{13,14},{14,13},{17,18},{18,... | collective-permute-start | bytes 4227080 | tf_op jit(solution)/shard_map/ppermute | solution.py:1308
  217.8 16.2 %collective-permute-start.24 = (bf16[64,4096]{1,0:T(8,128)(2,1)}, bf16[64,4096]{1,0:T(8,128)(2,1)S(1)}, u32[]{:S(2)}, u32[]{:S(2)}) collective-permute-start(bf16[64,4096]{1,0:T(8,128)(2,1)} %get-tuple-element.124.refs_8_), channel_id=1, source_target_pairs={{0,8},{2,10},{8,16},{10,18},{16,24},{18,26},{24,28},{26,30},{28,20... | collective-permute-start | bytes 1572872 | tf_op jit(solution)/shard_map/ppermute | solution.py:1113
  220.1 14.1 %collective-permute-start.25 = (bf16[64,4096]{1,0:T(8,128)(2,1)}, bf16[64,4096]{1,0:T(8,128)(2,1)S(1)}, u32[]{:S(2)}, u32[]{:S(2)}) collective-permute-start(bf16[64,4096]{1,0:T(8,128)(2,1)} %get-tuple-element.125.refs_9_), channel_id=1, source_target_pairs={{0,4},{2,6},{8,0},{10,2},{16,8},{18,10},{24,16},{26,18},{28,24},{3... | collective-permute-start | bytes 1572872 | tf_op jit(solution)/shard_map/ppermute | solution.py:1113
  239.4 24.6 %collective-permute-start.27 = (bf16[64,8192]{1,0:T(8,128)(2,1)}, bf16[64,8192]{1,0:T(8,128)(2,1)S(1)}, u32[]{:S(2)}, u32[]{:S(2)}) collective-permute-start(bf16[64,8192]{1,0:T(8,128)(2,1)} %get-tuple-element.128.refs_10_), channel_id=1, source_target_pairs={{0,8},{2,10},{8,16},{10,18},{16,24},{18,26},{24,28},{26,30},{28,20... | collective-permute-start | bytes 3145736 | tf_op jit(solution)/shard_map/ppermute | solution.py:1113
  241.4 25.4 %collective-permute-start.28 = (bf16[64,8192]{1,0:T(8,128)(2,1)}, bf16[64,8192]{1,0:T(8,128)(2,1)}, u32[]{:S(2)}, u32[]{:S(2)}) collective-permute-start(bf16[64,8192]{1,0:T(8,128)(2,1)} %get-tuple-element.129.refs_11_), channel_id=1, source_target_pairs={{0,4},{2,6},{8,0},{10,2},{16,8},{18,10},{24,16},{26,18},{28,24},{3... | collective-permute-start | bytes 3145736 | tf_op jit(solution)/shard_map/ppermute | solution.py:1113
  270.9 26.5 %collective-permute-start.29 = (bf16[64,8192]{1,0:T(8,128)(2,1)}, bf16[64,8192]{1,0:T(8,128)(2,1)}, u32[]{:S(2)}, u32[]{:S(2)}) collective-permute-start(bf16[64,8192]{1,0:T(8,128)(2,1)} %get-tuple-element.133.refs_10_), channel_id=1, source_target_pairs={{0,8},{2,10},{8,16},{10,18},{16,24},{18,26},{24,28},{26,30},{28,20... | collective-permute-start | bytes 3145736 | tf_op jit(solution)/shard_map/ppermute | solution.py:1113
  272.2 26.4 %collective-permute-start.30 = (bf16[64,8192]{1,0:T(8,128)(2,1)}, bf16[64,8192]{1,0:T(8,128)(2,1)}, u32[]{:S(2)}, u32[]{:S(2)}) collective-permute-start(bf16[64,8192]{1,0:T(8,128)(2,1)} %get-tuple-element.134.refs_11_), channel_id=1, source_target_pairs={{0,4},{2,6},{8,0},{10,2},{16,8},{18,10},{24,16},{26,18},{28,24},{3... | collective-permute-start | bytes 3145736 | tf_op jit(solution)/shard_map/ppermute | solution.py:1113
  302.7 4.6 %collective-permute-start.31 = (bf16[3,688,512]{2,1,0:T(8,128)(2,1)}, bf16[3,688,512]{2,1,0:T(8,128)(2,1)}, u32[]{:S(2)}, u32[]{:S(2)}) collective-permute-start(bf16[3,688,512]{2,1,0:T(8,128)(2,1)} %get-tuple-element.137), channel_id=1, source_target_pairs={{0,2},{2,0},{4,6},{6,4},{8,10},{10,8},{12,14},{14,12},{16,18},{18,... | collective-permute-start | bytes 6340616 | tf_op jit(solution)/shard_map/ppermute | solution.py:1314
  302.8 25.8 %collective-permute-start.32 = (bf16[64,8192]{1,0:T(8,128)(2,1)}, bf16[64,8192]{1,0:T(8,128)(2,1)S(1)}, u32[]{:S(2)}, u32[]{:S(2)}) collective-permute-start(bf16[64,8192]{1,0:T(8,128)(2,1)} %get-tuple-element.144), channel_id=1, source_target_pairs={{0,8},{2,10},{8,16},{10,18},{16,24},{18,26},{24,28},{26,30},{28,20... | collective-permute-start | bytes 3145736 | tf_op jit(solution)/shard_map/ppermute | solution.py:1113
  304.5 25.7 %collective-permute-start.33 = (bf16[64,8192]{1,0:T(8,128)(2,1)}, bf16[64,8192]{1,0:T(8,128)(2,1)S(1)}, u32[]{:S(2)}, u32[]{:S(2)}) collective-permute-start(bf16[64,8192]{1,0:T(8,128)(2,1)} %get-tuple-element.145), channel_id=1, source_target_pairs={{0,4},{2,6},{8,0},{10,2},{16,8},{18,10},{24,16},{26,18},{28,24},{3... | collective-permute-start | bytes 3145736 | tf_op jit(solution)/shard_map/ppermute | solution.py:1113
  331.1 6.1 %collective-permute-start.35 = (bf16[8,64,3072]{2,1,0:T(8,128)(2,1)}, bf16[8,64,3072]{2,1,0:T(8,128)(2,1)}, u32[]{:S(2)}, u32[]{:S(2)}) collective-permute-start(bf16[8,64,3072]{2,1,0:T(8,128)(2,1)} %get-tuple-element.148), channel_id=1, source_target_pairs={{0,2},{2,0},{4,6},{6,4},{8,10},{10,8},{12,14},{14,12},{16,18},{18,... | collective-permute-start | bytes 9437192 | tf_op jit(solution)/shard_map/ppermute | solution.py:1314
  331.1 24.1 %collective-permute-start.34 = (bf16[688,1024]{1,0:T(8,128)(2,1)}, bf16[688,1024]{1,0:T(8,128)(2,1)}, u32[]{:S(2)}, u32[]{:S(2)}) collective-permute-start(bf16[688,1024]{1,0:T(8,128)(2,1)} %get-tuple-element.146), channel_id=1, source_target_pairs={{1,2},{2,1},{5,6},{6,5},{9,10},{10,9},{13,14},{14,13},{17,18},{18,... | collective-permute-start | bytes 4227080 | tf_op jit(solution)/shard_map/ppermute | solution.py:1308
  332.9 4.3 %collective-permute-start.36 = (bf16[8,64,128]{2,1,0:T(8,128)(2,1)}, bf16[8,64,128]{2,1,0:T(8,128)(2,1)S(1)}, u32[]{:S(2)}, u32[]{:S(2)}) collective-permute-start(bf16[8,64,128]{2,1,0:T(8,128)(2,1)} %get-tuple-element.151), channel_id=1, source_target_pairs={{0,2},{2,0},{4,6},{6,4},{8,10},{10,8},{12,14},{14,12},{16,18},{18,... | collective-permute-start | bytes 393224 | tf_op jit(solution)/shard_map/ppermute | solution.py:1314
  340.7 6.2 %collective-permute-start.38 = (bf16[64,1024]{1,0:T(8,128)(2,1)S(1)}, bf16[64,1024]{1,0:T(8,128)(2,1)S(1)}, u32[]{:S(2)}, u32[]{:S(2)}) collective-permute-start(bf16[64,1024]{1,0:T(8,128)(2,1)S(1)} %get-tuple-element.153.refs_5_), channel_id=1, source_target_pairs={{0,4},{2,6},{8,0},{10,2},{16,8},{18,10},{24,16},{26,18},{28,24},{3... | collective-permute-start | bytes 393224 | tf_op jit(solution)/shard_map/ppermute | solution.py:1113
  341.1 41.4 %collective-permute-start.55 = (bf16[64,8192]{1,0:T(8,128)(2,1)}, bf16[64,8192]{1,0:T(8,128)(2,1)S(1)}, u32[]{:S(2)}, u32[]{:S(2)}) collective-permute-start(bf16[64,8192]{1,0:T(8,128)(2,1)} %ring_add.19.refs_6_.part_ref), channel_id=1, source_target_pairs={{0,1},{1,0},{2,3},{3,2},{4,5},{5,4},{6,7},{7,6},{8,9},{9,8},{10,11... | collective-permute-start | bytes 3145736 | tf_op jit(solution)/shard_map/ppermute | solution.py:1317
  342.6 6.4 %collective-permute-start.37 = (bf16[64,1152]{1,0:T(8,128)(2,1)S(1)}, bf16[64,1152]{1,0:T(8,128)(2,1)S(1)}, u32[]{:S(2)}, u32[]{:S(2)}) collective-permute-start(bf16[64,1152]{1,0:T(8,128)(2,1)S(1)} %get-tuple-element.152.refs_4_), channel_id=1, source_target_pairs={{0,8},{2,10},{8,16},{10,18},{16,24},{18,26},{24,28},{26,30},{28,20... | collective-permute-start | bytes 442376 | tf_op jit(solution)/shard_map/ppermute | solution.py:1113
  345.2 6.7 %collective-permute-start.41 = (bf16[64,1024]{1,0:T(8,128)(2,1)S(1)}, bf16[64,1024]{1,0:T(8,128)(2,1)S(1)}, u32[]{:S(2)}, u32[]{:S(2)}) collective-permute-start(bf16[64,1024]{1,0:T(8,128)(2,1)S(1)} %get-tuple-element.154.refs_14_), channel_id=1, source_target_pairs={{0,8},{2,10},{8,16},{10,18},{16,24},{18,26},{24,28},{26,30},{28,20... | collective-permute-start | bytes 393224 | tf_op jit(solution)/shard_map/ppermute | solution.py:1113
  346.8 5.4 %collective-permute-start.42 = (bf16[64,1024]{1,0:T(8,128)(2,1)S(1)}, bf16[64,1024]{1,0:T(8,128)(2,1)S(1)}, u32[]{:S(2)}, u32[]{:S(2)}) collective-permute-start(bf16[64,1024]{1,0:T(8,128)(2,1)S(1)} %get-tuple-element.155.refs_15_), channel_id=1, source_target_pairs={{0,4},{2,6},{8,0},{10,2},{16,8},{18,10},{24,16},{26,18},{28,24},{3... | collective-permute-start | bytes 393224 | tf_op jit(solution)/shard_map/ppermute | solution.py:1113
  350.2 9.6 %collective-permute-start.39 = (bf16[64,2176]{1,0:T(8,128)(2,1)S(1)}, bf16[64,2176]{1,0:T(8,128)(2,1)S(1)}, u32[]{:S(2)}, u32[]{:S(2)}) collective-permute-start(bf16[64,2176]{1,0:T(8,128)(2,1)S(1)} %get-tuple-element.156.refs_10_), channel_id=1, source_target_pairs={{0,8},{2,10},{8,16},{10,18},{16,24},{18,26},{24,28},{26,30},{28,20... | collective-permute-start | bytes 835592 | tf_op jit(solution)/shard_map/ppermute | solution.py:1113
  351.9 7.9 %collective-permute-start.40 = (bf16[64,2176]{1,0:T(8,128)(2,1)S(1)}, bf16[64,2176]{1,0:T(8,128)(2,1)S(1)}, u32[]{:S(2)}, u32[]{:S(2)}) collective-permute-start(bf16[64,2176]{1,0:T(8,128)(2,1)S(1)} %get-tuple-element.157.refs_11_), channel_id=1, source_target_pairs={{0,4},{2,6},{8,0},{10,2},{16,8},{18,10},{24,16},{26,18},{28,24},{3... | collective-permute-start | bytes 835592 | tf_op jit(solution)/shard_map/ppermute | solution.py:1113
  353.5 9.7 %collective-permute-start.45 = (bf16[64,2048]{1,0:T(8,128)(2,1)S(1)}, bf16[64,2048]{1,0:T(8,128)(2,1)S(1)}, u32[]{:S(2)}, u32[]{:S(2)}) collective-permute-start(bf16[64,2048]{1,0:T(8,128)(2,1)S(1)} %get-tuple-element.158.refs_14_), channel_id=1, source_target_pairs={{0,8},{2,10},{8,16},{10,18},{16,24},{18,26},{24,28},{26,30},{28,20... | collective-permute-start | bytes 786440 | tf_op jit(solution)/shard_map/ppermute | solution.py:1113
  355.2 7.9 %collective-permute-start.46 = (bf16[64,2048]{1,0:T(8,128)(2,1)S(1)}, bf16[64,2048]{1,0:T(8,128)(2,1)S(1)}, u32[]{:S(2)}, u32[]{:S(2)}) collective-permute-start(bf16[64,2048]{1,0:T(8,128)(2,1)S(1)} %get-tuple-element.159.refs_15_), channel_id=1, source_target_pairs={{0,4},{2,6},{8,0},{10,2},{16,8},{18,10},{24,16},{26,18},{28,24},{3... | collective-permute-start | bytes 786440 | tf_op jit(solution)/shard_map/ppermute | solution.py:1113
  361.1 9.5 %collective-permute-start.43 = (bf16[64,2176]{1,0:T(8,128)(2,1)S(1)}, bf16[64,2176]{1,0:T(8,128)(2,1)S(1)}, u32[]{:S(2)}, u32[]{:S(2)}) collective-permute-start(bf16[64,2176]{1,0:T(8,128)(2,1)S(1)} %get-tuple-element.160.refs_10_), channel_id=1, source_target_pairs={{0,8},{2,10},{8,16},{10,18},{16,24},{18,26},{24,28},{26,30},{28,20... | collective-permute-start | bytes 835592 | tf_op jit(solution)/shard_map/ppermute | solution.py:1113
  362.7 9.6 %collective-permute-start.44 = (bf16[64,2176]{1,0:T(8,128)(2,1)S(1)}, bf16[64,2176]{1,0:T(8,128)(2,1)S(1)}, u32[]{:S(2)}, u32[]{:S(2)}) collective-permute-start(bf16[64,2176]{1,0:T(8,128)(2,1)S(1)} %get-tuple-element.161.refs_11_), channel_id=1, source_target_pairs={{0,4},{2,6},{8,0},{10,2},{16,8},{18,10},{24,16},{26,18},{28,24},{3... | collective-permute-start | bytes 835592 | tf_op jit(solution)/shard_map/ppermute | solution.py:1113
  364.4 11.8 %collective-permute-start.49 = (bf16[64,2048]{1,0:T(8,128)(2,1)S(1)}, bf16[64,2048]{1,0:T(8,128)(2,1)S(1)}, u32[]{:S(2)}, u32[]{:S(2)}) collective-permute-start(bf16[64,2048]{1,0:T(8,128)(2,1)S(1)} %get-tuple-element.162.refs_14_), channel_id=1, source_target_pairs={{0,8},{2,10},{8,16},{10,18},{16,24},{18,26},{24,28},{26,30},{28,20... | collective-permute-start | bytes 786440 | tf_op jit(solution)/shard_map/ppermute | solution.py:1113
  366.1 11.9 %collective-permute-start.50 = (bf16[64,2048]{1,0:T(8,128)(2,1)S(1)}, bf16[64,2048]{1,0:T(8,128)(2,1)S(1)}, u32[]{:S(2)}, u32[]{:S(2)}) collective-permute-start(bf16[64,2048]{1,0:T(8,128)(2,1)S(1)} %get-tuple-element.163.refs_15_), channel_id=1, source_target_pairs={{0,4},{2,6},{8,0},{10,2},{16,8},{18,10},{24,16},{26,18},{28,24},{3... | collective-permute-start | bytes 786440 | tf_op jit(solution)/shard_map/ppermute | solution.py:1113
  373.6 11.8 %collective-permute-start.47 = (bf16[64,2176]{1,0:T(8,128)(2,1)S(1)}, bf16[64,2176]{1,0:T(8,128)(2,1)S(1)}, u32[]{:S(2)}, u32[]{:S(2)}) collective-permute-start(bf16[64,2176]{1,0:T(8,128)(2,1)S(1)} %get-tuple-element.164.refs_10_), channel_id=1, source_target_pairs={{0,8},{2,10},{8,16},{10,18},{16,24},{18,26},{24,28},{26,30},{28,20... | collective-permute-start | bytes 835592 | tf_op jit(solution)/shard_map/ppermute | solution.py:1113
  375.2 6.1 %copy-start.13 = (bf16[688,1024]{1,0:T(8,128)(2,1)S(1)}, bf16[688,1024]{1,0:T(8,128)(2,1)}, u32[]{:S(2)}) copy-start(bf16[688,1024]{1,0:T(8,128)(2,1)} %get-tuple-element.113) | copy-start | bytes 4227076
  375.2 6.1 %copy-start.15 = (bf16[688,1024]{1,0:T(8,128)(2,1)S(1)}, bf16[688,1024]{1,0:T(8,128)(2,1)}, u32[]{:S(2)}) copy-start(bf16[688,1024]{1,0:T(8,128)(2,1)} %copy-done.14) | copy-start | bytes 4227076
  375.2 10.2 %collective-permute-start.48 = (bf16[64,2176]{1,0:T(8,128)(2,1)S(1)}, bf16[64,2176]{1,0:T(8,128)(2,1)S(1)}, u32[]{:S(2)}, u32[]{:S(2)}) collective-permute-start(bf16[64,2176]{1,0:T(8,128)(2,1)S(1)} %get-tuple-element.165.refs_11_), channel_id=1, source_target_pairs={{0,4},{2,6},{8,0},{10,2},{16,8},{18,10},{24,16},{26,18},{28,24},{3... | collective-permute-start | bytes 835592 | tf_op jit(solution)/shard_map/ppermute | solution.py:1113
  379.2 10.3 %collective-permute-start.51 = (bf16[64,2048]{1,0:T(8,128)(2,1)S(1)}, bf16[64,2048]{1,0:T(8,128)(2,1)S(1)}, u32[]{:S(2)}, u32[]{:S(2)}) collective-permute-start(bf16[64,2048]{1,0:T(8,128)(2,1)S(1)} %get-tuple-element.166), channel_id=1, source_target_pairs={{0,8},{2,10},{8,16},{10,18},{16,24},{18,26},{24,28},{26,30},{28,20... | collective-permute-start | bytes 786440 | tf_op jit(solution)/shard_map/ppermute | solution.py:1113
  380.8 8.7 %collective-permute-start.52 = (bf16[64,2048]{1,0:T(8,128)(2,1)S(1)}, bf16[64,2048]{1,0:T(8,128)(2,1)S(1)}, u32[]{:S(2)}, u32[]{:S(2)}) collective-permute-start(bf16[64,2048]{1,0:T(8,128)(2,1)S(1)} %get-tuple-element.167), channel_id=1, source_target_pairs={{0,4},{2,6},{8,0},{10,2},{16,8},{18,10},{24,16},{26,18},{28,24},{3... | collective-permute-start | bytes 786440 | tf_op jit(solution)/shard_map/ppermute | solution.py:1113
  386.5 13.1 %collective-permute-start.53 = (bf16[64,2176]{1,0:T(8,128)(2,1)S(1)}, bf16[64,2176]{1,0:T(8,128)(2,1)S(1)}, u32[]{:S(2)}, u32[]{:S(2)}) collective-permute-start(bf16[64,2176]{1,0:T(8,128)(2,1)S(1)} %ring_add.27.refs_6_.refs_0_), channel_id=1, source_target_pairs={{0,1},{1,0},{2,3},{3,2},{4,5},{5,4},{6,7},{7,6},{8,9},{9,8},{10,11... | collective-permute-start | bytes 835592 | tf_op jit(solution)/shard_map/ppermute | solution.py:1317
  390.6 9.1 %copy-start.9 = (s32[15]{0:T(128)S(1)}, s32[15]{0:T(128)}, u32[]{:S(2)}) copy-start(s32[15]{0:T(128)} %dynamic-slice_bitcast_fusion.place) | copy-start | bytes 184
  390.6 9.0 %collective-permute-start.54 = (bf16[64,2048]{1,0:T(8,128)(2,1)S(1)}, bf16[64,2048]{1,0:T(8,128)(2,1)S(1)}, u32[]{:S(2)}, u32[]{:S(2)}) collective-permute-start(bf16[64,2048]{1,0:T(8,128)(2,1)S(1)} %ring_add.29.refs_1_), channel_id=1, source_target_pairs={{0,1},{1,0},{2,3},{3,2},{4,5},{5,4},{6,7},{7,6},{8,9},{9,8},{10,11... | collective-permute-start | bytes 786440 | tf_op jit(solution)/shard_map/ppermute | solution.py:1317
  (16 other events, 31.3 us)
Sparse Core Ops, SparseCore 0:
  10.2 129.2 all-gather.1
